TPU v7x, 32 devices: a whole 2x2x4 slice. The times are simulated.
32 devices in a mesh: hid: 16 (over z, y, x), seq: 2 (over core).
Axes of the slice: x: 2, y: 2, z: 4, core: 2. Of those that a mesh axis runs over, the one named last changes fastest.
Arguments:
- pre_act: bfloat16 [192, 4096], P(('hid', 'seq')), may hold values from -6 to 6
- butterfly: bfloat16 [16, 5, 256, 256], P('hid'), may hold values from -0.15625 to 0.15625
- low_u: bfloat16 [4096, 256], P('hid'), may hold values from -0.75 to 0.75
- low_v: bfloat16 [256, 4096], P(None, 'hid'), may hold values from -0.1875 to 0.1875
- grad_out: bfloat16 [192, 4096], P(('hid', 'seq')), may hold values from -6 to 6
Outputs:
- output: bfloat16 [192, 4096], P(('hid', 'seq'))
- grad_pre: bfloat16 [192, 4096], P(('hid', 'seq'))
- grad_butterfly: float32 [16, 5, 256, 256], P('hid', None, 'seq')
- grad_low_u: float32 [4096, 256], P('hid', 'seq')
- grad_low_v: float32 [256, 4096], P('seq', 'hid')
All inputs are finite; a program needn't handle non-finite values.
Results may differ from a plain program's by a relative error of at most 0.0075.
Values may be sent and summed in bfloat16 or wider, within the bound.
No kernel may reach another device: no remote copies, remote signals or barrier semaphores. Data moves between devices by JAX's collectives and lax.ppermute only.
A program may use at most 64 MiB of HBM per device.

v0:
```python
import math

import jax
import jax.numpy as jnp
from jax import lax
from jax.sharding import PartitionSpec as P

LEVELS = 4


def swapped(x, axis, stride):
    return lax.ppermute(x, axis, [(i, i ^ 1 << stride) for i in range(lax.axis_size(axis))])


def gelu_tanh(value):
    return jax.nn.gelu(value, approximate=True)


def reduce_latent(partial_value):
    return lax.psum(partial_value, "hid").astype(jnp.bfloat16)


def inner_rows(left, right):
    return lax.dot_general(
        left, right, (((0,), (0,)), ((), ())), preferred_element_type=jnp.float32
    )


def on_device(pre_act, butterfly, low_u, low_v, grad_out):
    pre_f = pre_act.astype(jnp.float32)
    act_tok = gelu_tanh(pre_f).astype(jnp.bfloat16)
    act_rows = lax.all_to_all(act_tok, "hid", split_axis=1, concat_axis=0, tiled=True)
    partners = [act_rows]
    for level in range(LEVELS):
        partners.append(swapped(act_rows, "hid", level))
    latent = reduce_latent(jnp.dot(act_rows, low_u, preferred_element_type=jnp.float32))
    total = jnp.dot(latent, low_v, preferred_element_type=jnp.float32)
    for level in range(LEVELS + 1):
        total = total + jnp.dot(
            partners[level], butterfly[0, level], preferred_element_type=jnp.float32
        )
    output_rows = total.astype(jnp.bfloat16)
    output_tok = lax.all_to_all(output_rows, "hid", split_axis=0, concat_axis=1, tiled=True)
    grad_rows = lax.all_to_all(grad_out, "hid", split_axis=1, concat_axis=0, tiled=True)
    dlatent = reduce_latent(jnp.dot(grad_rows, low_v.T, preferred_element_type=jnp.float32))
    backward = jnp.dot(dlatent, low_u.T, preferred_element_type=jnp.float32)
    backward = backward + jnp.dot(grad_rows, butterfly[0, 0].T, preferred_element_type=jnp.float32)
    for level in range(1, LEVELS + 1):
        grad_far, weight_far = swapped((grad_rows, butterfly[0, level]), "hid", level - 1)
        backward = backward + jnp.dot(grad_far, weight_far.T, preferred_element_type=jnp.float32)
    grad_act = backward.astype(jnp.bfloat16)
    tokens_all = pre_act.shape[0] * lax.axis_size("hid") * lax.axis_size("seq")
    factor = 1.0 / math.sqrt(tokens_all)
    block_grads = jnp.stack(
        [inner_rows(partners[level], grad_rows) for level in range(LEVELS + 1)], axis=0
    )
    block_grads = block_grads[None] * factor
    low_u_grad = inner_rows(act_rows, dlatent) * factor
    low_v_grad = inner_rows(latent, grad_rows) * factor
    grad_butterfly, grad_low_u, grad_low_v = (
        lax.psum_scatter(
            block_grads.astype(jnp.bfloat16), "seq", scatter_dimension=2, tiled=True
        ).astype(jnp.float32),
        lax.psum_scatter(
            low_u_grad.astype(jnp.bfloat16), "seq", scatter_dimension=1, tiled=True
        ).astype(jnp.float32),
        lax.psum_scatter(
            low_v_grad.astype(jnp.bfloat16), "seq", scatter_dimension=0, tiled=True
        ).astype(jnp.float32),
    )
    grad_act_tok = lax.all_to_all(grad_act, "hid", split_axis=0, concat_axis=1, tiled=True)
    unused, pullback = jax.vjp(gelu_tanh, pre_f)
    grad_pre = pullback(grad_act_tok.astype(jnp.float32))[0].astype(jnp.bfloat16)
    return (output_tok, grad_pre, grad_butterfly, grad_low_u, grad_low_v)


def solution(mesh):
    in_specs = (
        P(("hid", "seq"), None),
        P("hid", None, None, None),
        P("hid", None),
        P(None, "hid"),
        P(("hid", "seq"), None),
    )
    out_specs = (
        P(("hid", "seq"), None),
        P(("hid", "seq"), None),
        P("hid", None, "seq", None),
        P("hid", "seq"),
        P("seq", "hid"),
    )
    return jax.shard_map(
        on_device, mesh=mesh, in_specs=in_specs, out_specs=out_specs, check_vma=False
    )
```

profile of v0, /device:TPU:0, one launch (start us, length us, event | category | flops | bytes accessed | tf_op | source)
XLA Modules:
  0.0 169.8 jit_solution(16581253652692597492)
XLA Ops:
  7.2 8.5 %all-to-all-start.2 = ((bf16[6,16,256]{2,0,1:T(8,128)(2,1)}), bf16[6,16,256]{2,0,1:T(8,128)(2,1)S(1)}, u32[]{:S(2)}, u32[]{:S(2)}) async-start(bf16[6,16,256]{2,0,1:T(8,128)(2,1)} %bitcast.96), calls=%async_computation.2 | async-start | bytes 131072 | tf_op jit(solution)/shard_map/all_to_all | solution.py:44
  15.7 1.2 slice_bitcast_fusion.3
  16.9 2.0 %collective-permute-start.7 = (bf16[256,256]{1,0:T(8,128)(2,1)S(1)}, bf16[256,256]{1,0:T(8,128)(2,1)S(1)}, u32[]{:S(2)}, u32[]{:S(2)}) collective-permute-start(bf16[256,256]{1,0:T(8,128)(2,1)S(1)} %get-tuple-element.8), channel_id=1, source_target_pairs={{0,4},{2,6},{4,0},{6,2},{8,12},{10,14},{12,8},{14,10},{16,20},{18,... | collective-permute-start | bytes 393224 | tf_op jit(solution)/shard_map/ppermute | solution.py:12
  18.9 1.5 collective-permute-start.9
  20.3 2.4 %collective-permute-start.11 = (bf16[256,256]{1,0:T(8,128)(2,1)S(1)}, bf16[256,256]{1,0:T(8,128)(2,1)S(1)}, u32[]{:S(2)}, u32[]{:S(2)}) collective-permute-start(bf16[256,256]{1,0:T(8,128)(2,1)S(1)} %get-tuple-element.9), channel_id=1, source_target_pairs={{0,16},{2,18},{4,20},{6,22},{8,24},{10,26},{12,28},{14,30},{16,0},... | collective-permute-start | bytes 393224 | tf_op jit(solution)/shard_map/ppermute | solution.py:12
  22.7 1.5 collective-permute-start.5
  24.1 1.5 fusion.22
  25.7 3.5 %all-to-all-start = ((bf16[6,16,256]{2,0,1:T(8,128)(2,1)}), bf16[6,16,256]{2,0,1:T(8,128)(2,1)S(1)}, u32[]{:S(2)}, u32[]{:S(2)}) async-start(bf16[6,16,256]{2,0,1:T(8,128)(2,1)} %bitcast), calls=%async_computation | async-start | bytes 131072 | tf_op jit(solution)/shard_map/all_to_all | solution.py:32
  29.2 0.0 reduce-scatter.10.cloned.1.call-start
  29.3 0.2 fusion.43
  29.4 7.4 %all-to-all-done = bf16[6,16,256]{2,0,1:T(8,128)(2,1)S(1)} async-done(((bf16[6,16,256]{2,0,1:T(8,128)(2,1)}), bf16[6,16,256]{2,0,1:T(8,128)(2,1)S(1)}, u32[]{:S(2)}, u32[]{:S(2)}) %all-to-all-start) | async-done | bytes 49184 | tf_op jit(solution)/shard_map/all_to_all | solution.py:32
  36.8 0.8 collective-permute-start
  37.6 0.1 fusion.42
  37.7 75.0 %all-reduce.2 = (bf16[96,256]{1,0:T(8,128)(2,1)S(1)}, bf16[96,256]{1,0:T(8,128)(2,1)S(1)}) all-reduce(f32[96,256]{1,0:T(8,128)S(1)} %fusion.42, f32[96,256]{1,0:T(8,128)S(1)} %fusion.43), channel_id=1, replica_groups=mesh['hid'=16,'seq'=2] {'hid'}, use_global_device_ids=true, to_apply=%region_0.0 | all-reduce | flops 49152 | bytes 294912 | tf_op jit(solution)/shard_map/psum | solution.py:20
  112.8 0.2 fusion.47
  112.9 0.2 fusion.5
  113.2 0.2 convolution_add_fusion.1
  113.4 0.1 fusion.48
  113.5 0.8 copy.18
  114.3 0.0 reduce-scatter.10.cloned.1.call-update
  114.3 0.0 reduce-scatter.8.cloned.1.call-start
  114.4 0.9 fusion.6
  115.2 0.2 convolution_add_fusion.3
  115.4 0.0 reduce-scatter.8.cloned.1.call-update
  115.4 0.2 fusion.4
  115.7 0.1 collective-permute-start.1
  115.7 0.2 fusion.3
  115.9 3.9 %collective-permute-done.1 = bf16[96,256]{1,0:T(8,128)(2,1)S(1)} collective-permute-done((bf16[96,256]{1,0:T(8,128)(2,1)S(1)}, bf16[96,256]{1,0:T(8,128)(2,1)S(1)}, u32[]{:S(2)}, u32[]{:S(2)}) %collective-permute-start.1) | collective-permute-done | bytes 49184 | tf_op jit(solution)/shard_map/ppermute | solution.py:12
  119.8 0.2 fusion.2
  120.0 3.9 %collective-permute-done.2 = bf16[96,256]{1,0:T(8,128)(2,1)S(1)} collective-permute-done((bf16[96,256]{1,0:T(8,128)(2,1)S(1)}, bf16[96,256]{1,0:T(8,128)(2,1)S(1)}, u32[]{:S(2)}, u32[]{:S(2)}) %collective-permute-start.2) | collective-permute-done | bytes 49184 | tf_op jit(solution)/shard_map/ppermute | solution.py:12
  123.9 0.2 fusion.1
  124.1 4.8 %collective-permute-done.3 = bf16[96,256]{1,0:T(8,128)(2,1)S(1)} collective-permute-done((bf16[96,256]{1,0:T(8,128)(2,1)S(1)}, bf16[96,256]{1,0:T(8,128)(2,1)S(1)}, u32[]{:S(2)}, u32[]{:S(2)}) %collective-permute-start.3) | collective-permute-done | bytes 49184 | tf_op jit(solution)/shard_map/ppermute | solution.py:12
  128.9 0.2 collective-permute-start.6
  129.1 0.2 fusion
  129.3 1.0 multiply_convert_fusion
  130.3 0.1 fusion.39
  130.4 0.2 fusion.40
  130.6 0.2 fusion.41
  130.7 0.2 fusion.14
  130.9 0.7 all_to_all.56
  131.6 3.5 %all-to-all-start.1 = ((bf16[16,6,256]{2,1,0:T(8,128)(2,1)}), bf16[16,6,256]{2,1,0:T(8,128)(2,1)S(1)}, u32[]{:S(2)}, u32[]{:S(2)}) async-start(bf16[16,6,256]{2,1,0:T(8,128)(2,1)} %all_to_all.56), calls=%async_computation.1 | async-start | bytes 131072 | tf_op jit(solution)/shard_map/all_to_all | solution.py:43
  135.1 0.0 reduce-scatter.6.cloned.1.call-start
  135.1 0.7 reduce-scatter.6.cloned.1.call-update
  135.8 1.9 %collective-permute-start.8 = (bf16[96,256]{1,0:T(8,128)(2,1)S(1)}, bf16[96,256]{1,0:T(8,128)(2,1)S(1)}, u32[]{:S(2)}, u32[]{:S(2)}) collective-permute-start(bf16[96,256]{1,0:T(8,128)(2,1)S(1)} %all_to_all.63), channel_id=1, source_target_pairs={{0,8},{2,10},{4,12},{6,14},{8,0},{10,2},{12,4},{14,6},{16,24},{18,... | collective-permute-start | bytes 147464 | tf_op jit(solution)/shard_map/ppermute | solution.py:12
  137.7 2.4 %collective-permute-start.10 = (bf16[96,256]{1,0:T(8,128)(2,1)S(1)}, bf16[96,256]{1,0:T(8,128)(2,1)S(1)}, u32[]{:S(2)}, u32[]{:S(2)}) collective-permute-start(bf16[96,256]{1,0:T(8,128)(2,1)S(1)} %all_to_all.63), channel_id=1, source_target_pairs={{0,16},{2,18},{4,20},{6,22},{8,24},{10,26},{12,28},{14,30},{16,0},... | collective-permute-start | bytes 147464 | tf_op jit(solution)/shard_map/ppermute | solution.py:12
  140.1 0.2 fusion.44
  140.3 0.0 collective-permute-done.9
  140.3 1.5 collective-permute-start.4
  141.9 0.2 fusion.45
  142.0 0.0 collective-permute-done.11
  142.1 1.2 collective-permute-done.10
  143.2 0.2 fusion.46
  143.4 0.0 collective-permute-done.5
  143.4 1.1 collective-permute-done.4
  144.5 0.2 fusion.13
  144.7 0.7 all_to_all.64
  145.3 4.0 %all-to-all-start.3 = ((bf16[16,6,256]{2,1,0:T(8,128)(2,1)}), bf16[16,6,256]{2,1,0:T(8,128)(2,1)S(1)}, u32[]{:S(2)}, u32[]{:S(2)}) async-start(bf16[16,6,256]{2,1,0:T(8,128)(2,1)} %all_to_all.64), calls=%async_computation.3 | async-start | bytes 131072 | tf_op jit(solution)/shard_map/all_to_all | solution.py:71
  149.4 7.5 %all-to-all-done.3 = bf16[16,6,256]{2,1,0:T(8,128)(2,1)S(1)} async-done(((bf16[16,6,256]{2,1,0:T(8,128)(2,1)}), bf16[16,6,256]{2,1,0:T(8,128)(2,1)S(1)}, u32[]{:S(2)}, u32[]{:S(2)}) %all-to-all-start.3) | async-done | bytes 49184 | tf_op jit(solution)/shard_map/all_to_all | solution.py:71
  157.0 0.7 fusion.18
  157.7 0.9 copy.19
  158.6 0.7 convert_element_type.69
  159.3 1.5 convert_element_type.71
  160.8 1.9 %convert_element_type.67 = f32[1,5,128,256]{3,2,1,0:T(8,128)} convert(bf16[1,5,128,256]{3,2,1,0:T(8,128)(2,1)} %reduce-scatter.6.cloned.1.call-done) | non-fusion elementwise | flops 163840 | bytes 983040 | tf_op jit(solution)/shard_map/convert_element_type | solution.py:63
  162.7 0.6 copy.37
  (22 shorter events, 0.1 us)
Async XLA Ops:
  7.2 30.4 %copy-start = (bf16[256,256]{1,0:T(8,128)(2,1)S(1)}, bf16[256,256]{1,0:T(8,128)(2,1)}, u32[]{:S(2)}) copy-start(bf16[256,256]{1,0:T(8,128)(2,1)} %param.7) | copy-start | bytes 393220
  7.2 22.1 %copy-start.2 = (bf16[256,256]{1,0:T(8,128)(2,1)S(1)}, bf16[256,256]{1,0:T(8,128)(2,1)}, u32[]{:S(2)}) copy-start(bf16[256,256]{1,0:T(8,128)(2,1)} %param.8) | copy-start | bytes 393220
  7.2 18.5 %all-to-all-start.2 = ((bf16[6,16,256]{2,0,1:T(8,128)(2,1)}), bf16[6,16,256]{2,0,1:T(8,128)(2,1)S(1)}, u32[]{:S(2)}, u32[]{:S(2)}) async-start(bf16[6,16,256]{2,0,1:T(8,128)(2,1)} %bitcast.96), calls=%async_computation.2 | async-start | bytes 131072 | tf_op jit(solution)/shard_map/all_to_all | solution.py:44
  15.7 97.5 %copy-start.1 = (bf16[1,5,256,256]{3,2,1,0:T(8,128)(2,1)S(1)}, bf16[1,5,256,256]{3,2,1,0:T(8,128)(2,1)}, u32[]{:S(2)}) copy-start(bf16[1,5,256,256]{3,2,1,0:T(8,128)(2,1)} %param.6) | copy-start | bytes 1966084
  16.9 119.0 %collective-permute-start.7 = (bf16[256,256]{1,0:T(8,128)(2,1)S(1)}, bf16[256,256]{1,0:T(8,128)(2,1)S(1)}, u32[]{:S(2)}, u32[]{:S(2)}) collective-permute-start(bf16[256,256]{1,0:T(8,128)(2,1)S(1)} %get-tuple-element.8), channel_id=1, source_target_pairs={{0,4},{2,6},{4,0},{6,2},{8,12},{10,14},{12,8},{14,10},{16,20},{18,... | collective-permute-start | bytes 393224 | tf_op jit(solution)/shard_map/ppermute | solution.py:12
  18.9 121.5 %collective-permute-start.9 = (bf16[256,256]{1,0:T(8,128)(2,1)S(1)}, bf16[256,256]{1,0:T(8,128)(2,1)S(1)}, u32[]{:S(2)}, u32[]{:S(2)}) collective-permute-start(bf16[256,256]{1,0:T(8,128)(2,1)S(1)} %get-tuple-element.10), channel_id=1, source_target_pairs={{0,8},{2,10},{4,12},{6,14},{8,0},{10,2},{12,4},{14,6},{16,24},{18,... | collective-permute-start | bytes 393224 | tf_op jit(solution)/shard_map/ppermute | solution.py:12
  20.3 121.7 %collective-permute-start.11 = (bf16[256,256]{1,0:T(8,128)(2,1)S(1)}, bf16[256,256]{1,0:T(8,128)(2,1)S(1)}, u32[]{:S(2)}, u32[]{:S(2)}) collective-permute-start(bf16[256,256]{1,0:T(8,128)(2,1)S(1)} %get-tuple-element.9), channel_id=1, source_target_pairs={{0,16},{2,18},{4,20},{6,22},{8,24},{10,26},{12,28},{14,30},{16,0},... | collective-permute-start | bytes 393224 | tf_op jit(solution)/shard_map/ppermute | solution.py:12
  22.7 120.7 %collective-permute-start.5 = (bf16[256,256]{1,0:T(8,128)(2,1)S(1)}, bf16[256,256]{1,0:T(8,128)(2,1)S(1)}, u32[]{:S(2)}, u32[]{:S(2)}) collective-permute-start(bf16[256,256]{1,0:T(8,128)(2,1)S(1)} %get-tuple-element.7), channel_id=1, source_target_pairs={{0,2},{2,0},{4,6},{6,4},{8,10},{10,8},{12,14},{14,12},{16,18},{18,... | collective-permute-start | bytes 393224 | tf_op jit(solution)/shard_map/ppermute | solution.py:12
  25.7 11.1 %all-to-all-start = ((bf16[6,16,256]{2,0,1:T(8,128)(2,1)}), bf16[6,16,256]{2,0,1:T(8,128)(2,1)S(1)}, u32[]{:S(2)}, u32[]{:S(2)}) async-start(bf16[6,16,256]{2,0,1:T(8,128)(2,1)} %bitcast), calls=%async_computation | async-start | bytes 131072 | tf_op jit(solution)/shard_map/all_to_all | solution.py:32
  29.2 128.5 %reduce-scatter.10.cloned.1.call-start = ((), (), s32[]{:S(2)}) async-start(), calls=%async_computation.9 | async-start | bytes 196608
  36.8 78.8 %collective-permute-start = (bf16[96,256]{1,0:T(8,128)(2,1)S(1)}, bf16[96,256]{1,0:T(8,128)(2,1)S(1)}, u32[]{:S(2)}, u32[]{:S(2)}) collective-permute-start(bf16[96,256]{1,0:T(8,128)(2,1)S(1)} %all_to_all.55), channel_id=1, source_target_pairs={{0,2},{2,0},{4,6},{6,4},{8,10},{10,8},{12,14},{14,12},{16,18},{18,... | collective-permute-start | bytes 147464 | tf_op jit(solution)/shard_map/ppermute | solution.py:12
  114.3 45.0 %reduce-scatter.8.cloned.1.call-start = ((), (), s32[]{:S(2)}) async-start(), calls=%async_computation.8 | async-start | bytes 196608 | tf_op jit(solution)/shard_map/reduce_scatter | solution.py:67
  115.7 4.2 %collective-permute-start.1 = (bf16[96,256]{1,0:T(8,128)(2,1)S(1)}, bf16[96,256]{1,0:T(8,128)(2,1)S(1)}, u32[]{:S(2)}, u32[]{:S(2)}) collective-permute-start(bf16[96,256]{1,0:T(8,128)(2,1)S(1)} %all_to_all.55), channel_id=1, source_target_pairs={{0,4},{2,6},{4,0},{6,2},{8,12},{10,14},{12,8},{14,10},{16,20},{18,... | collective-permute-start | bytes 147464 | tf_op jit(solution)/shard_map/ppermute | solution.py:12
  119.8 4.1 %collective-permute-start.2 = (bf16[96,256]{1,0:T(8,128)(2,1)S(1)}, bf16[96,256]{1,0:T(8,128)(2,1)S(1)}, u32[]{:S(2)}, u32[]{:S(2)}) collective-permute-start(bf16[96,256]{1,0:T(8,128)(2,1)S(1)} %all_to_all.55), channel_id=1, source_target_pairs={{0,8},{2,10},{4,12},{6,14},{8,0},{10,2},{12,4},{14,6},{16,24},{18,... | collective-permute-start | bytes 147464 | tf_op jit(solution)/shard_map/ppermute | solution.py:12
  123.9 5.0 %collective-permute-start.3 = (bf16[96,256]{1,0:T(8,128)(2,1)S(1)}, bf16[96,256]{1,0:T(8,128)(2,1)S(1)}, u32[]{:S(2)}, u32[]{:S(2)}) collective-permute-start(bf16[96,256]{1,0:T(8,128)(2,1)S(1)} %all_to_all.55), channel_id=1, source_target_pairs={{0,16},{2,18},{4,20},{6,22},{8,24},{10,26},{12,28},{14,30},{16,0},... | collective-permute-start | bytes 147464 | tf_op jit(solution)/shard_map/ppermute | solution.py:12
  128.9 8.8 %collective-permute-start.6 = (bf16[96,256]{1,0:T(8,128)(2,1)S(1)}, bf16[96,256]{1,0:T(8,128)(2,1)S(1)}, u32[]{:S(2)}, u32[]{:S(2)}) collective-permute-start(bf16[96,256]{1,0:T(8,128)(2,1)S(1)} %all_to_all.63), channel_id=1, source_target_pairs={{0,4},{2,6},{4,0},{6,2},{8,12},{10,14},{12,8},{14,10},{16,20},{18,... | collective-permute-start | bytes 147464 | tf_op jit(solution)/shard_map/ppermute | solution.py:12
  131.6 13.8 %all-to-all-start.1 = ((bf16[16,6,256]{2,1,0:T(8,128)(2,1)}), bf16[16,6,256]{2,1,0:T(8,128)(2,1)S(1)}, u32[]{:S(2)}, u32[]{:S(2)}) async-start(bf16[16,6,256]{2,1,0:T(8,128)(2,1)} %all_to_all.56), calls=%async_computation.1 | async-start | bytes 131072 | tf_op jit(solution)/shard_map/all_to_all | solution.py:43
  135.1 21.9 %copy-start.3 = (bf16[6,4096]{1,0:T(8,128)(2,1)S(1)}, bf16[6,4096]{1,0:T(8,128)(2,1)}, u32[]{:S(2)}) copy-start(bf16[6,4096]{1,0:T(8,128)(2,1)} %param.5) | copy-start | bytes 147460
  135.1 25.7 %reduce-scatter.6.cloned.1.call-start = ((), (), s32[]{:S(2)}) async-start(), calls=%async_computation.7 | async-start | bytes 983040 | tf_op jit(solution)/shard_map/reduce_scatter | solution.py:61
  135.8 6.0 %collective-permute-start.8 = (bf16[96,256]{1,0:T(8,128)(2,1)S(1)}, bf16[96,256]{1,0:T(8,128)(2,1)S(1)}, u32[]{:S(2)}, u32[]{:S(2)}) collective-permute-start(bf16[96,256]{1,0:T(8,128)(2,1)S(1)} %all_to_all.63), channel_id=1, source_target_pairs={{0,8},{2,10},{4,12},{6,14},{8,0},{10,2},{12,4},{14,6},{16,24},{18,... | collective-permute-start | bytes 147464 | tf_op jit(solution)/shard_map/ppermute | solution.py:12
  137.7 5.5 %collective-permute-start.10 = (bf16[96,256]{1,0:T(8,128)(2,1)S(1)}, bf16[96,256]{1,0:T(8,128)(2,1)S(1)}, u32[]{:S(2)}, u32[]{:S(2)}) collective-permute-start(bf16[96,256]{1,0:T(8,128)(2,1)S(1)} %all_to_all.63), channel_id=1, source_target_pairs={{0,16},{2,18},{4,20},{6,22},{8,24},{10,26},{12,28},{14,30},{16,0},... | collective-permute-start | bytes 147464 | tf_op jit(solution)/shard_map/ppermute | solution.py:12
  140.3 4.2 %collective-permute-start.4 = (bf16[96,256]{1,0:T(8,128)(2,1)S(1)}, bf16[96,256]{1,0:T(8,128)(2,1)S(1)}, u32[]{:S(2)}, u32[]{:S(2)}) collective-permute-start(bf16[96,256]{1,0:T(8,128)(2,1)S(1)} %all_to_all.63), channel_id=1, source_target_pairs={{0,2},{2,0},{4,6},{6,4},{8,10},{10,8},{12,14},{14,12},{16,18},{18,... | collective-permute-start | bytes 147464 | tf_op jit(solution)/shard_map/ppermute | solution.py:12
  145.3 11.6 %all-to-all-start.3 = ((bf16[16,6,256]{2,1,0:T(8,128)(2,1)}), bf16[16,6,256]{2,1,0:T(8,128)(2,1)S(1)}, u32[]{:S(2)}, u32[]{:S(2)}) async-start(bf16[16,6,256]{2,1,0:T(8,128)(2,1)} %all_to_all.64), calls=%async_computation.3 | async-start | bytes 131072 | tf_op jit(solution)/shard_map/all_to_all | solution.py:71
Sparse Core Ops, SparseCore 0:
  114.5 3.8 reduce-scatter.9
  120.6 8.6 reduce-scatter.7
  138.7 9.3 reduce-scatter.5
where the time goes:
time: 170 us
  blocking collectives  75 us (44%)
  starting transfers between devices  33.8 us (20%)
  waiting for transfers between devices  30.5 us (18%)
  between operations  14 us (8%)
  other arithmetic  7.27 us (4%)
  local copies, waits for them, and re-layouts  4.92 us (3%)
  matrix products  4.36 us (3%)
    psum x1, blocking collectives, reduce_latent(): return lax.psum(partial_value, 'hid').astype(jnp.bfloat16)  75 us
    ppermute x12, waiting for transfers between devices, swapped(): lax.ppermute(x, axis, [(i, i ^ 1 << stride) for i in range(lax.axis_size(...  14.9 us
    ppermute x12, starting transfers between devices, swapped(): lax.ppermute(x, axis, [(i, i ^ 1 << stride) for i in range(lax.axis_size(...  14.2 us
    all_to_all x1, starting transfers between devices, on_device(): lax.all_to_all(grad_out, 'hid', split_axis=1, concat_axis=0, tiled=True)  8.46 us
    all_to_all x1, waiting for transfers between devices, on_device(): lax.all_to_all(grad_act, 'hid', split_axis=0, concat_axis=1, tiled=True)  7.53 us
    all_to_all x1, waiting for transfers between devices, on_device(): lax.all_to_all(act_tok, 'hid', split_axis=1, concat_axis=0, tiled=True)  7.35 us
    all_to_all x1, starting transfers between devices, on_device(): lax.all_to_all(grad_act, 'hid', split_axis=0, concat_axis=1, tiled=True)  4.05 us
    convert_element_type x3, other arithmetic, on_device(): grad_butterfly, grad_low_u, grad_low_v = (lax.psum_scatter(block_grads.as...  4.04 us
  transfers between devices with their start and end apart: 19, of which 7 were waited for; matrix products, arithmetic and copies ran while one was open for 7% of the time, Pallas kernels for 0%

commit v1 on v0

v1 whole, which is shorter than its diff:
```python
import math

import jax
import jax.numpy as jnp
from jax import lax
from jax.sharding import PartitionSpec as P


def exchange(x, mask):
    return lax.ppermute(x, "hid", [(i, i ^ mask) for i in range(lax.axis_size("hid"))])


def mate(x):
    return lax.ppermute(x, "seq", [(0, 1), (1, 0)])


def gelu_tanh(value):
    return jax.nn.gelu(value, approximate=True)


def dot(left, right):
    return jnp.dot(left, right, preferred_element_type=jnp.float32)


def dot_t(left, right):
    return lax.dot_general(
        left, right, (((1,), (1,)), ((), ())), preferred_element_type=jnp.float32
    )


def inner_rows(left, right):
    return lax.dot_general(
        left, right, (((0,), (0,)), ((), ())), preferred_element_type=jnp.float32
    )


def sum_over_hid(part):
    bits = (lax.axis_size("hid") - 1).bit_length()
    total = part
    for low in range(0, bits, 2):
        sent = total.astype(jnp.bfloat16)
        masks = [1 << low]
        if low + 1 < bits:
            masks += [2 << low, 3 << low]
        total = total + sum(exchange(sent, mask).astype(jnp.float32) for mask in masks)
    return total.astype(jnp.bfloat16)


def half(x, which):
    width = x.shape[1] // 2
    return jnp.where(which == 0, x[:, :width], x[:, width:])


def on_device(pre_act, butterfly, low_u, low_v, grad_out):
    tokens = pre_act.shape[0]
    hid = lax.axis_size("hid")
    core = lax.axis_index("seq")
    side = butterfly.shape[-1]
    levels = butterfly.shape[1] - 1
    rank = low_u.shape[1]
    factor = 1.0 / math.sqrt(tokens * hid * lax.axis_size("seq"))

    both = jnp.concatenate(
        [pre_act.reshape(tokens, hid, side), grad_out.reshape(tokens, hid, side)], axis=2
    ).reshape(tokens, hid * 2 * side)
    rows = lax.all_to_all(both, "hid", split_axis=1, concat_axis=0, tiled=True)
    pre_f = rows[:, :side].astype(jnp.float32)
    grad = rows[:, side:]
    act_f, pullback = jax.vjp(gelu_tanh, pre_f)
    act = act_f.astype(jnp.bfloat16)

    latents = sum_over_hid(jnp.concatenate([dot(act, low_u), dot_t(grad, low_v)], axis=1))
    latent, dlatent = latents[:, :rank], latents[:, rank:]

    acts = [act]
    total = dot(act, butterfly[0, 0])
    back = dot_t(grad, butterfly[0, 0])
    for level in range(1, levels + 1):
        term = dot_t(grad, butterfly[0, level]).astype(jnp.bfloat16)
        far = exchange(jnp.concatenate([act, term], axis=1), 1 << level - 1)
        acts.append(far[:, :side])
        total = total + dot(far[:, :side], butterfly[0, level])
        back = back + far[:, side:].astype(jnp.float32)

    output_rows = (total + dot(latent, low_v)).astype(jnp.bfloat16)
    grad_act = (back + dot_t(dlatent, low_u)).astype(jnp.bfloat16)
    grad_pre_rows = pullback(grad_act.astype(jnp.float32))[0].astype(jnp.bfloat16)
    results = jnp.concatenate([output_rows, grad_pre_rows], axis=1)
    results = lax.all_to_all(results, "hid", split_axis=0, concat_axis=1, tiled=True)
    results = results.reshape(tokens, hid, 2 * side)
    output = results[:, :, :side].reshape(tokens, hid * side)
    grad_pre = results[:, :, side:].reshape(tokens, hid * side)

    other = 1 - core
    sent = jnp.concatenate(
        [grad, act] + [half(x, other) for x in acts[1:]], axis=1
    )
    got = mate(sent)
    own = jnp.concatenate([half(x, core) for x in acts], axis=1)
    far = jnp.concatenate(
        [half(got[:, side : 2 * side], core), got[:, 2 * side :]], axis=1
    )
    grad_butterfly = (inner_rows(own, grad) + inner_rows(far, got[:, :side])) * factor
    grad_butterfly = grad_butterfly.reshape(1, levels + 1, side // 2, side)
    far_latents = mate(jnp.concatenate([half(latent, other), half(dlatent, other)], axis=1))
    far_latent, far_dlatent = far_latents[:, : rank // 2], far_latents[:, rank // 2 :]
    grad_low_u = (
        inner_rows(act, half(dlatent, core)) + inner_rows(got[:, side : 2 * side], far_dlatent)
    ) * factor
    grad_low_v = (
        inner_rows(half(latent, core), grad) + inner_rows(far_latent, got[:, :side])
    ) * factor
    return (output, grad_pre, grad_butterfly, grad_low_u, grad_low_v)


def solution(mesh):
    in_specs = (
        P(("hid", "seq"), None),
        P("hid", None, None, None),
        P("hid", None),
        P(None, "hid"),
        P(("hid", "seq"), None),
    )
    out_specs = (
        P(("hid", "seq"), None),
        P(("hid", "seq"), None),
        P("hid", None, "seq", None),
        P("hid", "seq"),
        P("seq", "hid"),
    )
    return jax.shard_map(
        on_device, mesh=mesh, in_specs=in_specs, out_specs=out_specs, check_vma=False
    )
```

time: 170 us -> 52.9 us (0.31)
  blocking collectives: 75 us -> 0 us
  waiting for transfers between devices: 30.5 us -> 16.6 us
  between operations: 14 us -> 1.02 us
  starting transfers between devices: 33.8 us -> 25.6 us
  other arithmetic: 7.27 us -> 2 us
  local copies, waits for them, and re-layouts: 4.92 us -> 1.43 us
    psum x1 -> x0, blocking collectives: 75 us -> none  [reduce_latent(): return lax.psum(partial_value, 'hid').astype(jnp.bfloat16)]
    ppermute x12, waiting for transfers between devices: 14.9 us -> 4.52 us  [the longest x10 4.51 us: exchange(): lax.ppermute(x, 'hid', [(i, i ^ mask) for i in range(lax.axis_size('hid'))])]
    convert_element_type x7 -> x4, other arithmetic: 7.27 us -> 0.19 us  [the longest x1 0.09 us: sum_over_hid(): return total.astype(jnp.bfloat16)]
    all_to_all x4 -> x2, starting transfers between devices: 19.5 us -> 12.9 us  [the longest x1 8.44 us: on_device(): rows = lax.all_to_all(both, 'hid', split_axis=1, concat_axis=0, tiled=True)]
    all_to_all x4 -> x2, waiting for transfers between devices: 14.9 us -> 12.1 us  [the longest x1 7.78 us: on_device(): rows = lax.all_to_all(both, 'hid', split_axis=1, concat_axis=0, tiled=True)]
    unnamed x11 -> x7, local copies, waits for them, and re-layouts: 2.38 us -> 0.05 us
    dot_general x7 -> x6, matrix products: 2.11 us -> 3.54 us  [inner_rows(): lax.dot_general(left, right, (((0,), (0,)), ((), ())), preferred_element_...]
  transfers between devices with their start and end apart: 19 -> 14, of which waited for: 7 -> 5; matrix products, arithmetic and copies ran while one was open for 7% -> 11% of each run, Pallas kernels for 0% -> 0%
where the time goes in v1:
time: 52.9 us; the launch traced here: 52.6 us
  starting transfers between devices  25.6 us (48%)
  waiting for transfers between devices  16.6 us (31%)
  matrix products  5.87 us (11%)
  other arithmetic  2 us (4%)
  local copies, waits for them, and re-layouts  1.43 us (3%)
  between operations  1.02 us (2%)
    ppermute x10, starting transfers between devices, exchange(): lax.ppermute(x, 'hid', [(i, i ^ mask) for i in range(lax.axis_size('hid'))])  12.6 us
    all_to_all x1, starting transfers between devices, on_device(): rows = lax.all_to_all(both, 'hid', split_axis=1, concat_axis=0, tiled=True)  8.44 us
    all_to_all x1, waiting for transfers between devices, on_device(): rows = lax.all_to_all(both, 'hid', split_axis=1, concat_axis=0, tiled=True)  7.78 us
    ppermute x10, waiting for transfers between devices, exchange(): lax.ppermute(x, 'hid', [(i, i ^ mask) for i in range(lax.axis_size('hid'))])  4.51 us
    all_to_all x1, starting transfers between devices, on_device(): lax.all_to_all(results, 'hid', split_axis=0, concat_axis=1, tiled=True)  4.41 us
    all_to_all x1, waiting for transfers between devices, on_device(): lax.all_to_all(results, 'hid', split_axis=0, concat_axis=1, tiled=True)  4.35 us
    dot_general x6, matrix products, inner_rows(): lax.dot_general(left, right, (((0,), (0,)), ((), ())), preferred_element_...  3.54 us
    concatenate x1, other arithmetic, on_device(): jnp.concatenate([pre_act.reshape(tokens, hid, side), grad_out.reshape(tok...  1.59 us
  transfers between devices with their start and end apart: 14, of which 5 were waited for; matrix products, arithmetic and copies ran while one was open for 11% of the time, Pallas kernels for 0%

profile of v1, /device:TPU:0, one launch (start us, length us, event | category | flops | bytes accessed | tf_op | source)
XLA Modules:
  0.0 52.6 jit_solution(6170507459105208117)
XLA Ops:
  0.6 0.0 copy-start
  0.6 1.6 %pad_maximum_fusion.5 = bf16[6,16,512]{2,0,1:T(8,128)(2,1)} fusion(bf16[6,16,256]{2,0,1:T(8,128)(2,1)} %bitcast.40, bf16[6,16,256]{2,0,1:T(8,128)(2,1)} %bitcast.41), kind=kLoop, calls=%fused_computation.30 | loop fusion | flops 196608 | bytes 196608 | tf_op jit(solution)/shard_map/concatenate | solution.py:63
  2.2 0.0 copy-start.2
  2.2 8.4 %all-to-all-start = ((bf16[6,16,512]{2,0,1:T(8,128)(2,1)}), bf16[6,16,512]{2,0,1:T(8,128)(2,1)S(1)}, u32[]{:S(2)}, u32[]{:S(2)}) async-start(bf16[6,16,512]{2,0,1:T(8,128)(2,1)} %pad_maximum_fusion.5), calls=%async_computation | async-start | bytes 262144 | tf_op jit(solution)/shard_map/all_to_all | solution.py:66
  10.7 0.0 copy-start.1
  10.7 7.8 %all-to-all-done = bf16[6,16,512]{2,0,1:T(8,128)(2,1)S(1)} async-done(((bf16[6,16,512]{2,0,1:T(8,128)(2,1)}), bf16[6,16,512]{2,0,1:T(8,128)(2,1)S(1)}, u32[]{:S(2)}, u32[]{:S(2)}) %all-to-all-start) | async-done | bytes 98336 | tf_op jit(solution)/shard_map/all_to_all | solution.py:66
  18.5 0.0 copy-done
  18.5 0.2 fusion.76
  18.7 0.0 copy-done.2
  18.7 0.2 fusion.84
  18.9 0.8 %collective-permute-start.6 = (bf16[96,512]{1,0:T(8,128)(2,1)S(1)}, bf16[96,512]{1,0:T(8,128)(2,1)S(1)}, u32[]{:S(2)}, u32[]{:S(2)}) collective-permute-start(bf16[96,512]{1,0:T(8,128)(2,1)S(1)} %fusion.7), channel_id=1, source_target_pairs={{0,6},{2,4},{4,2},{6,0},{8,14},{10,12},{12,10},{14,8},{16,22},{18,... | collective-permute-start | bytes 294920 | tf_op jit(solution)/shard_map/ppermute | solution.py:10
  19.7 1.8 %collective-permute-start.5 = (bf16[96,512]{1,0:T(8,128)(2,1)S(1)}, bf16[96,512]{1,0:T(8,128)(2,1)S(1)}, u32[]{:S(2)}, u32[]{:S(2)}) collective-permute-start(bf16[96,512]{1,0:T(8,128)(2,1)S(1)} %fusion.7), channel_id=1, source_target_pairs={{0,4},{2,6},{4,0},{6,2},{8,12},{10,14},{12,8},{14,10},{16,20},{18,... | collective-permute-start | bytes 294920 | tf_op jit(solution)/shard_map/ppermute | solution.py:10
  21.5 0.9 %collective-permute-start.4 = (bf16[96,512]{1,0:T(8,128)(2,1)S(1)}, bf16[96,512]{1,0:T(8,128)(2,1)S(1)}, u32[]{:S(2)}, u32[]{:S(2)}) collective-permute-start(bf16[96,512]{1,0:T(8,128)(2,1)S(1)} %fusion.7), channel_id=1, source_target_pairs={{0,2},{2,0},{4,6},{6,4},{8,10},{10,8},{12,14},{14,12},{16,18},{18,... | collective-permute-start | bytes 294920 | tf_op jit(solution)/shard_map/ppermute | solution.py:10
  22.5 0.0 copy-done.1
  22.5 0.2 fusion.19
  22.7 0.2 convolution_convert_fusion.3
  22.9 0.2 convolution_convert_fusion
  23.1 0.2 convolution_convert_fusion.2
  23.3 0.2 convolution_convert_fusion.1
  23.5 0.2 fusion.21
  23.7 1.0 %collective-permute-start.3 = (bf16[96,512]{1,0:T(8,128)(2,1)S(1)}, bf16[96,512]{1,0:T(8,128)(2,1)S(1)}, u32[]{:S(2)}, u32[]{:S(2)}) collective-permute-start(bf16[96,512]{1,0:T(8,128)(2,1)S(1)} %get-tuple-element.18), channel_id=1, source_target_pairs={{0,16},{2,18},{4,20},{6,22},{8,24},{10,26},{12,28},{14,30},{16,0},... | collective-permute-start | bytes 294920 | tf_op jit(solution)/shard_map/ppermute | solution.py:10
  24.7 0.9 %collective-permute-start.2 = (bf16[96,512]{1,0:T(8,128)(2,1)S(1)}, bf16[96,512]{1,0:T(8,128)(2,1)S(1)}, u32[]{:S(2)}, u32[]{:S(2)}) collective-permute-start(bf16[96,512]{1,0:T(8,128)(2,1)S(1)} %get-tuple-element.20), channel_id=1, source_target_pairs={{0,8},{2,10},{4,12},{6,14},{8,0},{10,2},{12,4},{14,6},{16,24},{18,... | collective-permute-start | bytes 294920 | tf_op jit(solution)/shard_map/ppermute | solution.py:10
  25.7 0.0 collective-permute-done.6
  25.7 0.8 %collective-permute-start.1 = (bf16[96,512]{1,0:T(8,128)(2,1)S(1)}, bf16[96,512]{1,0:T(8,128)(2,1)S(1)}, u32[]{:S(2)}, u32[]{:S(2)}) collective-permute-start(bf16[96,512]{1,0:T(8,128)(2,1)S(1)} %get-tuple-element.19), channel_id=1, source_target_pairs={{0,4},{2,6},{4,0},{6,2},{8,12},{10,14},{12,8},{14,10},{16,20},{18,... | collective-permute-start | bytes 294920 | tf_op jit(solution)/shard_map/ppermute | solution.py:10
  26.5 0.0 collective-permute-done.5
  26.5 0.9 %collective-permute-start = (bf16[96,512]{1,0:T(8,128)(2,1)S(1)}, bf16[96,512]{1,0:T(8,128)(2,1)S(1)}, u32[]{:S(2)}, u32[]{:S(2)}) collective-permute-start(bf16[96,512]{1,0:T(8,128)(2,1)S(1)} %get-tuple-element.17), channel_id=1, source_target_pairs={{0,2},{2,0},{4,6},{6,4},{8,10},{10,8},{12,14},{14,12},{16,18},{18,... | collective-permute-start | bytes 294920 | tf_op jit(solution)/shard_map/ppermute | solution.py:10
  27.4 0.0 collective-permute-done.4
  27.4 2.3 %collective-permute-start.9 = (bf16[96,512]{1,0:T(8,128)(2,1)S(1)}, bf16[96,512]{1,0:T(8,128)(2,1)S(1)}, u32[]{:S(2)}, u32[]{:S(2)}) collective-permute-start(bf16[96,512]{1,0:T(8,128)(2,1)S(1)} %fusion.83), channel_id=1, source_target_pairs={{0,24},{2,26},{4,28},{6,30},{8,16},{10,18},{12,20},{14,22},{16,8},... | collective-permute-start | bytes 294920 | tf_op jit(solution)/shard_map/ppermute | solution.py:10
  29.7 1.4 %collective-permute-done = bf16[96,512]{1,0:T(8,128)(2,1)S(1)} collective-permute-done((bf16[96,512]{1,0:T(8,128)(2,1)S(1)}, bf16[96,512]{1,0:T(8,128)(2,1)S(1)}, u32[]{:S(2)}, u32[]{:S(2)}) %collective-permute-start) | collective-permute-done | bytes 98336 | tf_op jit(solution)/shard_map/ppermute | solution.py:10
  31.1 1.8 %collective-permute-start.8 = (bf16[96,512]{1,0:T(8,128)(2,1)S(1)}, bf16[96,512]{1,0:T(8,128)(2,1)S(1)}, u32[]{:S(2)}, u32[]{:S(2)}) collective-permute-start(bf16[96,512]{1,0:T(8,128)(2,1)S(1)} %fusion.83), channel_id=1, source_target_pairs={{0,16},{2,18},{4,20},{6,22},{8,24},{10,26},{12,28},{14,30},{16,0},... | collective-permute-start | bytes 294920 | tf_op jit(solution)/shard_map/ppermute | solution.py:10
  33.0 0.0 collective-permute-done.1
  33.0 1.4 %collective-permute-start.7 = (bf16[96,512]{1,0:T(8,128)(2,1)S(1)}, bf16[96,512]{1,0:T(8,128)(2,1)S(1)}, u32[]{:S(2)}, u32[]{:S(2)}) collective-permute-start(bf16[96,512]{1,0:T(8,128)(2,1)S(1)} %fusion.83), channel_id=1, source_target_pairs={{0,8},{2,10},{4,12},{6,14},{8,0},{10,2},{12,4},{14,6},{16,24},{18,... | collective-permute-start | bytes 294920 | tf_op jit(solution)/shard_map/ppermute | solution.py:10
  34.4 0.0 collective-permute-done.2
  34.4 0.0 collective-permute-done.3
  34.4 0.1 collective-permute-start.10
  34.5 0.1 fusion.9
  34.7 0.2 convolution_add_fusion.4
  34.8 0.1 fusion.12
  35.0 0.0 collective-permute-done.9
  35.0 2.8 %collective-permute-done.8 = bf16[96,512]{1,0:T(8,128)(2,1)S(1)} collective-permute-done((bf16[96,512]{1,0:T(8,128)(2,1)S(1)}, bf16[96,512]{1,0:T(8,128)(2,1)S(1)}, u32[]{:S(2)}, u32[]{:S(2)}) %collective-permute-start.8) | collective-permute-done | bytes 98336 | tf_op jit(solution)/shard_map/ppermute | solution.py:10
  37.8 0.3 collective-permute-done.7
  38.1 0.1 add_convert_fusion
  38.2 0.1 fusion.52
  38.4 0.2 fusion.65
  38.6 0.2 fusion.39
  38.8 0.2 fusion.6
  39.0 0.7 %all_to_all.27 = bf16[16,6,512]{2,1,0:T(8,128)(2,1)} reshape(bf16[96,512]{1,0:T(8,128)(2,1)S(1)} %pad_maximum_fusion.6) | data formatting | bytes 196608 | tf_op jit(solution)/shard_map/all_to_all | solution.py:89
  39.7 4.4 %all-to-all-start.1 = ((bf16[16,6,512]{2,1,0:T(8,128)(2,1)}), bf16[16,6,512]{2,1,0:T(8,128)(2,1)S(1)}, u32[]{:S(2)}, u32[]{:S(2)}) async-start(bf16[16,6,512]{2,1,0:T(8,128)(2,1)} %all_to_all.27), calls=%async_computation.1 | async-start | bytes 262144 | tf_op jit(solution)/shard_map/all_to_all | solution.py:89
  44.1 0.1 collective-permute-start.11
  44.2 0.2 fusion.63
  44.4 0.0 collective-permute-done.10
  44.5 0.3 fusion.23
  44.7 1.1 %fusion = f32[640,256]{1,0:T(8,128)} fusion(f32[640,256]{1,0:T(8,128)S(1)} %fusion.23, bf16[96,640]{1,0:T(8,128)(2,1)S(1)} %get-tuple-element.9, bf16[96,512]{1,0:T(8,128)(2,1)S(1)} %all_to_all.26), kind=kOutput, calls=%fused_computation.1 | convolution fusion | flops 31784960 | bytes 1482752 | tf_op jit(solution)/shard_map/dot_general | solution.py:32
  45.9 0.0 collective-permute-done.11
  45.9 0.9 %fusion.2 = f32[256,128]{1,0:T(8,128)} fusion(f32[256,128]{1,0:T(8,128)S(1)} %fusion.65, bf16[96,1024]{1,0:T(8,128)(2,1)S(1)} %collective-permute-done.10, bf16[96,256]{1,0:T(8,128)(2,1)S(1)} %collective-permute-done.11), kind=kOutput, calls=%fused_computation.5 | convolution fusion | flops 6356992 | bytes 335872 | tf_op jit(solution)/shard_map/dot_general | solution.py:32
  46.7 0.9 %fusion.1 = f32[128,256]{1,0:T(8,128)} fusion(f32[128,256]{1,0:T(8,128)S(1)} %fusion.63, bf16[96,1024]{1,0:T(8,128)(2,1)S(1)} %collective-permute-done.10, bf16[96,256]{1,0:T(8,128)(2,1)S(1)} %collective-permute-done.11), kind=kOutput, calls=%fused_computation.3 | convolution fusion | flops 6356992 | bytes 335872 | tf_op jit(solution)/shard_map/dot_general | solution.py:32
  47.6 4.3 %all-to-all-done.1 = bf16[16,6,512]{2,1,0:T(8,128)(2,1)S(1)} async-done(((bf16[16,6,512]{2,1,0:T(8,128)(2,1)}), bf16[16,6,512]{2,1,0:T(8,128)(2,1)S(1)}, u32[]{:S(2)}, u32[]{:S(2)}) %all-to-all-start.1) | async-done | bytes 98336 | tf_op jit(solution)/shard_map/all_to_all | solution.py:89
  51.9 0.7 %fusion.88 = (bf16[6,16,256]{2,0,1:T(8,128)(2,1)}, bf16[6,16,256]{2,0,1:T(8,128)(2,1)}) fusion(bf16[6,16,512]{2,0,1:T(8,128)(2,1)S(1)} %bitcast.39), kind=kLoop, calls=%fused_computation.123 | loop fusion | bytes 196608 | tf_op jit(solution)/shard_map/slice | solution.py:92
  (17 shorter events, 0.4 us)
Async XLA Ops:
  0.6 17.9 %copy-start = (bf16[256,256]{1,0:T(8,128)(2,1)S(1)}, bf16[256,256]{1,0:T(8,128)(2,1)}, u32[]{:S(2)}) copy-start(bf16[256,256]{1,0:T(8,128)(2,1)} %param.8) | copy-start | bytes 393220
  2.2 16.5 %copy-start.2 = (bf16[256,256]{1,0:T(8,128)(2,1)S(1)}, bf16[256,256]{1,0:T(8,128)(2,1)}, u32[]{:S(2)}) copy-start(bf16[256,256]{1,0:T(8,128)(2,1)} %param.7) | copy-start | bytes 393220
  2.2 16.2 %all-to-all-start = ((bf16[6,16,512]{2,0,1:T(8,128)(2,1)}), bf16[6,16,512]{2,0,1:T(8,128)(2,1)S(1)}, u32[]{:S(2)}, u32[]{:S(2)}) async-start(bf16[6,16,512]{2,0,1:T(8,128)(2,1)} %pad_maximum_fusion.5), calls=%async_computation | async-start | bytes 262144 | tf_op jit(solution)/shard_map/all_to_all | solution.py:66
  10.7 11.8 %copy-start.1 = (bf16[1,5,256,256]{3,2,1,0:T(8,128)(2,1)S(1)}, bf16[1,5,256,256]{3,2,1,0:T(8,128)(2,1)}, u32[]{:S(2)}) copy-start(bf16[1,5,256,256]{3,2,1,0:T(8,128)(2,1)} %param.6) | copy-start | bytes 1966084
  18.9 6.7 %collective-permute-start.6 = (bf16[96,512]{1,0:T(8,128)(2,1)S(1)}, bf16[96,512]{1,0:T(8,128)(2,1)S(1)}, u32[]{:S(2)}, u32[]{:S(2)}) collective-permute-start(bf16[96,512]{1,0:T(8,128)(2,1)S(1)} %fusion.7), channel_id=1, source_target_pairs={{0,6},{2,4},{4,2},{6,0},{8,14},{10,12},{12,10},{14,8},{16,22},{18,... | collective-permute-start | bytes 294920 | tf_op jit(solution)/shard_map/ppermute | solution.py:10
  19.7 6.8 %collective-permute-start.5 = (bf16[96,512]{1,0:T(8,128)(2,1)S(1)}, bf16[96,512]{1,0:T(8,128)(2,1)S(1)}, u32[]{:S(2)}, u32[]{:S(2)}) collective-permute-start(bf16[96,512]{1,0:T(8,128)(2,1)S(1)} %fusion.7), channel_id=1, source_target_pairs={{0,4},{2,6},{4,0},{6,2},{8,12},{10,14},{12,8},{14,10},{16,20},{18,... | collective-permute-start | bytes 294920 | tf_op jit(solution)/shard_map/ppermute | solution.py:10
  21.5 5.8 %collective-permute-start.4 = (bf16[96,512]{1,0:T(8,128)(2,1)S(1)}, bf16[96,512]{1,0:T(8,128)(2,1)S(1)}, u32[]{:S(2)}, u32[]{:S(2)}) collective-permute-start(bf16[96,512]{1,0:T(8,128)(2,1)S(1)} %fusion.7), channel_id=1, source_target_pairs={{0,2},{2,0},{4,6},{6,4},{8,10},{10,8},{12,14},{14,12},{16,18},{18,... | collective-permute-start | bytes 294920 | tf_op jit(solution)/shard_map/ppermute | solution.py:10
  23.7 10.7 %collective-permute-start.3 = (bf16[96,512]{1,0:T(8,128)(2,1)S(1)}, bf16[96,512]{1,0:T(8,128)(2,1)S(1)}, u32[]{:S(2)}, u32[]{:S(2)}) collective-permute-start(bf16[96,512]{1,0:T(8,128)(2,1)S(1)} %get-tuple-element.18), channel_id=1, source_target_pairs={{0,16},{2,18},{4,20},{6,22},{8,24},{10,26},{12,28},{14,30},{16,0},... | collective-permute-start | bytes 294920 | tf_op jit(solution)/shard_map/ppermute | solution.py:10
  24.7 9.7 %collective-permute-start.2 = (bf16[96,512]{1,0:T(8,128)(2,1)S(1)}, bf16[96,512]{1,0:T(8,128)(2,1)S(1)}, u32[]{:S(2)}, u32[]{:S(2)}) collective-permute-start(bf16[96,512]{1,0:T(8,128)(2,1)S(1)} %get-tuple-element.20), channel_id=1, source_target_pairs={{0,8},{2,10},{4,12},{6,14},{8,0},{10,2},{12,4},{14,6},{16,24},{18,... | collective-permute-start | bytes 294920 | tf_op jit(solution)/shard_map/ppermute | solution.py:10
  25.7 7.3 %collective-permute-start.1 = (bf16[96,512]{1,0:T(8,128)(2,1)S(1)}, bf16[96,512]{1,0:T(8,128)(2,1)S(1)}, u32[]{:S(2)}, u32[]{:S(2)}) collective-permute-start(bf16[96,512]{1,0:T(8,128)(2,1)S(1)} %get-tuple-element.19), channel_id=1, source_target_pairs={{0,4},{2,6},{4,0},{6,2},{8,12},{10,14},{12,8},{14,10},{16,20},{18,... | collective-permute-start | bytes 294920 | tf_op jit(solution)/shard_map/ppermute | solution.py:10
  26.5 4.6 %collective-permute-start = (bf16[96,512]{1,0:T(8,128)(2,1)S(1)}, bf16[96,512]{1,0:T(8,128)(2,1)S(1)}, u32[]{:S(2)}, u32[]{:S(2)}) collective-permute-start(bf16[96,512]{1,0:T(8,128)(2,1)S(1)} %get-tuple-element.17), channel_id=1, source_target_pairs={{0,2},{2,0},{4,6},{6,4},{8,10},{10,8},{12,14},{14,12},{16,18},{18,... | collective-permute-start | bytes 294920 | tf_op jit(solution)/shard_map/ppermute | solution.py:10
  27.4 7.6 %collective-permute-start.9 = (bf16[96,512]{1,0:T(8,128)(2,1)S(1)}, bf16[96,512]{1,0:T(8,128)(2,1)S(1)}, u32[]{:S(2)}, u32[]{:S(2)}) collective-permute-start(bf16[96,512]{1,0:T(8,128)(2,1)S(1)} %fusion.83), channel_id=1, source_target_pairs={{0,24},{2,26},{4,28},{6,30},{8,16},{10,18},{12,20},{14,22},{16,8},... | collective-permute-start | bytes 294920 | tf_op jit(solution)/shard_map/ppermute | solution.py:10
  31.1 6.7 %collective-permute-start.8 = (bf16[96,512]{1,0:T(8,128)(2,1)S(1)}, bf16[96,512]{1,0:T(8,128)(2,1)S(1)}, u32[]{:S(2)}, u32[]{:S(2)}) collective-permute-start(bf16[96,512]{1,0:T(8,128)(2,1)S(1)} %fusion.83), channel_id=1, source_target_pairs={{0,16},{2,18},{4,20},{6,22},{8,24},{10,26},{12,28},{14,30},{16,0},... | collective-permute-start | bytes 294920 | tf_op jit(solution)/shard_map/ppermute | solution.py:10
  33.0 5.1 %collective-permute-start.7 = (bf16[96,512]{1,0:T(8,128)(2,1)S(1)}, bf16[96,512]{1,0:T(8,128)(2,1)S(1)}, u32[]{:S(2)}, u32[]{:S(2)}) collective-permute-start(bf16[96,512]{1,0:T(8,128)(2,1)S(1)} %fusion.83), channel_id=1, source_target_pairs={{0,8},{2,10},{4,12},{6,14},{8,0},{10,2},{12,4},{14,6},{16,24},{18,... | collective-permute-start | bytes 294920 | tf_op jit(solution)/shard_map/ppermute | solution.py:10
  34.4 10.0 %collective-permute-start.10 = (bf16[96,1024]{1,0:T(8,128)(2,1)S(1)}, bf16[96,1024]{1,0:T(8,128)(2,1)S(1)}, u32[]{:S(2)}, u32[]{:S(2)}) collective-permute-start(bf16[96,1024]{1,0:T(8,128)(2,1)S(1)} %get-tuple-element.10), channel_id=1, source_target_pairs={{0,1},{1,0},{2,3},{3,2},{4,5},{5,4},{6,7},{7,6},{8,9},{9,8},{10,11... | collective-permute-start | bytes 589832 | tf_op jit(solution)/shard_map/ppermute | solution.py:14
  39.7 12.2 %all-to-all-start.1 = ((bf16[16,6,512]{2,1,0:T(8,128)(2,1)}), bf16[16,6,512]{2,1,0:T(8,128)(2,1)S(1)}, u32[]{:S(2)}, u32[]{:S(2)}) async-start(bf16[16,6,512]{2,1,0:T(8,128)(2,1)} %all_to_all.27), calls=%async_computation.1 | async-start | bytes 262144 | tf_op jit(solution)/shard_map/all_to_all | solution.py:89
  44.1 1.7 %collective-permute-start.11 = (bf16[96,256]{1,0:T(8,128)(2,1)S(1)}, bf16[96,256]{1,0:T(8,128)(2,1)S(1)}, u32[]{:S(2)}, u32[]{:S(2)}) collective-permute-start(bf16[96,256]{1,0:T(8,128)(2,1)S(1)} %pad_maximum_fusion.7), channel_id=1, source_target_pairs={{0,1},{1,0},{2,3},{3,2},{4,5},{5,4},{6,7},{7,6},{8,9},{9,8},{10,11... | collective-permute-start | bytes 147464 | tf_op jit(solution)/shard_map/ppermute | solution.py:14

commit v2 on v1

--- a/solution.py
+++ b/solution.py
@@ -34,16 +34,33 @@
     )
 
 
+def split_hid():
+    hid = lax.axis_size("hid")
+    low = 1 << ((hid - 1).bit_length() // 2)
+    return hid // low, low
+
+
+def swap_slow(x):
+    high, low = split_hid()
+    groups = [[i * low + j for i in range(high)] for j in range(low)]
+    return lax.all_to_all(x, "hid", 0, 0, axis_index_groups=groups, tiled=True)
+
+
+def swap_fast(x):
+    high, low = split_hid()
+    groups = [[i * low + j for j in range(low)] for i in range(high)]
+    return lax.all_to_all(x, "hid", 0, 0, axis_index_groups=groups, tiled=True)
+
+
 def sum_over_hid(part):
-    bits = (lax.axis_size("hid") - 1).bit_length()
-    total = part
-    for low in range(0, bits, 2):
-        sent = total.astype(jnp.bfloat16)
-        masks = [1 << low]
-        if low + 1 < bits:
-            masks += [2 << low, 3 << low]
-        total = total + sum(exchange(sent, mask).astype(jnp.float32) for mask in masks)
-    return total.astype(jnp.bfloat16)
+    high, low = split_hid()
+    tokens, width = part.shape
+    pieces = part.astype(jnp.bfloat16).reshape(low, tokens // low, width)
+    piece = jnp.sum(swap_fast(pieces).astype(jnp.float32), axis=0).astype(jnp.bfloat16)
+    pieces = swap_slow(jnp.broadcast_to(piece[None], (high,) + piece.shape))
+    piece = jnp.sum(pieces.astype(jnp.float32), axis=0).astype(jnp.bfloat16)
+    pieces = swap_fast(jnp.broadcast_to(piece[None], (low,) + piece.shape))
+    return pieces.reshape(tokens, width)
 
 
 def half(x, which):
@@ -60,10 +77,13 @@
     rank = low_u.shape[1]
     factor = 1.0 / math.sqrt(tokens * hid * lax.axis_size("seq"))
 
+    high, low = split_hid()
     both = jnp.concatenate(
-        [pre_act.reshape(tokens, hid, side), grad_out.reshape(tokens, hid, side)], axis=2
-    ).reshape(tokens, hid * 2 * side)
-    rows = lax.all_to_all(both, "hid", split_axis=1, concat_axis=0, tiled=True)
+        [pre_act.reshape(tokens, high, low, side), grad_out.reshape(tokens, high, low, side)],
+        axis=3,
+    )
+    rows = swap_fast(both.transpose(2, 1, 0, 3))
+    rows = swap_slow(rows.transpose(1, 0, 2, 3)).reshape(hid * tokens, 2 * side)
     pre_f = rows[:, :side].astype(jnp.float32)
     grad = rows[:, side:]
     act_f, pullback = jax.vjp(gelu_tanh, pre_f)
@@ -86,8 +106,9 @@
     grad_act = (back + dot_t(dlatent, low_u)).astype(jnp.bfloat16)
     grad_pre_rows = pullback(grad_act.astype(jnp.float32))[0].astype(jnp.bfloat16)
     results = jnp.concatenate([output_rows, grad_pre_rows], axis=1)
-    results = lax.all_to_all(results, "hid", split_axis=0, concat_axis=1, tiled=True)
-    results = results.reshape(tokens, hid, 2 * side)
+    results = swap_slow(results.reshape(high, low, tokens, 2 * side))
+    results = swap_fast(results.transpose(1, 0, 2, 3))
+    results = results.transpose(2, 1, 0, 3).reshape(tokens, hid, 2 * side)
     output = results[:, :, :side].reshape(tokens, hid * side)
     grad_pre = results[:, :, side:].reshape(tokens, hid * side)
 

time: 52.9 us -> 75.8 us (1.43)
  blocking collectives: 0 us -> 10 us
  waiting for transfers between devices: 16.6 us -> 22.9 us
  local copies, waits for them, and re-layouts: 1.43 us -> 6.7 us
  starting transfers between devices: 25.6 us -> 27.4 us
  other arithmetic: 2 us -> 1.02 us
    all_to_all x2 -> x6, waiting for transfers between devices: 12.1 us -> 22.9 us  [the longest x3 14.1 us: swap_slow(): return lax.all_to_all(x, 'hid', 0, 0, axis_index_groups=groups, tiled=True)]
    all_to_all x0 -> x1, blocking collectives: none -> 10 us  [swap_fast(): return lax.all_to_all(x, 'hid', 0, 0, axis_index_groups=groups, tiled=True)]
    all_to_all x2 -> x6, starting transfers between devices: 12.9 us -> 22.1 us  [the longest x3 12.2 us: swap_slow(): return lax.all_to_all(x, 'hid', 0, 0, axis_index_groups=groups, tiled=True)]
    ppermute x10 -> x4, starting transfers between devices: 12.6 us -> 5.13 us  [exchange(): lax.ppermute(x, 'hid', [(i, i ^ mask) for i in range(lax.axis_size('hid'))])]
    ppermute x10 -> x4, waiting for transfers between devices: 4.51 us -> 0.01 us  [exchange(): lax.ppermute(x, 'hid', [(i, i ^ mask) for i in range(lax.axis_size('hid'))])]
    unnamed x7 -> x12, local copies, waits for them, and re-layouts: 0.05 us -> 2.06 us
    reshape x0 -> x6, local copies, waits for them, and re-layouts: none -> 1.85 us  [the longest x1 0.97 us: on_device(): grad_out.reshape(tokens, high, low, side)]
    transpose x0 -> x4, local copies, waits for them, and re-layouts: none -> 1.47 us  [the longest x1 0.69 us: on_device(): rows = swap_slow(rows.transpose(1, 0, 2, 3)).reshape(hid * tokens, 2 * side)]
  transfers between devices with their start and end apart: 14 -> 12, of which waited for: 5 -> 5; matrix products, arithmetic and copies ran while one was open for 11% -> 9% of each run, Pallas kernels for 0% -> 0%
where the time goes in v2:
time: 75.8 us; the launch traced here: 75 us
  starting transfers between devices  27.4 us (36%)
  waiting for transfers between devices  22.9 us (30%)
  blocking collectives  10 us (13%)
  local copies, waits for them, and re-layouts  6.7 us (9%)
  matrix products  5.85 us (8%)
  between operations  1.12 us (1%)
  other arithmetic  1.02 us (1%)
    all_to_all x3, waiting for transfers between devices, swap_slow(): return lax.all_to_all(x, 'hid', 0, 0, axis_index_groups=groups, tiled=True)  14.1 us
    all_to_all x3, starting transfers between devices, swap_slow(): return lax.all_to_all(x, 'hid', 0, 0, axis_index_groups=groups, tiled=True)  12.2 us
    all_to_all x1, blocking collectives, swap_fast(): return lax.all_to_all(x, 'hid', 0, 0, axis_index_groups=groups, tiled=True)  10 us
    all_to_all x3, starting transfers between devices, swap_fast(): return lax.all_to_all(x, 'hid', 0, 0, axis_index_groups=groups, tiled=True)  9.91 us
    all_to_all x3, waiting for transfers between devices, swap_fast(): return lax.all_to_all(x, 'hid', 0, 0, axis_index_groups=groups, tiled=True)  8.8 us
    ppermute x4, starting transfers between devices, exchange(): lax.ppermute(x, 'hid', [(i, i ^ mask) for i in range(lax.axis_size('hid'))])  5.13 us
    dot_general x6, matrix products, inner_rows(): lax.dot_general(left, right, (((0,), (0,)), ((), ())), preferred_element_...  3.52 us
    unnamed x12, local copies, waits for them, and re-layouts  2.06 us
  transfers between devices with their start and end apart: 12, of which 5 were waited for; matrix products, arithmetic and copies ran while one was open for 9% of the time, Pallas kernels for 0%

profile of v2, /device:TPU:0, one launch (start us, length us, event | category | flops | bytes accessed | tf_op | source)
XLA Modules:
  0.0 75.0 jit_solution(1319526274840192006)
XLA Ops:
  0.6 0.0 copy-start
  0.6 0.0 copy-start.3
  0.7 1.0 %reshape.45 = bf16[6,4,4,256]{3,2,1,0:T(4,128)(2,1)S(1)} reshape(bf16[6,4096]{1,0:T(8,128)(2,1)} %param.9) | data formatting | bytes 98304 | tf_op jit(solution)/shard_map/reshape | solution.py:82
  1.6 0.0 copy-done.3
  1.6 0.1 reshape.44
  1.8 0.0 copy-start.1
  1.8 10.0 %all_to_all.35 = bf16[4,4,6,512]{3,1,2,0:T(4,128)(2,1)S(1)} all-to-all(bf16[4,4,6,512]{3,1,2,0:T(4,128)(2,1)S(1)} %copy.26), channel_id=1, replica_groups={{0,2,4,6},{8,10,12,14},{16,18,20,22},{24,26,28,30},{1,3,5,7},{9,11,13,1..., dimensions={0} | all-to-all | bytes 196608 | tf_op jit(solution)/shard_map/all_to_all | solution.py:52
  11.9 0.7 copy.27
  12.6 4.9 %all-to-all-start.1 = ((bf16[4,4,6,512]{3,1,2,0:T(4,128)(2,1)}), bf16[4,4,6,512]{3,1,2,0:T(4,128)(2,1)S(1)}, u32[]{:S(2)}, u32[]{:S(2)}) async-start(bf16[4,4,6,512]{3,1,2,0:T(4,128)(2,1)} %copy.27), calls=%async_computation.1 | async-start | bytes 196608 | tf_op jit(solution)/shard_map/all_to_all | solution.py:46
  17.4 5.8 %all-to-all-done.1 = bf16[4,4,6,512]{3,1,2,0:T(4,128)(2,1)S(1)} async-done(((bf16[4,4,6,512]{3,1,2,0:T(4,128)(2,1)}), bf16[4,4,6,512]{3,1,2,0:T(4,128)(2,1)S(1)}, u32[]{:S(2)}, u32[]{:S(2)}) %all-to-all-start.1) | async-done | bytes 98336 | tf_op jit(solution)/shard_map/all_to_all | solution.py:46
  23.4 0.0 copy-done.1
  23.4 0.2 convolution_convert_fusion.5
  23.6 0.2 convolution_convert_fusion.2
  23.8 0.2 convolution_convert_fusion.4
  24.0 0.2 convolution_convert_fusion.3
  24.2 0.0 copy-start.2
  24.2 0.2 fusion.20
  24.3 0.7 copy-done.2
  25.1 0.2 convolution_convert_fusion
  25.3 0.0 copy-done
  25.3 0.2 convolution_convert_fusion.1
  25.4 0.7 pad_maximum_fusion.4
  26.1 3.3 %all-to-all-start.2 = ((bf16[4,24,512]{2,1,0:T(8,128)(2,1)}), bf16[4,24,512]{2,1,0:T(8,128)(2,1)S(1)}, u32[]{:S(2)}, u32[]{:S(2)}) async-start(bf16[4,24,512]{2,1,0:T(8,128)(2,1)} %pad_maximum_fusion.4), calls=%async_computation.2 | async-start | bytes 196608 | tf_op jit(solution)/shard_map/all_to_all | solution.py:52
  29.4 0.9 %collective-permute-start.3 = (bf16[96,512]{1,0:T(8,128)(2,1)S(1)}, bf16[96,512]{1,0:T(8,128)(2,1)S(1)}, u32[]{:S(2)}, u32[]{:S(2)}) collective-permute-start(bf16[96,512]{1,0:T(8,128)(2,1)S(1)} %get-tuple-element.18), channel_id=1, source_target_pairs={{0,16},{2,18},{4,20},{6,22},{8,24},{10,26},{12,28},{14,30},{16,0},... | collective-permute-start | bytes 294920 | tf_op jit(solution)/shard_map/ppermute | solution.py:10
  30.3 0.8 %collective-permute-start.2 = (bf16[96,512]{1,0:T(8,128)(2,1)S(1)}, bf16[96,512]{1,0:T(8,128)(2,1)S(1)}, u32[]{:S(2)}, u32[]{:S(2)}) collective-permute-start(bf16[96,512]{1,0:T(8,128)(2,1)S(1)} %get-tuple-element.20), channel_id=1, source_target_pairs={{0,8},{2,10},{4,12},{6,14},{8,0},{10,2},{12,4},{14,6},{16,24},{18,... | collective-permute-start | bytes 294920 | tf_op jit(solution)/shard_map/ppermute | solution.py:10
  31.1 2.0 %collective-permute-start.1 = (bf16[96,512]{1,0:T(8,128)(2,1)S(1)}, bf16[96,512]{1,0:T(8,128)(2,1)S(1)}, u32[]{:S(2)}, u32[]{:S(2)}) collective-permute-start(bf16[96,512]{1,0:T(8,128)(2,1)S(1)} %get-tuple-element.19), channel_id=1, source_target_pairs={{0,4},{2,6},{4,0},{6,2},{8,12},{10,14},{12,8},{14,10},{16,20},{18,... | collective-permute-start | bytes 294920 | tf_op jit(solution)/shard_map/ppermute | solution.py:10
  33.1 1.5 %collective-permute-start = (bf16[96,512]{1,0:T(8,128)(2,1)S(1)}, bf16[96,512]{1,0:T(8,128)(2,1)S(1)}, u32[]{:S(2)}, u32[]{:S(2)}) collective-permute-start(bf16[96,512]{1,0:T(8,128)(2,1)S(1)} %get-tuple-element.17), channel_id=1, source_target_pairs={{0,2},{2,0},{4,6},{6,4},{8,10},{10,8},{12,14},{14,12},{16,18},{18,... | collective-permute-start | bytes 294920 | tf_op jit(solution)/shard_map/ppermute | solution.py:10
  34.6 0.0 all-to-all-done.2
  34.7 0.6 broadcast_in_dim.4
  35.3 4.0 %all-to-all-start.3 = ((bf16[4,24,512]{2,1,0:T(8,128)(2,1)}), bf16[4,24,512]{2,1,0:T(8,128)(2,1)S(1)}, u32[]{:S(2)}, u32[]{:S(2)}) async-start(bf16[4,24,512]{2,1,0:T(8,128)(2,1)} %broadcast_in_dim.4), calls=%async_computation.3 | async-start | bytes 196608 | tf_op jit(solution)/shard_map/all_to_all | solution.py:46
  39.4 0.0 collective-permute-done
  39.4 0.0 collective-permute-done.1
  39.4 0.0 collective-permute-done.2
  39.5 0.0 collective-permute-done.3
  39.5 0.1 collective-permute-start.4
  39.6 0.2 convolution_add_fusion.4
  39.8 0.1 fusion.8
  39.9 5.3 %all-to-all-done.3 = bf16[4,24,512]{2,1,0:T(8,128)(2,1)S(1)} async-done(((bf16[4,24,512]{2,1,0:T(8,128)(2,1)}), bf16[4,24,512]{2,1,0:T(8,128)(2,1)S(1)}, u32[]{:S(2)}, u32[]{:S(2)}) %all-to-all-start.3) | async-done | bytes 98336 | tf_op jit(solution)/shard_map/all_to_all | solution.py:46
  45.2 0.6 broadcast_in_dim.5
  45.9 3.3 %all-to-all-start.4 = ((bf16[4,24,512]{2,1,0:T(8,128)(2,1)}), bf16[4,24,512]{2,1,0:T(8,128)(2,1)S(1)}, u32[]{:S(2)}, u32[]{:S(2)}) async-start(bf16[4,24,512]{2,1,0:T(8,128)(2,1)} %broadcast_in_dim.5), calls=%async_computation.4 | async-start | bytes 196608 | tf_op jit(solution)/shard_map/all_to_all | solution.py:52
  49.2 0.1 fusion.11
  49.3 4.8 %all-to-all-done.4 = bf16[4,24,512]{2,1,0:T(8,128)(2,1)S(1)} async-done(((bf16[4,24,512]{2,1,0:T(8,128)(2,1)}), bf16[4,24,512]{2,1,0:T(8,128)(2,1)S(1)}, u32[]{:S(2)}, u32[]{:S(2)}) %all-to-all-start.4) | async-done | bytes 98336 | tf_op jit(solution)/shard_map/all_to_all | solution.py:52
  54.1 0.2 fusion.47
  54.2 0.2 fusion.49
  54.4 0.3 fusion.38
  54.7 0.2 fusion.6
  54.9 0.7 copy.29
  55.6 3.3 %all-to-all-start.5 = ((bf16[4,4,6,512]{3,1,2,0:T(4,128)(2,1)}), bf16[4,4,6,512]{3,1,2,0:T(4,128)(2,1)S(1)}, u32[]{:S(2)}, u32[]{:S(2)}) async-start(bf16[4,4,6,512]{3,1,2,0:T(4,128)(2,1)} %copy.29), calls=%async_computation.5 | async-start | bytes 196608 | tf_op jit(solution)/shard_map/all_to_all | solution.py:46
  59.0 0.1 collective-permute-start.5
  59.0 0.2 fusion.60
  59.2 0.0 collective-permute-done.4
  59.3 0.3 fusion.22
  59.6 1.1 %fusion = f32[640,256]{1,0:T(8,128)} fusion(f32[640,256]{1,0:T(8,128)S(1)} %fusion.22, bf16[96,640]{1,0:T(8,128)(2,1)S(1)} %get-tuple-element.7, bf16[96,512]{1,0:T(8,128)(2,1)S(1)} %reshape.46), kind=kOutput, calls=%fused_computation.1 | convolution fusion | flops 31784960 | bytes 1482752 | tf_op jit(solution)/shard_map/dot_general | solution.py:32
  60.7 0.2 fusion.62
  60.9 0.0 collective-permute-done.5
  60.9 0.9 %fusion.2 = f32[256,128]{1,0:T(8,128)} fusion(f32[256,128]{1,0:T(8,128)S(1)} %fusion.62, bf16[96,1024]{1,0:T(8,128)(2,1)S(1)} %collective-permute-done.4, bf16[96,256]{1,0:T(8,128)(2,1)S(1)} %collective-permute-done.5), kind=kOutput, calls=%fused_computation.5 | convolution fusion | flops 6356992 | bytes 335872 | tf_op jit(solution)/shard_map/dot_general | solution.py:32
  61.8 3.0 %all-to-all-done.5 = bf16[4,4,6,512]{3,1,2,0:T(4,128)(2,1)S(1)} async-done(((bf16[4,4,6,512]{3,1,2,0:T(4,128)(2,1)}), bf16[4,4,6,512]{3,1,2,0:T(4,128)(2,1)S(1)}, u32[]{:S(2)}, u32[]{:S(2)}) %all-to-all-start.5) | async-done | bytes 98336 | tf_op jit(solution)/shard_map/all_to_all | solution.py:46
  64.7 0.7 copy.30
  65.4 3.3 %all-to-all-start.6 = ((bf16[4,4,6,512]{3,1,2,0:T(4,128)(2,1)}), bf16[4,4,6,512]{3,1,2,0:T(4,128)(2,1)S(1)}, u32[]{:S(2)}, u32[]{:S(2)}) async-start(bf16[4,4,6,512]{3,1,2,0:T(4,128)(2,1)} %copy.30), calls=%async_computation.6 | async-start | bytes 196608 | tf_op jit(solution)/shard_map/all_to_all | solution.py:52
  68.7 0.9 %fusion.1 = f32[128,256]{1,0:T(8,128)} fusion(f32[128,256]{1,0:T(8,128)S(1)} %fusion.60, bf16[96,1024]{1,0:T(8,128)(2,1)S(1)} %collective-permute-done.4, bf16[96,256]{1,0:T(8,128)(2,1)S(1)} %collective-permute-done.5), kind=kOutput, calls=%fused_computation.3 | convolution fusion | flops 6356992 | bytes 335872 | tf_op jit(solution)/shard_map/dot_general | solution.py:32
  69.6 4.0 %all-to-all-done.6 = bf16[4,4,6,512]{3,1,2,0:T(4,128)(2,1)S(1)} async-done(((bf16[4,4,6,512]{3,1,2,0:T(4,128)(2,1)}), bf16[4,4,6,512]{3,1,2,0:T(4,128)(2,1)S(1)}, u32[]{:S(2)}, u32[]{:S(2)}) %all-to-all-start.6) | async-done | bytes 98336 | tf_op jit(solution)/shard_map/all_to_all | solution.py:52
  73.6 0.1 copy.31
  73.7 0.6 copy.32
  74.4 0.6 copy.33
  (23 shorter events, 0.6 us)
Async XLA Ops:
  0.6 24.6 %copy-start = (bf16[256,256]{1,0:T(8,128)(2,1)S(1)}, bf16[256,256]{1,0:T(8,128)(2,1)}, u32[]{:S(2)}) copy-start(bf16[256,256]{1,0:T(8,128)(2,1)} %param.7) | copy-start | bytes 393220
  0.6 1.0 %copy-start.3 = (bf16[6,4096]{1,0:T(8,128)(2,1)S(1)}, bf16[6,4096]{1,0:T(8,128)(2,1)}, u32[]{:S(2)}) copy-start(bf16[6,4096]{1,0:T(8,128)(2,1)} %param.5) | copy-start | bytes 147460
  1.8 21.6 %copy-start.1 = (bf16[1,5,256,256]{3,2,1,0:T(8,128)(2,1)S(1)}, bf16[1,5,256,256]{3,2,1,0:T(8,128)(2,1)}, u32[]{:S(2)}) copy-start(bf16[1,5,256,256]{3,2,1,0:T(8,128)(2,1)} %param.6) | copy-start | bytes 1966084
  12.6 10.7 %all-to-all-start.1 = ((bf16[4,4,6,512]{3,1,2,0:T(4,128)(2,1)}), bf16[4,4,6,512]{3,1,2,0:T(4,128)(2,1)S(1)}, u32[]{:S(2)}, u32[]{:S(2)}) async-start(bf16[4,4,6,512]{3,1,2,0:T(4,128)(2,1)} %copy.27), calls=%async_computation.1 | async-start | bytes 196608 | tf_op jit(solution)/shard_map/all_to_all | solution.py:46
  24.2 0.9 %copy-start.2 = (bf16[256,256]{1,0:T(8,128)(2,1)S(1)}, bf16[256,256]{1,0:T(8,128)(2,1)}, u32[]{:S(2)}) copy-start(bf16[256,256]{1,0:T(8,128)(2,1)} %param.8) | copy-start | bytes 393220
  26.1 8.5 %all-to-all-start.2 = ((bf16[4,24,512]{2,1,0:T(8,128)(2,1)}), bf16[4,24,512]{2,1,0:T(8,128)(2,1)S(1)}, u32[]{:S(2)}, u32[]{:S(2)}) async-start(bf16[4,24,512]{2,1,0:T(8,128)(2,1)} %pad_maximum_fusion.4), calls=%async_computation.2 | async-start | bytes 196608 | tf_op jit(solution)/shard_map/all_to_all | solution.py:52
  29.4 10.0 %collective-permute-start.3 = (bf16[96,512]{1,0:T(8,128)(2,1)S(1)}, bf16[96,512]{1,0:T(8,128)(2,1)S(1)}, u32[]{:S(2)}, u32[]{:S(2)}) collective-permute-start(bf16[96,512]{1,0:T(8,128)(2,1)S(1)} %get-tuple-element.18), channel_id=1, source_target_pairs={{0,16},{2,18},{4,20},{6,22},{8,24},{10,26},{12,28},{14,30},{16,0},... | collective-permute-start | bytes 294920 | tf_op jit(solution)/shard_map/ppermute | solution.py:10
  30.3 9.1 %collective-permute-start.2 = (bf16[96,512]{1,0:T(8,128)(2,1)S(1)}, bf16[96,512]{1,0:T(8,128)(2,1)S(1)}, u32[]{:S(2)}, u32[]{:S(2)}) collective-permute-start(bf16[96,512]{1,0:T(8,128)(2,1)S(1)} %get-tuple-element.20), channel_id=1, source_target_pairs={{0,8},{2,10},{4,12},{6,14},{8,0},{10,2},{12,4},{14,6},{16,24},{18,... | collective-permute-start | bytes 294920 | tf_op jit(solution)/shard_map/ppermute | solution.py:10
  31.1 8.3 %collective-permute-start.1 = (bf16[96,512]{1,0:T(8,128)(2,1)S(1)}, bf16[96,512]{1,0:T(8,128)(2,1)S(1)}, u32[]{:S(2)}, u32[]{:S(2)}) collective-permute-start(bf16[96,512]{1,0:T(8,128)(2,1)S(1)} %get-tuple-element.19), channel_id=1, source_target_pairs={{0,4},{2,6},{4,0},{6,2},{8,12},{10,14},{12,8},{14,10},{16,20},{18,... | collective-permute-start | bytes 294920 | tf_op jit(solution)/shard_map/ppermute | solution.py:10
  33.1 6.3 %collective-permute-start = (bf16[96,512]{1,0:T(8,128)(2,1)S(1)}, bf16[96,512]{1,0:T(8,128)(2,1)S(1)}, u32[]{:S(2)}, u32[]{:S(2)}) collective-permute-start(bf16[96,512]{1,0:T(8,128)(2,1)S(1)} %get-tuple-element.17), channel_id=1, source_target_pairs={{0,2},{2,0},{4,6},{6,4},{8,10},{10,8},{12,14},{14,12},{16,18},{18,... | collective-permute-start | bytes 294920 | tf_op jit(solution)/shard_map/ppermute | solution.py:10
  35.3 9.9 %all-to-all-start.3 = ((bf16[4,24,512]{2,1,0:T(8,128)(2,1)}), bf16[4,24,512]{2,1,0:T(8,128)(2,1)S(1)}, u32[]{:S(2)}, u32[]{:S(2)}) async-start(bf16[4,24,512]{2,1,0:T(8,128)(2,1)} %broadcast_in_dim.4), calls=%async_computation.3 | async-start | bytes 196608 | tf_op jit(solution)/shard_map/all_to_all | solution.py:46
  39.5 19.7 %collective-permute-start.4 = (bf16[96,1024]{1,0:T(8,128)(2,1)S(1)}, bf16[96,1024]{1,0:T(8,128)(2,1)S(1)}, u32[]{:S(2)}, u32[]{:S(2)}) collective-permute-start(bf16[96,1024]{1,0:T(8,128)(2,1)S(1)} %get-tuple-element.8), channel_id=1, source_target_pairs={{0,1},{1,0},{2,3},{3,2},{4,5},{5,4},{6,7},{7,6},{8,9},{9,8},{10,11... | collective-permute-start | bytes 589832 | tf_op jit(solution)/shard_map/ppermute | solution.py:14
  45.9 8.2 %all-to-all-start.4 = ((bf16[4,24,512]{2,1,0:T(8,128)(2,1)}), bf16[4,24,512]{2,1,0:T(8,128)(2,1)S(1)}, u32[]{:S(2)}, u32[]{:S(2)}) async-start(bf16[4,24,512]{2,1,0:T(8,128)(2,1)} %broadcast_in_dim.5), calls=%async_computation.4 | async-start | bytes 196608 | tf_op jit(solution)/shard_map/all_to_all | solution.py:52
  55.6 9.1 %all-to-all-start.5 = ((bf16[4,4,6,512]{3,1,2,0:T(4,128)(2,1)}), bf16[4,4,6,512]{3,1,2,0:T(4,128)(2,1)S(1)}, u32[]{:S(2)}, u32[]{:S(2)}) async-start(bf16[4,4,6,512]{3,1,2,0:T(4,128)(2,1)} %copy.29), calls=%async_computation.5 | async-start | bytes 196608 | tf_op jit(solution)/shard_map/all_to_all | solution.py:46
  59.0 1.9 %collective-permute-start.5 = (bf16[96,256]{1,0:T(8,128)(2,1)S(1)}, bf16[96,256]{1,0:T(8,128)(2,1)S(1)}, u32[]{:S(2)}, u32[]{:S(2)}) collective-permute-start(bf16[96,256]{1,0:T(8,128)(2,1)S(1)} %pad_maximum_fusion.6), channel_id=1, source_target_pairs={{0,1},{1,0},{2,3},{3,2},{4,5},{5,4},{6,7},{7,6},{8,9},{9,8},{10,11... | collective-permute-start | bytes 147464 | tf_op jit(solution)/shard_map/ppermute | solution.py:14
  65.4 8.2 %all-to-all-start.6 = ((bf16[4,4,6,512]{3,1,2,0:T(4,128)(2,1)}), bf16[4,4,6,512]{3,1,2,0:T(4,128)(2,1)S(1)}, u32[]{:S(2)}, u32[]{:S(2)}) async-start(bf16[4,4,6,512]{3,1,2,0:T(4,128)(2,1)} %copy.30), calls=%async_computation.6 | async-start | bytes 196608 | tf_op jit(solution)/shard_map/all_to_all | solution.py:52

commit v3 on v1

--- a/solution.py
+++ b/solution.py
@@ -35,15 +35,28 @@
 
 
 def sum_over_hid(part):
-    bits = (lax.axis_size("hid") - 1).bit_length()
-    total = part
-    for low in range(0, bits, 2):
-        sent = total.astype(jnp.bfloat16)
-        masks = [1 << low]
-        if low + 1 < bits:
-            masks += [2 << low, 3 << low]
-        total = total + sum(exchange(sent, mask).astype(jnp.float32) for mask in masks)
-    return total.astype(jnp.bfloat16)
+    hid = lax.axis_size("hid")
+    low = 1 << ((hid - 1).bit_length() // 2)
+    rows = part.shape[0] // low
+    place = lax.axis_index("hid") % low
+    sent = part.astype(jnp.bfloat16)
+
+    def take(x, at):
+        return lax.dynamic_slice_in_dim(x, at * rows, rows, 0)
+
+    piece = take(part, place)
+    got = [exchange(take(sent, place ^ mask), mask) for mask in range(1, low)]
+    got = lax.optimization_barrier(got)
+    piece = piece + sum(x.astype(jnp.float32) for x in got)
+    sent = piece.astype(jnp.bfloat16)
+    got = [exchange(sent, mask) for mask in range(low, hid, low)]
+    got = lax.optimization_barrier(got)
+    piece = (piece + sum(x.astype(jnp.float32) for x in got)).astype(jnp.bfloat16)
+    got = [exchange(piece, mask) for mask in range(1, low)]
+    total = jnp.zeros(part.shape, jnp.bfloat16)
+    for mask, x in enumerate(lax.optimization_barrier([piece] + got)):
+        total = lax.dynamic_update_slice_in_dim(total, x, (place ^ mask) * rows, 0)
+    return total
 
 
 def half(x, which):
@@ -86,15 +99,17 @@
     grad_act = (back + dot_t(dlatent, low_u)).astype(jnp.bfloat16)
     grad_pre_rows = pullback(grad_act.astype(jnp.float32))[0].astype(jnp.bfloat16)
     results = jnp.concatenate([output_rows, grad_pre_rows], axis=1)
+    other = 1 - core
+    sent = jnp.concatenate(
+        [grad, act] + [half(x, other) for x in acts[1:]], axis=1
+    )
+    sent_latents = jnp.concatenate([half(latent, other), half(dlatent, other)], axis=1)
+    results, sent, sent_latents = lax.optimization_barrier((results, sent, sent_latents))
     results = lax.all_to_all(results, "hid", split_axis=0, concat_axis=1, tiled=True)
     results = results.reshape(tokens, hid, 2 * side)
     output = results[:, :, :side].reshape(tokens, hid * side)
     grad_pre = results[:, :, side:].reshape(tokens, hid * side)
 
-    other = 1 - core
-    sent = jnp.concatenate(
-        [grad, act] + [half(x, other) for x in acts[1:]], axis=1
-    )
     got = mate(sent)
     own = jnp.concatenate([half(x, core) for x in acts], axis=1)
     far = jnp.concatenate(
@@ -102,7 +117,7 @@
     )
     grad_butterfly = (inner_rows(own, grad) + inner_rows(far, got[:, :side])) * factor
     grad_butterfly = grad_butterfly.reshape(1, levels + 1, side // 2, side)
-    far_latents = mate(jnp.concatenate([half(latent, other), half(dlatent, other)], axis=1))
+    far_latents = mate(sent_latents)
     far_latent, far_dlatent = far_latents[:, : rank // 2], far_latents[:, rank // 2 :]
     grad_low_u = (
         inner_rows(act, half(dlatent, core)) + inner_rows(got[:, side : 2 * side], far_dlatent)

time: 52.9 us -> 63.3 us (1.20)
  waiting for transfers between devices: 16.6 us -> 23 us
  starting transfers between devices: 25.6 us -> 28.9 us
  local copies, waits for them, and re-layouts: 1.43 us -> 2.22 us
    ppermute x10 -> x13, waiting for transfers between devices: 4.51 us -> 8.24 us  [exchange(): lax.ppermute(x, 'hid', [(i, i ^ mask) for i in range(lax.axis_size('hid'))])]
    all_to_all x1, waiting for transfers between devices: 4.35 us -> 7.02 us  [on_device(): lax.all_to_all(results, 'hid', split_axis=0, concat_axis=1, tiled=True)]
    ppermute x10 -> x13, starting transfers between devices: 12.6 us -> 15.1 us  [exchange(): lax.ppermute(x, 'hid', [(i, i ^ mask) for i in range(lax.axis_size('hid'))])]
    unnamed x7, local copies, waits for them, and re-layouts: 0.05 us -> 0.76 us
  transfers between devices with their start and end apart: 14 -> 17, of which waited for: 5 -> 10; matrix products, arithmetic and copies ran while one was open for 11% -> 5% of each run, Pallas kernels for 0% -> 0%
where the time goes in v3:
time: 63.3 us; the launch traced here: 63 us
  starting transfers between devices  28.9 us (46%)
  waiting for transfers between devices  23 us (36%)
  matrix products  5.84 us (9%)
  local copies, waits for them, and re-layouts  2.22 us (4%)
  other arithmetic  1.94 us (3%)
  between operations  1.06 us (2%)
    ppermute x13, starting transfers between devices, exchange(): lax.ppermute(x, 'hid', [(i, i ^ mask) for i in range(lax.axis_size('hid'))])  15.1 us
    all_to_all x1, starting transfers between devices, on_device(): rows = lax.all_to_all(both, 'hid', split_axis=1, concat_axis=0, tiled=True)  8.31 us
    ppermute x13, waiting for transfers between devices, exchange(): lax.ppermute(x, 'hid', [(i, i ^ mask) for i in range(lax.axis_size('hid'))])  8.24 us
    all_to_all x1, waiting for transfers between devices, on_device(): rows = lax.all_to_all(both, 'hid', split_axis=1, concat_axis=0, tiled=True)  7.75 us
    all_to_all x1, waiting for transfers between devices, on_device(): lax.all_to_all(results, 'hid', split_axis=0, concat_axis=1, tiled=True)  7.02 us
    all_to_all x1, starting transfers between devices, on_device(): lax.all_to_all(results, 'hid', split_axis=0, concat_axis=1, tiled=True)  4.86 us
    dot_general x6, matrix products, inner_rows(): lax.dot_general(left, right, (((0,), (0,)), ((), ())), preferred_element_...  3.54 us
    concatenate x1, other arithmetic, on_device(): jnp.concatenate([pre_act.reshape(tokens, hid, side), grad_out.reshape(tok...  1.62 us
  transfers between devices with their start and end apart: 17, of which 10 were waited for; matrix products, arithmetic and copies ran while one was open for 5% of the time, Pallas kernels for 0%

profile of v3, /device:TPU:0, one launch (start us, length us, event | category | flops | bytes accessed | tf_op | source)
XLA Modules:
  0.0 63.0 jit_solution(4120195933960492599)
XLA Ops:
  0.6 0.0 copy-start
  0.6 0.0 copy-start.1
  0.7 1.6 %pad_maximum_fusion.5 = bf16[6,16,512]{2,0,1:T(8,128)(2,1)} fusion(bf16[6,16,256]{2,0,1:T(8,128)(2,1)} %bitcast.40, bf16[6,16,256]{2,0,1:T(8,128)(2,1)} %bitcast.41), kind=kLoop, calls=%fused_computation.30 | loop fusion | flops 196608 | bytes 196608 | tf_op jit(solution)/shard_map/concatenate | solution.py:76
  2.3 8.3 %all-to-all-start = ((bf16[6,16,512]{2,0,1:T(8,128)(2,1)}), bf16[6,16,512]{2,0,1:T(8,128)(2,1)S(1)}, u32[]{:S(2)}, u32[]{:S(2)}) async-start(bf16[6,16,512]{2,0,1:T(8,128)(2,1)} %pad_maximum_fusion.5), calls=%async_computation | async-start | bytes 262144 | tf_op jit(solution)/shard_map/all_to_all | solution.py:79
  10.6 7.8 %all-to-all-done = bf16[6,16,512]{2,0,1:T(8,128)(2,1)S(1)} async-done(((bf16[6,16,512]{2,0,1:T(8,128)(2,1)}), bf16[6,16,512]{2,0,1:T(8,128)(2,1)S(1)}, u32[]{:S(2)}, u32[]{:S(2)}) %all-to-all-start) | async-done | bytes 98336 | tf_op jit(solution)/shard_map/all_to_all | solution.py:79
  18.5 0.0 copy-done.1
  18.5 0.2 fusion.19
  18.7 0.2 convolution_convert_fusion.3
  18.9 0.2 convolution_convert_fusion.2
  19.1 0.2 convolution_convert_fusion.1
  19.3 0.2 convolution_convert_fusion
  19.5 0.2 fusion.21
  19.6 0.0 copy-done
  19.7 0.0 copy-start.2
  19.7 0.2 fusion.78
  19.8 0.7 %copy-done.2 = bf16[256,256]{1,0:T(8,128)(2,1)S(1)} copy-done((bf16[256,256]{1,0:T(8,128)(2,1)S(1)}, bf16[256,256]{1,0:T(8,128)(2,1)}, u32[]{:S(2)}) %copy-start.2) | copy-done | bytes 131096
  20.6 0.2 fusion.85
  20.8 1.2 %collective-permute-start.4 = (bf16[24,512]{1,0:T(8,128)(2,1)S(1)}, bf16[24,512]{1,0:T(8,128)(2,1)S(1)}, u32[]{:S(2)}, u32[]{:S(2)}) collective-permute-start(bf16[24,512]{1,0:T(8,128)(2,1)S(1)} %get-tuple-element.47), channel_id=1, source_target_pairs={{0,2},{2,0},{4,6},{6,4},{8,10},{10,8},{12,14},{14,12},{16,18},{18,... | collective-permute-start | bytes 73736 | tf_op jit(solution)/shard_map/ppermute | solution.py:10
  21.9 0.2 collective-permute-start.5
  22.2 2.2 %collective-permute-start.6 = (bf16[24,512]{1,0:T(8,128)(2,1)S(1)}, bf16[24,512]{1,0:T(8,128)(2,1)S(1)}, u32[]{:S(2)}, u32[]{:S(2)}) collective-permute-start(bf16[24,512]{1,0:T(8,128)(2,1)S(1)} %get-tuple-element.45), channel_id=1, source_target_pairs={{0,6},{2,4},{4,2},{6,0},{8,14},{10,12},{12,10},{14,8},{16,22},{18,... | collective-permute-start | bytes 73736 | tf_op jit(solution)/shard_map/ppermute | solution.py:10
  24.4 1.0 %collective-permute-start.3 = (bf16[96,512]{1,0:T(8,128)(2,1)S(1)}, bf16[96,512]{1,0:T(8,128)(2,1)S(1)}, u32[]{:S(2)}, u32[]{:S(2)}) collective-permute-start(bf16[96,512]{1,0:T(8,128)(2,1)S(1)} %get-tuple-element.51), channel_id=1, source_target_pairs={{0,16},{2,18},{4,20},{6,22},{8,24},{10,26},{12,28},{14,30},{16,0},... | collective-permute-start | bytes 294920 | tf_op jit(solution)/shard_map/ppermute | solution.py:10
  25.4 0.9 %collective-permute-start.2 = (bf16[96,512]{1,0:T(8,128)(2,1)S(1)}, bf16[96,512]{1,0:T(8,128)(2,1)S(1)}, u32[]{:S(2)}, u32[]{:S(2)}) collective-permute-start(bf16[96,512]{1,0:T(8,128)(2,1)S(1)} %get-tuple-element.50), channel_id=1, source_target_pairs={{0,8},{2,10},{4,12},{6,14},{8,0},{10,2},{12,4},{14,6},{16,24},{18,... | collective-permute-start | bytes 294920 | tf_op jit(solution)/shard_map/ppermute | solution.py:10
  26.3 0.0 collective-permute-done.4
  26.3 0.0 collective-permute-done.5
  26.3 0.6 collective-permute-done.6
  26.9 0.8 %collective-permute-start.7 = (bf16[24,512]{1,0:T(8,128)(2,1)S(1)}, bf16[24,512]{1,0:T(8,128)(2,1)S(1)}, u32[]{:S(2)}, u32[]{:S(2)}) collective-permute-start(bf16[24,512]{1,0:T(8,128)(2,1)S(1)} %get-tuple-element.31), channel_id=1, source_target_pairs={{0,8},{2,10},{4,12},{6,14},{8,0},{10,2},{12,4},{14,6},{16,24},{18,... | collective-permute-start | bytes 73736 | tf_op jit(solution)/shard_map/ppermute | solution.py:10
  27.7 1.8 %collective-permute-start.8 = (bf16[24,512]{1,0:T(8,128)(2,1)S(1)}, bf16[24,512]{1,0:T(8,128)(2,1)S(1)}, u32[]{:S(2)}, u32[]{:S(2)}) collective-permute-start(bf16[24,512]{1,0:T(8,128)(2,1)S(1)} %get-tuple-element.31), channel_id=1, source_target_pairs={{0,16},{2,18},{4,20},{6,22},{8,24},{10,26},{12,28},{14,30},{16,0},... | collective-permute-start | bytes 73736 | tf_op jit(solution)/shard_map/ppermute | solution.py:10
  29.5 1.9 %collective-permute-start.9 = (bf16[24,512]{1,0:T(8,128)(2,1)S(1)}, bf16[24,512]{1,0:T(8,128)(2,1)S(1)}, u32[]{:S(2)}, u32[]{:S(2)}) collective-permute-start(bf16[24,512]{1,0:T(8,128)(2,1)S(1)} %get-tuple-element.31), channel_id=1, source_target_pairs={{0,24},{2,26},{4,28},{6,30},{8,16},{10,18},{12,20},{14,22},{16,8},... | collective-permute-start | bytes 73736 | tf_op jit(solution)/shard_map/ppermute | solution.py:10
  31.4 0.4 collective-permute-done.7
  31.8 0.6 collective-permute-done.8
  32.4 2.7 %collective-permute-done.9 = bf16[24,512]{1,0:T(8,128)(2,1)S(1)} collective-permute-done((bf16[24,512]{1,0:T(8,128)(2,1)S(1)}, bf16[24,512]{1,0:T(8,128)(2,1)S(1)}, u32[]{:S(2)}, u32[]{:S(2)}) %collective-permute-start.9) | collective-permute-done | bytes 24608 | tf_op jit(solution)/shard_map/ppermute | solution.py:10
  35.1 1.2 %collective-permute-start.10 = (bf16[24,512]{1,0:T(8,128)(2,1)S(1)}, bf16[24,512]{1,0:T(8,128)(2,1)S(1)}, u32[]{:S(2)}, u32[]{:S(2)}) collective-permute-start(bf16[24,512]{1,0:T(8,128)(2,1)S(1)} %add_convert_fusion.1), channel_id=1, source_target_pairs={{0,2},{2,0},{4,6},{6,4},{8,10},{10,8},{12,14},{14,12},{16,18},{18,... | collective-permute-start | bytes 73736 | tf_op jit(solution)/shard_map/ppermute | solution.py:10
  36.3 1.0 %collective-permute-start.11 = (bf16[24,512]{1,0:T(8,128)(2,1)S(1)}, bf16[24,512]{1,0:T(8,128)(2,1)S(1)}, u32[]{:S(2)}, u32[]{:S(2)}) collective-permute-start(bf16[24,512]{1,0:T(8,128)(2,1)S(1)} %add_convert_fusion.1), channel_id=1, source_target_pairs={{0,4},{2,6},{4,0},{6,2},{8,12},{10,14},{12,8},{14,10},{16,20},{18,... | collective-permute-start | bytes 73736 | tf_op jit(solution)/shard_map/ppermute | solution.py:10
  37.2 1.4 %collective-permute-start.12 = (bf16[24,512]{1,0:T(8,128)(2,1)S(1)}, bf16[24,512]{1,0:T(8,128)(2,1)S(1)}, u32[]{:S(2)}, u32[]{:S(2)}) collective-permute-start(bf16[24,512]{1,0:T(8,128)(2,1)S(1)} %add_convert_fusion.1), channel_id=1, source_target_pairs={{0,6},{2,4},{4,2},{6,0},{8,14},{10,12},{12,10},{14,8},{16,22},{18,... | collective-permute-start | bytes 73736 | tf_op jit(solution)/shard_map/ppermute | solution.py:10
  38.7 0.3 collective-permute-done.10
  39.0 0.7 %collective-permute-start.1 = (bf16[96,512]{1,0:T(8,128)(2,1)S(1)}, bf16[96,512]{1,0:T(8,128)(2,1)S(1)}, u32[]{:S(2)}, u32[]{:S(2)}) collective-permute-start(bf16[96,512]{1,0:T(8,128)(2,1)S(1)} %get-tuple-element.49), channel_id=1, source_target_pairs={{0,4},{2,6},{4,0},{6,2},{8,12},{10,14},{12,8},{14,10},{16,20},{18,... | collective-permute-start | bytes 294920 | tf_op jit(solution)/shard_map/ppermute | solution.py:10
  39.8 0.4 collective-permute-done.11
  40.1 1.0 %collective-permute-start = (bf16[96,512]{1,0:T(8,128)(2,1)S(1)}, bf16[96,512]{1,0:T(8,128)(2,1)S(1)}, u32[]{:S(2)}, u32[]{:S(2)}) collective-permute-start(bf16[96,512]{1,0:T(8,128)(2,1)S(1)} %get-tuple-element.48), channel_id=1, source_target_pairs={{0,2},{2,0},{4,6},{6,4},{8,10},{10,8},{12,14},{14,12},{16,18},{18,... | collective-permute-start | bytes 294920 | tf_op jit(solution)/shard_map/ppermute | solution.py:10
  41.1 0.9 %collective-permute-done.12 = bf16[24,512]{1,0:T(8,128)(2,1)S(1)} collective-permute-done((bf16[24,512]{1,0:T(8,128)(2,1)S(1)}, bf16[24,512]{1,0:T(8,128)(2,1)S(1)}, u32[]{:S(2)}, u32[]{:S(2)}) %collective-permute-start.12) | collective-permute-done | bytes 24608 | tf_op jit(solution)/shard_map/ppermute | solution.py:10
  42.1 0.1 fusion.54
  42.2 0.2 fusion.67
  42.4 2.3 %collective-permute-done = bf16[96,512]{1,0:T(8,128)(2,1)S(1)} collective-permute-done((bf16[96,512]{1,0:T(8,128)(2,1)S(1)}, bf16[96,512]{1,0:T(8,128)(2,1)S(1)}, u32[]{:S(2)}, u32[]{:S(2)}) %collective-permute-start) | collective-permute-done | bytes 98336 | tf_op jit(solution)/shard_map/ppermute | solution.py:10
  44.7 0.2 convolution_add_fusion.4
  44.9 0.0 collective-permute-done.3
  44.9 0.1 fusion.9
  45.1 0.0 collective-permute-done.2
  45.1 0.1 fusion.12
  45.2 0.0 collective-permute-done.1
  45.2 0.2 fusion.39
  45.5 0.2 fusion.6
  45.8 0.7 %all_to_all.27 = bf16[16,6,512]{2,1,0:T(8,128)(2,1)} reshape(bf16[96,512]{1,0:T(8,128)(2,1)S(1)} %pad_maximum_fusion.6) | data formatting | bytes 196608 | tf_op jit(solution)/shard_map/all_to_all | solution.py:108
  46.5 4.9 %all-to-all-start.1 = ((bf16[16,6,512]{2,1,0:T(8,128)(2,1)}), bf16[16,6,512]{2,1,0:T(8,128)(2,1)S(1)}, u32[]{:S(2)}, u32[]{:S(2)}) async-start(bf16[16,6,512]{2,1,0:T(8,128)(2,1)} %all_to_all.27), calls=%async_computation.1 | async-start | bytes 262144 | tf_op jit(solution)/shard_map/all_to_all | solution.py:108
  51.4 0.2 fusion.65
  51.6 0.1 collective-permute-start.13
  51.6 0.5 collective-permute-start.14
  52.1 7.0 %all-to-all-done.1 = bf16[16,6,512]{2,1,0:T(8,128)(2,1)S(1)} async-done(((bf16[16,6,512]{2,1,0:T(8,128)(2,1)}), bf16[16,6,512]{2,1,0:T(8,128)(2,1)S(1)}, u32[]{:S(2)}, u32[]{:S(2)}) %all-to-all-start.1) | async-done | bytes 98336 | tf_op jit(solution)/shard_map/all_to_all | solution.py:108
  59.2 0.7 %fusion.91 = (bf16[6,16,256]{2,0,1:T(8,128)(2,1)}, bf16[6,16,256]{2,0,1:T(8,128)(2,1)}) fusion(bf16[6,16,512]{2,0,1:T(8,128)(2,1)S(1)} %bitcast.39), kind=kLoop, calls=%fused_computation.133 | loop fusion | bytes 196608 | tf_op jit(solution)/shard_map/slice | solution.py:111
  59.8 0.0 collective-permute-done.13
  59.9 0.3 fusion.23
  60.1 1.1 %fusion = f32[640,256]{1,0:T(8,128)} fusion(f32[640,256]{1,0:T(8,128)S(1)} %fusion.23, bf16[96,640]{1,0:T(8,128)(2,1)S(1)} %get-tuple-element.35, bf16[96,512]{1,0:T(8,128)(2,1)S(1)} %all_to_all.26), kind=kOutput, calls=%fused_computation.1 | convolution fusion | flops 31784960 | bytes 1482752 | tf_op jit(solution)/shard_map/dot_general | solution.py:32
  61.3 0.0 collective-permute-done.14
  61.3 0.9 %fusion.2 = f32[256,128]{1,0:T(8,128)} fusion(f32[256,128]{1,0:T(8,128)S(1)} %fusion.67, bf16[96,1024]{1,0:T(8,128)(2,1)S(1)} %collective-permute-done.13, bf16[96,256]{1,0:T(8,128)(2,1)S(1)} %collective-permute-done.14), kind=kOutput, calls=%fused_computation.5 | convolution fusion | flops 6356992 | bytes 335872 | tf_op jit(solution)/shard_map/dot_general | solution.py:32
  62.1 0.9 %fusion.1 = f32[128,256]{1,0:T(8,128)} fusion(f32[128,256]{1,0:T(8,128)S(1)} %fusion.65, bf16[96,1024]{1,0:T(8,128)(2,1)S(1)} %collective-permute-done.13, bf16[96,256]{1,0:T(8,128)(2,1)S(1)} %collective-permute-done.14), kind=kOutput, calls=%fused_computation.3 | convolution fusion | flops 6356992 | bytes 335872 | tf_op jit(solution)/shard_map/dot_general | solution.py:32
  (23 shorter events, 0.4 us)
Async XLA Ops:
  0.6 19.0 %copy-start = (bf16[256,256]{1,0:T(8,128)(2,1)S(1)}, bf16[256,256]{1,0:T(8,128)(2,1)}, u32[]{:S(2)}) copy-start(bf16[256,256]{1,0:T(8,128)(2,1)} %param.8) | copy-start | bytes 393220
  0.6 17.8 %copy-start.1 = (bf16[1,5,256,256]{3,2,1,0:T(8,128)(2,1)S(1)}, bf16[1,5,256,256]{3,2,1,0:T(8,128)(2,1)}, u32[]{:S(2)}) copy-start(bf16[1,5,256,256]{3,2,1,0:T(8,128)(2,1)} %param.6) | copy-start | bytes 1966084
  2.3 16.1 %all-to-all-start = ((bf16[6,16,512]{2,0,1:T(8,128)(2,1)}), bf16[6,16,512]{2,0,1:T(8,128)(2,1)S(1)}, u32[]{:S(2)}, u32[]{:S(2)}) async-start(bf16[6,16,512]{2,0,1:T(8,128)(2,1)} %pad_maximum_fusion.5), calls=%async_computation | async-start | bytes 262144 | tf_op jit(solution)/shard_map/all_to_all | solution.py:79
  19.7 0.9 %copy-start.2 = (bf16[256,256]{1,0:T(8,128)(2,1)S(1)}, bf16[256,256]{1,0:T(8,128)(2,1)}, u32[]{:S(2)}) copy-start(bf16[256,256]{1,0:T(8,128)(2,1)} %param.7) | copy-start | bytes 393220
  20.8 5.5 %collective-permute-start.4 = (bf16[24,512]{1,0:T(8,128)(2,1)S(1)}, bf16[24,512]{1,0:T(8,128)(2,1)S(1)}, u32[]{:S(2)}, u32[]{:S(2)}) collective-permute-start(bf16[24,512]{1,0:T(8,128)(2,1)S(1)} %get-tuple-element.47), channel_id=1, source_target_pairs={{0,2},{2,0},{4,6},{6,4},{8,10},{10,8},{12,14},{14,12},{16,18},{18,... | collective-permute-start | bytes 73736 | tf_op jit(solution)/shard_map/ppermute | solution.py:10
  21.9 4.3 %collective-permute-start.5 = (bf16[24,512]{1,0:T(8,128)(2,1)S(1)}, bf16[24,512]{1,0:T(8,128)(2,1)S(1)}, u32[]{:S(2)}, u32[]{:S(2)}) collective-permute-start(bf16[24,512]{1,0:T(8,128)(2,1)S(1)} %get-tuple-element.46), channel_id=1, source_target_pairs={{0,4},{2,6},{4,0},{6,2},{8,12},{10,14},{12,8},{14,10},{16,20},{18,... | collective-permute-start | bytes 73736 | tf_op jit(solution)/shard_map/ppermute | solution.py:10
  22.2 4.7 %collective-permute-start.6 = (bf16[24,512]{1,0:T(8,128)(2,1)S(1)}, bf16[24,512]{1,0:T(8,128)(2,1)S(1)}, u32[]{:S(2)}, u32[]{:S(2)}) collective-permute-start(bf16[24,512]{1,0:T(8,128)(2,1)S(1)} %get-tuple-element.45), channel_id=1, source_target_pairs={{0,6},{2,4},{4,2},{6,0},{8,14},{10,12},{12,10},{14,8},{16,22},{18,... | collective-permute-start | bytes 73736 | tf_op jit(solution)/shard_map/ppermute | solution.py:10
  24.4 20.5 %collective-permute-start.3 = (bf16[96,512]{1,0:T(8,128)(2,1)S(1)}, bf16[96,512]{1,0:T(8,128)(2,1)S(1)}, u32[]{:S(2)}, u32[]{:S(2)}) collective-permute-start(bf16[96,512]{1,0:T(8,128)(2,1)S(1)} %get-tuple-element.51), channel_id=1, source_target_pairs={{0,16},{2,18},{4,20},{6,22},{8,24},{10,26},{12,28},{14,30},{16,0},... | collective-permute-start | bytes 294920 | tf_op jit(solution)/shard_map/ppermute | solution.py:10
  25.4 19.7 %collective-permute-start.2 = (bf16[96,512]{1,0:T(8,128)(2,1)S(1)}, bf16[96,512]{1,0:T(8,128)(2,1)S(1)}, u32[]{:S(2)}, u32[]{:S(2)}) collective-permute-start(bf16[96,512]{1,0:T(8,128)(2,1)S(1)} %get-tuple-element.50), channel_id=1, source_target_pairs={{0,8},{2,10},{4,12},{6,14},{8,0},{10,2},{12,4},{14,6},{16,24},{18,... | collective-permute-start | bytes 294920 | tf_op jit(solution)/shard_map/ppermute | solution.py:10
  26.9 4.9 %collective-permute-start.7 = (bf16[24,512]{1,0:T(8,128)(2,1)S(1)}, bf16[24,512]{1,0:T(8,128)(2,1)S(1)}, u32[]{:S(2)}, u32[]{:S(2)}) collective-permute-start(bf16[24,512]{1,0:T(8,128)(2,1)S(1)} %get-tuple-element.31), channel_id=1, source_target_pairs={{0,8},{2,10},{4,12},{6,14},{8,0},{10,2},{12,4},{14,6},{16,24},{18,... | collective-permute-start | bytes 73736 | tf_op jit(solution)/shard_map/ppermute | solution.py:10
  27.7 4.7 %collective-permute-start.8 = (bf16[24,512]{1,0:T(8,128)(2,1)S(1)}, bf16[24,512]{1,0:T(8,128)(2,1)S(1)}, u32[]{:S(2)}, u32[]{:S(2)}) collective-permute-start(bf16[24,512]{1,0:T(8,128)(2,1)S(1)} %get-tuple-element.31), channel_id=1, source_target_pairs={{0,16},{2,18},{4,20},{6,22},{8,24},{10,26},{12,28},{14,30},{16,0},... | collective-permute-start | bytes 73736 | tf_op jit(solution)/shard_map/ppermute | solution.py:10
  29.5 5.6 %collective-permute-start.9 = (bf16[24,512]{1,0:T(8,128)(2,1)S(1)}, bf16[24,512]{1,0:T(8,128)(2,1)S(1)}, u32[]{:S(2)}, u32[]{:S(2)}) collective-permute-start(bf16[24,512]{1,0:T(8,128)(2,1)S(1)} %get-tuple-element.31), channel_id=1, source_target_pairs={{0,24},{2,26},{4,28},{6,30},{8,16},{10,18},{12,20},{14,22},{16,8},... | collective-permute-start | bytes 73736 | tf_op jit(solution)/shard_map/ppermute | solution.py:10
  35.1 3.9 %collective-permute-start.10 = (bf16[24,512]{1,0:T(8,128)(2,1)S(1)}, bf16[24,512]{1,0:T(8,128)(2,1)S(1)}, u32[]{:S(2)}, u32[]{:S(2)}) collective-permute-start(bf16[24,512]{1,0:T(8,128)(2,1)S(1)} %add_convert_fusion.1), channel_id=1, source_target_pairs={{0,2},{2,0},{4,6},{6,4},{8,10},{10,8},{12,14},{14,12},{16,18},{18,... | collective-permute-start | bytes 73736 | tf_op jit(solution)/shard_map/ppermute | solution.py:10
  36.3 3.8 %collective-permute-start.11 = (bf16[24,512]{1,0:T(8,128)(2,1)S(1)}, bf16[24,512]{1,0:T(8,128)(2,1)S(1)}, u32[]{:S(2)}, u32[]{:S(2)}) collective-permute-start(bf16[24,512]{1,0:T(8,128)(2,1)S(1)} %add_convert_fusion.1), channel_id=1, source_target_pairs={{0,4},{2,6},{4,0},{6,2},{8,12},{10,14},{12,8},{14,10},{16,20},{18,... | collective-permute-start | bytes 73736 | tf_op jit(solution)/shard_map/ppermute | solution.py:10
  37.2 4.7 %collective-permute-start.12 = (bf16[24,512]{1,0:T(8,128)(2,1)S(1)}, bf16[24,512]{1,0:T(8,128)(2,1)S(1)}, u32[]{:S(2)}, u32[]{:S(2)}) collective-permute-start(bf16[24,512]{1,0:T(8,128)(2,1)S(1)} %add_convert_fusion.1), channel_id=1, source_target_pairs={{0,6},{2,4},{4,2},{6,0},{8,14},{10,12},{12,10},{14,8},{16,22},{18,... | collective-permute-start | bytes 73736 | tf_op jit(solution)/shard_map/ppermute | solution.py:10
  39.0 6.2 %collective-permute-start.1 = (bf16[96,512]{1,0:T(8,128)(2,1)S(1)}, bf16[96,512]{1,0:T(8,128)(2,1)S(1)}, u32[]{:S(2)}, u32[]{:S(2)}) collective-permute-start(bf16[96,512]{1,0:T(8,128)(2,1)S(1)} %get-tuple-element.49), channel_id=1, source_target_pairs={{0,4},{2,6},{4,0},{6,2},{8,12},{10,14},{12,8},{14,10},{16,20},{18,... | collective-permute-start | bytes 294920 | tf_op jit(solution)/shard_map/ppermute | solution.py:10
  40.1 4.6 %collective-permute-start = (bf16[96,512]{1,0:T(8,128)(2,1)S(1)}, bf16[96,512]{1,0:T(8,128)(2,1)S(1)}, u32[]{:S(2)}, u32[]{:S(2)}) collective-permute-start(bf16[96,512]{1,0:T(8,128)(2,1)S(1)} %get-tuple-element.48), channel_id=1, source_target_pairs={{0,2},{2,0},{4,6},{6,4},{8,10},{10,8},{12,14},{14,12},{16,18},{18,... | collective-permute-start | bytes 294920 | tf_op jit(solution)/shard_map/ppermute | solution.py:10
  46.5 12.7 %all-to-all-start.1 = ((bf16[16,6,512]{2,1,0:T(8,128)(2,1)}), bf16[16,6,512]{2,1,0:T(8,128)(2,1)S(1)}, u32[]{:S(2)}, u32[]{:S(2)}) async-start(bf16[16,6,512]{2,1,0:T(8,128)(2,1)} %all_to_all.27), calls=%async_computation.1 | async-start | bytes 262144 | tf_op jit(solution)/shard_map/all_to_all | solution.py:108
  51.6 8.3 %collective-permute-start.13 = (bf16[96,1024]{1,0:T(8,128)(2,1)S(1)}, bf16[96,1024]{1,0:T(8,128)(2,1)S(1)}, u32[]{:S(2)}, u32[]{:S(2)}) collective-permute-start(bf16[96,1024]{1,0:T(8,128)(2,1)S(1)} %get-tuple-element.29), channel_id=1, source_target_pairs={{0,1},{1,0},{2,3},{3,2},{4,5},{5,4},{6,7},{7,6},{8,9},{9,8},{10,11... | collective-permute-start | bytes 589832 | tf_op jit(solution)/shard_map/ppermute | solution.py:14
  51.6 9.6 %collective-permute-start.14 = (bf16[96,256]{1,0:T(8,128)(2,1)S(1)}, bf16[96,256]{1,0:T(8,128)(2,1)S(1)}, u32[]{:S(2)}, u32[]{:S(2)}) collective-permute-start(bf16[96,256]{1,0:T(8,128)(2,1)S(1)} %pad_maximum_fusion.7), channel_id=1, source_target_pairs={{0,1},{1,0},{2,3},{3,2},{4,5},{5,4},{6,7},{7,6},{8,9},{9,8},{10,11... | collective-permute-start | bytes 147464 | tf_op jit(solution)/shard_map/ppermute | solution.py:14

commit v4 on v1

--- a/solution.py
+++ b/solution.py
@@ -34,16 +34,27 @@
     )
 
 
-def sum_over_hid(part):
+def sum_over_hid(part, blocks):
     bits = (lax.axis_size("hid") - 1).bit_length()
-    total = part
+    width = part.shape[1]
+    total, far = part, {}
     for low in range(0, bits, 2):
         sent = total.astype(jnp.bfloat16)
-        masks = [1 << low]
-        if low + 1 < bits:
-            masks += [2 << low, 3 << low]
-        total = total + sum(exchange(sent, mask).astype(jnp.float32) for mask in masks)
-    return total.astype(jnp.bfloat16)
+        got = {}
+        for mask in range(1 << low, min(4 << low, 1 << bits), 1 << low):
+            if low == 0 and mask in blocks:
+                got[mask] = exchange(jnp.concatenate([sent, blocks[mask]], axis=1), mask)
+            else:
+                got[mask] = exchange(sent, mask)
+        if low == 0:
+            apart = {mask: exchange(blocks[mask], mask) for mask in blocks if mask not in got}
+            got = lax.optimization_barrier(got)
+            far = {mask: got[mask][:, width:] for mask in blocks if mask in got}
+        if low + 2 >= bits:
+            got, apart = lax.optimization_barrier((got, apart))
+        total = total + sum(x[:, :width].astype(jnp.float32) for x in got.values())
+    far.update(apart)
+    return total.astype(jnp.bfloat16), [far[mask] for mask in blocks]
 
 
 def half(x, which):
@@ -69,17 +80,18 @@
     act_f, pullback = jax.vjp(gelu_tanh, pre_f)
     act = act_f.astype(jnp.bfloat16)
 
-    latents = sum_over_hid(jnp.concatenate([dot(act, low_u), dot_t(grad, low_v)], axis=1))
+    part = jnp.concatenate([dot(act, low_u), dot_t(grad, low_v)], axis=1)
+    blocks = {}
+    for level in range(1, levels + 1):
+        term = dot_t(grad, butterfly[0, level]).astype(jnp.bfloat16)
+        blocks[1 << level - 1] = jnp.concatenate([act, term], axis=1)
+    latents, fars = sum_over_hid(part, blocks)
     latent, dlatent = latents[:, :rank], latents[:, rank:]
 
-    acts = [act]
-    total = dot(act, butterfly[0, 0])
+    acts = [act] + [far[:, :side] for far in fars]
+    total = dot(jnp.concatenate(acts, axis=1), butterfly[0].reshape(-1, side))
     back = dot_t(grad, butterfly[0, 0])
-    for level in range(1, levels + 1):
-        term = dot_t(grad, butterfly[0, level]).astype(jnp.bfloat16)
-        far = exchange(jnp.concatenate([act, term], axis=1), 1 << level - 1)
-        acts.append(far[:, :side])
-        total = total + dot(far[:, :side], butterfly[0, level])
+    for far in fars:
         back = back + far[:, side:].astype(jnp.float32)
 
     output_rows = (total + dot(latent, low_v)).astype(jnp.bfloat16)

time: 52.9 us -> 56 us (1.059)
  waiting for transfers between devices: 16.6 us -> 22.6 us
  starting transfers between devices: 25.6 us -> 22.5 us
  local copies, waits for them, and re-layouts: 1.43 us -> 2.18 us
  matrix products: 5.87 us -> 5.29 us
    ppermute x10 -> x8, waiting for transfers between devices: 4.51 us -> 8.19 us  [exchange(): lax.ppermute(x, 'hid', [(i, i ^ mask) for i in range(lax.axis_size('hid'))])]
    ppermute x10 -> x8, starting transfers between devices: 12.6 us -> 9.96 us  [exchange(): lax.ppermute(x, 'hid', [(i, i ^ mask) for i in range(lax.axis_size('hid'))])]
    all_to_all x1, waiting for transfers between devices: 4.35 us -> 6.62 us  [on_device(): lax.all_to_all(results, 'hid', split_axis=0, concat_axis=1, tiled=True)]
    all_to_all x1, starting transfers between devices: 4.41 us -> 3.63 us  [on_device(): lax.all_to_all(results, 'hid', split_axis=0, concat_axis=1, tiled=True)]
    unnamed x7 -> x10, local copies, waits for them, and re-layouts: 0.05 us -> 0.77 us
  transfers between devices with their start and end apart: 14 -> 12, of which waited for: 5 -> 7; matrix products, arithmetic and copies ran while one was open for 11% -> 3% of each run, Pallas kernels for 0% -> 0%
where the time goes in v4:
time: 56 us; the launch traced here: 55.7 us
  waiting for transfers between devices  22.6 us (40%)
  starting transfers between devices  22.5 us (40%)
  matrix products  5.29 us (9%)
  local copies, waits for them, and re-layouts  2.18 us (4%)
  other arithmetic  2.07 us (4%)
  between operations  1.02 us (2%)
    ppermute x8, starting transfers between devices, exchange(): lax.ppermute(x, 'hid', [(i, i ^ mask) for i in range(lax.axis_size('hid'))])  9.96 us
    all_to_all x1, starting transfers between devices, on_device(): rows = lax.all_to_all(both, 'hid', split_axis=1, concat_axis=0, tiled=True)  8.31 us
    ppermute x8, waiting for transfers between devices, exchange(): lax.ppermute(x, 'hid', [(i, i ^ mask) for i in range(lax.axis_size('hid'))])  8.19 us
    all_to_all x1, waiting for transfers between devices, on_device(): rows = lax.all_to_all(both, 'hid', split_axis=1, concat_axis=0, tiled=True)  7.79 us
    all_to_all x1, waiting for transfers between devices, on_device(): lax.all_to_all(results, 'hid', split_axis=0, concat_axis=1, tiled=True)  6.62 us
    all_to_all x1, starting transfers between devices, on_device(): lax.all_to_all(results, 'hid', split_axis=0, concat_axis=1, tiled=True)  3.63 us
    dot_general x6, matrix products, inner_rows(): lax.dot_general(left, right, (((0,), (0,)), ((), ())), preferred_element_...  3.51 us
    concatenate x1, other arithmetic, on_device(): jnp.concatenate([pre_act.reshape(tokens, hid, side), grad_out.reshape(tok...  1.62 us
  transfers between devices with their start and end apart: 12, of which 7 were waited for; matrix products, arithmetic and copies ran while one was open for 3% of the time, Pallas kernels for 0%

profile of v4, /device:TPU:0, one launch (start us, length us, event | category | flops | bytes accessed | tf_op | source)
XLA Modules:
  0.0 55.7 jit_solution(12878967374673994089)
XLA Ops:
  0.6 0.0 copy-start
  0.6 0.0 copy-start.1
  0.7 1.6 %pad_maximum_fusion.4 = bf16[6,16,512]{2,0,1:T(8,128)(2,1)} fusion(bf16[6,16,256]{2,0,1:T(8,128)(2,1)} %bitcast.34, bf16[6,16,256]{2,0,1:T(8,128)(2,1)} %bitcast.35), kind=kLoop, calls=%fused_computation.28 | loop fusion | flops 196608 | bytes 196608 | tf_op jit(solution)/shard_map/concatenate | solution.py:74
  2.3 8.3 %all-to-all-start = ((bf16[6,16,512]{2,0,1:T(8,128)(2,1)}), bf16[6,16,512]{2,0,1:T(8,128)(2,1)S(1)}, u32[]{:S(2)}, u32[]{:S(2)}) async-start(bf16[6,16,512]{2,0,1:T(8,128)(2,1)} %pad_maximum_fusion.4), calls=%async_computation | async-start | bytes 262144 | tf_op jit(solution)/shard_map/all_to_all | solution.py:77
  10.6 7.8 %all-to-all-done = bf16[6,16,512]{2,0,1:T(8,128)(2,1)S(1)} async-done(((bf16[6,16,512]{2,0,1:T(8,128)(2,1)}), bf16[6,16,512]{2,0,1:T(8,128)(2,1)S(1)}, u32[]{:S(2)}, u32[]{:S(2)}) %all-to-all-start) | async-done | bytes 98336 | tf_op jit(solution)/shard_map/all_to_all | solution.py:77
  18.4 0.0 copy-done.1
  18.5 0.2 fusion.8
  18.6 0.2 convolution_convert_fusion.2
  18.9 0.2 convolution_convert_fusion.3
  19.1 0.2 convolution_convert_fusion
  19.3 0.0 copy-start.2
  19.3 0.2 convolution_convert_fusion.1
  19.5 0.7 %copy-done.2 = bf16[256,256]{1,0:T(8,128)(2,1)S(1)} copy-done((bf16[256,256]{1,0:T(8,128)(2,1)S(1)}, bf16[256,256]{1,0:T(8,128)(2,1)}, u32[]{:S(2)}) %copy-start.2) | copy-done | bytes 131096
  20.2 0.2 fusion.56
  20.3 0.0 copy-done
  20.4 0.2 fusion.61
  20.6 0.8 %collective-permute-start.2 = (bf16[96,512]{1,0:T(8,128)(2,1)S(1)}, bf16[96,512]{1,0:T(8,128)(2,1)S(1)}, u32[]{:S(2)}, u32[]{:S(2)}) collective-permute-start(bf16[96,512]{1,0:T(8,128)(2,1)S(1)} %fusion.6), channel_id=1, source_target_pairs={{0,6},{2,4},{4,2},{6,0},{8,14},{10,12},{12,10},{14,8},{16,22},{18,... | collective-permute-start | bytes 294920 | tf_op jit(solution)/shard_map/ppermute | solution.py:10
  21.4 1.5 %collective-permute-start = (bf16[96,1024]{1,0:T(8,128)(2,1)S(1)}, bf16[96,1024]{1,0:T(8,128)(2,1)S(1)}, u32[]{:S(2)}, u32[]{:S(2)}) collective-permute-start(bf16[96,1024]{1,0:T(8,128)(2,1)S(1)} %get-tuple-element.26), channel_id=1, source_target_pairs={{0,2},{2,0},{4,6},{6,4},{8,10},{10,8},{12,14},{14,12},{16,18},{18,... | collective-permute-start | bytes 589832 | tf_op jit(solution)/shard_map/ppermute | solution.py:10
  22.9 1.3 %collective-permute-start.1 = (bf16[96,1024]{1,0:T(8,128)(2,1)S(1)}, bf16[96,1024]{1,0:T(8,128)(2,1)S(1)}, u32[]{:S(2)}, u32[]{:S(2)}) collective-permute-start(bf16[96,1024]{1,0:T(8,128)(2,1)S(1)} %get-tuple-element.25), channel_id=1, source_target_pairs={{0,4},{2,6},{4,0},{6,2},{8,12},{10,14},{12,8},{14,10},{16,20},{18,... | collective-permute-start | bytes 589832 | tf_op jit(solution)/shard_map/ppermute | solution.py:10
  24.2 0.8 %collective-permute-start.6 = (bf16[96,512]{1,0:T(8,128)(2,1)S(1)}, bf16[96,512]{1,0:T(8,128)(2,1)S(1)}, u32[]{:S(2)}, u32[]{:S(2)}) collective-permute-start(bf16[96,512]{1,0:T(8,128)(2,1)S(1)} %get-tuple-element.38), channel_id=1, source_target_pairs={{0,8},{2,10},{4,12},{6,14},{8,0},{10,2},{12,4},{14,6},{16,24},{18,... | collective-permute-start | bytes 294920 | tf_op jit(solution)/shard_map/ppermute | solution.py:10
  25.0 1.1 %collective-permute-start.7 = (bf16[96,512]{1,0:T(8,128)(2,1)S(1)}, bf16[96,512]{1,0:T(8,128)(2,1)S(1)}, u32[]{:S(2)}, u32[]{:S(2)}) collective-permute-start(bf16[96,512]{1,0:T(8,128)(2,1)S(1)} %get-tuple-element.37), channel_id=1, source_target_pairs={{0,16},{2,18},{4,20},{6,22},{8,24},{10,26},{12,28},{14,30},{16,0},... | collective-permute-start | bytes 294920 | tf_op jit(solution)/shard_map/ppermute | solution.py:10
  26.2 0.8 %collective-permute-done.2 = bf16[96,512]{1,0:T(8,128)(2,1)S(1)} collective-permute-done((bf16[96,512]{1,0:T(8,128)(2,1)S(1)}, bf16[96,512]{1,0:T(8,128)(2,1)S(1)}, u32[]{:S(2)}, u32[]{:S(2)}) %collective-permute-start.2) | collective-permute-done | bytes 98336 | tf_op jit(solution)/shard_map/ppermute | solution.py:10
  27.0 1.3 %collective-permute-done = bf16[96,1024]{1,0:T(8,128)(2,1)S(1)} collective-permute-done((bf16[96,1024]{1,0:T(8,128)(2,1)S(1)}, bf16[96,1024]{1,0:T(8,128)(2,1)S(1)}, u32[]{:S(2)}, u32[]{:S(2)}) %collective-permute-start) | collective-permute-done | bytes 196640 | tf_op jit(solution)/shard_map/ppermute | solution.py:10
  28.3 0.6 %collective-permute-done.1 = bf16[96,1024]{1,0:T(8,128)(2,1)S(1)} collective-permute-done((bf16[96,1024]{1,0:T(8,128)(2,1)S(1)}, bf16[96,1024]{1,0:T(8,128)(2,1)S(1)}, u32[]{:S(2)}, u32[]{:S(2)}) %collective-permute-start.1) | collective-permute-done | bytes 196640 | tf_op jit(solution)/shard_map/ppermute | solution.py:10
  29.0 0.7 %collective-permute-start.3 = (bf16[96,512]{1,0:T(8,128)(2,1)S(1)}, bf16[96,512]{1,0:T(8,128)(2,1)S(1)}, u32[]{:S(2)}, u32[]{:S(2)}) collective-permute-start(bf16[96,512]{1,0:T(8,128)(2,1)S(1)} %fusion.59), channel_id=1, source_target_pairs={{0,8},{2,10},{4,12},{6,14},{8,0},{10,2},{12,4},{14,6},{16,24},{18,... | collective-permute-start | bytes 294920 | tf_op jit(solution)/shard_map/ppermute | solution.py:10
  29.8 1.1 %collective-permute-start.4 = (bf16[96,512]{1,0:T(8,128)(2,1)S(1)}, bf16[96,512]{1,0:T(8,128)(2,1)S(1)}, u32[]{:S(2)}, u32[]{:S(2)}) collective-permute-start(bf16[96,512]{1,0:T(8,128)(2,1)S(1)} %fusion.59), channel_id=1, source_target_pairs={{0,16},{2,18},{4,20},{6,22},{8,24},{10,26},{12,28},{14,30},{16,0},... | collective-permute-start | bytes 294920 | tf_op jit(solution)/shard_map/ppermute | solution.py:10
  30.9 2.6 %collective-permute-start.5 = (bf16[96,512]{1,0:T(8,128)(2,1)S(1)}, bf16[96,512]{1,0:T(8,128)(2,1)S(1)}, u32[]{:S(2)}, u32[]{:S(2)}) collective-permute-start(bf16[96,512]{1,0:T(8,128)(2,1)S(1)} %fusion.59), channel_id=1, source_target_pairs={{0,24},{2,26},{4,28},{6,30},{8,16},{10,18},{12,20},{14,22},{16,8},... | collective-permute-start | bytes 294920 | tf_op jit(solution)/shard_map/ppermute | solution.py:10
  33.6 0.0 collective-permute-done.6
  33.6 0.0 collective-permute-done.7
  33.6 1.8 %collective-permute-done.3 = bf16[96,512]{1,0:T(8,128)(2,1)S(1)} collective-permute-done((bf16[96,512]{1,0:T(8,128)(2,1)S(1)}, bf16[96,512]{1,0:T(8,128)(2,1)S(1)}, u32[]{:S(2)}, u32[]{:S(2)}) %collective-permute-start.3) | collective-permute-done | bytes 98336 | tf_op jit(solution)/shard_map/ppermute | solution.py:10
  35.3 3.6 %collective-permute-done.4 = bf16[96,512]{1,0:T(8,128)(2,1)S(1)} collective-permute-done((bf16[96,512]{1,0:T(8,128)(2,1)S(1)}, bf16[96,512]{1,0:T(8,128)(2,1)S(1)}, u32[]{:S(2)}, u32[]{:S(2)}) %collective-permute-start.4) | collective-permute-done | bytes 98336 | tf_op jit(solution)/shard_map/ppermute | solution.py:10
  39.0 0.0 collective-permute-done.5
  39.0 0.1 add_convert_fusion
  39.1 0.2 fusion.40
  39.3 0.2 fusion.24
  39.6 0.2 fusion.64
  39.8 0.2 fusion.3
  40.0 0.7 %all_to_all.27 = bf16[16,6,512]{2,1,0:T(8,128)(2,1)} reshape(bf16[96,512]{1,0:T(8,128)(2,1)S(1)} %pad_maximum_fusion.7) | data formatting | bytes 196608 | tf_op jit(solution)/shard_map/all_to_all | solution.py:101
  40.7 3.6 %all-to-all-start.1 = ((bf16[16,6,512]{2,1,0:T(8,128)(2,1)}), bf16[16,6,512]{2,1,0:T(8,128)(2,1)S(1)}, u32[]{:S(2)}, u32[]{:S(2)}) async-start(bf16[16,6,512]{2,1,0:T(8,128)(2,1)} %all_to_all.27), calls=%async_computation.1 | async-start | bytes 262144 | tf_op jit(solution)/shard_map/all_to_all | solution.py:101
  44.4 0.3 fusion.49
  44.7 0.1 collective-permute-start.8
  44.8 0.5 collective-permute-start.9
  45.3 0.2 fusion.38
  45.5 6.6 %all-to-all-done.1 = bf16[16,6,512]{2,1,0:T(8,128)(2,1)S(1)} async-done(((bf16[16,6,512]{2,1,0:T(8,128)(2,1)}), bf16[16,6,512]{2,1,0:T(8,128)(2,1)S(1)}, u32[]{:S(2)}, u32[]{:S(2)}) %all-to-all-start.1) | async-done | bytes 98336 | tf_op jit(solution)/shard_map/all_to_all | solution.py:101
  52.2 0.7 %fusion.63 = (bf16[6,16,256]{2,0,1:T(8,128)(2,1)}, bf16[6,16,256]{2,0,1:T(8,128)(2,1)}) fusion(bf16[6,16,512]{2,0,1:T(8,128)(2,1)S(1)} %bitcast.33), kind=kLoop, calls=%fused_computation.106 | loop fusion | bytes 196608 | tf_op jit(solution)/shard_map/slice | solution.py:104
  52.8 0.0 collective-permute-done.8
  52.8 0.0 collective-permute-done.9
  52.9 0.9 %fusion.2 = f32[256,128]{1,0:T(8,128)} fusion(f32[256,128]{1,0:T(8,128)S(1)} %fusion.40, bf16[96,1024]{1,0:T(8,128)(2,1)S(1)} %collective-permute-done.8, bf16[96,256]{1,0:T(8,128)(2,1)S(1)} %collective-permute-done.9), kind=kOutput, calls=%fused_computation.5 | convolution fusion | flops 6356992 | bytes 335872 | tf_op jit(solution)/shard_map/dot_general | solution.py:32
  53.7 0.9 %fusion.1 = f32[128,256]{1,0:T(8,128)} fusion(f32[128,256]{1,0:T(8,128)S(1)} %fusion.38, bf16[96,1024]{1,0:T(8,128)(2,1)S(1)} %collective-permute-done.8, bf16[96,256]{1,0:T(8,128)(2,1)S(1)} %collective-permute-done.9), kind=kOutput, calls=%fused_computation.3 | convolution fusion | flops 6356992 | bytes 335872 | tf_op jit(solution)/shard_map/dot_general | solution.py:32
  54.6 1.1 %fusion = f32[640,256]{1,0:T(8,128)} fusion(f32[640,256]{1,0:T(8,128)S(1)} %fusion.49, bf16[96,512]{1,0:T(8,128)(2,1)S(1)} %slice.212, bf16[96,128]{1,0:T(8,128)(2,1)S(1)} %slice_select_fusion, bf16[96,1024]{1,0:T(8,128)(2,1)S(1)} %collective-permute-done.8), kind=kOutput, calls=%fused_computation.1 | convolution fusion | flops 32030720 | bytes 1482752 | tf_op jit(solution)/shard_map/dot_general | solution.py:32
  (22 shorter events, 0.4 us)
Async XLA Ops:
  0.6 19.7 %copy-start = (bf16[256,256]{1,0:T(8,128)(2,1)S(1)}, bf16[256,256]{1,0:T(8,128)(2,1)}, u32[]{:S(2)}) copy-start(bf16[256,256]{1,0:T(8,128)(2,1)} %param.7) | copy-start | bytes 393220
  0.6 17.8 %copy-start.1 = (bf16[1,5,256,256]{3,2,1,0:T(8,128)(2,1)S(1)}, bf16[1,5,256,256]{3,2,1,0:T(8,128)(2,1)}, u32[]{:S(2)}) copy-start(bf16[1,5,256,256]{3,2,1,0:T(8,128)(2,1)} %param.6) | copy-start | bytes 1966084
  2.3 16.1 %all-to-all-start = ((bf16[6,16,512]{2,0,1:T(8,128)(2,1)}), bf16[6,16,512]{2,0,1:T(8,128)(2,1)S(1)}, u32[]{:S(2)}, u32[]{:S(2)}) async-start(bf16[6,16,512]{2,0,1:T(8,128)(2,1)} %pad_maximum_fusion.4), calls=%async_computation | async-start | bytes 262144 | tf_op jit(solution)/shard_map/all_to_all | solution.py:77
  19.3 0.9 %copy-start.2 = (bf16[256,256]{1,0:T(8,128)(2,1)S(1)}, bf16[256,256]{1,0:T(8,128)(2,1)}, u32[]{:S(2)}) copy-start(bf16[256,256]{1,0:T(8,128)(2,1)} %param.8) | copy-start | bytes 393220
  20.6 6.4 %collective-permute-start.2 = (bf16[96,512]{1,0:T(8,128)(2,1)S(1)}, bf16[96,512]{1,0:T(8,128)(2,1)S(1)}, u32[]{:S(2)}, u32[]{:S(2)}) collective-permute-start(bf16[96,512]{1,0:T(8,128)(2,1)S(1)} %fusion.6), channel_id=1, source_target_pairs={{0,6},{2,4},{4,2},{6,0},{8,14},{10,12},{12,10},{14,8},{16,22},{18,... | collective-permute-start | bytes 294920 | tf_op jit(solution)/shard_map/ppermute | solution.py:10
  21.4 6.9 %collective-permute-start = (bf16[96,1024]{1,0:T(8,128)(2,1)S(1)}, bf16[96,1024]{1,0:T(8,128)(2,1)S(1)}, u32[]{:S(2)}, u32[]{:S(2)}) collective-permute-start(bf16[96,1024]{1,0:T(8,128)(2,1)S(1)} %get-tuple-element.26), channel_id=1, source_target_pairs={{0,2},{2,0},{4,6},{6,4},{8,10},{10,8},{12,14},{14,12},{16,18},{18,... | collective-permute-start | bytes 589832 | tf_op jit(solution)/shard_map/ppermute | solution.py:10
  22.9 6.0 %collective-permute-start.1 = (bf16[96,1024]{1,0:T(8,128)(2,1)S(1)}, bf16[96,1024]{1,0:T(8,128)(2,1)S(1)}, u32[]{:S(2)}, u32[]{:S(2)}) collective-permute-start(bf16[96,1024]{1,0:T(8,128)(2,1)S(1)} %get-tuple-element.25), channel_id=1, source_target_pairs={{0,4},{2,6},{4,0},{6,2},{8,12},{10,14},{12,8},{14,10},{16,20},{18,... | collective-permute-start | bytes 589832 | tf_op jit(solution)/shard_map/ppermute | solution.py:10
  24.2 9.3 %collective-permute-start.6 = (bf16[96,512]{1,0:T(8,128)(2,1)S(1)}, bf16[96,512]{1,0:T(8,128)(2,1)S(1)}, u32[]{:S(2)}, u32[]{:S(2)}) collective-permute-start(bf16[96,512]{1,0:T(8,128)(2,1)S(1)} %get-tuple-element.38), channel_id=1, source_target_pairs={{0,8},{2,10},{4,12},{6,14},{8,0},{10,2},{12,4},{14,6},{16,24},{18,... | collective-permute-start | bytes 294920 | tf_op jit(solution)/shard_map/ppermute | solution.py:10
  25.0 8.5 %collective-permute-start.7 = (bf16[96,512]{1,0:T(8,128)(2,1)S(1)}, bf16[96,512]{1,0:T(8,128)(2,1)S(1)}, u32[]{:S(2)}, u32[]{:S(2)}) collective-permute-start(bf16[96,512]{1,0:T(8,128)(2,1)S(1)} %get-tuple-element.37), channel_id=1, source_target_pairs={{0,16},{2,18},{4,20},{6,22},{8,24},{10,26},{12,28},{14,30},{16,0},... | collective-permute-start | bytes 294920 | tf_op jit(solution)/shard_map/ppermute | solution.py:10
  29.0 6.3 %collective-permute-start.3 = (bf16[96,512]{1,0:T(8,128)(2,1)S(1)}, bf16[96,512]{1,0:T(8,128)(2,1)S(1)}, u32[]{:S(2)}, u32[]{:S(2)}) collective-permute-start(bf16[96,512]{1,0:T(8,128)(2,1)S(1)} %fusion.59), channel_id=1, source_target_pairs={{0,8},{2,10},{4,12},{6,14},{8,0},{10,2},{12,4},{14,6},{16,24},{18,... | collective-permute-start | bytes 294920 | tf_op jit(solution)/shard_map/ppermute | solution.py:10
  29.8 9.2 %collective-permute-start.4 = (bf16[96,512]{1,0:T(8,128)(2,1)S(1)}, bf16[96,512]{1,0:T(8,128)(2,1)S(1)}, u32[]{:S(2)}, u32[]{:S(2)}) collective-permute-start(bf16[96,512]{1,0:T(8,128)(2,1)S(1)} %fusion.59), channel_id=1, source_target_pairs={{0,16},{2,18},{4,20},{6,22},{8,24},{10,26},{12,28},{14,30},{16,0},... | collective-permute-start | bytes 294920 | tf_op jit(solution)/shard_map/ppermute | solution.py:10
  30.9 8.1 %collective-permute-start.5 = (bf16[96,512]{1,0:T(8,128)(2,1)S(1)}, bf16[96,512]{1,0:T(8,128)(2,1)S(1)}, u32[]{:S(2)}, u32[]{:S(2)}) collective-permute-start(bf16[96,512]{1,0:T(8,128)(2,1)S(1)} %fusion.59), channel_id=1, source_target_pairs={{0,24},{2,26},{4,28},{6,30},{8,16},{10,18},{12,20},{14,22},{16,8},... | collective-permute-start | bytes 294920 | tf_op jit(solution)/shard_map/ppermute | solution.py:10
  40.7 11.4 %all-to-all-start.1 = ((bf16[16,6,512]{2,1,0:T(8,128)(2,1)}), bf16[16,6,512]{2,1,0:T(8,128)(2,1)S(1)}, u32[]{:S(2)}, u32[]{:S(2)}) async-start(bf16[16,6,512]{2,1,0:T(8,128)(2,1)} %all_to_all.27), calls=%async_computation.1 | async-start | bytes 262144 | tf_op jit(solution)/shard_map/all_to_all | solution.py:101
  44.7 8.1 %collective-permute-start.8 = (bf16[96,1024]{1,0:T(8,128)(2,1)S(1)}, bf16[96,1024]{1,0:T(8,128)(2,1)S(1)}, u32[]{:S(2)}, u32[]{:S(2)}) collective-permute-start(bf16[96,1024]{1,0:T(8,128)(2,1)S(1)} %get-tuple-element.31), channel_id=1, source_target_pairs={{0,1},{1,0},{2,3},{3,2},{4,5},{5,4},{6,7},{7,6},{8,9},{9,8},{10,11... | collective-permute-start | bytes 589832 | tf_op jit(solution)/shard_map/ppermute | solution.py:14
  44.8 8.1 %collective-permute-start.9 = (bf16[96,256]{1,0:T(8,128)(2,1)S(1)}, bf16[96,256]{1,0:T(8,128)(2,1)S(1)}, u32[]{:S(2)}, u32[]{:S(2)}) collective-permute-start(bf16[96,256]{1,0:T(8,128)(2,1)S(1)} %pad_maximum_fusion.8), channel_id=1, source_target_pairs={{0,1},{1,0},{2,3},{3,2},{4,5},{5,4},{6,7},{7,6},{8,9},{9,8},{10,11... | collective-permute-start | bytes 147464 | tf_op jit(solution)/shard_map/ppermute | solution.py:14

commit v5 on v1

--- a/solution.py
+++ b/solution.py
@@ -35,15 +35,7 @@
 
 
 def sum_over_hid(part):
-    bits = (lax.axis_size("hid") - 1).bit_length()
-    total = part
-    for low in range(0, bits, 2):
-        sent = total.astype(jnp.bfloat16)
-        masks = [1 << low]
-        if low + 1 < bits:
-            masks += [2 << low, 3 << low]
-        total = total + sum(exchange(sent, mask).astype(jnp.float32) for mask in masks)
-    return total.astype(jnp.bfloat16)
+    return lax.psum(part.astype(jnp.bfloat16), "hid")
 
 
 def half(x, which):

time: 52.9 us -> 156 us (2.95)
  waiting for transfers between devices: 16.6 us -> 112 us
  between operations: 1.02 us -> 14.4 us
  starting transfers between devices: 25.6 us -> 17.7 us
    psum x0 -> x1, waiting for transfers between devices: none -> 97.5 us  [sum_over_hid(): return lax.psum(part.astype(jnp.bfloat16), 'hid')]
    ppermute x10 -> x4, starting transfers between devices: 12.6 us -> 3.1 us  [exchange(): lax.ppermute(x, 'hid', [(i, i ^ mask) for i in range(lax.axis_size('hid'))])]
    ppermute x10 -> x4, waiting for transfers between devices: 4.51 us -> 0.04 us  [exchange(): lax.ppermute(x, 'hid', [(i, i ^ mask) for i in range(lax.axis_size('hid'))])]
    all_to_all x1, waiting for transfers between devices: 4.35 us -> 6.59 us  [on_device(): lax.all_to_all(results, 'hid', split_axis=0, concat_axis=1, tiled=True)]
  transfers between devices with their start and end apart: 14 -> 9, of which waited for: 5 -> 3; matrix products, arithmetic and copies ran while one was open for 11% -> 3% of each run, Pallas kernels for 0% -> 0%
where the time goes in v5:
time: 156 us
  waiting for transfers between devices  112 us (72%)
  starting transfers between devices  17.7 us (11%)
  between operations  14.4 us (9%)
  matrix products  6.65 us (4%)
  local copies, waits for them, and re-layouts  2.89 us (2%)
  other arithmetic  2.54 us (2%)
    psum x1, waiting for transfers between devices, sum_over_hid(): return lax.psum(part.astype(jnp.bfloat16), 'hid')  97.5 us
    all_to_all x1, starting transfers between devices, on_device(): rows = lax.all_to_all(both, 'hid', split_axis=1, concat_axis=0, tiled=True)  8.31 us
    all_to_all x1, waiting for transfers between devices, on_device(): rows = lax.all_to_all(both, 'hid', split_axis=1, concat_axis=0, tiled=True)  7.74 us
    all_to_all x1, waiting for transfers between devices, on_device(): lax.all_to_all(results, 'hid', split_axis=0, concat_axis=1, tiled=True)  6.59 us
    all_to_all x1, starting transfers between devices, on_device(): lax.all_to_all(results, 'hid', split_axis=0, concat_axis=1, tiled=True)  5.63 us
    dot_general x6, matrix products, inner_rows(): lax.dot_general(left, right, (((0,), (0,)), ((), ())), preferred_element_...  3.51 us
  transfers between devices with their start and end apart: 9, of which 3 were waited for; matrix products, arithmetic and copies ran while one was open for 3% of the time, Pallas kernels for 0%

profile of v5, /device:TPU:0, one launch (start us, length us, event | category | flops | bytes accessed | tf_op | source)
XLA Modules:
  0.0 156.1 jit_solution(14272075647211215061)
XLA Ops:
  7.2 0.0 copy-start
  7.2 0.0 copy-start.1
  7.2 1.6 %pad_maximum_fusion.4 = bf16[6,16,512]{2,0,1:T(8,128)(2,1)} fusion(bf16[6,16,256]{2,0,1:T(8,128)(2,1)} %bitcast.42, bf16[6,16,256]{2,0,1:T(8,128)(2,1)} %bitcast.43), kind=kLoop, calls=%fused_computation.28 | loop fusion | flops 196608 | bytes 196608 | tf_op jit(solution)/shard_map/concatenate | solution.py:55
  8.8 8.3 %all-to-all-start = ((bf16[6,16,512]{2,0,1:T(8,128)(2,1)}), bf16[6,16,512]{2,0,1:T(8,128)(2,1)S(1)}, u32[]{:S(2)}, u32[]{:S(2)}) async-start(bf16[6,16,512]{2,0,1:T(8,128)(2,1)} %pad_maximum_fusion.4), calls=%async_computation | async-start | bytes 262144 | tf_op jit(solution)/shard_map/all_to_all | solution.py:58
  17.1 0.0 all-reduce.2.cloned.1.call-start
  17.2 7.7 %all-to-all-done = bf16[6,16,512]{2,0,1:T(8,128)(2,1)S(1)} async-done(((bf16[6,16,512]{2,0,1:T(8,128)(2,1)}), bf16[6,16,512]{2,0,1:T(8,128)(2,1)S(1)}, u32[]{:S(2)}, u32[]{:S(2)}) %all-to-all-start) | async-done | bytes 98336 | tf_op jit(solution)/shard_map/all_to_all | solution.py:58
  25.0 0.0 copy-done.1
  25.0 0.2 convolution_convert_fusion.5
  25.2 0.2 convolution_convert_fusion.2
  25.4 0.2 convolution_convert_fusion.4
  25.6 0.2 convolution_convert_fusion.3
  25.8 0.0 copy-start.2
  25.8 0.2 fusion.20
  26.0 0.7 copy-done.2
  26.7 0.2 convolution_convert_fusion
  26.9 0.0 copy-done
  26.9 0.2 convolution_convert_fusion.1
  27.1 0.7 pad_maximum_fusion.5
  27.7 0.0 all-reduce.2.cloned.1.call-update
  27.8 1.0 collective-permute-start.3
  28.8 0.9 collective-permute-start.2
  29.7 0.7 collective-permute-start.1
  30.4 0.5 collective-permute-start
  31.0 97.5 %all-reduce.2.cloned.1.call-done = bf16[96,512]{1,0:T(8,128)(2,1)} async-done(((bf16[96,512]{1,0:T(8,128)(2,1)}), bf16[96,512]{1,0:T(8,128)(2,1)}) %all-reduce.2.cloned.1.call-update) | async-done | bytes 98320 | tf_op jit(solution)/shard_map/psum | solution.py:38
  128.5 1.0 fusion.47
  129.4 0.0 copy-start.3
  129.5 0.0 collective-permute-done
  129.5 0.2 convolution_add_fusion.4
  129.6 0.7 copy-done.3
  130.4 0.1 fusion.49
  130.5 0.0 collective-permute-done.3
  130.5 0.1 fusion.8
  130.7 0.0 collective-permute-done.2
  130.7 0.1 fusion.11
  130.8 0.0 collective-permute-done.1
  130.9 0.2 fusion.38
  131.1 0.2 fusion.6
  131.3 0.7 all_to_all.27
  132.0 5.6 %all-to-all-start.1 = ((bf16[16,6,512]{2,1,0:T(8,128)(2,1)}), bf16[16,6,512]{2,1,0:T(8,128)(2,1)S(1)}, u32[]{:S(2)}, u32[]{:S(2)}) async-start(bf16[16,6,512]{2,1,0:T(8,128)(2,1)} %all_to_all.27), calls=%async_computation.1 | async-start | bytes 262144 | tf_op jit(solution)/shard_map/all_to_all | solution.py:81
  137.8 0.1 collective-permute-start.4
  137.9 0.6 collective-permute-start.5
  138.4 0.2 fusion.62
  138.6 0.2 fusion.60
  138.8 6.6 %all-to-all-done.1 = bf16[16,6,512]{2,1,0:T(8,128)(2,1)S(1)} async-done(((bf16[16,6,512]{2,1,0:T(8,128)(2,1)}), bf16[16,6,512]{2,1,0:T(8,128)(2,1)S(1)}, u32[]{:S(2)}, u32[]{:S(2)}) %all-to-all-start.1) | async-done | bytes 98336 | tf_op jit(solution)/shard_map/all_to_all | solution.py:81
  145.4 0.7 fusion.86
  146.1 0.0 collective-permute-done.4
  146.1 0.3 fusion.22
  146.4 1.1 fusion
  147.5 0.0 collective-permute-done.5
  147.5 0.9 fusion.2
  148.4 0.9 fusion.1
  (15 shorter events, 0.3 us)
Async XLA Ops:
  7.2 19.7 %copy-start = (bf16[256,256]{1,0:T(8,128)(2,1)S(1)}, bf16[256,256]{1,0:T(8,128)(2,1)}, u32[]{:S(2)}) copy-start(bf16[256,256]{1,0:T(8,128)(2,1)} %param.7) | copy-start | bytes 393220
  7.2 17.8 %copy-start.1 = (bf16[1,5,256,256]{3,2,1,0:T(8,128)(2,1)S(1)}, bf16[1,5,256,256]{3,2,1,0:T(8,128)(2,1)}, u32[]{:S(2)}) copy-start(bf16[1,5,256,256]{3,2,1,0:T(8,128)(2,1)} %param.6) | copy-start | bytes 1966084
  8.8 16.1 %all-to-all-start = ((bf16[6,16,512]{2,0,1:T(8,128)(2,1)}), bf16[6,16,512]{2,0,1:T(8,128)(2,1)S(1)}, u32[]{:S(2)}, u32[]{:S(2)}) async-start(bf16[6,16,512]{2,0,1:T(8,128)(2,1)} %pad_maximum_fusion.4), calls=%async_computation | async-start | bytes 262144 | tf_op jit(solution)/shard_map/all_to_all | solution.py:58
  17.1 111.3 %all-reduce.2.cloned.1.call-start = ((), (), s32[]{:S(2)}) async-start(), calls=%async_computation.2 | async-start | bytes 196608 | tf_op jit(solution)/shard_map/psum | solution.py:38
  25.8 0.9 copy-start.2
  27.8 102.7 %collective-permute-start.3 = (bf16[96,512]{1,0:T(8,128)(2,1)S(1)}, bf16[96,512]{1,0:T(8,128)(2,1)S(1)}, u32[]{:S(2)}, u32[]{:S(2)}) collective-permute-start(bf16[96,512]{1,0:T(8,128)(2,1)S(1)} %get-tuple-element.18), channel_id=1, source_target_pairs={{0,16},{2,18},{4,20},{6,22},{8,24},{10,26},{12,28},{14,30},{16,0},... | collective-permute-start | bytes 294920 | tf_op jit(solution)/shard_map/ppermute | solution.py:10
  28.8 101.9 %collective-permute-start.2 = (bf16[96,512]{1,0:T(8,128)(2,1)S(1)}, bf16[96,512]{1,0:T(8,128)(2,1)S(1)}, u32[]{:S(2)}, u32[]{:S(2)}) collective-permute-start(bf16[96,512]{1,0:T(8,128)(2,1)S(1)} %get-tuple-element.20), channel_id=1, source_target_pairs={{0,8},{2,10},{4,12},{6,14},{8,0},{10,2},{12,4},{14,6},{16,24},{18,... | collective-permute-start | bytes 294920 | tf_op jit(solution)/shard_map/ppermute | solution.py:10
  29.7 101.2 %collective-permute-start.1 = (bf16[96,512]{1,0:T(8,128)(2,1)S(1)}, bf16[96,512]{1,0:T(8,128)(2,1)S(1)}, u32[]{:S(2)}, u32[]{:S(2)}) collective-permute-start(bf16[96,512]{1,0:T(8,128)(2,1)S(1)} %get-tuple-element.19), channel_id=1, source_target_pairs={{0,4},{2,6},{4,0},{6,2},{8,12},{10,14},{12,8},{14,10},{16,20},{18,... | collective-permute-start | bytes 294920 | tf_op jit(solution)/shard_map/ppermute | solution.py:10
  30.4 99.0 %collective-permute-start = (bf16[96,512]{1,0:T(8,128)(2,1)S(1)}, bf16[96,512]{1,0:T(8,128)(2,1)S(1)}, u32[]{:S(2)}, u32[]{:S(2)}) collective-permute-start(bf16[96,512]{1,0:T(8,128)(2,1)S(1)} %get-tuple-element.17), channel_id=1, source_target_pairs={{0,2},{2,0},{4,6},{6,4},{8,10},{10,8},{12,14},{14,12},{16,18},{18,... | collective-permute-start | bytes 294920 | tf_op jit(solution)/shard_map/ppermute | solution.py:10
  129.4 0.9 copy-start.3
  132.0 13.4 %all-to-all-start.1 = ((bf16[16,6,512]{2,1,0:T(8,128)(2,1)}), bf16[16,6,512]{2,1,0:T(8,128)(2,1)S(1)}, u32[]{:S(2)}, u32[]{:S(2)}) async-start(bf16[16,6,512]{2,1,0:T(8,128)(2,1)} %all_to_all.27), calls=%async_computation.1 | async-start | bytes 262144 | tf_op jit(solution)/shard_map/all_to_all | solution.py:81
  137.8 8.3 %collective-permute-start.4 = (bf16[96,1024]{1,0:T(8,128)(2,1)S(1)}, bf16[96,1024]{1,0:T(8,128)(2,1)S(1)}, u32[]{:S(2)}, u32[]{:S(2)}) collective-permute-start(bf16[96,1024]{1,0:T(8,128)(2,1)S(1)} %get-tuple-element.10), channel_id=1, source_target_pairs={{0,1},{1,0},{2,3},{3,2},{4,5},{5,4},{6,7},{7,6},{8,9},{9,8},{10,11... | collective-permute-start | bytes 589832 | tf_op jit(solution)/shard_map/ppermute | solution.py:14
  137.9 9.7 %collective-permute-start.5 = (bf16[96,256]{1,0:T(8,128)(2,1)S(1)}, bf16[96,256]{1,0:T(8,128)(2,1)S(1)}, u32[]{:S(2)}, u32[]{:S(2)}) collective-permute-start(bf16[96,256]{1,0:T(8,128)(2,1)S(1)} %pad_maximum_fusion.7), channel_id=1, source_target_pairs={{0,1},{1,0},{2,3},{3,2},{4,5},{5,4},{6,7},{7,6},{8,9},{9,8},{10,11... | collective-permute-start | bytes 147464 | tf_op jit(solution)/shard_map/ppermute | solution.py:14
Sparse Core Ops, SparseCore 0:
  27.9 100.5 all-reduce.1

commit v6 on v5

v6 whole, which is shorter than its diff:
```python
import math

import jax
import jax.numpy as jnp
from jax import lax
from jax.sharding import PartitionSpec as P


def exchange(x, mask):
    return lax.ppermute(x, "hid", [(i, i ^ mask) for i in range(lax.axis_size("hid"))])


def mate(x):
    return lax.ppermute(x, "seq", [(0, 1), (1, 0)])


def gelu_tanh(value):
    return jax.nn.gelu(value, approximate=True)


def dot(left, right):
    return jnp.dot(left, right, preferred_element_type=jnp.float32)


def dot_t(left, right):
    return lax.dot_general(
        left, right, (((1,), (1,)), ((), ())), preferred_element_type=jnp.float32
    )


def inner_rows(left, right):
    return lax.dot_general(
        left, right, (((0,), (0,)), ((), ())), preferred_element_type=jnp.float32
    )


def sum_over_hid(part, blocks):
    bits = (lax.axis_size("hid") - 1).bit_length()
    total, far, late = part, {}, {}
    for low in range(0, bits, 2):
        sent = total.astype(jnp.bfloat16)
        if low == 2:
            late = {mask: blocks[mask] for mask in blocks if mask not in far}
            sent, late = lax.optimization_barrier((sent, late))
        masks = [mask << low for mask in (1, 2, 3) if mask << low < 1 << bits]
        got = {mask: exchange(sent, mask) for mask in masks}
        if low == 0:
            far = {mask: exchange(blocks[mask], mask) for mask in blocks if mask not in masks}
        elif low == 2:
            late = {mask: exchange(late[mask], mask) for mask in late}
        if low + 2 < bits:
            got = lax.optimization_barrier(got)
        else:
            got, late = lax.optimization_barrier((got, late))
        total = total + sum(x.astype(jnp.float32) for x in got.values())
    return total.astype(jnp.bfloat16), far, late


def halves(x, first):
    width = x.shape[1] // 2
    low, high = x[:, :width], x[:, width:]
    return jnp.where(first, low, high), jnp.where(first, high, low)


def on_device(pre_act, butterfly, low_u, low_v, grad_out):
    tokens = pre_act.shape[0]
    hid = lax.axis_size("hid")
    first = lax.axis_index("seq") == 0
    side = butterfly.shape[-1]
    levels = butterfly.shape[1] - 1
    rank = low_u.shape[1]
    factor = 1.0 / math.sqrt(tokens * hid * lax.axis_size("seq"))

    pre_act, grad_out, first = lax.optimization_barrier((pre_act, grad_out, first))
    both = jnp.concatenate(
        [pre_act.reshape(tokens, hid, side), grad_out.reshape(tokens, hid, side)], axis=2
    ).reshape(tokens, hid * 2 * side)
    rows = lax.all_to_all(both, "hid", split_axis=1, concat_axis=0, tiled=True)
    pre_f = rows[:, :side].astype(jnp.float32)
    grad = rows[:, side:]
    act_f, pullback = jax.vjp(gelu_tanh, pre_f)
    act = act_f.astype(jnp.bfloat16)

    part = jnp.concatenate([dot(act, low_u), dot_t(grad, low_v)], axis=1)
    part, grad = lax.optimization_barrier((part, grad))
    blocks = {}
    for level in range(1, levels + 1):
        term = dot_t(grad, butterfly[0, level]).astype(jnp.bfloat16)
        blocks[1 << level - 1] = jnp.concatenate([act, term], axis=1)
    latents, early, late = sum_over_hid(part, blocks)
    fars = [(early | late)[mask] for mask in blocks]
    latent, dlatent = latents[:, :rank], latents[:, rank:]

    acts = [act] + [far[:, :side] for far in fars]
    total = dot(act, butterfly[0, 0])
    back = dot_t(grad, butterfly[0, 0])
    for level in range(1, levels + 1):
        total = total + dot(acts[level], butterfly[0, level])
        back = back + fars[level - 1][:, side:].astype(jnp.float32)

    output_rows = (total + dot(latent, low_v)).astype(jnp.bfloat16)
    grad_act = (back + dot_t(dlatent, low_u)).astype(jnp.bfloat16)
    grad_pre_rows = pullback(grad_act.astype(jnp.float32))[0].astype(jnp.bfloat16)
    results = jnp.concatenate([output_rows, grad_pre_rows], axis=1)
    results = lax.all_to_all(results, "hid", split_axis=0, concat_axis=1, tiled=True)

    def theirs(received):
        return [halves(x[:, :side], first)[1] for x in received.values()]

    def ours(received):
        return [halves(x[:, :side], first)[0] for x in received.values()]

    half = side // 2
    got = mate(jnp.concatenate([grad, act] + theirs(early), axis=1))
    far_grad, far_act = got[:, :side], got[:, side : 2 * side]
    latent, sent_latent = halves(latent, first)
    dlatent, sent_dlatent = halves(dlatent, first)
    last = mate(jnp.concatenate([sent_latent, sent_dlatent] + theirs(late), axis=1))
    far_latent, far_dlatent = last[:, : rank // 2], last[:, rank // 2 : rank]
    far = dict(zip(early, jnp.split(got[:, 2 * side :], len(early), axis=1)))
    far.update(zip(late, jnp.split(last[:, rank:], len(late), axis=1)))
    own = jnp.concatenate(ours({0: act}) + ours({mask: (early | late)[mask] for mask in blocks}), axis=1)
    far = jnp.concatenate(ours({0: far_act}) + [far[mask] for mask in blocks], axis=1)
    grad_butterfly = (inner_rows(own, grad) + inner_rows(far, far_grad)) * factor
    grad_butterfly = grad_butterfly.reshape(1, levels + 1, half, side)
    grad_low_u = (inner_rows(act, dlatent) + inner_rows(far_act, far_dlatent)) * factor
    grad_low_v = (inner_rows(latent, grad) + inner_rows(far_latent, far_grad)) * factor

    results = results.reshape(tokens, hid, 2 * side)
    output = results[:, :, :side].reshape(tokens, hid * side)
    grad_pre = results[:, :, side:].reshape(tokens, hid * side)
    return (output, grad_pre, grad_butterfly, grad_low_u, grad_low_v)


def solution(mesh):
    in_specs = (
        P(("hid", "seq"), None),
        P("hid", None, None, None),
        P("hid", None),
        P(None, "hid"),
        P(("hid", "seq"), None),
    )
    out_specs = (
        P(("hid", "seq"), None),
        P(("hid", "seq"), None),
        P("hid", None, "seq", None),
        P("hid", "seq"),
        P("seq", "hid"),
    )
    return jax.shard_map(
        on_device, mesh=mesh, in_specs=in_specs, out_specs=out_specs, check_vma=False
    )
```

time: 156 us -> 54.3 us (0.35)
  waiting for transfers between devices: 112 us -> 10.6 us
  blocking collectives: 0 us -> 15.9 us
  between operations: 14.4 us -> 1.04 us
  starting transfers between devices: 17.7 us -> 15.6 us
    psum x1 -> x0, waiting for transfers between devices: 97.5 us -> none  [sum_over_hid(): return lax.psum(part.astype(jnp.bfloat16), 'hid')]
    all_to_all x0 -> x1, blocking collectives: none -> 15.9 us  [on_device(): rows = lax.all_to_all(both, 'hid', split_axis=1, concat_axis=0, tiled=True)]
    all_to_all x1 -> x0, starting transfers between devices: 8.31 us -> none  [on_device(): rows = lax.all_to_all(both, 'hid', split_axis=1, concat_axis=0, tiled=True)]
    ppermute x4 -> x10, starting transfers between devices: 3.1 us -> 11 us  [exchange(): lax.ppermute(x, 'hid', [(i, i ^ mask) for i in range(lax.axis_size('hid'))])]
    all_to_all x1 -> x0, waiting for transfers between devices: 7.74 us -> none  [on_device(): rows = lax.all_to_all(both, 'hid', split_axis=1, concat_axis=0, tiled=True)]
    ppermute x4 -> x10, waiting for transfers between devices: 0.04 us -> 7.39 us  [exchange(): lax.ppermute(x, 'hid', [(i, i ^ mask) for i in range(lax.axis_size('hid'))])]
    all_to_all x1, waiting for transfers between devices: 6.59 us -> 3.22 us  [on_device(): lax.all_to_all(results, 'hid', split_axis=0, concat_axis=1, tiled=True)]
    all_to_all x1, starting transfers between devices: 5.63 us -> 4 us  [on_device(): lax.all_to_all(results, 'hid', split_axis=0, concat_axis=1, tiled=True)]
  transfers between devices with their start and end apart: 9 -> 13, of which waited for: 3 -> 5; matrix products, arithmetic and copies ran while one was open for 3% -> 11% of each run, Pallas kernels for 0% -> 0%
where the time goes in v6:
time: 54.3 us; the launch traced here: 53.9 us
  blocking collectives  15.9 us (29%)
  starting transfers between devices  15.6 us (29%)
  waiting for transfers between devices  10.6 us (20%)
  matrix products  5.85 us (11%)
  local copies, waits for them, and re-layouts  3.53 us (7%)
  other arithmetic  1.36 us (3%)
  between operations  1.04 us (2%)
    all_to_all x1, blocking collectives, on_device(): rows = lax.all_to_all(both, 'hid', split_axis=1, concat_axis=0, tiled=True)  15.9 us
    ppermute x10, starting transfers between devices, exchange(): lax.ppermute(x, 'hid', [(i, i ^ mask) for i in range(lax.axis_size('hid'))])  11 us
    ppermute x10, waiting for transfers between devices, exchange(): lax.ppermute(x, 'hid', [(i, i ^ mask) for i in range(lax.axis_size('hid'))])  7.39 us
    all_to_all x1, starting transfers between devices, on_device(): lax.all_to_all(results, 'hid', split_axis=0, concat_axis=1, tiled=True)  4 us
    dot_general x6, matrix products, inner_rows(): lax.dot_general(left, right, (((0,), (0,)), ((), ())), preferred_element_...  3.52 us
    all_to_all x1, waiting for transfers between devices, on_device(): lax.all_to_all(results, 'hid', split_axis=0, concat_axis=1, tiled=True)  3.22 us
    unnamed x10, local copies, waits for them, and re-layouts  1.36 us
    dot_general x7, matrix products, dot_t(): lax.dot_general(left, right, (((1,), (1,)), ((), ())), preferred_element_...  1.23 us
  transfers between devices with their start and end apart: 13, of which 5 were waited for; matrix products, arithmetic and copies ran while one was open for 11% of the time, Pallas kernels for 0%

profile of v6, /device:TPU:0, one launch (start us, length us, event | category | flops | bytes accessed | tf_op | source)
XLA Modules:
  0.0 53.9 jit_solution(17540672705525937501)
XLA Ops:
  0.6 0.0 copy-start
  0.7 0.9 %pad_maximum_fusion.6 = bf16[6,16,512]{2,0,1:T(8,128)(2,1)S(1)} fusion(bf16[6,16,256]{2,0,1:T(8,128)(2,1)} %bitcast.47, bf16[6,16,256]{2,0,1:T(8,128)(2,1)} %bitcast.48), kind=kLoop, calls=%fused_computation.30 | loop fusion | flops 196608 | bytes 196608 | tf_op jit(solution)/shard_map/concatenate | solution.py:75
  1.6 15.9 %all_to_all.32 = bf16[6,16,512]{2,0,1:T(8,128)(2,1)S(1)} all-to-all(bf16[6,16,512]{2,0,1:T(8,128)(2,1)S(1)} %pad_maximum_fusion.6), channel_id=1, replica_groups=mesh['hid'=16,'seq'=2] {'hid'}, dimensions={1} | all-to-all | bytes 196608 | tf_op jit(solution)/shard_map/all_to_all | solution.py:78
  17.5 0.0 copy-start.4
  17.6 0.0 copy-done
  17.6 0.0 copy-start.1
  17.6 0.2 fusion.74
  17.7 0.7 %copy-done.4 = bf16[256,256]{1,0:T(8,128)(2,1)S(1)} copy-done((bf16[256,256]{1,0:T(8,128)(2,1)S(1)}, bf16[256,256]{1,0:T(8,128)(2,1)}, u32[]{:S(2)}) %copy-start.4) | copy-done | bytes 131096
  18.4 0.2 fusion.77
  18.7 1.2 %collective-permute-start = (bf16[96,512]{1,0:T(8,128)(2,1)S(1)}, bf16[96,512]{1,0:T(8,128)(2,1)S(1)}, u32[]{:S(2)}, u32[]{:S(2)}) collective-permute-start(bf16[96,512]{1,0:T(8,128)(2,1)S(1)} %convert_element_type.71), channel_id=1, source_target_pairs={{0,2},{2,0},{4,6},{6,4},{8,10},{10,8},{12,14},{14,12},{16,18},{18,... | collective-permute-start | bytes 294920 | tf_op jit(solution)/shard_map/ppermute | solution.py:10
  19.8 0.2 collective-permute-start.1
  20.0 2.2 %collective-permute-start.2 = (bf16[96,512]{1,0:T(8,128)(2,1)S(1)}, bf16[96,512]{1,0:T(8,128)(2,1)S(1)}, u32[]{:S(2)}, u32[]{:S(2)}) collective-permute-start(bf16[96,512]{1,0:T(8,128)(2,1)S(1)} %convert_element_type.71), channel_id=1, source_target_pairs={{0,6},{2,4},{4,2},{6,0},{8,14},{10,12},{12,10},{14,8},{16,22},{18,... | collective-permute-start | bytes 294920 | tf_op jit(solution)/shard_map/ppermute | solution.py:10
  22.3 0.0 copy-done.1
  22.3 0.2 fusion.16
  22.4 0.2 convolution_convert_fusion.1
  22.7 0.2 convolution_convert_fusion.3
  22.9 0.2 convolution_convert_fusion
  23.0 0.2 convolution_convert_fusion.2
  23.2 0.2 fusion.18
  23.5 1.0 %collective-permute-start.9 = (bf16[96,512]{1,0:T(8,128)(2,1)S(1)}, bf16[96,512]{1,0:T(8,128)(2,1)S(1)}, u32[]{:S(2)}, u32[]{:S(2)}) collective-permute-start(bf16[96,512]{1,0:T(8,128)(2,1)S(1)} %get-tuple-element.51), channel_id=1, source_target_pairs={{0,16},{2,18},{4,20},{6,22},{8,24},{10,26},{12,28},{14,30},{16,0},... | collective-permute-start | bytes 294920 | tf_op jit(solution)/shard_map/ppermute | solution.py:10
  24.5 0.0 collective-permute-done
  24.5 0.0 collective-permute-done.1
  24.5 1.1 %collective-permute-done.2 = bf16[96,512]{1,0:T(8,128)(2,1)S(1)} collective-permute-done((bf16[96,512]{1,0:T(8,128)(2,1)S(1)}, bf16[96,512]{1,0:T(8,128)(2,1)S(1)}, u32[]{:S(2)}, u32[]{:S(2)}) %collective-permute-start.2) | collective-permute-done | bytes 98336 | tf_op jit(solution)/shard_map/ppermute | solution.py:10
  25.6 0.8 %collective-permute-start.3 = (bf16[96,512]{1,0:T(8,128)(2,1)S(1)}, bf16[96,512]{1,0:T(8,128)(2,1)S(1)}, u32[]{:S(2)}, u32[]{:S(2)}) collective-permute-start(bf16[96,512]{1,0:T(8,128)(2,1)S(1)} %fusion.72), channel_id=1, source_target_pairs={{0,8},{2,10},{4,12},{6,14},{8,0},{10,2},{12,4},{14,6},{16,24},{18,... | collective-permute-start | bytes 294920 | tf_op jit(solution)/shard_map/ppermute | solution.py:10
  26.4 1.1 %collective-permute-start.4 = (bf16[96,512]{1,0:T(8,128)(2,1)S(1)}, bf16[96,512]{1,0:T(8,128)(2,1)S(1)}, u32[]{:S(2)}, u32[]{:S(2)}) collective-permute-start(bf16[96,512]{1,0:T(8,128)(2,1)S(1)} %fusion.72), channel_id=1, source_target_pairs={{0,16},{2,18},{4,20},{6,22},{8,24},{10,26},{12,28},{14,30},{16,0},... | collective-permute-start | bytes 294920 | tf_op jit(solution)/shard_map/ppermute | solution.py:10
  27.5 2.5 %collective-permute-start.5 = (bf16[96,512]{1,0:T(8,128)(2,1)S(1)}, bf16[96,512]{1,0:T(8,128)(2,1)S(1)}, u32[]{:S(2)}, u32[]{:S(2)}) collective-permute-start(bf16[96,512]{1,0:T(8,128)(2,1)S(1)} %fusion.72), channel_id=1, source_target_pairs={{0,24},{2,26},{4,28},{6,30},{8,16},{10,18},{12,20},{14,22},{16,8},... | collective-permute-start | bytes 294920 | tf_op jit(solution)/shard_map/ppermute | solution.py:10
  30.1 1.5 %collective-permute-start.6 = (bf16[96,512]{1,0:T(8,128)(2,1)S(1)}, bf16[96,512]{1,0:T(8,128)(2,1)S(1)}, u32[]{:S(2)}, u32[]{:S(2)}) collective-permute-start(bf16[96,512]{1,0:T(8,128)(2,1)S(1)} %get-tuple-element.29), channel_id=1, source_target_pairs={{0,2},{2,0},{4,6},{6,4},{8,10},{10,8},{12,14},{14,12},{16,18},{18,... | collective-permute-start | bytes 294920 | tf_op jit(solution)/shard_map/ppermute | solution.py:10
  31.5 2.4 %collective-permute-done.9 = bf16[96,512]{1,0:T(8,128)(2,1)S(1)} collective-permute-done((bf16[96,512]{1,0:T(8,128)(2,1)S(1)}, bf16[96,512]{1,0:T(8,128)(2,1)S(1)}, u32[]{:S(2)}, u32[]{:S(2)}) %collective-permute-start.9) | collective-permute-done | bytes 98336 | tf_op jit(solution)/shard_map/ppermute | solution.py:10
  33.9 0.5 collective-permute-start.7
  34.4 0.1 fusion.7
  34.6 0.0 collective-permute-done.3
  34.6 0.1 collective-permute-start.8
  34.7 1.6 %collective-permute-done.4 = bf16[96,512]{1,0:T(8,128)(2,1)S(1)} collective-permute-done((bf16[96,512]{1,0:T(8,128)(2,1)S(1)}, bf16[96,512]{1,0:T(8,128)(2,1)S(1)}, u32[]{:S(2)}, u32[]{:S(2)}) %collective-permute-start.4) | collective-permute-done | bytes 98336 | tf_op jit(solution)/shard_map/ppermute | solution.py:10
  36.2 0.0 collective-permute-done.5
  36.2 0.0 collective-permute-done.6
  36.2 2.3 %collective-permute-done.7 = bf16[96,512]{1,0:T(8,128)(2,1)S(1)} collective-permute-done((bf16[96,512]{1,0:T(8,128)(2,1)S(1)}, bf16[96,512]{1,0:T(8,128)(2,1)S(1)}, u32[]{:S(2)}, u32[]{:S(2)}) %collective-permute-start.7) | collective-permute-done | bytes 98336 | tf_op jit(solution)/shard_map/ppermute | solution.py:10
  38.5 0.1 add_convert_fusion
  38.6 0.1 fusion.51
  38.8 0.2 fusion.64
  39.0 0.2 fusion.62
  39.2 0.2 convolution_add_fusion.5
  39.4 0.2 convolution_add_fusion.4
  39.6 0.0 collective-permute-done.8
  39.7 0.1 collective-permute-start.10
  39.8 0.6 %collective-permute-start.11 = (bf16[96,512]{1,0:T(8,128)(2,1)S(1)}, bf16[96,512]{1,0:T(8,128)(2,1)S(1)}, u32[]{:S(2)}, u32[]{:S(2)}) collective-permute-start(bf16[96,512]{1,0:T(8,128)(2,1)S(1)} %pad_maximum_fusion.8), channel_id=1, source_target_pairs={{0,1},{1,0},{2,3},{3,2},{4,5},{5,4},{6,7},{7,6},{8,9},{9,8},{10,11... | collective-permute-start | bytes 294920 | tf_op jit(solution)/shard_map/ppermute | solution.py:14
  40.4 0.2 fusion.38
  40.6 0.2 fusion.5
  40.8 0.7 %all_to_all.27 = bf16[16,6,512]{2,1,0:T(8,128)(2,1)} reshape(bf16[96,512]{1,0:T(8,128)(2,1)S(1)} %pad_maximum_fusion.7) | data formatting | bytes 196608 | tf_op jit(solution)/shard_map/all_to_all | solution.py:105
  41.5 4.0 %all-to-all-start.1 = ((bf16[16,6,512]{2,1,0:T(8,128)(2,1)}), bf16[16,6,512]{2,1,0:T(8,128)(2,1)S(1)}, u32[]{:S(2)}, u32[]{:S(2)}) async-start(bf16[16,6,512]{2,1,0:T(8,128)(2,1)} %all_to_all.27), calls=%async_computation.1 | async-start | bytes 262144 | tf_op jit(solution)/shard_map/all_to_all | solution.py:105
  45.5 0.0 collective-permute-done.11
  45.5 0.0 copy-start.2
  45.5 0.6 %copy-done.2 = bf16[96,512]{1,0:T(8,128)(2,1)} copy-done((bf16[96,512]{1,0:T(8,128)(2,1)}, bf16[96,512]{1,0:T(8,128)(2,1)S(1)}, u32[]{:S(2)}) %copy-start.2) | copy-done | bytes 98328
  46.1 0.0 collective-permute-done.10
  46.1 0.0 slice-start
  46.2 0.8 %slice-done = bf16[96,256]{1,0:T(8,128)(2,1)S(1)} async-done(((bf16[96,512]{1,0:T(8,128)(2,1)}), bf16[96,256]{1,0:T(8,128)(2,1)S(1)}, s32[]{:S(2)}) %slice-start) | async-done | bytes 49176 | tf_op jit(solution)/shard_map/split | solution.py:121
  46.9 0.3 fusion.20
  47.2 0.0 copy-start.3
  47.2 1.1 %fusion = f32[640,256]{1,0:T(8,128)} fusion(f32[640,256]{1,0:T(8,128)S(1)} %fusion.20, bf16[96,640]{1,0:T(8,128)(2,1)S(1)} %get-tuple-element.39, bf16[96,256]{1,0:T(8,128)(2,1)S(1)} %slice.200), kind=kOutput, calls=%fused_computation.1 | convolution fusion | flops 31784960 | bytes 1482752 | tf_op jit(solution)/shard_map/dot_general | solution.py:32
  48.3 0.0 copy-done.3
  48.4 0.9 %fusion.2 = f32[256,128]{1,0:T(8,128)} fusion(f32[256,128]{1,0:T(8,128)S(1)} %fusion.64, bf16[96,768]{1,0:T(8,128)(2,1)S(1)} %collective-permute-done.10, bf16[96,512]{1,0:T(8,128)(2,1)S(1)} %copy-done.3), kind=kOutput, calls=%fused_computation.5 | convolution fusion | flops 6356992 | bytes 335872 | tf_op jit(solution)/shard_map/dot_general | solution.py:32
  49.2 0.9 %fusion.1 = f32[128,256]{1,0:T(8,128)} fusion(f32[128,256]{1,0:T(8,128)S(1)} %fusion.62, bf16[96,768]{1,0:T(8,128)(2,1)S(1)} %collective-permute-done.10, bf16[96,512]{1,0:T(8,128)(2,1)S(1)} %copy-done.3), kind=kOutput, calls=%fused_computation.3 | convolution fusion | flops 6356992 | bytes 335872 | tf_op jit(solution)/shard_map/dot_general | solution.py:32
  50.1 3.2 %all-to-all-done.1 = bf16[16,6,512]{2,1,0:T(8,128)(2,1)S(1)} async-done(((bf16[16,6,512]{2,1,0:T(8,128)(2,1)}), bf16[16,6,512]{2,1,0:T(8,128)(2,1)S(1)}, u32[]{:S(2)}, u32[]{:S(2)}) %all-to-all-start.1) | async-done | bytes 98336 | tf_op jit(solution)/shard_map/all_to_all | solution.py:105
  53.3 0.7 %fusion.80 = (bf16[6,16,256]{2,0,1:T(8,128)(2,1)}, bf16[6,16,256]{2,0,1:T(8,128)(2,1)}) fusion(bf16[6,16,512]{2,0,1:T(8,128)(2,1)S(1)} %bitcast.46), kind=kLoop, calls=%fused_computation.115 | loop fusion | bytes 196608 | tf_op jit(solution)/shard_map/slice | solution.py:131
  (18 shorter events, 0.4 us)
Async XLA Ops:
  0.6 16.9 %copy-start = (bf16[256,256]{1,0:T(8,128)(2,1)S(1)}, bf16[256,256]{1,0:T(8,128)(2,1)}, u32[]{:S(2)}) copy-start(bf16[256,256]{1,0:T(8,128)(2,1)} %param.8) | copy-start | bytes 393220
  17.5 0.9 %copy-start.4 = (bf16[256,256]{1,0:T(8,128)(2,1)S(1)}, bf16[256,256]{1,0:T(8,128)(2,1)}, u32[]{:S(2)}) copy-start(bf16[256,256]{1,0:T(8,128)(2,1)} %param.7) | copy-start | bytes 393220
  17.6 4.7 %copy-start.1 = (bf16[1,5,256,256]{3,2,1,0:T(8,128)(2,1)S(1)}, bf16[1,5,256,256]{3,2,1,0:T(8,128)(2,1)}, u32[]{:S(2)}) copy-start(bf16[1,5,256,256]{3,2,1,0:T(8,128)(2,1)} %param.6) | copy-start | bytes 1966084
  18.7 5.8 %collective-permute-start = (bf16[96,512]{1,0:T(8,128)(2,1)S(1)}, bf16[96,512]{1,0:T(8,128)(2,1)S(1)}, u32[]{:S(2)}, u32[]{:S(2)}) collective-permute-start(bf16[96,512]{1,0:T(8,128)(2,1)S(1)} %convert_element_type.71), channel_id=1, source_target_pairs={{0,2},{2,0},{4,6},{6,4},{8,10},{10,8},{12,14},{14,12},{16,18},{18,... | collective-permute-start | bytes 294920 | tf_op jit(solution)/shard_map/ppermute | solution.py:10
  19.8 4.6 %collective-permute-start.1 = (bf16[96,512]{1,0:T(8,128)(2,1)S(1)}, bf16[96,512]{1,0:T(8,128)(2,1)S(1)}, u32[]{:S(2)}, u32[]{:S(2)}) collective-permute-start(bf16[96,512]{1,0:T(8,128)(2,1)S(1)} %convert_element_type.71), channel_id=1, source_target_pairs={{0,4},{2,6},{4,0},{6,2},{8,12},{10,14},{12,8},{14,10},{16,20},{18,... | collective-permute-start | bytes 294920 | tf_op jit(solution)/shard_map/ppermute | solution.py:10
  20.0 5.5 %collective-permute-start.2 = (bf16[96,512]{1,0:T(8,128)(2,1)S(1)}, bf16[96,512]{1,0:T(8,128)(2,1)S(1)}, u32[]{:S(2)}, u32[]{:S(2)}) collective-permute-start(bf16[96,512]{1,0:T(8,128)(2,1)S(1)} %convert_element_type.71), channel_id=1, source_target_pairs={{0,6},{2,4},{4,2},{6,0},{8,14},{10,12},{12,10},{14,8},{16,22},{18,... | collective-permute-start | bytes 294920 | tf_op jit(solution)/shard_map/ppermute | solution.py:10
  23.5 10.5 %collective-permute-start.9 = (bf16[96,512]{1,0:T(8,128)(2,1)S(1)}, bf16[96,512]{1,0:T(8,128)(2,1)S(1)}, u32[]{:S(2)}, u32[]{:S(2)}) collective-permute-start(bf16[96,512]{1,0:T(8,128)(2,1)S(1)} %get-tuple-element.51), channel_id=1, source_target_pairs={{0,16},{2,18},{4,20},{6,22},{8,24},{10,26},{12,28},{14,30},{16,0},... | collective-permute-start | bytes 294920 | tf_op jit(solution)/shard_map/ppermute | solution.py:10
  25.6 9.0 %collective-permute-start.3 = (bf16[96,512]{1,0:T(8,128)(2,1)S(1)}, bf16[96,512]{1,0:T(8,128)(2,1)S(1)}, u32[]{:S(2)}, u32[]{:S(2)}) collective-permute-start(bf16[96,512]{1,0:T(8,128)(2,1)S(1)} %fusion.72), channel_id=1, source_target_pairs={{0,8},{2,10},{4,12},{6,14},{8,0},{10,2},{12,4},{14,6},{16,24},{18,... | collective-permute-start | bytes 294920 | tf_op jit(solution)/shard_map/ppermute | solution.py:10
  26.4 9.8 %collective-permute-start.4 = (bf16[96,512]{1,0:T(8,128)(2,1)S(1)}, bf16[96,512]{1,0:T(8,128)(2,1)S(1)}, u32[]{:S(2)}, u32[]{:S(2)}) collective-permute-start(bf16[96,512]{1,0:T(8,128)(2,1)S(1)} %fusion.72), channel_id=1, source_target_pairs={{0,16},{2,18},{4,20},{6,22},{8,24},{10,26},{12,28},{14,30},{16,0},... | collective-permute-start | bytes 294920 | tf_op jit(solution)/shard_map/ppermute | solution.py:10
  27.5 8.7 %collective-permute-start.5 = (bf16[96,512]{1,0:T(8,128)(2,1)S(1)}, bf16[96,512]{1,0:T(8,128)(2,1)S(1)}, u32[]{:S(2)}, u32[]{:S(2)}) collective-permute-start(bf16[96,512]{1,0:T(8,128)(2,1)S(1)} %fusion.72), channel_id=1, source_target_pairs={{0,24},{2,26},{4,28},{6,30},{8,16},{10,18},{12,20},{14,22},{16,8},... | collective-permute-start | bytes 294920 | tf_op jit(solution)/shard_map/ppermute | solution.py:10
  30.1 6.2 %collective-permute-start.6 = (bf16[96,512]{1,0:T(8,128)(2,1)S(1)}, bf16[96,512]{1,0:T(8,128)(2,1)S(1)}, u32[]{:S(2)}, u32[]{:S(2)}) collective-permute-start(bf16[96,512]{1,0:T(8,128)(2,1)S(1)} %get-tuple-element.29), channel_id=1, source_target_pairs={{0,2},{2,0},{4,6},{6,4},{8,10},{10,8},{12,14},{14,12},{16,18},{18,... | collective-permute-start | bytes 294920 | tf_op jit(solution)/shard_map/ppermute | solution.py:10
  33.9 4.6 %collective-permute-start.7 = (bf16[96,512]{1,0:T(8,128)(2,1)S(1)}, bf16[96,512]{1,0:T(8,128)(2,1)S(1)}, u32[]{:S(2)}, u32[]{:S(2)}) collective-permute-start(bf16[96,512]{1,0:T(8,128)(2,1)S(1)} %get-tuple-element.30), channel_id=1, source_target_pairs={{0,4},{2,6},{4,0},{6,2},{8,12},{10,14},{12,8},{14,10},{16,20},{18,... | collective-permute-start | bytes 294920 | tf_op jit(solution)/shard_map/ppermute | solution.py:10
  34.6 5.0 %collective-permute-start.8 = (bf16[96,512]{1,0:T(8,128)(2,1)S(1)}, bf16[96,512]{1,0:T(8,128)(2,1)S(1)}, u32[]{:S(2)}, u32[]{:S(2)}) collective-permute-start(bf16[96,512]{1,0:T(8,128)(2,1)S(1)} %get-tuple-element.49), channel_id=1, source_target_pairs={{0,8},{2,10},{4,12},{6,14},{8,0},{10,2},{12,4},{14,6},{16,24},{18,... | collective-permute-start | bytes 294920 | tf_op jit(solution)/shard_map/ppermute | solution.py:10
  39.7 6.4 %collective-permute-start.10 = (bf16[96,768]{1,0:T(8,128)(2,1)S(1)}, bf16[96,768]{1,0:T(8,128)(2,1)S(1)}, u32[]{:S(2)}, u32[]{:S(2)}) collective-permute-start(bf16[96,768]{1,0:T(8,128)(2,1)S(1)} %pad_maximum_fusion.1), channel_id=1, source_target_pairs={{0,1},{1,0},{2,3},{3,2},{4,5},{5,4},{6,7},{7,6},{8,9},{9,8},{10,11... | collective-permute-start | bytes 442376 | tf_op jit(solution)/shard_map/ppermute | solution.py:14
  39.8 5.7 %collective-permute-start.11 = (bf16[96,512]{1,0:T(8,128)(2,1)S(1)}, bf16[96,512]{1,0:T(8,128)(2,1)S(1)}, u32[]{:S(2)}, u32[]{:S(2)}) collective-permute-start(bf16[96,512]{1,0:T(8,128)(2,1)S(1)} %pad_maximum_fusion.8), channel_id=1, source_target_pairs={{0,1},{1,0},{2,3},{3,2},{4,5},{5,4},{6,7},{7,6},{8,9},{9,8},{10,11... | collective-permute-start | bytes 294920 | tf_op jit(solution)/shard_map/ppermute | solution.py:14
  41.5 11.8 %all-to-all-start.1 = ((bf16[16,6,512]{2,1,0:T(8,128)(2,1)}), bf16[16,6,512]{2,1,0:T(8,128)(2,1)S(1)}, u32[]{:S(2)}, u32[]{:S(2)}) async-start(bf16[16,6,512]{2,1,0:T(8,128)(2,1)} %all_to_all.27), calls=%async_computation.1 | async-start | bytes 262144 | tf_op jit(solution)/shard_map/all_to_all | solution.py:105
  45.5 0.6 %copy-start.2 = (bf16[96,512]{1,0:T(8,128)(2,1)}, bf16[96,512]{1,0:T(8,128)(2,1)S(1)}, u32[]{:S(2)}) copy-start(bf16[96,512]{1,0:T(8,128)(2,1)S(1)} %collective-permute-done.11) | copy-start | bytes 294916
  46.1 0.8 %slice-start = ((bf16[96,512]{1,0:T(8,128)(2,1)}), bf16[96,256]{1,0:T(8,128)(2,1)S(1)}, s32[]{:S(2)}) async-start(bf16[96,512]{1,0:T(8,128)(2,1)} %copy-done.2), calls=%async_computation.2 | async-start | bytes 98304 | tf_op jit(solution)/shard_map/split | solution.py:121
  47.2 1.1 %copy-start.3 = (bf16[96,512]{1,0:T(8,128)(2,1)S(1)}, bf16[96,512]{1,0:T(8,128)(2,1)}, u32[]{:S(2)}) copy-start(bf16[96,512]{1,0:T(8,128)(2,1)} %copy-done.2) | copy-start | bytes 294916

commit v7 on v1

--- a/solution.py
+++ b/solution.py
@@ -46,20 +46,22 @@
     return total.astype(jnp.bfloat16)
 
 
-def half(x, which):
+def halves(x, first):
     width = x.shape[1] // 2
-    return jnp.where(which == 0, x[:, :width], x[:, width:])
+    low, high = x[:, :width], x[:, width:]
+    return jnp.where(first, low, high), jnp.where(first, high, low)
 
 
 def on_device(pre_act, butterfly, low_u, low_v, grad_out):
     tokens = pre_act.shape[0]
     hid = lax.axis_size("hid")
-    core = lax.axis_index("seq")
+    first = lax.axis_index("seq") == 0
     side = butterfly.shape[-1]
     levels = butterfly.shape[1] - 1
     rank = low_u.shape[1]
     factor = 1.0 / math.sqrt(tokens * hid * lax.axis_size("seq"))
 
+    pre_act, grad_out, first = lax.optimization_barrier((pre_act, grad_out, first))
     both = jnp.concatenate(
         [pre_act.reshape(tokens, hid, side), grad_out.reshape(tokens, hid, side)], axis=2
     ).reshape(tokens, hid * 2 * side)
@@ -91,25 +93,24 @@
     output = results[:, :, :side].reshape(tokens, hid * side)
     grad_pre = results[:, :, side:].reshape(tokens, hid * side)
 
-    other = 1 - core
-    sent = jnp.concatenate(
-        [grad, act] + [half(x, other) for x in acts[1:]], axis=1
-    )
-    got = mate(sent)
-    own = jnp.concatenate([half(x, core) for x in acts], axis=1)
-    far = jnp.concatenate(
-        [half(got[:, side : 2 * side], core), got[:, 2 * side :]], axis=1
-    )
-    grad_butterfly = (inner_rows(own, grad) + inner_rows(far, got[:, :side])) * factor
+    split = [halves(x, first) for x in acts[1:]]
+    got = mate(jnp.concatenate([grad, act] + [theirs for ours, theirs in split[::-1]], axis=1))
+    far_grad, far_act = got[:, :side], got[:, side : 2 * side]
+    far_halves = jnp.split(got[:, 2 * side :], levels, axis=1)[::-1]
+    latent, sent_latent = halves(latent, first)
+    dlatent, sent_dlatent = halves(dlatent, first)
+    got = mate(jnp.concatenate([sent_latent, sent_dlatent], axis=1))
+
+    def tokens_of(own, far):
+        return jnp.concatenate([own, far], axis=0)
+
+    grads = tokens_of(grad, far_grad)
+    own = jnp.concatenate([halves(act, first)[0]] + [ours for ours, theirs in split], axis=1)
+    far = jnp.concatenate([halves(far_act, first)[0]] + far_halves, axis=1)
+    grad_butterfly = inner_rows(tokens_of(own, far), grads) * factor
     grad_butterfly = grad_butterfly.reshape(1, levels + 1, side // 2, side)
-    far_latents = mate(jnp.concatenate([half(latent, other), half(dlatent, other)], axis=1))
-    far_latent, far_dlatent = far_latents[:, : rank // 2], far_latents[:, rank // 2 :]
-    grad_low_u = (
-        inner_rows(act, half(dlatent, core)) + inner_rows(got[:, side : 2 * side], far_dlatent)
-    ) * factor
-    grad_low_v = (
-        inner_rows(half(latent, core), grad) + inner_rows(far_latent, got[:, :side])
-    ) * factor
+    grad_low_u = inner_rows(tokens_of(act, far_act), tokens_of(dlatent, got[:, rank // 2 :])) * factor
+    grad_low_v = inner_rows(tokens_of(latent, got[:, : rank // 2]), grads) * factor
     return (output, grad_pre, grad_butterfly, grad_low_u, grad_low_v)
 
 

time: 52.9 us -> 52.2 us (0.987)
  blocking collectives: 0 us -> 16 us
  starting transfers between devices: 25.6 us -> 17.2 us
  waiting for transfers between devices: 16.6 us -> 9.52 us
  matrix products: 5.87 us -> 5.21 us
  other arithmetic: 2 us -> 1.4 us
    all_to_all x0 -> x1, blocking collectives: none -> 16 us  [on_device(): rows = lax.all_to_all(both, 'hid', split_axis=1, concat_axis=0, tiled=True)]
    all_to_all x1 -> x0, starting transfers between devices: 8.44 us -> none  [on_device(): rows = lax.all_to_all(both, 'hid', split_axis=1, concat_axis=0, tiled=True)]
    all_to_all x1 -> x0, waiting for transfers between devices: 7.78 us -> none  [on_device(): rows = lax.all_to_all(both, 'hid', split_axis=1, concat_axis=0, tiled=True)]
    all_to_all x1, waiting for transfers between devices: 4.35 us -> 5.06 us  [on_device(): lax.all_to_all(results, 'hid', split_axis=0, concat_axis=1, tiled=True)]
    dot_general x6 -> x3, matrix products: 3.54 us -> 2.88 us  [inner_rows(): lax.dot_general(left, right, (((0,), (0,)), ((), ())), preferred_element_...]
    concatenate x1, other arithmetic: 1.59 us -> 0.93 us  [on_device(): jnp.concatenate([pre_act.reshape(tokens, hid, side), grad_out.reshape(tok...]
  transfers between devices with their start and end apart: 14 -> 13, of which waited for: 5 -> 4; matrix products, arithmetic and copies ran while one was open for 11% -> 10% of each run, Pallas kernels for 0% -> 0%
where the time goes in v7:
time: 52.2 us; the launch traced here: 51.9 us
  starting transfers between devices  17.2 us (33%)
  blocking collectives  16 us (31%)
  waiting for transfers between devices  9.52 us (18%)
  matrix products  5.21 us (10%)
  local copies, waits for them, and re-layouts  1.52 us (3%)
  other arithmetic  1.4 us (3%)
  between operations  1.05 us (2%)
    all_to_all x1, blocking collectives, on_device(): rows = lax.all_to_all(both, 'hid', split_axis=1, concat_axis=0, tiled=True)  16 us
    ppermute x10, starting transfers between devices, exchange(): lax.ppermute(x, 'hid', [(i, i ^ mask) for i in range(lax.axis_size('hid'))])  12.6 us
    all_to_all x1, waiting for transfers between devices, on_device(): lax.all_to_all(results, 'hid', split_axis=0, concat_axis=1, tiled=True)  5.06 us
    ppermute x10, waiting for transfers between devices, exchange(): lax.ppermute(x, 'hid', [(i, i ^ mask) for i in range(lax.axis_size('hid'))])  4.45 us
    all_to_all x1, starting transfers between devices, on_device(): lax.all_to_all(results, 'hid', split_axis=0, concat_axis=1, tiled=True)  4.41 us
    dot_general x3, matrix products, inner_rows(): lax.dot_general(left, right, (((0,), (0,)), ((), ())), preferred_element_...  2.88 us
    dot_general x7, matrix products, dot_t(): lax.dot_general(left, right, (((1,), (1,)), ((), ())), preferred_element_...  1.22 us
    dot_general x7, matrix products, dot(): return jnp.dot(left, right, preferred_element_type=jnp.float32)  1.11 us
  transfers between devices with their start and end apart: 13, of which 4 were waited for; matrix products, arithmetic and copies ran while one was open for 10% of the time, Pallas kernels for 0%

profile of v7, /device:TPU:0, one launch (start us, length us, event | category | flops | bytes accessed | tf_op | source)
XLA Modules:
  0.0 51.9 jit_solution(11865333307961625681)
XLA Ops:
  0.6 0.0 copy-start
  0.7 0.9 %pad_maximum_fusion.5 = bf16[6,16,512]{2,0,1:T(8,128)(2,1)S(1)} fusion(bf16[6,16,256]{2,0,1:T(8,128)(2,1)} %bitcast.38, bf16[6,16,256]{2,0,1:T(8,128)(2,1)} %bitcast.39), kind=kLoop, calls=%fused_computation.30 | loop fusion | flops 196608 | bytes 196608 | tf_op jit(solution)/shard_map/concatenate | solution.py:65
  1.6 0.0 copy-start.2
  1.6 16.0 %all_to_all.32 = bf16[6,16,512]{2,0,1:T(8,128)(2,1)S(1)} all-to-all(bf16[6,16,512]{2,0,1:T(8,128)(2,1)S(1)} %pad_maximum_fusion.5), channel_id=1, replica_groups=mesh['hid'=16,'seq'=2] {'hid'}, dimensions={1} | all-to-all | bytes 196608 | tf_op jit(solution)/shard_map/all_to_all | solution.py:68
  17.6 0.0 copy-start.1
  17.7 0.0 copy-done
  17.7 0.2 fusion.67
  17.9 0.0 copy-done.2
  17.9 0.2 fusion.73
  18.1 0.8 %collective-permute-start.6 = (bf16[96,512]{1,0:T(8,128)(2,1)S(1)}, bf16[96,512]{1,0:T(8,128)(2,1)S(1)}, u32[]{:S(2)}, u32[]{:S(2)}) collective-permute-start(bf16[96,512]{1,0:T(8,128)(2,1)S(1)} %fusion.7), channel_id=1, source_target_pairs={{0,6},{2,4},{4,2},{6,0},{8,14},{10,12},{12,10},{14,8},{16,22},{18,... | collective-permute-start | bytes 294920 | tf_op jit(solution)/shard_map/ppermute | solution.py:10
  18.9 1.8 %collective-permute-start.5 = (bf16[96,512]{1,0:T(8,128)(2,1)S(1)}, bf16[96,512]{1,0:T(8,128)(2,1)S(1)}, u32[]{:S(2)}, u32[]{:S(2)}) collective-permute-start(bf16[96,512]{1,0:T(8,128)(2,1)S(1)} %fusion.7), channel_id=1, source_target_pairs={{0,4},{2,6},{4,0},{6,2},{8,12},{10,14},{12,8},{14,10},{16,20},{18,... | collective-permute-start | bytes 294920 | tf_op jit(solution)/shard_map/ppermute | solution.py:10
  20.7 0.9 %collective-permute-start.4 = (bf16[96,512]{1,0:T(8,128)(2,1)S(1)}, bf16[96,512]{1,0:T(8,128)(2,1)S(1)}, u32[]{:S(2)}, u32[]{:S(2)}) collective-permute-start(bf16[96,512]{1,0:T(8,128)(2,1)S(1)} %fusion.7), channel_id=1, source_target_pairs={{0,2},{2,0},{4,6},{6,4},{8,10},{10,8},{12,14},{14,12},{16,18},{18,... | collective-permute-start | bytes 294920 | tf_op jit(solution)/shard_map/ppermute | solution.py:10
  21.7 0.0 copy-done.1
  21.7 0.2 fusion.19
  21.9 0.2 convolution_convert_fusion.3
  22.1 0.2 convolution_convert_fusion.1
  22.3 0.2 convolution_convert_fusion
  22.5 0.2 convolution_convert_fusion.2
  22.7 0.2 fusion.21
  22.9 1.0 %collective-permute-start.3 = (bf16[96,512]{1,0:T(8,128)(2,1)S(1)}, bf16[96,512]{1,0:T(8,128)(2,1)S(1)}, u32[]{:S(2)}, u32[]{:S(2)}) collective-permute-start(bf16[96,512]{1,0:T(8,128)(2,1)S(1)} %get-tuple-element.27), channel_id=1, source_target_pairs={{0,16},{2,18},{4,20},{6,22},{8,24},{10,26},{12,28},{14,30},{16,0},... | collective-permute-start | bytes 294920 | tf_op jit(solution)/shard_map/ppermute | solution.py:10
  23.9 0.9 %collective-permute-start.2 = (bf16[96,512]{1,0:T(8,128)(2,1)S(1)}, bf16[96,512]{1,0:T(8,128)(2,1)S(1)}, u32[]{:S(2)}, u32[]{:S(2)}) collective-permute-start(bf16[96,512]{1,0:T(8,128)(2,1)S(1)} %get-tuple-element.26), channel_id=1, source_target_pairs={{0,8},{2,10},{4,12},{6,14},{8,0},{10,2},{12,4},{14,6},{16,24},{18,... | collective-permute-start | bytes 294920 | tf_op jit(solution)/shard_map/ppermute | solution.py:10
  24.8 0.0 collective-permute-done.6
  24.8 0.8 %collective-permute-start.1 = (bf16[96,512]{1,0:T(8,128)(2,1)S(1)}, bf16[96,512]{1,0:T(8,128)(2,1)S(1)}, u32[]{:S(2)}, u32[]{:S(2)}) collective-permute-start(bf16[96,512]{1,0:T(8,128)(2,1)S(1)} %get-tuple-element.28), channel_id=1, source_target_pairs={{0,4},{2,6},{4,0},{6,2},{8,12},{10,14},{12,8},{14,10},{16,20},{18,... | collective-permute-start | bytes 294920 | tf_op jit(solution)/shard_map/ppermute | solution.py:10
  25.6 0.0 collective-permute-done.5
  25.7 0.9 %collective-permute-start = (bf16[96,512]{1,0:T(8,128)(2,1)S(1)}, bf16[96,512]{1,0:T(8,128)(2,1)S(1)}, u32[]{:S(2)}, u32[]{:S(2)}) collective-permute-start(bf16[96,512]{1,0:T(8,128)(2,1)S(1)} %get-tuple-element.25), channel_id=1, source_target_pairs={{0,2},{2,0},{4,6},{6,4},{8,10},{10,8},{12,14},{14,12},{16,18},{18,... | collective-permute-start | bytes 294920 | tf_op jit(solution)/shard_map/ppermute | solution.py:10
  26.5 0.0 collective-permute-done.4
  26.6 2.3 %collective-permute-start.9 = (bf16[96,512]{1,0:T(8,128)(2,1)S(1)}, bf16[96,512]{1,0:T(8,128)(2,1)S(1)}, u32[]{:S(2)}, u32[]{:S(2)}) collective-permute-start(bf16[96,512]{1,0:T(8,128)(2,1)S(1)} %fusion.65), channel_id=1, source_target_pairs={{0,24},{2,26},{4,28},{6,30},{8,16},{10,18},{12,20},{14,22},{16,8},... | collective-permute-start | bytes 294920 | tf_op jit(solution)/shard_map/ppermute | solution.py:10
  28.9 1.4 %collective-permute-done = bf16[96,512]{1,0:T(8,128)(2,1)S(1)} collective-permute-done((bf16[96,512]{1,0:T(8,128)(2,1)S(1)}, bf16[96,512]{1,0:T(8,128)(2,1)S(1)}, u32[]{:S(2)}, u32[]{:S(2)}) %collective-permute-start) | collective-permute-done | bytes 98336 | tf_op jit(solution)/shard_map/ppermute | solution.py:10
  30.3 1.8 %collective-permute-start.8 = (bf16[96,512]{1,0:T(8,128)(2,1)S(1)}, bf16[96,512]{1,0:T(8,128)(2,1)S(1)}, u32[]{:S(2)}, u32[]{:S(2)}) collective-permute-start(bf16[96,512]{1,0:T(8,128)(2,1)S(1)} %fusion.65), channel_id=1, source_target_pairs={{0,16},{2,18},{4,20},{6,22},{8,24},{10,26},{12,28},{14,30},{16,0},... | collective-permute-start | bytes 294920 | tf_op jit(solution)/shard_map/ppermute | solution.py:10
  32.1 0.0 collective-permute-done.1
  32.1 1.4 %collective-permute-start.7 = (bf16[96,512]{1,0:T(8,128)(2,1)S(1)}, bf16[96,512]{1,0:T(8,128)(2,1)S(1)}, u32[]{:S(2)}, u32[]{:S(2)}) collective-permute-start(bf16[96,512]{1,0:T(8,128)(2,1)S(1)} %fusion.65), channel_id=1, source_target_pairs={{0,8},{2,10},{4,12},{6,14},{8,0},{10,2},{12,4},{14,6},{16,24},{18,... | collective-permute-start | bytes 294920 | tf_op jit(solution)/shard_map/ppermute | solution.py:10
  33.5 0.0 collective-permute-done.2
  33.5 0.0 collective-permute-done.3
  33.7 0.1 collective-permute-start.10
  33.7 0.1 fusion.9
  33.9 0.2 convolution_add_fusion.1
  34.1 0.1 fusion.12
  34.2 0.0 collective-permute-done.9
  34.2 2.8 %collective-permute-done.8 = bf16[96,512]{1,0:T(8,128)(2,1)S(1)} collective-permute-done((bf16[96,512]{1,0:T(8,128)(2,1)S(1)}, bf16[96,512]{1,0:T(8,128)(2,1)S(1)}, u32[]{:S(2)}, u32[]{:S(2)}) %collective-permute-start.8) | collective-permute-done | bytes 98336 | tf_op jit(solution)/shard_map/ppermute | solution.py:10
  37.0 0.3 collective-permute-done.7
  37.3 0.1 add_convert_fusion
  37.4 0.1 fusion.50
  37.6 0.1 collective-permute-start.11
  37.6 0.2 fusion.35
  37.9 0.2 fusion.3
  38.1 0.7 %all_to_all.27 = bf16[16,6,512]{2,1,0:T(8,128)(2,1)} reshape(bf16[96,512]{1,0:T(8,128)(2,1)S(1)} %pad_maximum_fusion.6) | data formatting | bytes 196608 | tf_op jit(solution)/shard_map/all_to_all | solution.py:91
  38.7 4.4 %all-to-all-start.1 = ((bf16[16,6,512]{2,1,0:T(8,128)(2,1)}), bf16[16,6,512]{2,1,0:T(8,128)(2,1)S(1)}, u32[]{:S(2)}, u32[]{:S(2)}) async-start(bf16[16,6,512]{2,1,0:T(8,128)(2,1)} %all_to_all.27), calls=%async_computation.1 | async-start | bytes 262144 | tf_op jit(solution)/shard_map/all_to_all | solution.py:91
  43.2 0.0 collective-permute-done.11
  43.2 0.0 collective-permute-done.10
  43.2 0.9 %convolution_multiply_fusion.2 = f32[256,128]{1,0:T(8,128)} fusion(bf16[96,256]{1,0:T(8,128)(2,1)S(1)} %get-tuple-element.11, bf16[96,256]{1,0:T(8,128)(2,1)S(1)} %fusion.40, bf16[96,128]{1,0:T(8,128)(2,1)S(1)} %get-tuple-element.24, bf16[96,128]{1,0:T(8,128)(2,1)S(1)} %get-tuple-element.16), kind=kOutput, calls=%fused_computation.2 | convolution fusion | flops 12910592 | bytes 278528 | tf_op jit(solution)/shard_map/dot_general | solution.py:32
  44.2 0.9 %convolution_multiply_fusion.1 = f32[128,256]{1,0:T(8,128)} fusion(bf16[96,256]{1,0:T(8,128)(2,1)S(1)} %get-tuple-element.12, bf16[96,256]{1,0:T(8,128)(2,1)S(1)} %get-tuple-element.19, bf16[96,128]{1,0:T(8,128)(2,1)S(1)} %get-tuple-element.23, bf16[96,128]{1,0:T(8,128)(2,1)S(1)} %get-tuple-element.15), kind=kOutput, calls=%fused_computation.1 | convolution fusion | flops 12910592 | bytes 278528 | tf_op jit(solution)/shard_map/dot_general | solution.py:32
  45.1 1.1 %convolution_multiply_fusion = f32[640,256]{1,0:T(8,128)} fusion(bf16[96,640]{1,0:T(8,128)(2,1)S(1)} %constant_dynamic-update-slice_fusion.11, bf16[96,640]{1,0:T(8,128)(2,1)S(1)} %get-tuple-element.21, bf16[96,256]{1,0:T(8,128)(2,1)S(1)} %get-tuple-element.12, bf16[96,256]{1,0:T(8,128)(2,1)S(1)} %get-tuple-element.19), kind=kOutput, calls=%fused_computation | convolution fusion | flops 63766528 | bytes 999424 | tf_op jit(solution)/shard_map/dot_general | solution.py:32
  46.2 5.1 %all-to-all-done.1 = bf16[16,6,512]{2,1,0:T(8,128)(2,1)S(1)} async-done(((bf16[16,6,512]{2,1,0:T(8,128)(2,1)}), bf16[16,6,512]{2,1,0:T(8,128)(2,1)S(1)}, u32[]{:S(2)}, u32[]{:S(2)}) %all-to-all-start.1) | async-done | bytes 98336 | tf_op jit(solution)/shard_map/all_to_all | solution.py:91
  51.3 0.7 %fusion.77 = (bf16[6,16,256]{2,0,1:T(8,128)(2,1)}, bf16[6,16,256]{2,0,1:T(8,128)(2,1)}) fusion(bf16[6,16,512]{2,0,1:T(8,128)(2,1)S(1)} %bitcast.37), kind=kLoop, calls=%fused_computation.122 | loop fusion | bytes 196608 | tf_op jit(solution)/shard_map/slice | solution.py:94
  (25 shorter events, 0.5 us)
Async XLA Ops:
  0.6 17.1 %copy-start = (bf16[256,256]{1,0:T(8,128)(2,1)S(1)}, bf16[256,256]{1,0:T(8,128)(2,1)}, u32[]{:S(2)}) copy-start(bf16[256,256]{1,0:T(8,128)(2,1)} %param.8) | copy-start | bytes 393220
  1.6 16.3 %copy-start.2 = (bf16[256,256]{1,0:T(8,128)(2,1)S(1)}, bf16[256,256]{1,0:T(8,128)(2,1)}, u32[]{:S(2)}) copy-start(bf16[256,256]{1,0:T(8,128)(2,1)} %param.7) | copy-start | bytes 393220
  17.6 4.0 %copy-start.1 = (bf16[1,5,256,256]{3,2,1,0:T(8,128)(2,1)S(1)}, bf16[1,5,256,256]{3,2,1,0:T(8,128)(2,1)}, u32[]{:S(2)}) copy-start(bf16[1,5,256,256]{3,2,1,0:T(8,128)(2,1)} %param.6) | copy-start | bytes 1966084
  18.1 6.7 %collective-permute-start.6 = (bf16[96,512]{1,0:T(8,128)(2,1)S(1)}, bf16[96,512]{1,0:T(8,128)(2,1)S(1)}, u32[]{:S(2)}, u32[]{:S(2)}) collective-permute-start(bf16[96,512]{1,0:T(8,128)(2,1)S(1)} %fusion.7), channel_id=1, source_target_pairs={{0,6},{2,4},{4,2},{6,0},{8,14},{10,12},{12,10},{14,8},{16,22},{18,... | collective-permute-start | bytes 294920 | tf_op jit(solution)/shard_map/ppermute | solution.py:10
  18.9 6.8 %collective-permute-start.5 = (bf16[96,512]{1,0:T(8,128)(2,1)S(1)}, bf16[96,512]{1,0:T(8,128)(2,1)S(1)}, u32[]{:S(2)}, u32[]{:S(2)}) collective-permute-start(bf16[96,512]{1,0:T(8,128)(2,1)S(1)} %fusion.7), channel_id=1, source_target_pairs={{0,4},{2,6},{4,0},{6,2},{8,12},{10,14},{12,8},{14,10},{16,20},{18,... | collective-permute-start | bytes 294920 | tf_op jit(solution)/shard_map/ppermute | solution.py:10
  20.7 5.8 %collective-permute-start.4 = (bf16[96,512]{1,0:T(8,128)(2,1)S(1)}, bf16[96,512]{1,0:T(8,128)(2,1)S(1)}, u32[]{:S(2)}, u32[]{:S(2)}) collective-permute-start(bf16[96,512]{1,0:T(8,128)(2,1)S(1)} %fusion.7), channel_id=1, source_target_pairs={{0,2},{2,0},{4,6},{6,4},{8,10},{10,8},{12,14},{14,12},{16,18},{18,... | collective-permute-start | bytes 294920 | tf_op jit(solution)/shard_map/ppermute | solution.py:10
  22.9 10.7 %collective-permute-start.3 = (bf16[96,512]{1,0:T(8,128)(2,1)S(1)}, bf16[96,512]{1,0:T(8,128)(2,1)S(1)}, u32[]{:S(2)}, u32[]{:S(2)}) collective-permute-start(bf16[96,512]{1,0:T(8,128)(2,1)S(1)} %get-tuple-element.27), channel_id=1, source_target_pairs={{0,16},{2,18},{4,20},{6,22},{8,24},{10,26},{12,28},{14,30},{16,0},... | collective-permute-start | bytes 294920 | tf_op jit(solution)/shard_map/ppermute | solution.py:10
  23.9 9.7 %collective-permute-start.2 = (bf16[96,512]{1,0:T(8,128)(2,1)S(1)}, bf16[96,512]{1,0:T(8,128)(2,1)S(1)}, u32[]{:S(2)}, u32[]{:S(2)}) collective-permute-start(bf16[96,512]{1,0:T(8,128)(2,1)S(1)} %get-tuple-element.26), channel_id=1, source_target_pairs={{0,8},{2,10},{4,12},{6,14},{8,0},{10,2},{12,4},{14,6},{16,24},{18,... | collective-permute-start | bytes 294920 | tf_op jit(solution)/shard_map/ppermute | solution.py:10
  24.8 7.3 %collective-permute-start.1 = (bf16[96,512]{1,0:T(8,128)(2,1)S(1)}, bf16[96,512]{1,0:T(8,128)(2,1)S(1)}, u32[]{:S(2)}, u32[]{:S(2)}) collective-permute-start(bf16[96,512]{1,0:T(8,128)(2,1)S(1)} %get-tuple-element.28), channel_id=1, source_target_pairs={{0,4},{2,6},{4,0},{6,2},{8,12},{10,14},{12,8},{14,10},{16,20},{18,... | collective-permute-start | bytes 294920 | tf_op jit(solution)/shard_map/ppermute | solution.py:10
  25.7 4.6 %collective-permute-start = (bf16[96,512]{1,0:T(8,128)(2,1)S(1)}, bf16[96,512]{1,0:T(8,128)(2,1)S(1)}, u32[]{:S(2)}, u32[]{:S(2)}) collective-permute-start(bf16[96,512]{1,0:T(8,128)(2,1)S(1)} %get-tuple-element.25), channel_id=1, source_target_pairs={{0,2},{2,0},{4,6},{6,4},{8,10},{10,8},{12,14},{14,12},{16,18},{18,... | collective-permute-start | bytes 294920 | tf_op jit(solution)/shard_map/ppermute | solution.py:10
  26.6 7.6 %collective-permute-start.9 = (bf16[96,512]{1,0:T(8,128)(2,1)S(1)}, bf16[96,512]{1,0:T(8,128)(2,1)S(1)}, u32[]{:S(2)}, u32[]{:S(2)}) collective-permute-start(bf16[96,512]{1,0:T(8,128)(2,1)S(1)} %fusion.65), channel_id=1, source_target_pairs={{0,24},{2,26},{4,28},{6,30},{8,16},{10,18},{12,20},{14,22},{16,8},... | collective-permute-start | bytes 294920 | tf_op jit(solution)/shard_map/ppermute | solution.py:10
  30.3 6.7 %collective-permute-start.8 = (bf16[96,512]{1,0:T(8,128)(2,1)S(1)}, bf16[96,512]{1,0:T(8,128)(2,1)S(1)}, u32[]{:S(2)}, u32[]{:S(2)}) collective-permute-start(bf16[96,512]{1,0:T(8,128)(2,1)S(1)} %fusion.65), channel_id=1, source_target_pairs={{0,16},{2,18},{4,20},{6,22},{8,24},{10,26},{12,28},{14,30},{16,0},... | collective-permute-start | bytes 294920 | tf_op jit(solution)/shard_map/ppermute | solution.py:10
  32.1 5.1 %collective-permute-start.7 = (bf16[96,512]{1,0:T(8,128)(2,1)S(1)}, bf16[96,512]{1,0:T(8,128)(2,1)S(1)}, u32[]{:S(2)}, u32[]{:S(2)}) collective-permute-start(bf16[96,512]{1,0:T(8,128)(2,1)S(1)} %fusion.65), channel_id=1, source_target_pairs={{0,8},{2,10},{4,12},{6,14},{8,0},{10,2},{12,4},{14,6},{16,24},{18,... | collective-permute-start | bytes 294920 | tf_op jit(solution)/shard_map/ppermute | solution.py:10
  33.7 9.5 %collective-permute-start.10 = (bf16[96,1024]{1,0:T(8,128)(2,1)S(1)}, bf16[96,1024]{1,0:T(8,128)(2,1)S(1)}, u32[]{:S(2)}, u32[]{:S(2)}) collective-permute-start(bf16[96,1024]{1,0:T(8,128)(2,1)S(1)} %constant_dynamic-update-slice_fusion.5), channel_id=1, source_target_pairs={{0,1},{1,0},{2,3},{3,2},{4,5},{5,4},{6,7},{7,6},{8,9},{9,8},{10,11... | collective-permute-start | bytes 589832 | tf_op jit(solution)/shard_map/ppermute | solution.py:14
  37.6 5.6 %collective-permute-start.11 = (bf16[96,256]{1,0:T(8,128)(2,1)S(1)}, bf16[96,256]{1,0:T(8,128)(2,1)S(1)}, u32[]{:S(2)}, u32[]{:S(2)}) collective-permute-start(bf16[96,256]{1,0:T(8,128)(2,1)S(1)} %pad_maximum_fusion.10), channel_id=1, source_target_pairs={{0,1},{1,0},{2,3},{3,2},{4,5},{5,4},{6,7},{7,6},{8,9},{9,8},{10,11... | collective-permute-start | bytes 147464 | tf_op jit(solution)/shard_map/ppermute | solution.py:14
  38.7 12.5 %all-to-all-start.1 = ((bf16[16,6,512]{2,1,0:T(8,128)(2,1)}), bf16[16,6,512]{2,1,0:T(8,128)(2,1)S(1)}, u32[]{:S(2)}, u32[]{:S(2)}) async-start(bf16[16,6,512]{2,1,0:T(8,128)(2,1)} %all_to_all.27), calls=%async_computation.1 | async-start | bytes 262144 | tf_op jit(solution)/shard_map/all_to_all | solution.py:91

commit v8 on v7

--- a/solution.py
+++ b/solution.py
@@ -34,16 +34,26 @@
     )
 
 
-def sum_over_hid(part):
+def sum_over_hid(part, blocks):
     bits = (lax.axis_size("hid") - 1).bit_length()
+    rounds = [(1, 2, 3)] + [(1 << bit,) for bit in range(2, bits)]
     total = part
-    for low in range(0, bits, 2):
+    for at, masks in enumerate(rounds):
         sent = total.astype(jnp.bfloat16)
-        masks = [1 << low]
-        if low + 1 < bits:
-            masks += [2 << low, 3 << low]
-        total = total + sum(exchange(sent, mask).astype(jnp.float32) for mask in masks)
-    return total.astype(jnp.bfloat16)
+        if at == 1:
+            late = {mask: blocks[mask] for mask in blocks if mask not in early}
+            sent, late = lax.optimization_barrier((sent, late))
+        got = [exchange(sent, mask) for mask in masks]
+        if at == 0:
+            early = {mask: exchange(blocks[mask], mask) for mask in blocks if mask not in masks}
+            got = lax.optimization_barrier(got)
+        elif at == 1:
+            late = {mask: exchange(late[mask], mask) for mask in late}
+            got, early = lax.optimization_barrier((got, early))
+        else:
+            got = lax.optimization_barrier(got)
+        total = total + sum(x.astype(jnp.float32) for x in got)
+    return total.astype(jnp.bfloat16), [(early | late)[mask] for mask in blocks]
 
 
 def halves(x, first):
@@ -71,18 +81,20 @@
     act_f, pullback = jax.vjp(gelu_tanh, pre_f)
     act = act_f.astype(jnp.bfloat16)
 
-    latents = sum_over_hid(jnp.concatenate([dot(act, low_u), dot_t(grad, low_v)], axis=1))
+    part = jnp.concatenate([dot(act, low_u), dot_t(grad, low_v)], axis=1)
+    blocks = {}
+    for level in range(1, levels + 1):
+        term = dot_t(grad, butterfly[0, level]).astype(jnp.bfloat16)
+        blocks[1 << level - 1] = jnp.concatenate([act, term], axis=1)
+    latents, fars = sum_over_hid(part, blocks)
     latent, dlatent = latents[:, :rank], latents[:, rank:]
 
-    acts = [act]
+    acts = [act] + [far[:, :side] for far in fars]
     total = dot(act, butterfly[0, 0])
     back = dot_t(grad, butterfly[0, 0])
     for level in range(1, levels + 1):
-        term = dot_t(grad, butterfly[0, level]).astype(jnp.bfloat16)
-        far = exchange(jnp.concatenate([act, term], axis=1), 1 << level - 1)
-        acts.append(far[:, :side])
-        total = total + dot(far[:, :side], butterfly[0, level])
-        back = back + far[:, side:].astype(jnp.float32)
+        total = total + dot(acts[level], butterfly[0, level])
+        back = back + fars[level - 1][:, side:].astype(jnp.float32)
 
     output_rows = (total + dot(latent, low_v)).astype(jnp.bfloat16)
     grad_act = (back + dot_t(dlatent, low_u)).astype(jnp.bfloat16)

time: 52.2 us -> 51.1 us (0.979)
  starting transfers between devices: 17.2 us -> 14.8 us
  waiting for transfers between devices: 9.52 us -> 10.8 us
    ppermute x10 -> x9, starting transfers between devices: 12.6 us -> 10.6 us  [exchange(): lax.ppermute(x, 'hid', [(i, i ^ mask) for i in range(lax.axis_size('hid'))])]
    ppermute x10 -> x9, waiting for transfers between devices: 4.45 us -> 5.76 us  [exchange(): lax.ppermute(x, 'hid', [(i, i ^ mask) for i in range(lax.axis_size('hid'))])]
  transfers between devices with their start and end apart: 13 -> 12, of which waited for: 4 -> 4; matrix products, arithmetic and copies ran while one was open for 10% -> 11% of each run, Pallas kernels for 0% -> 0%
where the time goes in v8:
time: 51.1 us; the launch traced here: 50.8 us
  blocking collectives  16 us (31%)
  starting transfers between devices  14.8 us (29%)
  waiting for transfers between devices  10.8 us (21%)
  matrix products  5.21 us (10%)
  local copies, waits for them, and re-layouts  1.52 us (3%)
  other arithmetic  1.36 us (3%)
  between operations  1.06 us (2%)
    all_to_all x1, blocking collectives, on_device(): rows = lax.all_to_all(both, 'hid', split_axis=1, concat_axis=0, tiled=True)  16 us
    ppermute x9, starting transfers between devices, exchange(): lax.ppermute(x, 'hid', [(i, i ^ mask) for i in range(lax.axis_size('hid'))])  10.6 us
    ppermute x9, waiting for transfers between devices, exchange(): lax.ppermute(x, 'hid', [(i, i ^ mask) for i in range(lax.axis_size('hid'))])  5.76 us
    all_to_all x1, waiting for transfers between devices, on_device(): lax.all_to_all(results, 'hid', split_axis=0, concat_axis=1, tiled=True)  5.06 us
    all_to_all x1, starting transfers between devices, on_device(): lax.all_to_all(results, 'hid', split_axis=0, concat_axis=1, tiled=True)  3.99 us
    dot_general x3, matrix products, inner_rows(): lax.dot_general(left, right, (((0,), (0,)), ((), ())), preferred_element_...  2.88 us
    dot_general x7, matrix products, dot_t(): lax.dot_general(left, right, (((1,), (1,)), ((), ())), preferred_element_...  1.22 us
    dot_general x7, matrix products, dot(): return jnp.dot(left, right, preferred_element_type=jnp.float32)  1.11 us
  transfers between devices with their start and end apart: 12, of which 4 were waited for; matrix products, arithmetic and copies ran while one was open for 11% of the time, Pallas kernels for 0%

profile of v8, /device:TPU:0, one launch (start us, length us, event | category | flops | bytes accessed | tf_op | source)
XLA Modules:
  0.0 50.8 jit_solution(14243237321344731083)
XLA Ops:
  0.6 0.0 copy-start
  0.7 0.9 %pad_maximum_fusion.5 = bf16[6,16,512]{2,0,1:T(8,128)(2,1)S(1)} fusion(bf16[6,16,256]{2,0,1:T(8,128)(2,1)} %bitcast.38, bf16[6,16,256]{2,0,1:T(8,128)(2,1)} %bitcast.39), kind=kLoop, calls=%fused_computation.32 | loop fusion | flops 196608 | bytes 196608 | tf_op jit(solution)/shard_map/concatenate | solution.py:75
  1.6 0.0 copy-start.2
  1.6 16.0 %all_to_all.32 = bf16[6,16,512]{2,0,1:T(8,128)(2,1)S(1)} all-to-all(bf16[6,16,512]{2,0,1:T(8,128)(2,1)S(1)} %pad_maximum_fusion.5), channel_id=1, replica_groups=mesh['hid'=16,'seq'=2] {'hid'}, dimensions={1} | all-to-all | bytes 196608 | tf_op jit(solution)/shard_map/all_to_all | solution.py:78
  17.6 0.0 copy-start.1
  17.7 0.0 copy-done
  17.7 0.2 fusion.67
  17.9 0.0 copy-done.2
  17.9 0.2 fusion.69
  18.1 1.2 %collective-permute-start = (bf16[96,512]{1,0:T(8,128)(2,1)S(1)}, bf16[96,512]{1,0:T(8,128)(2,1)S(1)}, u32[]{:S(2)}, u32[]{:S(2)}) collective-permute-start(bf16[96,512]{1,0:T(8,128)(2,1)S(1)} %fusion.5), channel_id=1, source_target_pairs={{0,2},{2,0},{4,6},{6,4},{8,10},{10,8},{12,14},{14,12},{16,18},{18,... | collective-permute-start | bytes 294920 | tf_op jit(solution)/shard_map/ppermute | solution.py:10
  19.2 0.2 collective-permute-start.1
  19.5 2.2 %collective-permute-start.2 = (bf16[96,512]{1,0:T(8,128)(2,1)S(1)}, bf16[96,512]{1,0:T(8,128)(2,1)S(1)}, u32[]{:S(2)}, u32[]{:S(2)}) collective-permute-start(bf16[96,512]{1,0:T(8,128)(2,1)S(1)} %fusion.5), channel_id=1, source_target_pairs={{0,6},{2,4},{4,2},{6,0},{8,14},{10,12},{12,10},{14,8},{16,22},{18,... | collective-permute-start | bytes 294920 | tf_op jit(solution)/shard_map/ppermute | solution.py:10
  21.7 0.0 copy-done.1
  21.7 0.2 fusion.17
  21.9 0.2 convolution_convert_fusion
  22.1 0.2 convolution_convert_fusion.1
  22.3 0.2 convolution_convert_fusion.3
  22.5 0.2 convolution_convert_fusion.2
  22.7 0.2 fusion.19
  22.9 0.8 %collective-permute-start.6 = (bf16[96,512]{1,0:T(8,128)(2,1)S(1)}, bf16[96,512]{1,0:T(8,128)(2,1)S(1)}, u32[]{:S(2)}, u32[]{:S(2)}) collective-permute-start(bf16[96,512]{1,0:T(8,128)(2,1)S(1)} %get-tuple-element.46), channel_id=1, source_target_pairs={{0,8},{2,10},{4,12},{6,14},{8,0},{10,2},{12,4},{14,6},{16,24},{18,... | collective-permute-start | bytes 294920 | tf_op jit(solution)/shard_map/ppermute | solution.py:10
  23.7 1.1 %collective-permute-start.7 = (bf16[96,512]{1,0:T(8,128)(2,1)S(1)}, bf16[96,512]{1,0:T(8,128)(2,1)S(1)}, u32[]{:S(2)}, u32[]{:S(2)}) collective-permute-start(bf16[96,512]{1,0:T(8,128)(2,1)S(1)} %get-tuple-element.45), channel_id=1, source_target_pairs={{0,16},{2,18},{4,20},{6,22},{8,24},{10,26},{12,28},{14,30},{16,0},... | collective-permute-start | bytes 294920 | tf_op jit(solution)/shard_map/ppermute | solution.py:10
  24.8 0.0 collective-permute-done
  24.8 0.0 collective-permute-done.1
  24.8 0.1 collective-permute-done.2
  25.0 1.1 %collective-permute-start.5 = (bf16[96,512]{1,0:T(8,128)(2,1)S(1)}, bf16[96,512]{1,0:T(8,128)(2,1)S(1)}, u32[]{:S(2)}, u32[]{:S(2)}) collective-permute-start(bf16[96,512]{1,0:T(8,128)(2,1)S(1)} %get-tuple-element.24), channel_id=1, source_target_pairs={{0,8},{2,10},{4,12},{6,14},{8,0},{10,2},{12,4},{14,6},{16,24},{18,... | collective-permute-start | bytes 294920 | tf_op jit(solution)/shard_map/ppermute | solution.py:10
  26.1 1.1 %collective-permute-start.4 = (bf16[96,512]{1,0:T(8,128)(2,1)S(1)}, bf16[96,512]{1,0:T(8,128)(2,1)S(1)}, u32[]{:S(2)}, u32[]{:S(2)}) collective-permute-start(bf16[96,512]{1,0:T(8,128)(2,1)S(1)} %get-tuple-element.23), channel_id=1, source_target_pairs={{0,4},{2,6},{4,0},{6,2},{8,12},{10,14},{12,8},{14,10},{16,20},{18,... | collective-permute-start | bytes 294920 | tf_op jit(solution)/shard_map/ppermute | solution.py:10
  27.2 1.5 %collective-permute-start.3 = (bf16[96,512]{1,0:T(8,128)(2,1)S(1)}, bf16[96,512]{1,0:T(8,128)(2,1)S(1)}, u32[]{:S(2)}, u32[]{:S(2)}) collective-permute-start(bf16[96,512]{1,0:T(8,128)(2,1)S(1)} %get-tuple-element.22), channel_id=1, source_target_pairs={{0,2},{2,0},{4,6},{6,4},{8,10},{10,8},{12,14},{14,12},{16,18},{18,... | collective-permute-start | bytes 294920 | tf_op jit(solution)/shard_map/ppermute | solution.py:10
  28.7 0.0 collective-permute-done.6
  28.7 1.7 %collective-permute-done.7 = bf16[96,512]{1,0:T(8,128)(2,1)S(1)} collective-permute-done((bf16[96,512]{1,0:T(8,128)(2,1)S(1)}, bf16[96,512]{1,0:T(8,128)(2,1)S(1)}, u32[]{:S(2)}, u32[]{:S(2)}) %collective-permute-start.7) | collective-permute-done | bytes 98336 | tf_op jit(solution)/shard_map/ppermute | solution.py:10
  30.4 0.0 collective-permute-done.5
  30.4 1.6 %collective-permute-start.8 = (bf16[96,512]{1,0:T(8,128)(2,1)S(1)}, bf16[96,512]{1,0:T(8,128)(2,1)S(1)}, u32[]{:S(2)}, u32[]{:S(2)}) collective-permute-start(bf16[96,512]{1,0:T(8,128)(2,1)S(1)} %fusion.7), channel_id=1, source_target_pairs={{0,16},{2,18},{4,20},{6,22},{8,24},{10,26},{12,28},{14,30},{16,0},... | collective-permute-start | bytes 294920 | tf_op jit(solution)/shard_map/ppermute | solution.py:10
  32.0 0.1 fusion.10
  32.1 0.0 collective-permute-done.3
  32.2 0.0 collective-permute-done.4
  32.2 0.2 convolution_add_fusion.3
  32.4 0.2 fusion
  32.6 0.2 convolution_add_fusion.1
  32.8 0.1 collective-permute-start.9
  32.9 3.9 %collective-permute-done.8 = bf16[96,512]{1,0:T(8,128)(2,1)S(1)} collective-permute-done((bf16[96,512]{1,0:T(8,128)(2,1)S(1)}, bf16[96,512]{1,0:T(8,128)(2,1)S(1)}, u32[]{:S(2)}, u32[]{:S(2)}) %collective-permute-start.8) | collective-permute-done | bytes 98336 | tf_op jit(solution)/shard_map/ppermute | solution.py:10
  36.9 0.2 fusion.1
  37.0 0.1 collective-permute-start.10
  37.1 0.2 fusion.33
  37.4 0.7 %all_to_all.27 = bf16[16,6,512]{2,1,0:T(8,128)(2,1)} reshape(bf16[96,512]{1,0:T(8,128)(2,1)S(1)} %pad_maximum_fusion.6) | data formatting | bytes 196608 | tf_op jit(solution)/shard_map/all_to_all | solution.py:103
  38.0 4.0 %all-to-all-start.1 = ((bf16[16,6,512]{2,1,0:T(8,128)(2,1)}), bf16[16,6,512]{2,1,0:T(8,128)(2,1)S(1)}, u32[]{:S(2)}, u32[]{:S(2)}) async-start(bf16[16,6,512]{2,1,0:T(8,128)(2,1)} %all_to_all.27), calls=%async_computation.1 | async-start | bytes 262144 | tf_op jit(solution)/shard_map/all_to_all | solution.py:103
  42.0 0.0 collective-permute-done.10
  42.1 0.0 collective-permute-done.9
  42.1 0.9 %convolution_multiply_fusion.2 = f32[256,128]{1,0:T(8,128)} fusion(bf16[96,256]{1,0:T(8,128)(2,1)S(1)} %get-tuple-element.31, bf16[96,256]{1,0:T(8,128)(2,1)S(1)} %fusion.38, bf16[96,128]{1,0:T(8,128)(2,1)S(1)} %get-tuple-element.44, bf16[96,128]{1,0:T(8,128)(2,1)S(1)} %get-tuple-element.36), kind=kOutput, calls=%fused_computation.2 | convolution fusion | flops 12910592 | bytes 278528 | tf_op jit(solution)/shard_map/dot_general | solution.py:32
  43.1 0.9 %convolution_multiply_fusion.1 = f32[128,256]{1,0:T(8,128)} fusion(bf16[96,256]{1,0:T(8,128)(2,1)S(1)} %get-tuple-element.32, bf16[96,256]{1,0:T(8,128)(2,1)S(1)} %get-tuple-element.39, bf16[96,128]{1,0:T(8,128)(2,1)S(1)} %get-tuple-element.43, bf16[96,128]{1,0:T(8,128)(2,1)S(1)} %get-tuple-element.35), kind=kOutput, calls=%fused_computation.1 | convolution fusion | flops 12910592 | bytes 278528 | tf_op jit(solution)/shard_map/dot_general | solution.py:32
  43.9 1.1 %convolution_multiply_fusion = f32[640,256]{1,0:T(8,128)} fusion(bf16[96,640]{1,0:T(8,128)(2,1)S(1)} %constant_dynamic-update-slice_fusion.11, bf16[96,640]{1,0:T(8,128)(2,1)S(1)} %get-tuple-element.41, bf16[96,256]{1,0:T(8,128)(2,1)S(1)} %get-tuple-element.32, bf16[96,256]{1,0:T(8,128)(2,1)S(1)} %get-tuple-element.39), kind=kOutput, calls=%fused_computation | convolution fusion | flops 63766528 | bytes 999424 | tf_op jit(solution)/shard_map/dot_general | solution.py:32
  45.1 5.1 %all-to-all-done.1 = bf16[16,6,512]{2,1,0:T(8,128)(2,1)S(1)} async-done(((bf16[16,6,512]{2,1,0:T(8,128)(2,1)}), bf16[16,6,512]{2,1,0:T(8,128)(2,1)S(1)}, u32[]{:S(2)}, u32[]{:S(2)}) %all-to-all-start.1) | async-done | bytes 98336 | tf_op jit(solution)/shard_map/all_to_all | solution.py:103
  50.1 0.7 %fusion.74 = (bf16[6,16,256]{2,0,1:T(8,128)(2,1)}, bf16[6,16,256]{2,0,1:T(8,128)(2,1)}) fusion(bf16[6,16,512]{2,0,1:T(8,128)(2,1)S(1)} %bitcast.37), kind=kLoop, calls=%fused_computation.122 | loop fusion | bytes 196608 | tf_op jit(solution)/shard_map/slice | solution.py:106
  (27 shorter events, 0.6 us)
Async XLA Ops:
  0.6 17.1 %copy-start = (bf16[256,256]{1,0:T(8,128)(2,1)S(1)}, bf16[256,256]{1,0:T(8,128)(2,1)}, u32[]{:S(2)}) copy-start(bf16[256,256]{1,0:T(8,128)(2,1)} %param.8) | copy-start | bytes 393220
  1.6 16.3 %copy-start.2 = (bf16[256,256]{1,0:T(8,128)(2,1)S(1)}, bf16[256,256]{1,0:T(8,128)(2,1)}, u32[]{:S(2)}) copy-start(bf16[256,256]{1,0:T(8,128)(2,1)} %param.7) | copy-start | bytes 393220
  17.6 4.0 %copy-start.1 = (bf16[1,5,256,256]{3,2,1,0:T(8,128)(2,1)S(1)}, bf16[1,5,256,256]{3,2,1,0:T(8,128)(2,1)}, u32[]{:S(2)}) copy-start(bf16[1,5,256,256]{3,2,1,0:T(8,128)(2,1)} %param.6) | copy-start | bytes 1966084
  18.1 6.7 %collective-permute-start = (bf16[96,512]{1,0:T(8,128)(2,1)S(1)}, bf16[96,512]{1,0:T(8,128)(2,1)S(1)}, u32[]{:S(2)}, u32[]{:S(2)}) collective-permute-start(bf16[96,512]{1,0:T(8,128)(2,1)S(1)} %fusion.5), channel_id=1, source_target_pairs={{0,2},{2,0},{4,6},{6,4},{8,10},{10,8},{12,14},{14,12},{16,18},{18,... | collective-permute-start | bytes 294920 | tf_op jit(solution)/shard_map/ppermute | solution.py:10
  19.2 5.6 %collective-permute-start.1 = (bf16[96,512]{1,0:T(8,128)(2,1)S(1)}, bf16[96,512]{1,0:T(8,128)(2,1)S(1)}, u32[]{:S(2)}, u32[]{:S(2)}) collective-permute-start(bf16[96,512]{1,0:T(8,128)(2,1)S(1)} %fusion.5), channel_id=1, source_target_pairs={{0,4},{2,6},{4,0},{6,2},{8,12},{10,14},{12,8},{14,10},{16,20},{18,... | collective-permute-start | bytes 294920 | tf_op jit(solution)/shard_map/ppermute | solution.py:10
  19.5 5.5 %collective-permute-start.2 = (bf16[96,512]{1,0:T(8,128)(2,1)S(1)}, bf16[96,512]{1,0:T(8,128)(2,1)S(1)}, u32[]{:S(2)}, u32[]{:S(2)}) collective-permute-start(bf16[96,512]{1,0:T(8,128)(2,1)S(1)} %fusion.5), channel_id=1, source_target_pairs={{0,6},{2,4},{4,2},{6,0},{8,14},{10,12},{12,10},{14,8},{16,22},{18,... | collective-permute-start | bytes 294920 | tf_op jit(solution)/shard_map/ppermute | solution.py:10
  22.9 5.8 %collective-permute-start.6 = (bf16[96,512]{1,0:T(8,128)(2,1)S(1)}, bf16[96,512]{1,0:T(8,128)(2,1)S(1)}, u32[]{:S(2)}, u32[]{:S(2)}) collective-permute-start(bf16[96,512]{1,0:T(8,128)(2,1)S(1)} %get-tuple-element.46), channel_id=1, source_target_pairs={{0,8},{2,10},{4,12},{6,14},{8,0},{10,2},{12,4},{14,6},{16,24},{18,... | collective-permute-start | bytes 294920 | tf_op jit(solution)/shard_map/ppermute | solution.py:10
  23.7 6.7 %collective-permute-start.7 = (bf16[96,512]{1,0:T(8,128)(2,1)S(1)}, bf16[96,512]{1,0:T(8,128)(2,1)S(1)}, u32[]{:S(2)}, u32[]{:S(2)}) collective-permute-start(bf16[96,512]{1,0:T(8,128)(2,1)S(1)} %get-tuple-element.45), channel_id=1, source_target_pairs={{0,16},{2,18},{4,20},{6,22},{8,24},{10,26},{12,28},{14,30},{16,0},... | collective-permute-start | bytes 294920 | tf_op jit(solution)/shard_map/ppermute | solution.py:10
  25.0 5.4 %collective-permute-start.5 = (bf16[96,512]{1,0:T(8,128)(2,1)S(1)}, bf16[96,512]{1,0:T(8,128)(2,1)S(1)}, u32[]{:S(2)}, u32[]{:S(2)}) collective-permute-start(bf16[96,512]{1,0:T(8,128)(2,1)S(1)} %get-tuple-element.24), channel_id=1, source_target_pairs={{0,8},{2,10},{4,12},{6,14},{8,0},{10,2},{12,4},{14,6},{16,24},{18,... | collective-permute-start | bytes 294920 | tf_op jit(solution)/shard_map/ppermute | solution.py:10
  26.1 6.1 %collective-permute-start.4 = (bf16[96,512]{1,0:T(8,128)(2,1)S(1)}, bf16[96,512]{1,0:T(8,128)(2,1)S(1)}, u32[]{:S(2)}, u32[]{:S(2)}) collective-permute-start(bf16[96,512]{1,0:T(8,128)(2,1)S(1)} %get-tuple-element.23), channel_id=1, source_target_pairs={{0,4},{2,6},{4,0},{6,2},{8,12},{10,14},{12,8},{14,10},{16,20},{18,... | collective-permute-start | bytes 294920 | tf_op jit(solution)/shard_map/ppermute | solution.py:10
  27.2 4.9 %collective-permute-start.3 = (bf16[96,512]{1,0:T(8,128)(2,1)S(1)}, bf16[96,512]{1,0:T(8,128)(2,1)S(1)}, u32[]{:S(2)}, u32[]{:S(2)}) collective-permute-start(bf16[96,512]{1,0:T(8,128)(2,1)S(1)} %get-tuple-element.22), channel_id=1, source_target_pairs={{0,2},{2,0},{4,6},{6,4},{8,10},{10,8},{12,14},{14,12},{16,18},{18,... | collective-permute-start | bytes 294920 | tf_op jit(solution)/shard_map/ppermute | solution.py:10
  30.4 6.4 %collective-permute-start.8 = (bf16[96,512]{1,0:T(8,128)(2,1)S(1)}, bf16[96,512]{1,0:T(8,128)(2,1)S(1)}, u32[]{:S(2)}, u32[]{:S(2)}) collective-permute-start(bf16[96,512]{1,0:T(8,128)(2,1)S(1)} %fusion.7), channel_id=1, source_target_pairs={{0,16},{2,18},{4,20},{6,22},{8,24},{10,26},{12,28},{14,30},{16,0},... | collective-permute-start | bytes 294920 | tf_op jit(solution)/shard_map/ppermute | solution.py:10
  32.8 9.2 %collective-permute-start.9 = (bf16[96,1024]{1,0:T(8,128)(2,1)S(1)}, bf16[96,1024]{1,0:T(8,128)(2,1)S(1)}, u32[]{:S(2)}, u32[]{:S(2)}) collective-permute-start(bf16[96,1024]{1,0:T(8,128)(2,1)S(1)} %constant_dynamic-update-slice_fusion.5), channel_id=1, source_target_pairs={{0,1},{1,0},{2,3},{3,2},{4,5},{5,4},{6,7},{7,6},{8,9},{9,8},{10,11... | collective-permute-start | bytes 589832 | tf_op jit(solution)/shard_map/ppermute | solution.py:14
  37.0 5.0 %collective-permute-start.10 = (bf16[96,256]{1,0:T(8,128)(2,1)S(1)}, bf16[96,256]{1,0:T(8,128)(2,1)S(1)}, u32[]{:S(2)}, u32[]{:S(2)}) collective-permute-start(bf16[96,256]{1,0:T(8,128)(2,1)S(1)} %pad_maximum_fusion.10), channel_id=1, source_target_pairs={{0,1},{1,0},{2,3},{3,2},{4,5},{5,4},{6,7},{7,6},{8,9},{9,8},{10,11... | collective-permute-start | bytes 147464 | tf_op jit(solution)/shard_map/ppermute | solution.py:14
  38.0 12.1 %all-to-all-start.1 = ((bf16[16,6,512]{2,1,0:T(8,128)(2,1)}), bf16[16,6,512]{2,1,0:T(8,128)(2,1)S(1)}, u32[]{:S(2)}, u32[]{:S(2)}) async-start(bf16[16,6,512]{2,1,0:T(8,128)(2,1)} %all_to_all.27), calls=%async_computation.1 | async-start | bytes 262144 | tf_op jit(solution)/shard_map/all_to_all | solution.py:103

commit v9 on v8

--- a/solution.py
+++ b/solution.py
@@ -34,26 +34,30 @@
     )
 
 
-def sum_over_hid(part, blocks):
+def sum_over_hid(part, blocks, data):
     bits = (lax.axis_size("hid") - 1).bit_length()
     rounds = [(1, 2, 3)] + [(1 << bit,) for bit in range(2, bits)]
-    total = part
+    total, far = part, {}
     for at, masks in enumerate(rounds):
         sent = total.astype(jnp.bfloat16)
+        if at == 0:
+            beside = {mask: blocks[mask] for mask in sorted(blocks, reverse=True) if mask > 3}
+        elif at == 1:
+            early, beside = far, {mask: blocks[mask] for mask in blocks if mask not in far}
+            sent, beside = lax.optimization_barrier((sent, beside))
+        else:
+            beside = {}
+        if at == len(rounds) - 1:
+            sent, data = lax.optimization_barrier((sent, data))
+        got = [exchange(sent, mask) for mask in masks]
+        far = far | {mask: exchange(beside[mask], mask) for mask in beside}
         if at == 1:
-            late = {mask: blocks[mask] for mask in blocks if mask not in early}
-            sent, late = lax.optimization_barrier((sent, late))
-        got = [exchange(sent, mask) for mask in masks]
-        if at == 0:
-            early = {mask: exchange(blocks[mask], mask) for mask in blocks if mask not in masks}
-            got = lax.optimization_barrier(got)
-        elif at == 1:
-            late = {mask: exchange(late[mask], mask) for mask in late}
             got, early = lax.optimization_barrier((got, early))
+            far = far | early
         else:
             got = lax.optimization_barrier(got)
         total = total + sum(x.astype(jnp.float32) for x in got)
-    return total.astype(jnp.bfloat16), [(early | late)[mask] for mask in blocks]
+    return total.astype(jnp.bfloat16), [far[mask] for mask in blocks], data
 
 
 def halves(x, first):
@@ -82,16 +86,17 @@
     act = act_f.astype(jnp.bfloat16)
 
     part = jnp.concatenate([dot(act, low_u), dot_t(grad, low_v)], axis=1)
-    blocks = {}
-    for level in range(1, levels + 1):
-        term = dot_t(grad, butterfly[0, level]).astype(jnp.bfloat16)
-        blocks[1 << level - 1] = jnp.concatenate([act, term], axis=1)
-    latents, fars = sum_over_hid(part, blocks)
+    terms = dot_t(grad, butterfly.reshape((levels + 1) * side, side))
+    back, *terms = jnp.split(terms, levels + 1, axis=1)
+    blocks = {
+        1 << level: jnp.concatenate([act, term.astype(jnp.bfloat16)], axis=1)
+        for level, term in enumerate(terms)
+    }
+    latents, fars, (act, grad) = sum_over_hid(part, blocks, (act, grad))
     latent, dlatent = latents[:, :rank], latents[:, rank:]
 
     acts = [act] + [far[:, :side] for far in fars]
     total = dot(act, butterfly[0, 0])
-    back = dot_t(grad, butterfly[0, 0])
     for level in range(1, levels + 1):
         total = total + dot(acts[level], butterfly[0, level])
         back = back + fars[level - 1][:, side:].astype(jnp.float32)

time: 51.1 us -> 50.9 us (level)
  waiting for transfers between devices: 10.8 us -> 11.9 us
  starting transfers between devices: 14.8 us -> 14.2 us
    ppermute x9, waiting for transfers between devices: 5.76 us -> 6.83 us  [exchange(): lax.ppermute(x, 'hid', [(i, i ^ mask) for i in range(lax.axis_size('hid'))])]
    ppermute x9, starting transfers between devices: 10.6 us -> 9.95 us  [exchange(): lax.ppermute(x, 'hid', [(i, i ^ mask) for i in range(lax.axis_size('hid'))])]
    dot_general x7 -> x3, matrix products: 1.22 us -> 0.73 us  [dot_t(): lax.dot_general(left, right, (((1,), (1,)), ((), ())), preferred_element_...]
  transfers between devices with their start and end apart: 12 -> 12, of which waited for: 4 -> 6; matrix products, arithmetic and copies ran while one was open for 11% -> 10% of each run, Pallas kernels for 0% -> 0%
where the time goes in v9:
time: 50.9 us; the launch traced here: 50.6 us
  blocking collectives  16 us (31%)
  starting transfers between devices  14.2 us (28%)
  waiting for transfers between devices  11.9 us (23%)
  matrix products  4.7 us (9%)
  local copies, waits for them, and re-layouts  1.54 us (3%)
  other arithmetic  1.33 us (3%)
  between operations  0.94 us (2%)
    all_to_all x1, blocking collectives, on_device(): rows = lax.all_to_all(both, 'hid', split_axis=1, concat_axis=0, tiled=True)  16 us
    ppermute x9, starting transfers between devices, exchange(): lax.ppermute(x, 'hid', [(i, i ^ mask) for i in range(lax.axis_size('hid'))])  9.95 us
    ppermute x9, waiting for transfers between devices, exchange(): lax.ppermute(x, 'hid', [(i, i ^ mask) for i in range(lax.axis_size('hid'))])  6.83 us
    all_to_all x1, waiting for transfers between devices, on_device(): lax.all_to_all(results, 'hid', split_axis=0, concat_axis=1, tiled=True)  5.07 us
    all_to_all x1, starting transfers between devices, on_device(): lax.all_to_all(results, 'hid', split_axis=0, concat_axis=1, tiled=True)  4.09 us
    dot_general x3, matrix products, inner_rows(): lax.dot_general(left, right, (((0,), (0,)), ((), ())), preferred_element_...  2.87 us
    dot_general x7, matrix products, dot(): return jnp.dot(left, right, preferred_element_type=jnp.float32)  1.1 us
  transfers between devices with their start and end apart: 12, of which 6 were waited for; matrix products, arithmetic and copies ran while one was open for 10% of the time, Pallas kernels for 0%

profile of v9, /device:TPU:0, one launch (start us, length us, event | category | flops | bytes accessed | tf_op | source)
XLA Modules:
  0.0 50.6 jit_solution(6782391904109701262)
XLA Ops:
  0.6 0.0 copy-start
  0.7 0.9 %pad_maximum_fusion.5 = bf16[6,16,512]{2,0,1:T(8,128)(2,1)S(1)} fusion(bf16[6,16,256]{2,0,1:T(8,128)(2,1)} %bitcast.32, bf16[6,16,256]{2,0,1:T(8,128)(2,1)} %bitcast.33), kind=kLoop, calls=%fused_computation.28 | loop fusion | flops 196608 | bytes 196608 | tf_op jit(solution)/shard_map/concatenate | solution.py:79
  1.6 0.0 copy-start.2
  1.6 16.0 %all_to_all.32 = bf16[6,16,512]{2,0,1:T(8,128)(2,1)S(1)} all-to-all(bf16[6,16,512]{2,0,1:T(8,128)(2,1)S(1)} %pad_maximum_fusion.5), channel_id=1, replica_groups=mesh['hid'=16,'seq'=2] {'hid'}, dimensions={1} | all-to-all | bytes 196608 | tf_op jit(solution)/shard_map/all_to_all | solution.py:82
  17.6 0.0 copy-start.1
  17.7 0.0 copy-done
  17.7 0.2 fusion.58
  17.9 0.0 copy-done.2
  17.9 0.2 fusion.60
  18.1 1.2 %collective-permute-start = (bf16[96,512]{1,0:T(8,128)(2,1)S(1)}, bf16[96,512]{1,0:T(8,128)(2,1)S(1)}, u32[]{:S(2)}, u32[]{:S(2)}) collective-permute-start(bf16[96,512]{1,0:T(8,128)(2,1)S(1)} %fusion.5), channel_id=1, source_target_pairs={{0,2},{2,0},{4,6},{6,4},{8,10},{10,8},{12,14},{14,12},{16,18},{18,... | collective-permute-start | bytes 294920 | tf_op jit(solution)/shard_map/ppermute | solution.py:10
  19.2 0.2 collective-permute-start.1
  19.5 2.2 %collective-permute-start.2 = (bf16[96,512]{1,0:T(8,128)(2,1)S(1)}, bf16[96,512]{1,0:T(8,128)(2,1)S(1)}, u32[]{:S(2)}, u32[]{:S(2)}) collective-permute-start(bf16[96,512]{1,0:T(8,128)(2,1)S(1)} %fusion.5), channel_id=1, source_target_pairs={{0,6},{2,4},{4,2},{6,0},{8,14},{10,12},{12,10},{14,8},{16,22},{18,... | collective-permute-start | bytes 294920 | tf_op jit(solution)/shard_map/ppermute | solution.py:10
  21.7 0.0 copy-done.1
  21.7 0.3 fusion.67
  22.1 0.8 %collective-permute-start.4 = (bf16[96,512]{1,0:T(8,128)(2,1)S(1)}, bf16[96,512]{1,0:T(8,128)(2,1)S(1)}, u32[]{:S(2)}, u32[]{:S(2)}) collective-permute-start(bf16[96,512]{1,0:T(8,128)(2,1)S(1)} %get-tuple-element.54), channel_id=1, source_target_pairs={{0,8},{2,10},{4,12},{6,14},{8,0},{10,2},{12,4},{14,6},{16,24},{18,... | collective-permute-start | bytes 294920 | tf_op jit(solution)/shard_map/ppermute | solution.py:10
  22.9 1.1 %collective-permute-start.5 = (bf16[96,512]{1,0:T(8,128)(2,1)S(1)}, bf16[96,512]{1,0:T(8,128)(2,1)S(1)}, u32[]{:S(2)}, u32[]{:S(2)}) collective-permute-start(bf16[96,512]{1,0:T(8,128)(2,1)S(1)} %get-tuple-element.53), channel_id=1, source_target_pairs={{0,16},{2,18},{4,20},{6,22},{8,24},{10,26},{12,28},{14,30},{16,0},... | collective-permute-start | bytes 294920 | tf_op jit(solution)/shard_map/ppermute | solution.py:10
  24.0 0.0 collective-permute-done
  24.0 0.0 collective-permute-done.1
  24.0 1.0 %collective-permute-done.2 = bf16[96,512]{1,0:T(8,128)(2,1)S(1)} collective-permute-done((bf16[96,512]{1,0:T(8,128)(2,1)S(1)}, bf16[96,512]{1,0:T(8,128)(2,1)S(1)}, u32[]{:S(2)}, u32[]{:S(2)}) %collective-permute-start.2) | collective-permute-done | bytes 98336 | tf_op jit(solution)/shard_map/ppermute | solution.py:10
  25.0 0.8 %collective-permute-start.3 = (bf16[96,512]{1,0:T(8,128)(2,1)S(1)}, bf16[96,512]{1,0:T(8,128)(2,1)S(1)}, u32[]{:S(2)}, u32[]{:S(2)}) collective-permute-start(bf16[96,512]{1,0:T(8,128)(2,1)S(1)} %get-tuple-element.25), channel_id=1, source_target_pairs={{0,8},{2,10},{4,12},{6,14},{8,0},{10,2},{12,4},{14,6},{16,24},{18,... | collective-permute-start | bytes 294920 | tf_op jit(solution)/shard_map/ppermute | solution.py:10
  25.8 1.3 %collective-permute-start.7 = (bf16[96,512]{1,0:T(8,128)(2,1)S(1)}, bf16[96,512]{1,0:T(8,128)(2,1)S(1)}, u32[]{:S(2)}, u32[]{:S(2)}) collective-permute-start(bf16[96,512]{1,0:T(8,128)(2,1)S(1)} %get-tuple-element.29), channel_id=1, source_target_pairs={{0,4},{2,6},{4,0},{6,2},{8,12},{10,14},{12,8},{14,10},{16,20},{18,... | collective-permute-start | bytes 294920 | tf_op jit(solution)/shard_map/ppermute | solution.py:10
  27.1 1.5 %collective-permute-start.6 = (bf16[96,512]{1,0:T(8,128)(2,1)S(1)}, bf16[96,512]{1,0:T(8,128)(2,1)S(1)}, u32[]{:S(2)}, u32[]{:S(2)}) collective-permute-start(bf16[96,512]{1,0:T(8,128)(2,1)S(1)} %get-tuple-element.28), channel_id=1, source_target_pairs={{0,2},{2,0},{4,6},{6,4},{8,10},{10,8},{12,14},{14,12},{16,18},{18,... | collective-permute-start | bytes 294920 | tf_op jit(solution)/shard_map/ppermute | solution.py:10
  28.6 0.0 collective-permute-done.4
  28.6 1.0 %collective-permute-done.5 = bf16[96,512]{1,0:T(8,128)(2,1)S(1)} collective-permute-done((bf16[96,512]{1,0:T(8,128)(2,1)S(1)}, bf16[96,512]{1,0:T(8,128)(2,1)S(1)}, u32[]{:S(2)}, u32[]{:S(2)}) %collective-permute-start.5) | collective-permute-done | bytes 98336 | tf_op jit(solution)/shard_map/ppermute | solution.py:10
  29.6 0.3 collective-permute-done.3
  30.0 0.9 %collective-permute-start.8 = (bf16[96,512]{1,0:T(8,128)(2,1)S(1)}, bf16[96,512]{1,0:T(8,128)(2,1)S(1)}, u32[]{:S(2)}, u32[]{:S(2)}) collective-permute-start(bf16[96,512]{1,0:T(8,128)(2,1)S(1)} %fusion.7), channel_id=1, source_target_pairs={{0,16},{2,18},{4,20},{6,22},{8,24},{10,26},{12,28},{14,30},{16,0},... | collective-permute-start | bytes 294920 | tf_op jit(solution)/shard_map/ppermute | solution.py:10
  30.9 0.1 fusion.9
  31.0 0.2 fusion.13
  31.2 0.5 collective-permute-done.6
  31.8 0.0 collective-permute-done.7
  31.8 0.2 convolution_add_fusion.3
  32.0 0.2 fusion
  32.2 0.2 convolution_add_fusion.1
  32.4 0.1 collective-permute-start.9
  32.5 4.0 %collective-permute-done.8 = bf16[96,512]{1,0:T(8,128)(2,1)S(1)} collective-permute-done((bf16[96,512]{1,0:T(8,128)(2,1)S(1)}, bf16[96,512]{1,0:T(8,128)(2,1)S(1)}, u32[]{:S(2)}, u32[]{:S(2)}) %collective-permute-start.8) | collective-permute-done | bytes 98336 | tf_op jit(solution)/shard_map/ppermute | solution.py:10
  36.6 0.2 fusion.1
  36.8 0.1 collective-permute-start.10
  36.9 0.2 fusion.22
  37.1 0.7 %all_to_all.27 = bf16[16,6,512]{2,1,0:T(8,128)(2,1)} reshape(bf16[96,512]{1,0:T(8,128)(2,1)S(1)} %pad_maximum_fusion.6) | data formatting | bytes 196608 | tf_op jit(solution)/shard_map/all_to_all | solution.py:108
  37.8 4.1 %all-to-all-start.1 = ((bf16[16,6,512]{2,1,0:T(8,128)(2,1)}), bf16[16,6,512]{2,1,0:T(8,128)(2,1)S(1)}, u32[]{:S(2)}, u32[]{:S(2)}) async-start(bf16[16,6,512]{2,1,0:T(8,128)(2,1)} %all_to_all.27), calls=%async_computation.1 | async-start | bytes 262144 | tf_op jit(solution)/shard_map/all_to_all | solution.py:108
  41.9 0.0 collective-permute-done.10
  41.9 0.0 collective-permute-done.9
  41.9 0.9 %convolution_multiply_fusion.2 = f32[256,128]{1,0:T(8,128)} fusion(bf16[96,256]{1,0:T(8,128)(2,1)S(1)} %get-tuple-element.41, bf16[96,256]{1,0:T(8,128)(2,1)S(1)} %fusion.27, bf16[96,128]{1,0:T(8,128)(2,1)S(1)} %get-tuple-element.52, bf16[96,128]{1,0:T(8,128)(2,1)S(1)} %get-tuple-element.46), kind=kOutput, calls=%fused_computation.2 | convolution fusion | flops 12910592 | bytes 278528 | tf_op jit(solution)/shard_map/dot_general | solution.py:32
  42.9 0.9 %convolution_multiply_fusion.1 = f32[128,256]{1,0:T(8,128)} fusion(bf16[96,256]{1,0:T(8,128)(2,1)S(1)} %get-tuple-element.42, bf16[96,256]{1,0:T(8,128)(2,1)S(1)} %slice.176, bf16[96,128]{1,0:T(8,128)(2,1)S(1)} %get-tuple-element.51, bf16[96,128]{1,0:T(8,128)(2,1)S(1)} %get-tuple-element.45), kind=kOutput, calls=%fused_computation.1 | convolution fusion | flops 12910592 | bytes 278528 | tf_op jit(solution)/shard_map/dot_general | solution.py:32
  43.8 1.1 %convolution_multiply_fusion = f32[640,256]{1,0:T(8,128)} fusion(bf16[96,640]{1,0:T(8,128)(2,1)S(1)} %constant_dynamic-update-slice_fusion.11, bf16[96,640]{1,0:T(8,128)(2,1)S(1)} %get-tuple-element.49, bf16[96,256]{1,0:T(8,128)(2,1)S(1)} %get-tuple-element.42, bf16[96,256]{1,0:T(8,128)(2,1)S(1)} %slice.176), kind=kOutput, calls=%fused_computation | convolution fusion | flops 63766528 | bytes 999424 | tf_op jit(solution)/shard_map/dot_general | solution.py:32
  44.9 5.1 %all-to-all-done.1 = bf16[16,6,512]{2,1,0:T(8,128)(2,1)S(1)} async-done(((bf16[16,6,512]{2,1,0:T(8,128)(2,1)}), bf16[16,6,512]{2,1,0:T(8,128)(2,1)S(1)}, u32[]{:S(2)}, u32[]{:S(2)}) %all-to-all-start.1) | async-done | bytes 98336 | tf_op jit(solution)/shard_map/all_to_all | solution.py:108
  50.0 0.7 %fusion.65 = (bf16[6,16,256]{2,0,1:T(8,128)(2,1)}, bf16[6,16,256]{2,0,1:T(8,128)(2,1)}) fusion(bf16[6,16,512]{2,0,1:T(8,128)(2,1)S(1)} %bitcast.31), kind=kLoop, calls=%fused_computation.109 | loop fusion | bytes 196608 | tf_op jit(solution)/shard_map/slice | solution.py:111
  (29 shorter events, 0.6 us)
Async XLA Ops:
  0.6 17.1 %copy-start = (bf16[256,256]{1,0:T(8,128)(2,1)S(1)}, bf16[256,256]{1,0:T(8,128)(2,1)}, u32[]{:S(2)}) copy-start(bf16[256,256]{1,0:T(8,128)(2,1)} %param.8) | copy-start | bytes 393220
  1.6 16.3 %copy-start.2 = (bf16[256,256]{1,0:T(8,128)(2,1)S(1)}, bf16[256,256]{1,0:T(8,128)(2,1)}, u32[]{:S(2)}) copy-start(bf16[256,256]{1,0:T(8,128)(2,1)} %param.7) | copy-start | bytes 393220
  17.6 4.0 %copy-start.1 = (bf16[1,5,256,256]{3,2,1,0:T(8,128)(2,1)S(1)}, bf16[1,5,256,256]{3,2,1,0:T(8,128)(2,1)}, u32[]{:S(2)}) copy-start(bf16[1,5,256,256]{3,2,1,0:T(8,128)(2,1)} %param.6) | copy-start | bytes 1966084
  18.1 5.9 %collective-permute-start = (bf16[96,512]{1,0:T(8,128)(2,1)S(1)}, bf16[96,512]{1,0:T(8,128)(2,1)S(1)}, u32[]{:S(2)}, u32[]{:S(2)}) collective-permute-start(bf16[96,512]{1,0:T(8,128)(2,1)S(1)} %fusion.5), channel_id=1, source_target_pairs={{0,2},{2,0},{4,6},{6,4},{8,10},{10,8},{12,14},{14,12},{16,18},{18,... | collective-permute-start | bytes 294920 | tf_op jit(solution)/shard_map/ppermute | solution.py:10
  19.2 4.8 %collective-permute-start.1 = (bf16[96,512]{1,0:T(8,128)(2,1)S(1)}, bf16[96,512]{1,0:T(8,128)(2,1)S(1)}, u32[]{:S(2)}, u32[]{:S(2)}) collective-permute-start(bf16[96,512]{1,0:T(8,128)(2,1)S(1)} %fusion.5), channel_id=1, source_target_pairs={{0,4},{2,6},{4,0},{6,2},{8,12},{10,14},{12,8},{14,10},{16,20},{18,... | collective-permute-start | bytes 294920 | tf_op jit(solution)/shard_map/ppermute | solution.py:10
  19.5 5.5 %collective-permute-start.2 = (bf16[96,512]{1,0:T(8,128)(2,1)S(1)}, bf16[96,512]{1,0:T(8,128)(2,1)S(1)}, u32[]{:S(2)}, u32[]{:S(2)}) collective-permute-start(bf16[96,512]{1,0:T(8,128)(2,1)S(1)} %fusion.5), channel_id=1, source_target_pairs={{0,6},{2,4},{4,2},{6,0},{8,14},{10,12},{12,10},{14,8},{16,22},{18,... | collective-permute-start | bytes 294920 | tf_op jit(solution)/shard_map/ppermute | solution.py:10
  22.1 6.5 %collective-permute-start.4 = (bf16[96,512]{1,0:T(8,128)(2,1)S(1)}, bf16[96,512]{1,0:T(8,128)(2,1)S(1)}, u32[]{:S(2)}, u32[]{:S(2)}) collective-permute-start(bf16[96,512]{1,0:T(8,128)(2,1)S(1)} %get-tuple-element.54), channel_id=1, source_target_pairs={{0,8},{2,10},{4,12},{6,14},{8,0},{10,2},{12,4},{14,6},{16,24},{18,... | collective-permute-start | bytes 294920 | tf_op jit(solution)/shard_map/ppermute | solution.py:10
  22.9 6.7 %collective-permute-start.5 = (bf16[96,512]{1,0:T(8,128)(2,1)S(1)}, bf16[96,512]{1,0:T(8,128)(2,1)S(1)}, u32[]{:S(2)}, u32[]{:S(2)}) collective-permute-start(bf16[96,512]{1,0:T(8,128)(2,1)S(1)} %get-tuple-element.53), channel_id=1, source_target_pairs={{0,16},{2,18},{4,20},{6,22},{8,24},{10,26},{12,28},{14,30},{16,0},... | collective-permute-start | bytes 294920 | tf_op jit(solution)/shard_map/ppermute | solution.py:10
  25.0 4.9 %collective-permute-start.3 = (bf16[96,512]{1,0:T(8,128)(2,1)S(1)}, bf16[96,512]{1,0:T(8,128)(2,1)S(1)}, u32[]{:S(2)}, u32[]{:S(2)}) collective-permute-start(bf16[96,512]{1,0:T(8,128)(2,1)S(1)} %get-tuple-element.25), channel_id=1, source_target_pairs={{0,8},{2,10},{4,12},{6,14},{8,0},{10,2},{12,4},{14,6},{16,24},{18,... | collective-permute-start | bytes 294920 | tf_op jit(solution)/shard_map/ppermute | solution.py:10
  25.8 5.9 %collective-permute-start.7 = (bf16[96,512]{1,0:T(8,128)(2,1)S(1)}, bf16[96,512]{1,0:T(8,128)(2,1)S(1)}, u32[]{:S(2)}, u32[]{:S(2)}) collective-permute-start(bf16[96,512]{1,0:T(8,128)(2,1)S(1)} %get-tuple-element.29), channel_id=1, source_target_pairs={{0,4},{2,6},{4,0},{6,2},{8,12},{10,14},{12,8},{14,10},{16,20},{18,... | collective-permute-start | bytes 294920 | tf_op jit(solution)/shard_map/ppermute | solution.py:10
  27.1 4.6 %collective-permute-start.6 = (bf16[96,512]{1,0:T(8,128)(2,1)S(1)}, bf16[96,512]{1,0:T(8,128)(2,1)S(1)}, u32[]{:S(2)}, u32[]{:S(2)}) collective-permute-start(bf16[96,512]{1,0:T(8,128)(2,1)S(1)} %get-tuple-element.28), channel_id=1, source_target_pairs={{0,2},{2,0},{4,6},{6,4},{8,10},{10,8},{12,14},{14,12},{16,18},{18,... | collective-permute-start | bytes 294920 | tf_op jit(solution)/shard_map/ppermute | solution.py:10
  30.0 6.6 %collective-permute-start.8 = (bf16[96,512]{1,0:T(8,128)(2,1)S(1)}, bf16[96,512]{1,0:T(8,128)(2,1)S(1)}, u32[]{:S(2)}, u32[]{:S(2)}) collective-permute-start(bf16[96,512]{1,0:T(8,128)(2,1)S(1)} %fusion.7), channel_id=1, source_target_pairs={{0,16},{2,18},{4,20},{6,22},{8,24},{10,26},{12,28},{14,30},{16,0},... | collective-permute-start | bytes 294920 | tf_op jit(solution)/shard_map/ppermute | solution.py:10
  32.4 9.5 %collective-permute-start.9 = (bf16[96,1024]{1,0:T(8,128)(2,1)S(1)}, bf16[96,1024]{1,0:T(8,128)(2,1)S(1)}, u32[]{:S(2)}, u32[]{:S(2)}) collective-permute-start(bf16[96,1024]{1,0:T(8,128)(2,1)S(1)} %constant_dynamic-update-slice_fusion.5), channel_id=1, source_target_pairs={{0,1},{1,0},{2,3},{3,2},{4,5},{5,4},{6,7},{7,6},{8,9},{9,8},{10,11... | collective-permute-start | bytes 589832 | tf_op jit(solution)/shard_map/ppermute | solution.py:14
  36.8 5.1 %collective-permute-start.10 = (bf16[96,256]{1,0:T(8,128)(2,1)S(1)}, bf16[96,256]{1,0:T(8,128)(2,1)S(1)}, u32[]{:S(2)}, u32[]{:S(2)}) collective-permute-start(bf16[96,256]{1,0:T(8,128)(2,1)S(1)} %pad_maximum_fusion.10), channel_id=1, source_target_pairs={{0,1},{1,0},{2,3},{3,2},{4,5},{5,4},{6,7},{7,6},{8,9},{9,8},{10,11... | collective-permute-start | bytes 147464 | tf_op jit(solution)/shard_map/ppermute | solution.py:14
  37.8 12.2 %all-to-all-start.1 = ((bf16[16,6,512]{2,1,0:T(8,128)(2,1)}), bf16[16,6,512]{2,1,0:T(8,128)(2,1)S(1)}, u32[]{:S(2)}, u32[]{:S(2)}) async-start(bf16[16,6,512]{2,1,0:T(8,128)(2,1)} %all_to_all.27), calls=%async_computation.1 | async-start | bytes 262144 | tf_op jit(solution)/shard_map/all_to_all | solution.py:108

commit v10 on v9

--- a/solution.py
+++ b/solution.py
@@ -105,29 +105,33 @@
     grad_act = (back + dot_t(dlatent, low_u)).astype(jnp.bfloat16)
     grad_pre_rows = pullback(grad_act.astype(jnp.float32))[0].astype(jnp.bfloat16)
     results = jnp.concatenate([output_rows, grad_pre_rows], axis=1)
-    results = lax.all_to_all(results, "hid", split_axis=0, concat_axis=1, tiled=True)
-    results = results.reshape(tokens, hid, 2 * side)
-    output = results[:, :, :side].reshape(tokens, hid * side)
-    grad_pre = results[:, :, side:].reshape(tokens, hid * side)
-
     split = [halves(x, first) for x in acts[1:]]
-    got = mate(jnp.concatenate([grad, act] + [theirs for ours, theirs in split[::-1]], axis=1))
-    far_grad, far_act = got[:, :side], got[:, side : 2 * side]
-    far_halves = jnp.split(got[:, 2 * side :], levels, axis=1)[::-1]
     latent, sent_latent = halves(latent, first)
     dlatent, sent_dlatent = halves(dlatent, first)
-    got = mate(jnp.concatenate([sent_latent, sent_dlatent], axis=1))
+    sent = [grad, act, sent_latent, sent_dlatent] + [theirs for ours, theirs in split]
+    results, sent = lax.optimization_barrier((results, jnp.concatenate(sent, axis=1)))
+    results = lax.all_to_all(results.reshape(hid, tokens, 2 * side), "hid", 0, 0, tiled=True)
+
+    got = mate(sent)
+    ends = [side, 2 * side, 2 * side + rank // 2, 2 * side + rank]
+    far_grad, far_act, far_latent, far_dlatent, far_halves = jnp.split(got, ends, axis=1)
 
     def tokens_of(own, far):
         return jnp.concatenate([own, far], axis=0)
 
     grads = tokens_of(grad, far_grad)
     own = jnp.concatenate([halves(act, first)[0]] + [ours for ours, theirs in split], axis=1)
-    far = jnp.concatenate([halves(far_act, first)[0]] + far_halves, axis=1)
+    far = jnp.concatenate([halves(far_act, first)[0], far_halves], axis=1)
     grad_butterfly = inner_rows(tokens_of(own, far), grads) * factor
     grad_butterfly = grad_butterfly.reshape(1, levels + 1, side // 2, side)
-    grad_low_u = inner_rows(tokens_of(act, far_act), tokens_of(dlatent, got[:, rank // 2 :])) * factor
-    grad_low_v = inner_rows(tokens_of(latent, got[:, : rank // 2]), grads) * factor
+    grad_low_u = inner_rows(tokens_of(act, far_act), tokens_of(dlatent, far_dlatent)) * factor
+    grad_low_v = inner_rows(tokens_of(latent, far_latent), grads) * factor
+
+    results, grad_butterfly, grad_low_u, grad_low_v = lax.optimization_barrier(
+        (results, grad_butterfly, grad_low_u, grad_low_v)
+    )
+    output = results[:, :, :side].transpose(1, 0, 2).reshape(tokens, hid * side)
+    grad_pre = results[:, :, side:].transpose(1, 0, 2).reshape(tokens, hid * side)
     return (output, grad_pre, grad_butterfly, grad_low_u, grad_low_v)
 
 

time: 50.9 us -> 51.1 us (level)
    reshape x0 -> x1, local copies, waits for them, and re-layouts: none -> 0.69 us  [on_device(): results.reshape(hid, tokens, 2 * side)]
    all_to_all x1 -> x0, local copies, waits for them, and re-layouts: 0.68 us -> none  [on_device(): lax.all_to_all(results, 'hid', split_axis=0, concat_axis=1, tiled=True)]
  transfers between devices with their start and end apart: 12 -> 11, of which waited for: 6 -> 6; matrix products, arithmetic and copies ran while one was open for 10% -> 10% of each run, Pallas kernels for 0% -> 0%
where the time goes in v10:
time: 51.1 us; the launch traced here: 50.8 us
  blocking collectives  16 us (31%)
  starting transfers between devices  14.1 us (28%)
  waiting for transfers between devices  12.3 us (24%)
  matrix products  4.7 us (9%)
  local copies, waits for them, and re-layouts  1.48 us (3%)
  other arithmetic  1.32 us (3%)
  between operations  0.88 us (2%)
    all_to_all x1, blocking collectives, on_device(): rows = lax.all_to_all(both, 'hid', split_axis=1, concat_axis=0, tiled=True)  16 us
    ppermute x9, starting transfers between devices, exchange(): lax.ppermute(x, 'hid', [(i, i ^ mask) for i in range(lax.axis_size('hid'))])  9.95 us
    ppermute x9, waiting for transfers between devices, exchange(): lax.ppermute(x, 'hid', [(i, i ^ mask) for i in range(lax.axis_size('hid'))])  7.09 us
    all_to_all x1, waiting for transfers between devices, on_device(): lax.all_to_all(results.reshape(hid, tokens, 2 * side), 'hid', 0, 0, tiled...  5.16 us
    all_to_all x1, starting transfers between devices, on_device(): lax.all_to_all(results.reshape(hid, tokens, 2 * side), 'hid', 0, 0, tiled...  4.09 us
    dot_general x3, matrix products, inner_rows(): lax.dot_general(left, right, (((0,), (0,)), ((), ())), preferred_element_...  2.88 us
    dot_general x7, matrix products, dot(): return jnp.dot(left, right, preferred_element_type=jnp.float32)  1.09 us
  transfers between devices with their start and end apart: 11, of which 6 were waited for; matrix products, arithmetic and copies ran while one was open for 10% of the time, Pallas kernels for 0%

profile of v10, /device:TPU:0, one launch (start us, length us, event | category | flops | bytes accessed | tf_op | source)
XLA Modules:
  0.0 50.8 jit_solution(1776149804421756041)
XLA Ops:
  0.6 0.0 copy-start
  0.7 0.9 %pad_maximum_fusion.5 = bf16[6,16,512]{2,0,1:T(8,128)(2,1)S(1)} fusion(bf16[6,16,256]{2,0,1:T(8,128)(2,1)} %bitcast.34, bf16[6,16,256]{2,0,1:T(8,128)(2,1)} %bitcast.35), kind=kLoop, calls=%fused_computation.30 | loop fusion | flops 196608 | bytes 196608 | tf_op jit(solution)/shard_map/concatenate | solution.py:79
  1.6 0.0 copy-start.2
  1.6 16.0 %all_to_all.21 = bf16[6,16,512]{2,0,1:T(8,128)(2,1)S(1)} all-to-all(bf16[6,16,512]{2,0,1:T(8,128)(2,1)S(1)} %pad_maximum_fusion.5), channel_id=1, replica_groups=mesh['hid'=16,'seq'=2] {'hid'}, dimensions={1} | all-to-all | bytes 196608 | tf_op jit(solution)/shard_map/all_to_all | solution.py:82
  17.6 0.0 copy-start.1
  17.7 0.0 copy-done
  17.7 0.2 fusion.60
  17.9 0.0 copy-done.2
  17.9 0.2 fusion.62
  18.1 1.2 %collective-permute-start = (bf16[96,512]{1,0:T(8,128)(2,1)S(1)}, bf16[96,512]{1,0:T(8,128)(2,1)S(1)}, u32[]{:S(2)}, u32[]{:S(2)}) collective-permute-start(bf16[96,512]{1,0:T(8,128)(2,1)S(1)} %fusion.7), channel_id=1, source_target_pairs={{0,2},{2,0},{4,6},{6,4},{8,10},{10,8},{12,14},{14,12},{16,18},{18,... | collective-permute-start | bytes 294920 | tf_op jit(solution)/shard_map/ppermute | solution.py:10
  19.2 0.2 collective-permute-start.1
  19.5 2.2 %collective-permute-start.2 = (bf16[96,512]{1,0:T(8,128)(2,1)S(1)}, bf16[96,512]{1,0:T(8,128)(2,1)S(1)}, u32[]{:S(2)}, u32[]{:S(2)}) collective-permute-start(bf16[96,512]{1,0:T(8,128)(2,1)S(1)} %fusion.7), channel_id=1, source_target_pairs={{0,6},{2,4},{4,2},{6,0},{8,14},{10,12},{12,10},{14,8},{16,22},{18,... | collective-permute-start | bytes 294920 | tf_op jit(solution)/shard_map/ppermute | solution.py:10
  21.7 0.0 copy-done.1
  21.7 0.3 fusion.69
  22.1 0.8 %collective-permute-start.4 = (bf16[96,512]{1,0:T(8,128)(2,1)S(1)}, bf16[96,512]{1,0:T(8,128)(2,1)S(1)}, u32[]{:S(2)}, u32[]{:S(2)}) collective-permute-start(bf16[96,512]{1,0:T(8,128)(2,1)S(1)} %get-tuple-element.72), channel_id=1, source_target_pairs={{0,8},{2,10},{4,12},{6,14},{8,0},{10,2},{12,4},{14,6},{16,24},{18,... | collective-permute-start | bytes 294920 | tf_op jit(solution)/shard_map/ppermute | solution.py:10
  22.9 1.1 %collective-permute-start.5 = (bf16[96,512]{1,0:T(8,128)(2,1)S(1)}, bf16[96,512]{1,0:T(8,128)(2,1)S(1)}, u32[]{:S(2)}, u32[]{:S(2)}) collective-permute-start(bf16[96,512]{1,0:T(8,128)(2,1)S(1)} %get-tuple-element.71), channel_id=1, source_target_pairs={{0,16},{2,18},{4,20},{6,22},{8,24},{10,26},{12,28},{14,30},{16,0},... | collective-permute-start | bytes 294920 | tf_op jit(solution)/shard_map/ppermute | solution.py:10
  24.0 0.0 collective-permute-done
  24.0 0.0 collective-permute-done.1
  24.0 1.0 %collective-permute-done.2 = bf16[96,512]{1,0:T(8,128)(2,1)S(1)} collective-permute-done((bf16[96,512]{1,0:T(8,128)(2,1)S(1)}, bf16[96,512]{1,0:T(8,128)(2,1)S(1)}, u32[]{:S(2)}, u32[]{:S(2)}) %collective-permute-start.2) | collective-permute-done | bytes 98336 | tf_op jit(solution)/shard_map/ppermute | solution.py:10
  25.0 0.8 %collective-permute-start.3 = (bf16[96,512]{1,0:T(8,128)(2,1)S(1)}, bf16[96,512]{1,0:T(8,128)(2,1)S(1)}, u32[]{:S(2)}, u32[]{:S(2)}) collective-permute-start(bf16[96,512]{1,0:T(8,128)(2,1)S(1)} %get-tuple-element.31), channel_id=1, source_target_pairs={{0,8},{2,10},{4,12},{6,14},{8,0},{10,2},{12,4},{14,6},{16,24},{18,... | collective-permute-start | bytes 294920 | tf_op jit(solution)/shard_map/ppermute | solution.py:10
  25.8 1.3 %collective-permute-start.7 = (bf16[96,512]{1,0:T(8,128)(2,1)S(1)}, bf16[96,512]{1,0:T(8,128)(2,1)S(1)}, u32[]{:S(2)}, u32[]{:S(2)}) collective-permute-start(bf16[96,512]{1,0:T(8,128)(2,1)S(1)} %get-tuple-element.35), channel_id=1, source_target_pairs={{0,4},{2,6},{4,0},{6,2},{8,12},{10,14},{12,8},{14,10},{16,20},{18,... | collective-permute-start | bytes 294920 | tf_op jit(solution)/shard_map/ppermute | solution.py:10
  27.1 1.5 %collective-permute-start.6 = (bf16[96,512]{1,0:T(8,128)(2,1)S(1)}, bf16[96,512]{1,0:T(8,128)(2,1)S(1)}, u32[]{:S(2)}, u32[]{:S(2)}) collective-permute-start(bf16[96,512]{1,0:T(8,128)(2,1)S(1)} %get-tuple-element.34), channel_id=1, source_target_pairs={{0,2},{2,0},{4,6},{6,4},{8,10},{10,8},{12,14},{14,12},{16,18},{18,... | collective-permute-start | bytes 294920 | tf_op jit(solution)/shard_map/ppermute | solution.py:10
  28.6 0.0 collective-permute-done.4
  28.6 1.0 %collective-permute-done.5 = bf16[96,512]{1,0:T(8,128)(2,1)S(1)} collective-permute-done((bf16[96,512]{1,0:T(8,128)(2,1)S(1)}, bf16[96,512]{1,0:T(8,128)(2,1)S(1)}, u32[]{:S(2)}, u32[]{:S(2)}) %collective-permute-start.5) | collective-permute-done | bytes 98336 | tf_op jit(solution)/shard_map/ppermute | solution.py:10
  29.6 0.3 collective-permute-done.3
  30.0 0.9 %collective-permute-start.8 = (bf16[96,512]{1,0:T(8,128)(2,1)S(1)}, bf16[96,512]{1,0:T(8,128)(2,1)S(1)}, u32[]{:S(2)}, u32[]{:S(2)}) collective-permute-start(bf16[96,512]{1,0:T(8,128)(2,1)S(1)} %fusion.9), channel_id=1, source_target_pairs={{0,16},{2,18},{4,20},{6,22},{8,24},{10,26},{12,28},{14,30},{16,0},... | collective-permute-start | bytes 294920 | tf_op jit(solution)/shard_map/ppermute | solution.py:10
  30.9 0.1 fusion.11
  31.0 0.2 fusion.15
  31.2 0.5 collective-permute-done.6
  31.7 0.2 convolution_add_fusion.3
  31.9 0.0 collective-permute-done.7
  31.9 0.2 fusion
  32.1 0.2 convolution_add_fusion.1
  32.3 4.3 %collective-permute-done.8 = bf16[96,512]{1,0:T(8,128)(2,1)S(1)} collective-permute-done((bf16[96,512]{1,0:T(8,128)(2,1)S(1)}, bf16[96,512]{1,0:T(8,128)(2,1)S(1)}, u32[]{:S(2)}, u32[]{:S(2)}) %collective-permute-start.8) | collective-permute-done | bytes 98336 | tf_op jit(solution)/shard_map/ppermute | solution.py:10
  36.6 0.2 fusion.1
  36.8 0.2 fusion.24
  37.2 0.1 collective-permute-start.9
  37.2 0.7 %reshape.39 = bf16[16,6,512]{2,1,0:T(8,128)(2,1)} reshape(bf16[96,512]{1,0:T(8,128)(2,1)S(1)} %pad_maximum_fusion.6) | data formatting | bytes 196608 | tf_op jit(solution)/shard_map/reshape | solution.py:113
  37.9 4.1 %all-to-all-start.1 = ((bf16[16,6,512]{2,1,0:T(8,128)(2,1)}), bf16[16,6,512]{2,1,0:T(8,128)(2,1)S(1)}, u32[]{:S(2)}, u32[]{:S(2)}) async-start(bf16[16,6,512]{2,1,0:T(8,128)(2,1)} %reshape.39), calls=%async_computation.1 | async-start | bytes 262144 | tf_op jit(solution)/shard_map/all_to_all | solution.py:113
  42.0 0.0 collective-permute-done.9
  42.1 0.9 %convolution_multiply_fusion.2 = f32[256,128]{1,0:T(8,128)} fusion(bf16[96,256]{1,0:T(8,128)(2,1)S(1)} %get-tuple-element.52, bf16[96,256]{1,0:T(8,128)(2,1)S(1)} %fusion.29, bf16[96,128]{1,0:T(8,128)(2,1)S(1)} %get-tuple-element.50, bf16[96,128]{1,0:T(8,128)(2,1)S(1)} %get-tuple-element.62), kind=kOutput, calls=%fused_computation.2 | convolution fusion | flops 12910592 | bytes 278528 | tf_op jit(solution)/shard_map/dot_general | solution.py:32
  43.0 0.9 %convolution_multiply_fusion.1 = f32[128,256]{1,0:T(8,128)} fusion(bf16[96,256]{1,0:T(8,128)(2,1)S(1)} %get-tuple-element.53, bf16[96,256]{1,0:T(8,128)(2,1)S(1)} %slice.155, bf16[96,128]{1,0:T(8,128)(2,1)S(1)} %get-tuple-element.49, bf16[96,128]{1,0:T(8,128)(2,1)S(1)} %get-tuple-element.60), kind=kOutput, calls=%fused_computation.1 | convolution fusion | flops 12910592 | bytes 278528 | tf_op jit(solution)/shard_map/dot_general | solution.py:32
  43.8 1.1 %convolution_multiply_fusion = f32[640,256]{1,0:T(8,128)} fusion(bf16[96,512]{1,0:T(8,128)(2,1)S(1)} %split.49, bf16[96,128]{1,0:T(8,128)(2,1)S(1)} %get-tuple-element.51, bf16[96,640]{1,0:T(8,128)(2,1)S(1)} %get-tuple-element.63, bf16[96,256]{1,0:T(8,128)(2,1)S(1)} %get-tuple-element.53, bf16[96,256]{1,0:T(8,128)(2,1)S(1)} %slice.155), kind=kOutput, calls=%fused_computation | convolution fusion | flops 64012288 | bytes 999424 | tf_op jit(solution)/shard_map/dot_general | solution.py:32
  45.0 5.2 %all-to-all-done.1 = bf16[16,6,512]{2,1,0:T(8,128)(2,1)S(1)} async-done(((bf16[16,6,512]{2,1,0:T(8,128)(2,1)}), bf16[16,6,512]{2,1,0:T(8,128)(2,1)S(1)}, u32[]{:S(2)}, u32[]{:S(2)}) %all-to-all-start.1) | async-done | bytes 98336 | tf_op jit(solution)/shard_map/all_to_all | solution.py:113
  50.1 0.7 %fusion.68 = (bf16[16,6,256]{2,1,0:T(8,128)(2,1)}, bf16[16,6,256]{2,1,0:T(8,128)(2,1)}) fusion(bf16[16,6,512]{2,1,0:T(8,128)(2,1)S(1)} %all-to-all-done.1), kind=kLoop, calls=%fused_computation.106 | loop fusion | bytes 196608 | tf_op jit(solution)/shard_map/slice | solution.py:134
  (22 shorter events, 0.5 us)
Async XLA Ops:
  0.6 17.1 %copy-start = (bf16[256,256]{1,0:T(8,128)(2,1)S(1)}, bf16[256,256]{1,0:T(8,128)(2,1)}, u32[]{:S(2)}) copy-start(bf16[256,256]{1,0:T(8,128)(2,1)} %param.8) | copy-start | bytes 393220
  1.6 16.3 %copy-start.2 = (bf16[256,256]{1,0:T(8,128)(2,1)S(1)}, bf16[256,256]{1,0:T(8,128)(2,1)}, u32[]{:S(2)}) copy-start(bf16[256,256]{1,0:T(8,128)(2,1)} %param.7) | copy-start | bytes 393220
  17.6 4.0 %copy-start.1 = (bf16[1,5,256,256]{3,2,1,0:T(8,128)(2,1)S(1)}, bf16[1,5,256,256]{3,2,1,0:T(8,128)(2,1)}, u32[]{:S(2)}) copy-start(bf16[1,5,256,256]{3,2,1,0:T(8,128)(2,1)} %param.6) | copy-start | bytes 1966084
  18.1 5.9 %collective-permute-start = (bf16[96,512]{1,0:T(8,128)(2,1)S(1)}, bf16[96,512]{1,0:T(8,128)(2,1)S(1)}, u32[]{:S(2)}, u32[]{:S(2)}) collective-permute-start(bf16[96,512]{1,0:T(8,128)(2,1)S(1)} %fusion.7), channel_id=1, source_target_pairs={{0,2},{2,0},{4,6},{6,4},{8,10},{10,8},{12,14},{14,12},{16,18},{18,... | collective-permute-start | bytes 294920 | tf_op jit(solution)/shard_map/ppermute | solution.py:10
  19.2 4.8 %collective-permute-start.1 = (bf16[96,512]{1,0:T(8,128)(2,1)S(1)}, bf16[96,512]{1,0:T(8,128)(2,1)S(1)}, u32[]{:S(2)}, u32[]{:S(2)}) collective-permute-start(bf16[96,512]{1,0:T(8,128)(2,1)S(1)} %fusion.7), channel_id=1, source_target_pairs={{0,4},{2,6},{4,0},{6,2},{8,12},{10,14},{12,8},{14,10},{16,20},{18,... | collective-permute-start | bytes 294920 | tf_op jit(solution)/shard_map/ppermute | solution.py:10
  19.5 5.5 %collective-permute-start.2 = (bf16[96,512]{1,0:T(8,128)(2,1)S(1)}, bf16[96,512]{1,0:T(8,128)(2,1)S(1)}, u32[]{:S(2)}, u32[]{:S(2)}) collective-permute-start(bf16[96,512]{1,0:T(8,128)(2,1)S(1)} %fusion.7), channel_id=1, source_target_pairs={{0,6},{2,4},{4,2},{6,0},{8,14},{10,12},{12,10},{14,8},{16,22},{18,... | collective-permute-start | bytes 294920 | tf_op jit(solution)/shard_map/ppermute | solution.py:10
  22.1 6.5 %collective-permute-start.4 = (bf16[96,512]{1,0:T(8,128)(2,1)S(1)}, bf16[96,512]{1,0:T(8,128)(2,1)S(1)}, u32[]{:S(2)}, u32[]{:S(2)}) collective-permute-start(bf16[96,512]{1,0:T(8,128)(2,1)S(1)} %get-tuple-element.72), channel_id=1, source_target_pairs={{0,8},{2,10},{4,12},{6,14},{8,0},{10,2},{12,4},{14,6},{16,24},{18,... | collective-permute-start | bytes 294920 | tf_op jit(solution)/shard_map/ppermute | solution.py:10
  22.9 6.7 %collective-permute-start.5 = (bf16[96,512]{1,0:T(8,128)(2,1)S(1)}, bf16[96,512]{1,0:T(8,128)(2,1)S(1)}, u32[]{:S(2)}, u32[]{:S(2)}) collective-permute-start(bf16[96,512]{1,0:T(8,128)(2,1)S(1)} %get-tuple-element.71), channel_id=1, source_target_pairs={{0,16},{2,18},{4,20},{6,22},{8,24},{10,26},{12,28},{14,30},{16,0},... | collective-permute-start | bytes 294920 | tf_op jit(solution)/shard_map/ppermute | solution.py:10
  25.0 4.9 %collective-permute-start.3 = (bf16[96,512]{1,0:T(8,128)(2,1)S(1)}, bf16[96,512]{1,0:T(8,128)(2,1)S(1)}, u32[]{:S(2)}, u32[]{:S(2)}) collective-permute-start(bf16[96,512]{1,0:T(8,128)(2,1)S(1)} %get-tuple-element.31), channel_id=1, source_target_pairs={{0,8},{2,10},{4,12},{6,14},{8,0},{10,2},{12,4},{14,6},{16,24},{18,... | collective-permute-start | bytes 294920 | tf_op jit(solution)/shard_map/ppermute | solution.py:10
  25.8 6.1 %collective-permute-start.7 = (bf16[96,512]{1,0:T(8,128)(2,1)S(1)}, bf16[96,512]{1,0:T(8,128)(2,1)S(1)}, u32[]{:S(2)}, u32[]{:S(2)}) collective-permute-start(bf16[96,512]{1,0:T(8,128)(2,1)S(1)} %get-tuple-element.35), channel_id=1, source_target_pairs={{0,4},{2,6},{4,0},{6,2},{8,12},{10,14},{12,8},{14,10},{16,20},{18,... | collective-permute-start | bytes 294920 | tf_op jit(solution)/shard_map/ppermute | solution.py:10
  27.1 4.6 %collective-permute-start.6 = (bf16[96,512]{1,0:T(8,128)(2,1)S(1)}, bf16[96,512]{1,0:T(8,128)(2,1)S(1)}, u32[]{:S(2)}, u32[]{:S(2)}) collective-permute-start(bf16[96,512]{1,0:T(8,128)(2,1)S(1)} %get-tuple-element.34), channel_id=1, source_target_pairs={{0,2},{2,0},{4,6},{6,4},{8,10},{10,8},{12,14},{14,12},{16,18},{18,... | collective-permute-start | bytes 294920 | tf_op jit(solution)/shard_map/ppermute | solution.py:10
  30.0 6.6 %collective-permute-start.8 = (bf16[96,512]{1,0:T(8,128)(2,1)S(1)}, bf16[96,512]{1,0:T(8,128)(2,1)S(1)}, u32[]{:S(2)}, u32[]{:S(2)}) collective-permute-start(bf16[96,512]{1,0:T(8,128)(2,1)S(1)} %fusion.9), channel_id=1, source_target_pairs={{0,16},{2,18},{4,20},{6,22},{8,24},{10,26},{12,28},{14,30},{16,0},... | collective-permute-start | bytes 294920 | tf_op jit(solution)/shard_map/ppermute | solution.py:10
  37.2 4.9 %collective-permute-start.9 = (bf16[96,1280]{1,0:T(8,128)(2,1)S(1)}, bf16[96,1280]{1,0:T(8,128)(2,1)S(1)}, u32[]{:S(2)}, u32[]{:S(2)}) collective-permute-start(bf16[96,1280]{1,0:T(8,128)(2,1)S(1)} %get-tuple-element.42), channel_id=1, source_target_pairs={{0,1},{1,0},{2,3},{3,2},{4,5},{5,4},{6,7},{7,6},{8,9},{9,8},{10,11... | collective-permute-start | bytes 737288 | tf_op jit(solution)/shard_map/ppermute | solution.py:14
  37.9 12.2 %all-to-all-start.1 = ((bf16[16,6,512]{2,1,0:T(8,128)(2,1)}), bf16[16,6,512]{2,1,0:T(8,128)(2,1)S(1)}, u32[]{:S(2)}, u32[]{:S(2)}) async-start(bf16[16,6,512]{2,1,0:T(8,128)(2,1)} %reshape.39), calls=%async_computation.1 | async-start | bytes 262144 | tf_op jit(solution)/shard_map/all_to_all | solution.py:113

commit v11 on v10

--- a/solution.py
+++ b/solution.py
@@ -109,10 +109,11 @@
     latent, sent_latent = halves(latent, first)
     dlatent, sent_dlatent = halves(dlatent, first)
     sent = [grad, act, sent_latent, sent_dlatent] + [theirs for ours, theirs in split]
-    results, sent = lax.optimization_barrier((results, jnp.concatenate(sent, axis=1)))
-    results = lax.all_to_all(results.reshape(hid, tokens, 2 * side), "hid", 0, 0, tiled=True)
+    results = results.reshape(hid, tokens, 2 * side)
+    results, sent = lax.optimization_barrier((results, sent))
+    results = lax.all_to_all(results, "hid", 0, 0, tiled=True)
 
-    got = mate(sent)
+    got = mate(jnp.concatenate(sent, axis=1))
     ends = [side, 2 * side, 2 * side + rank // 2, 2 * side + rank]
     far_grad, far_act, far_latent, far_dlatent, far_halves = jnp.split(got, ends, axis=1)
 

time: 51.1 us -> 51 us (level)
  transfers between devices with their start and end apart: 11 -> 11, of which waited for: 6 -> 6; matrix products, arithmetic and copies ran while one was open for 10% -> 8% of each run, Pallas kernels for 0% -> 0%
where the time goes in v11:
time: 51 us; the launch traced here: 50.7 us
  blocking collectives  16 us (31%)
  starting transfers between devices  14.1 us (28%)
  waiting for transfers between devices  12.2 us (24%)
  matrix products  4.7 us (9%)
  local copies, waits for them, and re-layouts  1.56 us (3%)
  other arithmetic  1.27 us (2%)
  between operations  0.89 us (2%)
    all_to_all x1, blocking collectives, on_device(): rows = lax.all_to_all(both, 'hid', split_axis=1, concat_axis=0, tiled=True)  16 us
    ppermute x9, starting transfers between devices, exchange(): lax.ppermute(x, 'hid', [(i, i ^ mask) for i in range(lax.axis_size('hid'))])  9.95 us
    ppermute x9, waiting for transfers between devices, exchange(): lax.ppermute(x, 'hid', [(i, i ^ mask) for i in range(lax.axis_size('hid'))])  7.01 us
    all_to_all x1, waiting for transfers between devices, on_device(): results = lax.all_to_all(results, 'hid', 0, 0, tiled=True)  5.15 us
    all_to_all x1, starting transfers between devices, on_device(): results = lax.all_to_all(results, 'hid', 0, 0, tiled=True)  4.1 us
    dot_general x3, matrix products, inner_rows(): lax.dot_general(left, right, (((0,), (0,)), ((), ())), preferred_element_...  2.88 us
    dot_general x7, matrix products, dot(): return jnp.dot(left, right, preferred_element_type=jnp.float32)  1.09 us
  transfers between devices with their start and end apart: 11, of which 6 were waited for; matrix products, arithmetic and copies ran while one was open for 8% of the time, Pallas kernels for 0%

profile of v11, /device:TPU:0, one launch (start us, length us, event | category | flops | bytes accessed | tf_op | source)
XLA Modules:
  0.0 50.7 jit_solution(14399086965874944804)
XLA Ops:
  0.6 0.0 copy-start
  0.7 0.9 %pad_maximum_fusion.5 = bf16[6,16,512]{2,0,1:T(8,128)(2,1)S(1)} fusion(bf16[6,16,256]{2,0,1:T(8,128)(2,1)} %bitcast.34, bf16[6,16,256]{2,0,1:T(8,128)(2,1)} %bitcast.35), kind=kLoop, calls=%fused_computation.30 | loop fusion | flops 196608 | bytes 196608 | tf_op jit(solution)/shard_map/concatenate | solution.py:79
  1.6 0.0 copy-start.2
  1.6 16.0 %all_to_all.21 = bf16[6,16,512]{2,0,1:T(8,128)(2,1)S(1)} all-to-all(bf16[6,16,512]{2,0,1:T(8,128)(2,1)S(1)} %pad_maximum_fusion.5), channel_id=1, replica_groups=mesh['hid'=16,'seq'=2] {'hid'}, dimensions={1} | all-to-all | bytes 196608 | tf_op jit(solution)/shard_map/all_to_all | solution.py:82
  17.6 0.0 copy-start.1
  17.7 0.0 copy-done
  17.7 0.2 fusion.60
  17.9 0.0 copy-done.2
  17.9 0.2 fusion.62
  18.1 1.2 %collective-permute-start = (bf16[96,512]{1,0:T(8,128)(2,1)S(1)}, bf16[96,512]{1,0:T(8,128)(2,1)S(1)}, u32[]{:S(2)}, u32[]{:S(2)}) collective-permute-start(bf16[96,512]{1,0:T(8,128)(2,1)S(1)} %fusion.7), channel_id=1, source_target_pairs={{0,2},{2,0},{4,6},{6,4},{8,10},{10,8},{12,14},{14,12},{16,18},{18,... | collective-permute-start | bytes 294920 | tf_op jit(solution)/shard_map/ppermute | solution.py:10
  19.2 0.2 collective-permute-start.1
  19.5 2.2 %collective-permute-start.2 = (bf16[96,512]{1,0:T(8,128)(2,1)S(1)}, bf16[96,512]{1,0:T(8,128)(2,1)S(1)}, u32[]{:S(2)}, u32[]{:S(2)}) collective-permute-start(bf16[96,512]{1,0:T(8,128)(2,1)S(1)} %fusion.7), channel_id=1, source_target_pairs={{0,6},{2,4},{4,2},{6,0},{8,14},{10,12},{12,10},{14,8},{16,22},{18,... | collective-permute-start | bytes 294920 | tf_op jit(solution)/shard_map/ppermute | solution.py:10
  21.7 0.0 copy-done.1
  21.7 0.3 fusion.69
  22.1 0.8 %collective-permute-start.4 = (bf16[96,512]{1,0:T(8,128)(2,1)S(1)}, bf16[96,512]{1,0:T(8,128)(2,1)S(1)}, u32[]{:S(2)}, u32[]{:S(2)}) collective-permute-start(bf16[96,512]{1,0:T(8,128)(2,1)S(1)} %get-tuple-element.87), channel_id=1, source_target_pairs={{0,8},{2,10},{4,12},{6,14},{8,0},{10,2},{12,4},{14,6},{16,24},{18,... | collective-permute-start | bytes 294920 | tf_op jit(solution)/shard_map/ppermute | solution.py:10
  22.9 1.1 %collective-permute-start.5 = (bf16[96,512]{1,0:T(8,128)(2,1)S(1)}, bf16[96,512]{1,0:T(8,128)(2,1)S(1)}, u32[]{:S(2)}, u32[]{:S(2)}) collective-permute-start(bf16[96,512]{1,0:T(8,128)(2,1)S(1)} %get-tuple-element.86), channel_id=1, source_target_pairs={{0,16},{2,18},{4,20},{6,22},{8,24},{10,26},{12,28},{14,30},{16,0},... | collective-permute-start | bytes 294920 | tf_op jit(solution)/shard_map/ppermute | solution.py:10
  24.0 0.0 collective-permute-done
  24.0 0.0 collective-permute-done.1
  24.0 1.0 %collective-permute-done.2 = bf16[96,512]{1,0:T(8,128)(2,1)S(1)} collective-permute-done((bf16[96,512]{1,0:T(8,128)(2,1)S(1)}, bf16[96,512]{1,0:T(8,128)(2,1)S(1)}, u32[]{:S(2)}, u32[]{:S(2)}) %collective-permute-start.2) | collective-permute-done | bytes 98336 | tf_op jit(solution)/shard_map/ppermute | solution.py:10
  25.0 0.8 %collective-permute-start.3 = (bf16[96,512]{1,0:T(8,128)(2,1)S(1)}, bf16[96,512]{1,0:T(8,128)(2,1)S(1)}, u32[]{:S(2)}, u32[]{:S(2)}) collective-permute-start(bf16[96,512]{1,0:T(8,128)(2,1)S(1)} %get-tuple-element.38), channel_id=1, source_target_pairs={{0,8},{2,10},{4,12},{6,14},{8,0},{10,2},{12,4},{14,6},{16,24},{18,... | collective-permute-start | bytes 294920 | tf_op jit(solution)/shard_map/ppermute | solution.py:10
  25.8 1.3 %collective-permute-start.7 = (bf16[96,512]{1,0:T(8,128)(2,1)S(1)}, bf16[96,512]{1,0:T(8,128)(2,1)S(1)}, u32[]{:S(2)}, u32[]{:S(2)}) collective-permute-start(bf16[96,512]{1,0:T(8,128)(2,1)S(1)} %get-tuple-element.42), channel_id=1, source_target_pairs={{0,4},{2,6},{4,0},{6,2},{8,12},{10,14},{12,8},{14,10},{16,20},{18,... | collective-permute-start | bytes 294920 | tf_op jit(solution)/shard_map/ppermute | solution.py:10
  27.1 1.5 %collective-permute-start.6 = (bf16[96,512]{1,0:T(8,128)(2,1)S(1)}, bf16[96,512]{1,0:T(8,128)(2,1)S(1)}, u32[]{:S(2)}, u32[]{:S(2)}) collective-permute-start(bf16[96,512]{1,0:T(8,128)(2,1)S(1)} %get-tuple-element.41), channel_id=1, source_target_pairs={{0,2},{2,0},{4,6},{6,4},{8,10},{10,8},{12,14},{14,12},{16,18},{18,... | collective-permute-start | bytes 294920 | tf_op jit(solution)/shard_map/ppermute | solution.py:10
  28.6 0.0 collective-permute-done.4
  28.6 1.0 %collective-permute-done.5 = bf16[96,512]{1,0:T(8,128)(2,1)S(1)} collective-permute-done((bf16[96,512]{1,0:T(8,128)(2,1)S(1)}, bf16[96,512]{1,0:T(8,128)(2,1)S(1)}, u32[]{:S(2)}, u32[]{:S(2)}) %collective-permute-start.5) | collective-permute-done | bytes 98336 | tf_op jit(solution)/shard_map/ppermute | solution.py:10
  29.6 0.3 collective-permute-done.3
  30.0 0.9 %collective-permute-start.8 = (bf16[96,512]{1,0:T(8,128)(2,1)S(1)}, bf16[96,512]{1,0:T(8,128)(2,1)S(1)}, u32[]{:S(2)}, u32[]{:S(2)}) collective-permute-start(bf16[96,512]{1,0:T(8,128)(2,1)S(1)} %fusion.9), channel_id=1, source_target_pairs={{0,16},{2,18},{4,20},{6,22},{8,24},{10,26},{12,28},{14,30},{16,0},... | collective-permute-start | bytes 294920 | tf_op jit(solution)/shard_map/ppermute | solution.py:10
  30.9 0.1 fusion.11
  31.0 0.2 fusion.15
  31.2 0.5 collective-permute-done.6
  31.8 0.0 collective-permute-done.7
  31.8 0.2 convolution_add_fusion.3
  32.0 0.2 fusion
  32.2 0.2 convolution_add_fusion.1
  32.3 4.2 %collective-permute-done.8 = bf16[96,512]{1,0:T(8,128)(2,1)S(1)} collective-permute-done((bf16[96,512]{1,0:T(8,128)(2,1)S(1)}, bf16[96,512]{1,0:T(8,128)(2,1)S(1)}, u32[]{:S(2)}, u32[]{:S(2)}) %collective-permute-start.8) | collective-permute-done | bytes 98336 | tf_op jit(solution)/shard_map/ppermute | solution.py:10
  36.6 0.2 fusion.1
  36.8 0.2 fusion.24
  37.0 0.7 %reshape.39 = bf16[16,6,512]{2,1,0:T(8,128)(2,1)} reshape(bf16[96,512]{1,0:T(8,128)(2,1)S(1)} %pad_maximum_fusion.6) | data formatting | bytes 196608 | tf_op jit(solution)/shard_map/reshape | solution.py:112
  37.8 0.1 collective-permute-start.9
  37.9 4.1 %all-to-all-start.1 = ((bf16[16,6,512]{2,1,0:T(8,128)(2,1)}), bf16[16,6,512]{2,1,0:T(8,128)(2,1)S(1)}, u32[]{:S(2)}, u32[]{:S(2)}) async-start(bf16[16,6,512]{2,1,0:T(8,128)(2,1)} %reshape.39), calls=%async_computation.1 | async-start | bytes 262144 | tf_op jit(solution)/shard_map/all_to_all | solution.py:114
  42.0 0.0 collective-permute-done.9
  42.0 0.9 %convolution_multiply_fusion.2 = f32[256,128]{1,0:T(8,128)} fusion(bf16[96,256]{1,0:T(8,128)(2,1)S(1)} %get-tuple-element.66, bf16[96,256]{1,0:T(8,128)(2,1)S(1)} %fusion.29, bf16[96,128]{1,0:T(8,128)(2,1)S(1)} %get-tuple-element.64, bf16[96,128]{1,0:T(8,128)(2,1)S(1)} %get-tuple-element.76), kind=kOutput, calls=%fused_computation.2 | convolution fusion | flops 12910592 | bytes 278528 | tf_op jit(solution)/shard_map/dot_general | solution.py:32
  42.9 0.9 %convolution_multiply_fusion.1 = f32[128,256]{1,0:T(8,128)} fusion(bf16[96,256]{1,0:T(8,128)(2,1)S(1)} %get-tuple-element.67, bf16[96,256]{1,0:T(8,128)(2,1)S(1)} %slice.155, bf16[96,128]{1,0:T(8,128)(2,1)S(1)} %get-tuple-element.63, bf16[96,128]{1,0:T(8,128)(2,1)S(1)} %get-tuple-element.74), kind=kOutput, calls=%fused_computation.1 | convolution fusion | flops 12910592 | bytes 278528 | tf_op jit(solution)/shard_map/dot_general | solution.py:32
  43.8 1.1 %convolution_multiply_fusion = f32[640,256]{1,0:T(8,128)} fusion(bf16[96,512]{1,0:T(8,128)(2,1)S(1)} %split.49, bf16[96,128]{1,0:T(8,128)(2,1)S(1)} %get-tuple-element.65, bf16[96,640]{1,0:T(8,128)(2,1)S(1)} %get-tuple-element.78, bf16[96,256]{1,0:T(8,128)(2,1)S(1)} %get-tuple-element.67, bf16[96,256]{1,0:T(8,128)(2,1)S(1)} %slice.155), kind=kOutput, calls=%fused_computation | convolution fusion | flops 64012288 | bytes 999424 | tf_op jit(solution)/shard_map/dot_general | solution.py:32
  44.9 5.2 %all-to-all-done.1 = bf16[16,6,512]{2,1,0:T(8,128)(2,1)S(1)} async-done(((bf16[16,6,512]{2,1,0:T(8,128)(2,1)}), bf16[16,6,512]{2,1,0:T(8,128)(2,1)S(1)}, u32[]{:S(2)}, u32[]{:S(2)}) %all-to-all-start.1) | async-done | bytes 98336 | tf_op jit(solution)/shard_map/all_to_all | solution.py:114
  50.1 0.7 %fusion.68 = (bf16[16,6,256]{2,1,0:T(8,128)(2,1)}, bf16[16,6,256]{2,1,0:T(8,128)(2,1)}) fusion(bf16[16,6,512]{2,1,0:T(8,128)(2,1)S(1)} %all-to-all-done.1), kind=kLoop, calls=%fused_computation.112 | loop fusion | bytes 196608 | tf_op jit(solution)/shard_map/slice | solution.py:135
  (27 shorter events, 0.5 us)
Async XLA Ops:
  0.6 17.1 %copy-start = (bf16[256,256]{1,0:T(8,128)(2,1)S(1)}, bf16[256,256]{1,0:T(8,128)(2,1)}, u32[]{:S(2)}) copy-start(bf16[256,256]{1,0:T(8,128)(2,1)} %param.8) | copy-start | bytes 393220
  1.6 16.3 %copy-start.2 = (bf16[256,256]{1,0:T(8,128)(2,1)S(1)}, bf16[256,256]{1,0:T(8,128)(2,1)}, u32[]{:S(2)}) copy-start(bf16[256,256]{1,0:T(8,128)(2,1)} %param.7) | copy-start | bytes 393220
  17.6 4.0 %copy-start.1 = (bf16[1,5,256,256]{3,2,1,0:T(8,128)(2,1)S(1)}, bf16[1,5,256,256]{3,2,1,0:T(8,128)(2,1)}, u32[]{:S(2)}) copy-start(bf16[1,5,256,256]{3,2,1,0:T(8,128)(2,1)} %param.6) | copy-start | bytes 1966084
  18.1 5.9 %collective-permute-start = (bf16[96,512]{1,0:T(8,128)(2,1)S(1)}, bf16[96,512]{1,0:T(8,128)(2,1)S(1)}, u32[]{:S(2)}, u32[]{:S(2)}) collective-permute-start(bf16[96,512]{1,0:T(8,128)(2,1)S(1)} %fusion.7), channel_id=1, source_target_pairs={{0,2},{2,0},{4,6},{6,4},{8,10},{10,8},{12,14},{14,12},{16,18},{18,... | collective-permute-start | bytes 294920 | tf_op jit(solution)/shard_map/ppermute | solution.py:10
  19.2 4.8 %collective-permute-start.1 = (bf16[96,512]{1,0:T(8,128)(2,1)S(1)}, bf16[96,512]{1,0:T(8,128)(2,1)S(1)}, u32[]{:S(2)}, u32[]{:S(2)}) collective-permute-start(bf16[96,512]{1,0:T(8,128)(2,1)S(1)} %fusion.7), channel_id=1, source_target_pairs={{0,4},{2,6},{4,0},{6,2},{8,12},{10,14},{12,8},{14,10},{16,20},{18,... | collective-permute-start | bytes 294920 | tf_op jit(solution)/shard_map/ppermute | solution.py:10
  19.5 5.5 %collective-permute-start.2 = (bf16[96,512]{1,0:T(8,128)(2,1)S(1)}, bf16[96,512]{1,0:T(8,128)(2,1)S(1)}, u32[]{:S(2)}, u32[]{:S(2)}) collective-permute-start(bf16[96,512]{1,0:T(8,128)(2,1)S(1)} %fusion.7), channel_id=1, source_target_pairs={{0,6},{2,4},{4,2},{6,0},{8,14},{10,12},{12,10},{14,8},{16,22},{18,... | collective-permute-start | bytes 294920 | tf_op jit(solution)/shard_map/ppermute | solution.py:10
  22.1 6.5 %collective-permute-start.4 = (bf16[96,512]{1,0:T(8,128)(2,1)S(1)}, bf16[96,512]{1,0:T(8,128)(2,1)S(1)}, u32[]{:S(2)}, u32[]{:S(2)}) collective-permute-start(bf16[96,512]{1,0:T(8,128)(2,1)S(1)} %get-tuple-element.87), channel_id=1, source_target_pairs={{0,8},{2,10},{4,12},{6,14},{8,0},{10,2},{12,4},{14,6},{16,24},{18,... | collective-permute-start | bytes 294920 | tf_op jit(solution)/shard_map/ppermute | solution.py:10
  22.9 6.7 %collective-permute-start.5 = (bf16[96,512]{1,0:T(8,128)(2,1)S(1)}, bf16[96,512]{1,0:T(8,128)(2,1)S(1)}, u32[]{:S(2)}, u32[]{:S(2)}) collective-permute-start(bf16[96,512]{1,0:T(8,128)(2,1)S(1)} %get-tuple-element.86), channel_id=1, source_target_pairs={{0,16},{2,18},{4,20},{6,22},{8,24},{10,26},{12,28},{14,30},{16,0},... | collective-permute-start | bytes 294920 | tf_op jit(solution)/shard_map/ppermute | solution.py:10
  25.0 4.9 %collective-permute-start.3 = (bf16[96,512]{1,0:T(8,128)(2,1)S(1)}, bf16[96,512]{1,0:T(8,128)(2,1)S(1)}, u32[]{:S(2)}, u32[]{:S(2)}) collective-permute-start(bf16[96,512]{1,0:T(8,128)(2,1)S(1)} %get-tuple-element.38), channel_id=1, source_target_pairs={{0,8},{2,10},{4,12},{6,14},{8,0},{10,2},{12,4},{14,6},{16,24},{18,... | collective-permute-start | bytes 294920 | tf_op jit(solution)/shard_map/ppermute | solution.py:10
  25.8 5.9 %collective-permute-start.7 = (bf16[96,512]{1,0:T(8,128)(2,1)S(1)}, bf16[96,512]{1,0:T(8,128)(2,1)S(1)}, u32[]{:S(2)}, u32[]{:S(2)}) collective-permute-start(bf16[96,512]{1,0:T(8,128)(2,1)S(1)} %get-tuple-element.42), channel_id=1, source_target_pairs={{0,4},{2,6},{4,0},{6,2},{8,12},{10,14},{12,8},{14,10},{16,20},{18,... | collective-permute-start | bytes 294920 | tf_op jit(solution)/shard_map/ppermute | solution.py:10
  27.1 4.6 %collective-permute-start.6 = (bf16[96,512]{1,0:T(8,128)(2,1)S(1)}, bf16[96,512]{1,0:T(8,128)(2,1)S(1)}, u32[]{:S(2)}, u32[]{:S(2)}) collective-permute-start(bf16[96,512]{1,0:T(8,128)(2,1)S(1)} %get-tuple-element.41), channel_id=1, source_target_pairs={{0,2},{2,0},{4,6},{6,4},{8,10},{10,8},{12,14},{14,12},{16,18},{18,... | collective-permute-start | bytes 294920 | tf_op jit(solution)/shard_map/ppermute | solution.py:10
  30.0 6.6 %collective-permute-start.8 = (bf16[96,512]{1,0:T(8,128)(2,1)S(1)}, bf16[96,512]{1,0:T(8,128)(2,1)S(1)}, u32[]{:S(2)}, u32[]{:S(2)}) collective-permute-start(bf16[96,512]{1,0:T(8,128)(2,1)S(1)} %fusion.9), channel_id=1, source_target_pairs={{0,16},{2,18},{4,20},{6,22},{8,24},{10,26},{12,28},{14,30},{16,0},... | collective-permute-start | bytes 294920 | tf_op jit(solution)/shard_map/ppermute | solution.py:10
  37.8 4.2 %collective-permute-start.9 = (bf16[96,1280]{1,0:T(8,128)(2,1)S(1)}, bf16[96,1280]{1,0:T(8,128)(2,1)S(1)}, u32[]{:S(2)}, u32[]{:S(2)}) collective-permute-start(bf16[96,1280]{1,0:T(8,128)(2,1)S(1)} %constant_dynamic-update-slice_fusion.5), channel_id=1, source_target_pairs={{0,1},{1,0},{2,3},{3,2},{4,5},{5,4},{6,7},{7,6},{8,9},{9,8},{10,11... | collective-permute-start | bytes 737288 | tf_op jit(solution)/shard_map/ppermute | solution.py:14
  37.9 12.2 %all-to-all-start.1 = ((bf16[16,6,512]{2,1,0:T(8,128)(2,1)}), bf16[16,6,512]{2,1,0:T(8,128)(2,1)S(1)}, u32[]{:S(2)}, u32[]{:S(2)}) async-start(bf16[16,6,512]{2,1,0:T(8,128)(2,1)} %reshape.39), calls=%async_computation.1 | async-start | bytes 262144 | tf_op jit(solution)/shard_map/all_to_all | solution.py:114

commit v12 on v9

--- a/solution.py
+++ b/solution.py
@@ -126,6 +126,7 @@
     far = jnp.concatenate([halves(far_act, first)[0]] + far_halves, axis=1)
     grad_butterfly = inner_rows(tokens_of(own, far), grads) * factor
     grad_butterfly = grad_butterfly.reshape(1, levels + 1, side // 2, side)
+    got, grad_butterfly = lax.optimization_barrier((got, grad_butterfly))
     grad_low_u = inner_rows(tokens_of(act, far_act), tokens_of(dlatent, got[:, rank // 2 :])) * factor
     grad_low_v = inner_rows(tokens_of(latent, got[:, : rank // 2]), grads) * factor
     return (output, grad_pre, grad_butterfly, grad_low_u, grad_low_v)

time: 50.9 us -> 50.5 us (level)
  no operation moved by 1% of the time
where the time goes in v12:
time: 50.5 us; the launch traced here: 50.2 us
  blocking collectives  16 us (32%)
  starting transfers between devices  14.2 us (28%)
  waiting for transfers between devices  11.5 us (23%)
  matrix products  4.7 us (9%)
  local copies, waits for them, and re-layouts  1.54 us (3%)
  other arithmetic  1.33 us (3%)
  between operations  0.94 us (2%)
    all_to_all x1, blocking collectives, on_device(): rows = lax.all_to_all(both, 'hid', split_axis=1, concat_axis=0, tiled=True)  16 us
    ppermute x9, starting transfers between devices, exchange(): lax.ppermute(x, 'hid', [(i, i ^ mask) for i in range(lax.axis_size('hid'))])  9.95 us
    ppermute x9, waiting for transfers between devices, exchange(): lax.ppermute(x, 'hid', [(i, i ^ mask) for i in range(lax.axis_size('hid'))])  6.83 us
    all_to_all x1, waiting for transfers between devices, on_device(): lax.all_to_all(results, 'hid', split_axis=0, concat_axis=1, tiled=True)  4.68 us
    all_to_all x1, starting transfers between devices, on_device(): lax.all_to_all(results, 'hid', split_axis=0, concat_axis=1, tiled=True)  4.09 us
    dot_general x3, matrix products, inner_rows(): lax.dot_general(left, right, (((0,), (0,)), ((), ())), preferred_element_...  2.87 us
    dot_general x7, matrix products, dot(): return jnp.dot(left, right, preferred_element_type=jnp.float32)  1.1 us
  transfers between devices with their start and end apart: 12, of which 6 were waited for; matrix products, arithmetic and copies ran while one was open for 10% of the time, Pallas kernels for 0%

profile of v12, /device:TPU:0, one launch (start us, length us, event | category | flops | bytes accessed | tf_op | source)
XLA Modules:
  0.0 50.2 jit_solution(282348534661424643)
XLA Ops:
  0.6 0.0 copy-start
  0.7 0.9 %pad_maximum_fusion.5 = bf16[6,16,512]{2,0,1:T(8,128)(2,1)S(1)} fusion(bf16[6,16,256]{2,0,1:T(8,128)(2,1)} %bitcast.32, bf16[6,16,256]{2,0,1:T(8,128)(2,1)} %bitcast.33), kind=kLoop, calls=%fused_computation.28 | loop fusion | flops 196608 | bytes 196608 | tf_op jit(solution)/shard_map/concatenate | solution.py:79
  1.6 0.0 copy-start.2
  1.6 16.0 %all_to_all.32 = bf16[6,16,512]{2,0,1:T(8,128)(2,1)S(1)} all-to-all(bf16[6,16,512]{2,0,1:T(8,128)(2,1)S(1)} %pad_maximum_fusion.5), channel_id=1, replica_groups=mesh['hid'=16,'seq'=2] {'hid'}, dimensions={1} | all-to-all | bytes 196608 | tf_op jit(solution)/shard_map/all_to_all | solution.py:82
  17.6 0.0 copy-start.1
  17.7 0.0 copy-done
  17.7 0.2 fusion.58
  17.9 0.0 copy-done.2
  17.9 0.2 fusion.60
  18.1 1.2 %collective-permute-start = (bf16[96,512]{1,0:T(8,128)(2,1)S(1)}, bf16[96,512]{1,0:T(8,128)(2,1)S(1)}, u32[]{:S(2)}, u32[]{:S(2)}) collective-permute-start(bf16[96,512]{1,0:T(8,128)(2,1)S(1)} %fusion.5), channel_id=1, source_target_pairs={{0,2},{2,0},{4,6},{6,4},{8,10},{10,8},{12,14},{14,12},{16,18},{18,... | collective-permute-start | bytes 294920 | tf_op jit(solution)/shard_map/ppermute | solution.py:10
  19.2 0.2 collective-permute-start.1
  19.5 2.2 %collective-permute-start.2 = (bf16[96,512]{1,0:T(8,128)(2,1)S(1)}, bf16[96,512]{1,0:T(8,128)(2,1)S(1)}, u32[]{:S(2)}, u32[]{:S(2)}) collective-permute-start(bf16[96,512]{1,0:T(8,128)(2,1)S(1)} %fusion.5), channel_id=1, source_target_pairs={{0,6},{2,4},{4,2},{6,0},{8,14},{10,12},{12,10},{14,8},{16,22},{18,... | collective-permute-start | bytes 294920 | tf_op jit(solution)/shard_map/ppermute | solution.py:10
  21.7 0.0 copy-done.1
  21.7 0.3 fusion.67
  22.1 0.8 %collective-permute-start.4 = (bf16[96,512]{1,0:T(8,128)(2,1)S(1)}, bf16[96,512]{1,0:T(8,128)(2,1)S(1)}, u32[]{:S(2)}, u32[]{:S(2)}) collective-permute-start(bf16[96,512]{1,0:T(8,128)(2,1)S(1)} %get-tuple-element.58), channel_id=1, source_target_pairs={{0,8},{2,10},{4,12},{6,14},{8,0},{10,2},{12,4},{14,6},{16,24},{18,... | collective-permute-start | bytes 294920 | tf_op jit(solution)/shard_map/ppermute | solution.py:10
  22.9 1.1 %collective-permute-start.5 = (bf16[96,512]{1,0:T(8,128)(2,1)S(1)}, bf16[96,512]{1,0:T(8,128)(2,1)S(1)}, u32[]{:S(2)}, u32[]{:S(2)}) collective-permute-start(bf16[96,512]{1,0:T(8,128)(2,1)S(1)} %get-tuple-element.57), channel_id=1, source_target_pairs={{0,16},{2,18},{4,20},{6,22},{8,24},{10,26},{12,28},{14,30},{16,0},... | collective-permute-start | bytes 294920 | tf_op jit(solution)/shard_map/ppermute | solution.py:10
  24.0 0.0 collective-permute-done
  24.0 0.0 collective-permute-done.1
  24.0 1.0 %collective-permute-done.2 = bf16[96,512]{1,0:T(8,128)(2,1)S(1)} collective-permute-done((bf16[96,512]{1,0:T(8,128)(2,1)S(1)}, bf16[96,512]{1,0:T(8,128)(2,1)S(1)}, u32[]{:S(2)}, u32[]{:S(2)}) %collective-permute-start.2) | collective-permute-done | bytes 98336 | tf_op jit(solution)/shard_map/ppermute | solution.py:10
  25.0 0.8 %collective-permute-start.3 = (bf16[96,512]{1,0:T(8,128)(2,1)S(1)}, bf16[96,512]{1,0:T(8,128)(2,1)S(1)}, u32[]{:S(2)}, u32[]{:S(2)}) collective-permute-start(bf16[96,512]{1,0:T(8,128)(2,1)S(1)} %get-tuple-element.27), channel_id=1, source_target_pairs={{0,8},{2,10},{4,12},{6,14},{8,0},{10,2},{12,4},{14,6},{16,24},{18,... | collective-permute-start | bytes 294920 | tf_op jit(solution)/shard_map/ppermute | solution.py:10
  25.8 1.3 %collective-permute-start.7 = (bf16[96,512]{1,0:T(8,128)(2,1)S(1)}, bf16[96,512]{1,0:T(8,128)(2,1)S(1)}, u32[]{:S(2)}, u32[]{:S(2)}) collective-permute-start(bf16[96,512]{1,0:T(8,128)(2,1)S(1)} %get-tuple-element.31), channel_id=1, source_target_pairs={{0,4},{2,6},{4,0},{6,2},{8,12},{10,14},{12,8},{14,10},{16,20},{18,... | collective-permute-start | bytes 294920 | tf_op jit(solution)/shard_map/ppermute | solution.py:10
  27.1 1.5 %collective-permute-start.6 = (bf16[96,512]{1,0:T(8,128)(2,1)S(1)}, bf16[96,512]{1,0:T(8,128)(2,1)S(1)}, u32[]{:S(2)}, u32[]{:S(2)}) collective-permute-start(bf16[96,512]{1,0:T(8,128)(2,1)S(1)} %get-tuple-element.30), channel_id=1, source_target_pairs={{0,2},{2,0},{4,6},{6,4},{8,10},{10,8},{12,14},{14,12},{16,18},{18,... | collective-permute-start | bytes 294920 | tf_op jit(solution)/shard_map/ppermute | solution.py:10
  28.6 0.0 collective-permute-done.4
  28.6 1.0 %collective-permute-done.5 = bf16[96,512]{1,0:T(8,128)(2,1)S(1)} collective-permute-done((bf16[96,512]{1,0:T(8,128)(2,1)S(1)}, bf16[96,512]{1,0:T(8,128)(2,1)S(1)}, u32[]{:S(2)}, u32[]{:S(2)}) %collective-permute-start.5) | collective-permute-done | bytes 98336 | tf_op jit(solution)/shard_map/ppermute | solution.py:10
  29.6 0.3 collective-permute-done.3
  30.0 0.9 %collective-permute-start.8 = (bf16[96,512]{1,0:T(8,128)(2,1)S(1)}, bf16[96,512]{1,0:T(8,128)(2,1)S(1)}, u32[]{:S(2)}, u32[]{:S(2)}) collective-permute-start(bf16[96,512]{1,0:T(8,128)(2,1)S(1)} %fusion.7), channel_id=1, source_target_pairs={{0,16},{2,18},{4,20},{6,22},{8,24},{10,26},{12,28},{14,30},{16,0},... | collective-permute-start | bytes 294920 | tf_op jit(solution)/shard_map/ppermute | solution.py:10
  30.9 0.1 fusion.9
  31.0 0.2 fusion.13
  31.2 0.5 collective-permute-done.6
  31.8 0.0 collective-permute-done.7
  31.8 0.2 convolution_add_fusion.3
  32.0 0.2 fusion
  32.2 0.2 convolution_add_fusion.1
  32.4 0.1 collective-permute-start.10
  32.5 4.0 %collective-permute-done.8 = bf16[96,512]{1,0:T(8,128)(2,1)S(1)} collective-permute-done((bf16[96,512]{1,0:T(8,128)(2,1)S(1)}, bf16[96,512]{1,0:T(8,128)(2,1)S(1)}, u32[]{:S(2)}, u32[]{:S(2)}) %collective-permute-start.8) | collective-permute-done | bytes 98336 | tf_op jit(solution)/shard_map/ppermute | solution.py:10
  36.6 0.2 fusion.1
  36.8 0.2 fusion.22
  37.0 0.7 %all_to_all.27 = bf16[16,6,512]{2,1,0:T(8,128)(2,1)} reshape(bf16[96,512]{1,0:T(8,128)(2,1)S(1)} %pad_maximum_fusion.6) | data formatting | bytes 196608 | tf_op jit(solution)/shard_map/all_to_all | solution.py:108
  37.7 4.1 %all-to-all-start.1 = ((bf16[16,6,512]{2,1,0:T(8,128)(2,1)}), bf16[16,6,512]{2,1,0:T(8,128)(2,1)S(1)}, u32[]{:S(2)}, u32[]{:S(2)}) async-start(bf16[16,6,512]{2,1,0:T(8,128)(2,1)} %all_to_all.27), calls=%async_computation.1 | async-start | bytes 262144 | tf_op jit(solution)/shard_map/all_to_all | solution.py:108
  41.8 0.1 collective-permute-start.9
  41.9 0.0 collective-permute-done.10
  42.0 1.1 %convolution_multiply_fusion = f32[640,256]{1,0:T(8,128)} fusion(bf16[96,640]{1,0:T(8,128)(2,1)S(1)} %constant_dynamic-update-slice_fusion.11, bf16[96,640]{1,0:T(8,128)(2,1)S(1)} %get-tuple-element.53, bf16[96,256]{1,0:T(8,128)(2,1)S(1)} %get-tuple-element.46, bf16[96,256]{1,0:T(8,128)(2,1)S(1)} %slice.176), kind=kOutput, calls=%fused_computation | convolution fusion | flops 63766528 | bytes 999424 | tf_op jit(solution)/shard_map/dot_general | solution.py:32
  43.1 0.0 collective-permute-done.9
  43.2 0.9 %convolution_multiply_fusion.1 = f32[128,256]{1,0:T(8,128)} fusion(bf16[96,256]{1,0:T(8,128)(2,1)S(1)} %get-tuple-element.46, bf16[96,256]{1,0:T(8,128)(2,1)S(1)} %slice.176, bf16[96,128]{1,0:T(8,128)(2,1)S(1)} %get-tuple-element.55, bf16[96,128]{1,0:T(8,128)(2,1)S(1)} %get-tuple-element.49), kind=kOutput, calls=%fused_computation.1 | convolution fusion | flops 12910592 | bytes 278528 | tf_op jit(solution)/shard_map/dot_general | solution.py:32
  44.0 0.9 %convolution_multiply_fusion.2 = f32[256,128]{1,0:T(8,128)} fusion(bf16[96,256]{1,0:T(8,128)(2,1)S(1)} %get-tuple-element.45, bf16[96,256]{1,0:T(8,128)(2,1)S(1)} %fusion.27, bf16[96,128]{1,0:T(8,128)(2,1)S(1)} %get-tuple-element.56, bf16[96,128]{1,0:T(8,128)(2,1)S(1)} %get-tuple-element.51), kind=kOutput, calls=%fused_computation.2 | convolution fusion | flops 12910592 | bytes 278528 | tf_op jit(solution)/shard_map/dot_general | solution.py:32
  44.9 4.7 %all-to-all-done.1 = bf16[16,6,512]{2,1,0:T(8,128)(2,1)S(1)} async-done(((bf16[16,6,512]{2,1,0:T(8,128)(2,1)}), bf16[16,6,512]{2,1,0:T(8,128)(2,1)S(1)}, u32[]{:S(2)}, u32[]{:S(2)}) %all-to-all-start.1) | async-done | bytes 98336 | tf_op jit(solution)/shard_map/all_to_all | solution.py:108
  49.6 0.7 %fusion.65 = (bf16[6,16,256]{2,0,1:T(8,128)(2,1)}, bf16[6,16,256]{2,0,1:T(8,128)(2,1)}) fusion(bf16[6,16,512]{2,0,1:T(8,128)(2,1)S(1)} %bitcast.31), kind=kLoop, calls=%fused_computation.109 | loop fusion | bytes 196608 | tf_op jit(solution)/shard_map/slice | solution.py:111
  (29 shorter events, 0.6 us)
Async XLA Ops:
  0.6 17.1 %copy-start = (bf16[256,256]{1,0:T(8,128)(2,1)S(1)}, bf16[256,256]{1,0:T(8,128)(2,1)}, u32[]{:S(2)}) copy-start(bf16[256,256]{1,0:T(8,128)(2,1)} %param.8) | copy-start | bytes 393220
  1.6 16.3 %copy-start.2 = (bf16[256,256]{1,0:T(8,128)(2,1)S(1)}, bf16[256,256]{1,0:T(8,128)(2,1)}, u32[]{:S(2)}) copy-start(bf16[256,256]{1,0:T(8,128)(2,1)} %param.7) | copy-start | bytes 393220
  17.6 4.0 %copy-start.1 = (bf16[1,5,256,256]{3,2,1,0:T(8,128)(2,1)S(1)}, bf16[1,5,256,256]{3,2,1,0:T(8,128)(2,1)}, u32[]{:S(2)}) copy-start(bf16[1,5,256,256]{3,2,1,0:T(8,128)(2,1)} %param.6) | copy-start | bytes 1966084
  18.1 5.9 %collective-permute-start = (bf16[96,512]{1,0:T(8,128)(2,1)S(1)}, bf16[96,512]{1,0:T(8,128)(2,1)S(1)}, u32[]{:S(2)}, u32[]{:S(2)}) collective-permute-start(bf16[96,512]{1,0:T(8,128)(2,1)S(1)} %fusion.5), channel_id=1, source_target_pairs={{0,2},{2,0},{4,6},{6,4},{8,10},{10,8},{12,14},{14,12},{16,18},{18,... | collective-permute-start | bytes 294920 | tf_op jit(solution)/shard_map/ppermute | solution.py:10
  19.2 4.8 %collective-permute-start.1 = (bf16[96,512]{1,0:T(8,128)(2,1)S(1)}, bf16[96,512]{1,0:T(8,128)(2,1)S(1)}, u32[]{:S(2)}, u32[]{:S(2)}) collective-permute-start(bf16[96,512]{1,0:T(8,128)(2,1)S(1)} %fusion.5), channel_id=1, source_target_pairs={{0,4},{2,6},{4,0},{6,2},{8,12},{10,14},{12,8},{14,10},{16,20},{18,... | collective-permute-start | bytes 294920 | tf_op jit(solution)/shard_map/ppermute | solution.py:10
  19.5 5.5 %collective-permute-start.2 = (bf16[96,512]{1,0:T(8,128)(2,1)S(1)}, bf16[96,512]{1,0:T(8,128)(2,1)S(1)}, u32[]{:S(2)}, u32[]{:S(2)}) collective-permute-start(bf16[96,512]{1,0:T(8,128)(2,1)S(1)} %fusion.5), channel_id=1, source_target_pairs={{0,6},{2,4},{4,2},{6,0},{8,14},{10,12},{12,10},{14,8},{16,22},{18,... | collective-permute-start | bytes 294920 | tf_op jit(solution)/shard_map/ppermute | solution.py:10
  22.1 6.5 %collective-permute-start.4 = (bf16[96,512]{1,0:T(8,128)(2,1)S(1)}, bf16[96,512]{1,0:T(8,128)(2,1)S(1)}, u32[]{:S(2)}, u32[]{:S(2)}) collective-permute-start(bf16[96,512]{1,0:T(8,128)(2,1)S(1)} %get-tuple-element.58), channel_id=1, source_target_pairs={{0,8},{2,10},{4,12},{6,14},{8,0},{10,2},{12,4},{14,6},{16,24},{18,... | collective-permute-start | bytes 294920 | tf_op jit(solution)/shard_map/ppermute | solution.py:10
  22.9 6.7 %collective-permute-start.5 = (bf16[96,512]{1,0:T(8,128)(2,1)S(1)}, bf16[96,512]{1,0:T(8,128)(2,1)S(1)}, u32[]{:S(2)}, u32[]{:S(2)}) collective-permute-start(bf16[96,512]{1,0:T(8,128)(2,1)S(1)} %get-tuple-element.57), channel_id=1, source_target_pairs={{0,16},{2,18},{4,20},{6,22},{8,24},{10,26},{12,28},{14,30},{16,0},... | collective-permute-start | bytes 294920 | tf_op jit(solution)/shard_map/ppermute | solution.py:10
  25.0 4.9 %collective-permute-start.3 = (bf16[96,512]{1,0:T(8,128)(2,1)S(1)}, bf16[96,512]{1,0:T(8,128)(2,1)S(1)}, u32[]{:S(2)}, u32[]{:S(2)}) collective-permute-start(bf16[96,512]{1,0:T(8,128)(2,1)S(1)} %get-tuple-element.27), channel_id=1, source_target_pairs={{0,8},{2,10},{4,12},{6,14},{8,0},{10,2},{12,4},{14,6},{16,24},{18,... | collective-permute-start | bytes 294920 | tf_op jit(solution)/shard_map/ppermute | solution.py:10
  25.8 5.9 %collective-permute-start.7 = (bf16[96,512]{1,0:T(8,128)(2,1)S(1)}, bf16[96,512]{1,0:T(8,128)(2,1)S(1)}, u32[]{:S(2)}, u32[]{:S(2)}) collective-permute-start(bf16[96,512]{1,0:T(8,128)(2,1)S(1)} %get-tuple-element.31), channel_id=1, source_target_pairs={{0,4},{2,6},{4,0},{6,2},{8,12},{10,14},{12,8},{14,10},{16,20},{18,... | collective-permute-start | bytes 294920 | tf_op jit(solution)/shard_map/ppermute | solution.py:10
  27.1 4.6 %collective-permute-start.6 = (bf16[96,512]{1,0:T(8,128)(2,1)S(1)}, bf16[96,512]{1,0:T(8,128)(2,1)S(1)}, u32[]{:S(2)}, u32[]{:S(2)}) collective-permute-start(bf16[96,512]{1,0:T(8,128)(2,1)S(1)} %get-tuple-element.30), channel_id=1, source_target_pairs={{0,2},{2,0},{4,6},{6,4},{8,10},{10,8},{12,14},{14,12},{16,18},{18,... | collective-permute-start | bytes 294920 | tf_op jit(solution)/shard_map/ppermute | solution.py:10
  30.0 6.6 %collective-permute-start.8 = (bf16[96,512]{1,0:T(8,128)(2,1)S(1)}, bf16[96,512]{1,0:T(8,128)(2,1)S(1)}, u32[]{:S(2)}, u32[]{:S(2)}) collective-permute-start(bf16[96,512]{1,0:T(8,128)(2,1)S(1)} %fusion.7), channel_id=1, source_target_pairs={{0,16},{2,18},{4,20},{6,22},{8,24},{10,26},{12,28},{14,30},{16,0},... | collective-permute-start | bytes 294920 | tf_op jit(solution)/shard_map/ppermute | solution.py:10
  32.4 9.4 %collective-permute-start.10 = (bf16[96,1024]{1,0:T(8,128)(2,1)S(1)}, bf16[96,1024]{1,0:T(8,128)(2,1)S(1)}, u32[]{:S(2)}, u32[]{:S(2)}) collective-permute-start(bf16[96,1024]{1,0:T(8,128)(2,1)S(1)} %constant_dynamic-update-slice_fusion.5), channel_id=1, source_target_pairs={{0,1},{1,0},{2,3},{3,2},{4,5},{5,4},{6,7},{7,6},{8,9},{9,8},{10,11... | collective-permute-start | bytes 589832 | tf_op jit(solution)/shard_map/ppermute | solution.py:14
  37.7 11.9 %all-to-all-start.1 = ((bf16[16,6,512]{2,1,0:T(8,128)(2,1)}), bf16[16,6,512]{2,1,0:T(8,128)(2,1)S(1)}, u32[]{:S(2)}, u32[]{:S(2)}) async-start(bf16[16,6,512]{2,1,0:T(8,128)(2,1)} %all_to_all.27), calls=%async_computation.1 | async-start | bytes 262144 | tf_op jit(solution)/shard_map/all_to_all | solution.py:108
  41.8 1.4 %collective-permute-start.9 = (bf16[96,256]{1,0:T(8,128)(2,1)S(1)}, bf16[96,256]{1,0:T(8,128)(2,1)S(1)}, u32[]{:S(2)}, u32[]{:S(2)}) collective-permute-start(bf16[96,256]{1,0:T(8,128)(2,1)S(1)} %pad_maximum_fusion.10), channel_id=1, source_target_pairs={{0,1},{1,0},{2,3},{3,2},{4,5},{5,4},{6,7},{7,6},{8,9},{9,8},{10,11... | collective-permute-start | bytes 147464 | tf_op jit(solution)/shard_map/ppermute | solution.py:14

commit v13 on v12

--- a/solution.py
+++ b/solution.py
@@ -41,21 +41,26 @@
     for at, masks in enumerate(rounds):
         sent = total.astype(jnp.bfloat16)
         if at == 0:
-            beside = {mask: blocks[mask] for mask in sorted(blocks, reverse=True) if mask > 3}
+            beside = {max(blocks): blocks[max(blocks)]}
         elif at == 1:
-            early, beside = far, {mask: blocks[mask] for mask in blocks if mask not in far}
+            early, beside = far, {mask: blocks[mask] for mask in rounds[0] if mask in blocks}
+        elif at == len(rounds) - 1:
+            early, beside = {}, {mask: blocks[mask] for mask in blocks if mask not in far}
+            sent, data = lax.optimization_barrier((sent, data))
+        else:
+            early, beside = {}, {}
+        if at:
             sent, beside = lax.optimization_barrier((sent, beside))
+        got = [exchange(sent, mask) for mask in masks]
+        moved = {mask: exchange(beside[mask], mask) for mask in beside}
+        if at == 0:
+            got = lax.optimization_barrier(got)
+        elif at == len(rounds) - 1:
+            got, moved = lax.optimization_barrier((got, moved))
         else:
-            beside = {}
-        if at == len(rounds) - 1:
-            sent, data = lax.optimization_barrier((sent, data))
-        got = [exchange(sent, mask) for mask in masks]
-        far = far | {mask: exchange(beside[mask], mask) for mask in beside}
-        if at == 1:
             got, early = lax.optimization_barrier((got, early))
             far = far | early
-        else:
-            got = lax.optimization_barrier(got)
+        far = far | moved
         total = total + sum(x.astype(jnp.float32) for x in got)
     return total.astype(jnp.bfloat16), [far[mask] for mask in blocks], data
 

time: 50.5 us -> 54.3 us (1.075)
  waiting for transfers between devices: 11.5 us -> 14.4 us
  starting transfers between devices: 14.2 us -> 15.1 us
    all_to_all x1, waiting for transfers between devices: 4.68 us -> 7.02 us  [on_device(): lax.all_to_all(results, 'hid', split_axis=0, concat_axis=1, tiled=True)]
    ppermute x9, waiting for transfers between devices: 6.83 us -> 7.41 us  [exchange(): lax.ppermute(x, 'hid', [(i, i ^ mask) for i in range(lax.axis_size('hid'))])]
  transfers between devices with their start and end apart: 12 -> 12, of which waited for: 6 -> 7; matrix products, arithmetic and copies ran while one was open for 10% -> 5% of each run, Pallas kernels for 0% -> 0%
where the time goes in v13:
time: 54.3 us; the launch traced here: 54 us
  blocking collectives  16 us (29%)
  starting transfers between devices  15.1 us (28%)
  waiting for transfers between devices  14.4 us (27%)
  matrix products  4.69 us (9%)
  local copies, waits for them, and re-layouts  1.55 us (3%)
  other arithmetic  1.34 us (2%)
  between operations  0.93 us (2%)
    all_to_all x1, blocking collectives, on_device(): rows = lax.all_to_all(both, 'hid', split_axis=1, concat_axis=0, tiled=True)  16 us
    ppermute x9, starting transfers between devices, exchange(): lax.ppermute(x, 'hid', [(i, i ^ mask) for i in range(lax.axis_size('hid'))])  9.98 us
    ppermute x9, waiting for transfers between devices, exchange(): lax.ppermute(x, 'hid', [(i, i ^ mask) for i in range(lax.axis_size('hid'))])  7.41 us
    all_to_all x1, waiting for transfers between devices, on_device(): lax.all_to_all(results, 'hid', split_axis=0, concat_axis=1, tiled=True)  7.02 us
    all_to_all x1, starting transfers between devices, on_device(): lax.all_to_all(results, 'hid', split_axis=0, concat_axis=1, tiled=True)  4.45 us
    dot_general x3, matrix products, inner_rows(): lax.dot_general(left, right, (((0,), (0,)), ((), ())), preferred_element_...  2.88 us
  transfers between devices with their start and end apart: 12, of which 7 were waited for; matrix products, arithmetic and copies ran while one was open for 5% of the time, Pallas kernels for 0%

profile of v13, /device:TPU:0, one launch (start us, length us, event | category | flops | bytes accessed | tf_op | source)
XLA Modules:
  0.0 54.0 jit_solution(13144741257519523162)
XLA Ops:
  0.6 0.0 copy-start
  0.7 0.9 %pad_maximum_fusion.5 = bf16[6,16,512]{2,0,1:T(8,128)(2,1)S(1)} fusion(bf16[6,16,256]{2,0,1:T(8,128)(2,1)} %bitcast.32, bf16[6,16,256]{2,0,1:T(8,128)(2,1)} %bitcast.33), kind=kLoop, calls=%fused_computation.28 | loop fusion | flops 196608 | bytes 196608 | tf_op jit(solution)/shard_map/concatenate | solution.py:84
  1.6 0.0 copy-start.2
  1.6 16.0 %all_to_all.32 = bf16[6,16,512]{2,0,1:T(8,128)(2,1)S(1)} all-to-all(bf16[6,16,512]{2,0,1:T(8,128)(2,1)S(1)} %pad_maximum_fusion.5), channel_id=1, replica_groups=mesh['hid'=16,'seq'=2] {'hid'}, dimensions={1} | all-to-all | bytes 196608 | tf_op jit(solution)/shard_map/all_to_all | solution.py:87
  17.6 0.0 copy-start.1
  17.7 0.0 copy-done
  17.7 0.2 fusion.58
  17.9 0.0 copy-done.2
  17.9 0.2 fusion.60
  18.1 1.2 %collective-permute-start = (bf16[96,512]{1,0:T(8,128)(2,1)S(1)}, bf16[96,512]{1,0:T(8,128)(2,1)S(1)}, u32[]{:S(2)}, u32[]{:S(2)}) collective-permute-start(bf16[96,512]{1,0:T(8,128)(2,1)S(1)} %fusion.5), channel_id=1, source_target_pairs={{0,2},{2,0},{4,6},{6,4},{8,10},{10,8},{12,14},{14,12},{16,18},{18,... | collective-permute-start | bytes 294920 | tf_op jit(solution)/shard_map/ppermute | solution.py:10
  19.2 0.2 collective-permute-start.1
  19.5 2.2 %collective-permute-start.2 = (bf16[96,512]{1,0:T(8,128)(2,1)S(1)}, bf16[96,512]{1,0:T(8,128)(2,1)S(1)}, u32[]{:S(2)}, u32[]{:S(2)}) collective-permute-start(bf16[96,512]{1,0:T(8,128)(2,1)S(1)} %fusion.5), channel_id=1, source_target_pairs={{0,6},{2,4},{4,2},{6,0},{8,14},{10,12},{12,10},{14,8},{16,22},{18,... | collective-permute-start | bytes 294920 | tf_op jit(solution)/shard_map/ppermute | solution.py:10
  21.7 0.0 copy-done.1
  21.7 0.3 fusion.67
  22.1 1.0 %collective-permute-start.4 = (bf16[96,512]{1,0:T(8,128)(2,1)S(1)}, bf16[96,512]{1,0:T(8,128)(2,1)S(1)}, u32[]{:S(2)}, u32[]{:S(2)}) collective-permute-start(bf16[96,512]{1,0:T(8,128)(2,1)S(1)} %get-tuple-element.64), channel_id=1, source_target_pairs={{0,16},{2,18},{4,20},{6,22},{8,24},{10,26},{12,28},{14,30},{16,0},... | collective-permute-start | bytes 294920 | tf_op jit(solution)/shard_map/ppermute | solution.py:10
  23.1 0.5 collective-permute-done
  23.5 0.3 collective-permute-done.1
  23.9 1.1 %collective-permute-done.2 = bf16[96,512]{1,0:T(8,128)(2,1)S(1)} collective-permute-done((bf16[96,512]{1,0:T(8,128)(2,1)S(1)}, bf16[96,512]{1,0:T(8,128)(2,1)S(1)}, u32[]{:S(2)}, u32[]{:S(2)}) %collective-permute-start.2) | collective-permute-done | bytes 98336 | tf_op jit(solution)/shard_map/ppermute | solution.py:10
  25.0 0.8 %collective-permute-start.3 = (bf16[96,512]{1,0:T(8,128)(2,1)S(1)}, bf16[96,512]{1,0:T(8,128)(2,1)S(1)}, u32[]{:S(2)}, u32[]{:S(2)}) collective-permute-start(bf16[96,512]{1,0:T(8,128)(2,1)S(1)} %get-tuple-element.30), channel_id=1, source_target_pairs={{0,8},{2,10},{4,12},{6,14},{8,0},{10,2},{12,4},{14,6},{16,24},{18,... | collective-permute-start | bytes 294920 | tf_op jit(solution)/shard_map/ppermute | solution.py:10
  25.8 1.3 %collective-permute-start.6 = (bf16[96,512]{1,0:T(8,128)(2,1)S(1)}, bf16[96,512]{1,0:T(8,128)(2,1)S(1)}, u32[]{:S(2)}, u32[]{:S(2)}) collective-permute-start(bf16[96,512]{1,0:T(8,128)(2,1)S(1)} %get-tuple-element.34), channel_id=1, source_target_pairs={{0,4},{2,6},{4,0},{6,2},{8,12},{10,14},{12,8},{14,10},{16,20},{18,... | collective-permute-start | bytes 294920 | tf_op jit(solution)/shard_map/ppermute | solution.py:10
  27.1 1.5 %collective-permute-start.5 = (bf16[96,512]{1,0:T(8,128)(2,1)S(1)}, bf16[96,512]{1,0:T(8,128)(2,1)S(1)}, u32[]{:S(2)}, u32[]{:S(2)}) collective-permute-start(bf16[96,512]{1,0:T(8,128)(2,1)S(1)} %get-tuple-element.33), channel_id=1, source_target_pairs={{0,2},{2,0},{4,6},{6,4},{8,10},{10,8},{12,14},{14,12},{16,18},{18,... | collective-permute-start | bytes 294920 | tf_op jit(solution)/shard_map/ppermute | solution.py:10
  28.6 0.2 collective-permute-done.4
  28.8 1.0 %collective-permute-done.3 = bf16[96,512]{1,0:T(8,128)(2,1)S(1)} collective-permute-done((bf16[96,512]{1,0:T(8,128)(2,1)S(1)}, bf16[96,512]{1,0:T(8,128)(2,1)S(1)}, u32[]{:S(2)}, u32[]{:S(2)}) %collective-permute-start.3) | collective-permute-done | bytes 98336 | tf_op jit(solution)/shard_map/ppermute | solution.py:10
  29.8 0.9 %collective-permute-start.7 = (bf16[96,512]{1,0:T(8,128)(2,1)S(1)}, bf16[96,512]{1,0:T(8,128)(2,1)S(1)}, u32[]{:S(2)}, u32[]{:S(2)}) collective-permute-start(bf16[96,512]{1,0:T(8,128)(2,1)S(1)} %fusion.7), channel_id=1, source_target_pairs={{0,16},{2,18},{4,20},{6,22},{8,24},{10,26},{12,28},{14,30},{16,0},... | collective-permute-start | bytes 294920 | tf_op jit(solution)/shard_map/ppermute | solution.py:10
  30.7 1.0 %collective-permute-start.8 = (bf16[96,512]{1,0:T(8,128)(2,1)S(1)}, bf16[96,512]{1,0:T(8,128)(2,1)S(1)}, u32[]{:S(2)}, u32[]{:S(2)}) collective-permute-start(bf16[96,512]{1,0:T(8,128)(2,1)S(1)} %get-tuple-element.37), channel_id=1, source_target_pairs={{0,8},{2,10},{4,12},{6,14},{8,0},{10,2},{12,4},{14,6},{16,24},{18,... | collective-permute-start | bytes 294920 | tf_op jit(solution)/shard_map/ppermute | solution.py:10
  31.7 0.1 fusion.13
  31.9 0.0 collective-permute-done.5
  31.9 0.2 convolution_add_fusion.3
  32.1 0.0 collective-permute-done.6
  32.2 4.3 %collective-permute-done.7 = bf16[96,512]{1,0:T(8,128)(2,1)S(1)} collective-permute-done((bf16[96,512]{1,0:T(8,128)(2,1)S(1)}, bf16[96,512]{1,0:T(8,128)(2,1)S(1)}, u32[]{:S(2)}, u32[]{:S(2)}) %collective-permute-start.7) | collective-permute-done | bytes 98336 | tf_op jit(solution)/shard_map/ppermute | solution.py:10
  36.5 0.0 collective-permute-done.8
  36.5 0.1 fusion.9
  36.7 0.2 fusion
  36.8 0.2 convolution_add_fusion.1
  37.0 0.2 fusion.1
  37.2 0.2 fusion.22
  37.4 0.7 %all_to_all.27 = bf16[16,6,512]{2,1,0:T(8,128)(2,1)} reshape(bf16[96,512]{1,0:T(8,128)(2,1)S(1)} %pad_maximum_fusion.6) | data formatting | bytes 196608 | tf_op jit(solution)/shard_map/all_to_all | solution.py:113
  38.1 4.5 %all-to-all-start.1 = ((bf16[16,6,512]{2,1,0:T(8,128)(2,1)}), bf16[16,6,512]{2,1,0:T(8,128)(2,1)S(1)}, u32[]{:S(2)}, u32[]{:S(2)}) async-start(bf16[16,6,512]{2,1,0:T(8,128)(2,1)} %all_to_all.27), calls=%async_computation.1 | async-start | bytes 262144 | tf_op jit(solution)/shard_map/all_to_all | solution.py:113
  42.6 0.1 collective-permute-start.9
  42.8 0.6 %collective-permute-start.10 = (bf16[96,1024]{1,0:T(8,128)(2,1)S(1)}, bf16[96,1024]{1,0:T(8,128)(2,1)S(1)}, u32[]{:S(2)}, u32[]{:S(2)}) collective-permute-start(bf16[96,1024]{1,0:T(8,128)(2,1)S(1)} %constant_dynamic-update-slice_fusion.5), channel_id=1, source_target_pairs={{0,1},{1,0},{2,3},{3,2},{4,5},{5,4},{6,7},{7,6},{8,9},{9,8},{10,11... | collective-permute-start | bytes 589832 | tf_op jit(solution)/shard_map/ppermute | solution.py:14
  43.4 7.0 %all-to-all-done.1 = bf16[16,6,512]{2,1,0:T(8,128)(2,1)S(1)} async-done(((bf16[16,6,512]{2,1,0:T(8,128)(2,1)}), bf16[16,6,512]{2,1,0:T(8,128)(2,1)S(1)}, u32[]{:S(2)}, u32[]{:S(2)}) %all-to-all-start.1) | async-done | bytes 98336 | tf_op jit(solution)/shard_map/all_to_all | solution.py:113
  50.4 0.7 %fusion.65 = (bf16[6,16,256]{2,0,1:T(8,128)(2,1)}, bf16[6,16,256]{2,0,1:T(8,128)(2,1)}) fusion(bf16[6,16,512]{2,0,1:T(8,128)(2,1)S(1)} %bitcast.31), kind=kLoop, calls=%fused_computation.109 | loop fusion | bytes 196608 | tf_op jit(solution)/shard_map/slice | solution.py:116
  51.0 0.0 collective-permute-done.10
  51.2 1.1 %convolution_multiply_fusion = f32[640,256]{1,0:T(8,128)} fusion(bf16[96,640]{1,0:T(8,128)(2,1)S(1)} %constant_dynamic-update-slice_fusion.11, bf16[96,640]{1,0:T(8,128)(2,1)S(1)} %get-tuple-element.59, bf16[96,256]{1,0:T(8,128)(2,1)S(1)} %get-tuple-element.52, bf16[96,256]{1,0:T(8,128)(2,1)S(1)} %slice.176), kind=kOutput, calls=%fused_computation | convolution fusion | flops 63766528 | bytes 999424 | tf_op jit(solution)/shard_map/dot_general | solution.py:32
  52.3 0.0 collective-permute-done.9
  52.3 0.9 %convolution_multiply_fusion.1 = f32[128,256]{1,0:T(8,128)} fusion(bf16[96,256]{1,0:T(8,128)(2,1)S(1)} %get-tuple-element.52, bf16[96,256]{1,0:T(8,128)(2,1)S(1)} %slice.176, bf16[96,128]{1,0:T(8,128)(2,1)S(1)} %get-tuple-element.61, bf16[96,128]{1,0:T(8,128)(2,1)S(1)} %get-tuple-element.55), kind=kOutput, calls=%fused_computation.1 | convolution fusion | flops 12910592 | bytes 278528 | tf_op jit(solution)/shard_map/dot_general | solution.py:32
  53.2 0.9 %convolution_multiply_fusion.2 = f32[256,128]{1,0:T(8,128)} fusion(bf16[96,256]{1,0:T(8,128)(2,1)S(1)} %get-tuple-element.51, bf16[96,256]{1,0:T(8,128)(2,1)S(1)} %fusion.27, bf16[96,128]{1,0:T(8,128)(2,1)S(1)} %get-tuple-element.62, bf16[96,128]{1,0:T(8,128)(2,1)S(1)} %get-tuple-element.57), kind=kOutput, calls=%fused_computation.2 | convolution fusion | flops 12910592 | bytes 278528 | tf_op jit(solution)/shard_map/dot_general | solution.py:32
  (29 shorter events, 0.6 us)
Async XLA Ops:
  0.6 17.1 %copy-start = (bf16[256,256]{1,0:T(8,128)(2,1)S(1)}, bf16[256,256]{1,0:T(8,128)(2,1)}, u32[]{:S(2)}) copy-start(bf16[256,256]{1,0:T(8,128)(2,1)} %param.8) | copy-start | bytes 393220
  1.6 16.3 %copy-start.2 = (bf16[256,256]{1,0:T(8,128)(2,1)S(1)}, bf16[256,256]{1,0:T(8,128)(2,1)}, u32[]{:S(2)}) copy-start(bf16[256,256]{1,0:T(8,128)(2,1)} %param.7) | copy-start | bytes 393220
  17.6 4.0 %copy-start.1 = (bf16[1,5,256,256]{3,2,1,0:T(8,128)(2,1)S(1)}, bf16[1,5,256,256]{3,2,1,0:T(8,128)(2,1)}, u32[]{:S(2)}) copy-start(bf16[1,5,256,256]{3,2,1,0:T(8,128)(2,1)} %param.6) | copy-start | bytes 1966084
  18.1 5.5 %collective-permute-start = (bf16[96,512]{1,0:T(8,128)(2,1)S(1)}, bf16[96,512]{1,0:T(8,128)(2,1)S(1)}, u32[]{:S(2)}, u32[]{:S(2)}) collective-permute-start(bf16[96,512]{1,0:T(8,128)(2,1)S(1)} %fusion.5), channel_id=1, source_target_pairs={{0,2},{2,0},{4,6},{6,4},{8,10},{10,8},{12,14},{14,12},{16,18},{18,... | collective-permute-start | bytes 294920 | tf_op jit(solution)/shard_map/ppermute | solution.py:10
  19.2 4.6 %collective-permute-start.1 = (bf16[96,512]{1,0:T(8,128)(2,1)S(1)}, bf16[96,512]{1,0:T(8,128)(2,1)S(1)}, u32[]{:S(2)}, u32[]{:S(2)}) collective-permute-start(bf16[96,512]{1,0:T(8,128)(2,1)S(1)} %fusion.5), channel_id=1, source_target_pairs={{0,4},{2,6},{4,0},{6,2},{8,12},{10,14},{12,8},{14,10},{16,20},{18,... | collective-permute-start | bytes 294920 | tf_op jit(solution)/shard_map/ppermute | solution.py:10
  19.5 5.5 %collective-permute-start.2 = (bf16[96,512]{1,0:T(8,128)(2,1)S(1)}, bf16[96,512]{1,0:T(8,128)(2,1)S(1)}, u32[]{:S(2)}, u32[]{:S(2)}) collective-permute-start(bf16[96,512]{1,0:T(8,128)(2,1)S(1)} %fusion.5), channel_id=1, source_target_pairs={{0,6},{2,4},{4,2},{6,0},{8,14},{10,12},{12,10},{14,8},{16,22},{18,... | collective-permute-start | bytes 294920 | tf_op jit(solution)/shard_map/ppermute | solution.py:10
  22.1 6.6 %collective-permute-start.4 = (bf16[96,512]{1,0:T(8,128)(2,1)S(1)}, bf16[96,512]{1,0:T(8,128)(2,1)S(1)}, u32[]{:S(2)}, u32[]{:S(2)}) collective-permute-start(bf16[96,512]{1,0:T(8,128)(2,1)S(1)} %get-tuple-element.64), channel_id=1, source_target_pairs={{0,16},{2,18},{4,20},{6,22},{8,24},{10,26},{12,28},{14,30},{16,0},... | collective-permute-start | bytes 294920 | tf_op jit(solution)/shard_map/ppermute | solution.py:10
  25.0 4.8 %collective-permute-start.3 = (bf16[96,512]{1,0:T(8,128)(2,1)S(1)}, bf16[96,512]{1,0:T(8,128)(2,1)S(1)}, u32[]{:S(2)}, u32[]{:S(2)}) collective-permute-start(bf16[96,512]{1,0:T(8,128)(2,1)S(1)} %get-tuple-element.30), channel_id=1, source_target_pairs={{0,8},{2,10},{4,12},{6,14},{8,0},{10,2},{12,4},{14,6},{16,24},{18,... | collective-permute-start | bytes 294920 | tf_op jit(solution)/shard_map/ppermute | solution.py:10
  25.8 6.3 %collective-permute-start.6 = (bf16[96,512]{1,0:T(8,128)(2,1)S(1)}, bf16[96,512]{1,0:T(8,128)(2,1)S(1)}, u32[]{:S(2)}, u32[]{:S(2)}) collective-permute-start(bf16[96,512]{1,0:T(8,128)(2,1)S(1)} %get-tuple-element.34), channel_id=1, source_target_pairs={{0,4},{2,6},{4,0},{6,2},{8,12},{10,14},{12,8},{14,10},{16,20},{18,... | collective-permute-start | bytes 294920 | tf_op jit(solution)/shard_map/ppermute | solution.py:10
  27.1 4.8 %collective-permute-start.5 = (bf16[96,512]{1,0:T(8,128)(2,1)S(1)}, bf16[96,512]{1,0:T(8,128)(2,1)S(1)}, u32[]{:S(2)}, u32[]{:S(2)}) collective-permute-start(bf16[96,512]{1,0:T(8,128)(2,1)S(1)} %get-tuple-element.33), channel_id=1, source_target_pairs={{0,2},{2,0},{4,6},{6,4},{8,10},{10,8},{12,14},{14,12},{16,18},{18,... | collective-permute-start | bytes 294920 | tf_op jit(solution)/shard_map/ppermute | solution.py:10
  29.8 6.6 %collective-permute-start.7 = (bf16[96,512]{1,0:T(8,128)(2,1)S(1)}, bf16[96,512]{1,0:T(8,128)(2,1)S(1)}, u32[]{:S(2)}, u32[]{:S(2)}) collective-permute-start(bf16[96,512]{1,0:T(8,128)(2,1)S(1)} %fusion.7), channel_id=1, source_target_pairs={{0,16},{2,18},{4,20},{6,22},{8,24},{10,26},{12,28},{14,30},{16,0},... | collective-permute-start | bytes 294920 | tf_op jit(solution)/shard_map/ppermute | solution.py:10
  30.7 5.8 %collective-permute-start.8 = (bf16[96,512]{1,0:T(8,128)(2,1)S(1)}, bf16[96,512]{1,0:T(8,128)(2,1)S(1)}, u32[]{:S(2)}, u32[]{:S(2)}) collective-permute-start(bf16[96,512]{1,0:T(8,128)(2,1)S(1)} %get-tuple-element.37), channel_id=1, source_target_pairs={{0,8},{2,10},{4,12},{6,14},{8,0},{10,2},{12,4},{14,6},{16,24},{18,... | collective-permute-start | bytes 294920 | tf_op jit(solution)/shard_map/ppermute | solution.py:10
  38.1 12.3 %all-to-all-start.1 = ((bf16[16,6,512]{2,1,0:T(8,128)(2,1)}), bf16[16,6,512]{2,1,0:T(8,128)(2,1)S(1)}, u32[]{:S(2)}, u32[]{:S(2)}) async-start(bf16[16,6,512]{2,1,0:T(8,128)(2,1)} %all_to_all.27), calls=%async_computation.1 | async-start | bytes 262144 | tf_op jit(solution)/shard_map/all_to_all | solution.py:113
  42.6 9.7 %collective-permute-start.9 = (bf16[96,256]{1,0:T(8,128)(2,1)S(1)}, bf16[96,256]{1,0:T(8,128)(2,1)S(1)}, u32[]{:S(2)}, u32[]{:S(2)}) collective-permute-start(bf16[96,256]{1,0:T(8,128)(2,1)S(1)} %pad_maximum_fusion.10), channel_id=1, source_target_pairs={{0,1},{1,0},{2,3},{3,2},{4,5},{5,4},{6,7},{7,6},{8,9},{9,8},{10,11... | collective-permute-start | bytes 147464 | tf_op jit(solution)/shard_map/ppermute | solution.py:14
  42.8 8.2 %collective-permute-start.10 = (bf16[96,1024]{1,0:T(8,128)(2,1)S(1)}, bf16[96,1024]{1,0:T(8,128)(2,1)S(1)}, u32[]{:S(2)}, u32[]{:S(2)}) collective-permute-start(bf16[96,1024]{1,0:T(8,128)(2,1)S(1)} %constant_dynamic-update-slice_fusion.5), channel_id=1, source_target_pairs={{0,1},{1,0},{2,3},{3,2},{4,5},{5,4},{6,7},{7,6},{8,9},{9,8},{10,11... | collective-permute-start | bytes 589832 | tf_op jit(solution)/shard_map/ppermute | solution.py:14

commit v14 on v12

--- a/solution.py
+++ b/solution.py
@@ -36,7 +36,7 @@
 
 def sum_over_hid(part, blocks, data):
     bits = (lax.axis_size("hid") - 1).bit_length()
-    rounds = [(1, 2, 3)] + [(1 << bit,) for bit in range(2, bits)]
+    rounds = [(3, 1, 2)] + [(1 << bit,) for bit in range(2, bits)]
     total, far = part, {}
     for at, masks in enumerate(rounds):
         sent = total.astype(jnp.bfloat16)

time: 50.5 us -> 50 us (0.990)
  starting transfers between devices: 14.2 us -> 12.4 us
  waiting for transfers between devices: 11.5 us -> 12.8 us
    ppermute x9, waiting for transfers between devices: 6.83 us -> 8.11 us  [exchange(): lax.ppermute(x, 'hid', [(i, i ^ mask) for i in range(lax.axis_size('hid'))])]
    ppermute x9, starting transfers between devices: 9.95 us -> 8.79 us  [exchange(): lax.ppermute(x, 'hid', [(i, i ^ mask) for i in range(lax.axis_size('hid'))])]
    all_to_all x1, starting transfers between devices: 4.09 us -> 3.51 us  [on_device(): lax.all_to_all(results, 'hid', split_axis=0, concat_axis=1, tiled=True)]
where the time goes in v14:
time: 50 us; the launch traced here: 49.8 us
  blocking collectives  16 us (32%)
  waiting for transfers between devices  12.8 us (26%)
  starting transfers between devices  12.4 us (25%)
  matrix products  4.7 us (9%)
  local copies, waits for them, and re-layouts  1.54 us (3%)
  other arithmetic  1.33 us (3%)
  between operations  0.94 us (2%)
    all_to_all x1, blocking collectives, on_device(): rows = lax.all_to_all(both, 'hid', split_axis=1, concat_axis=0, tiled=True)  16 us
    ppermute x9, starting transfers between devices, exchange(): lax.ppermute(x, 'hid', [(i, i ^ mask) for i in range(lax.axis_size('hid'))])  8.79 us
    ppermute x9, waiting for transfers between devices, exchange(): lax.ppermute(x, 'hid', [(i, i ^ mask) for i in range(lax.axis_size('hid'))])  8.11 us
    all_to_all x1, waiting for transfers between devices, on_device(): lax.all_to_all(results, 'hid', split_axis=0, concat_axis=1, tiled=True)  4.66 us
    all_to_all x1, starting transfers between devices, on_device(): lax.all_to_all(results, 'hid', split_axis=0, concat_axis=1, tiled=True)  3.51 us
    dot_general x3, matrix products, inner_rows(): lax.dot_general(left, right, (((0,), (0,)), ((), ())), preferred_element_...  2.88 us
    dot_general x7, matrix products, dot(): return jnp.dot(left, right, preferred_element_type=jnp.float32)  1.1 us
  transfers between devices with their start and end apart: 12, of which 6 were waited for; matrix products, arithmetic and copies ran while one was open for 10% of the time, Pallas kernels for 0%

profile of v14, /device:TPU:0, one launch (start us, length us, event | category | flops | bytes accessed | tf_op | source)
XLA Modules:
  0.0 49.8 jit_solution(14750389065950905054)
XLA Ops:
  0.6 0.0 copy-start
  0.7 0.9 %pad_maximum_fusion.5 = bf16[6,16,512]{2,0,1:T(8,128)(2,1)S(1)} fusion(bf16[6,16,256]{2,0,1:T(8,128)(2,1)} %bitcast.32, bf16[6,16,256]{2,0,1:T(8,128)(2,1)} %bitcast.33), kind=kLoop, calls=%fused_computation.28 | loop fusion | flops 196608 | bytes 196608 | tf_op jit(solution)/shard_map/concatenate | solution.py:79
  1.6 0.0 copy-start.2
  1.6 16.0 %all_to_all.32 = bf16[6,16,512]{2,0,1:T(8,128)(2,1)S(1)} all-to-all(bf16[6,16,512]{2,0,1:T(8,128)(2,1)S(1)} %pad_maximum_fusion.5), channel_id=1, replica_groups=mesh['hid'=16,'seq'=2] {'hid'}, dimensions={1} | all-to-all | bytes 196608 | tf_op jit(solution)/shard_map/all_to_all | solution.py:82
  17.6 0.0 copy-start.1
  17.7 0.0 copy-done
  17.7 0.2 fusion.58
  17.9 0.0 copy-done.2
  17.9 0.2 fusion.60
  18.1 0.8 %collective-permute-start = (bf16[96,512]{1,0:T(8,128)(2,1)S(1)}, bf16[96,512]{1,0:T(8,128)(2,1)S(1)}, u32[]{:S(2)}, u32[]{:S(2)}) collective-permute-start(bf16[96,512]{1,0:T(8,128)(2,1)S(1)} %fusion.5), channel_id=1, source_target_pairs={{0,6},{2,4},{4,2},{6,0},{8,14},{10,12},{12,10},{14,8},{16,22},{18,... | collective-permute-start | bytes 294920 | tf_op jit(solution)/shard_map/ppermute | solution.py:10
  18.9 1.5 %collective-permute-start.1 = (bf16[96,512]{1,0:T(8,128)(2,1)S(1)}, bf16[96,512]{1,0:T(8,128)(2,1)S(1)}, u32[]{:S(2)}, u32[]{:S(2)}) collective-permute-start(bf16[96,512]{1,0:T(8,128)(2,1)S(1)} %fusion.5), channel_id=1, source_target_pairs={{0,2},{2,0},{4,6},{6,4},{8,10},{10,8},{12,14},{14,12},{16,18},{18,... | collective-permute-start | bytes 294920 | tf_op jit(solution)/shard_map/ppermute | solution.py:10
  20.4 1.3 %collective-permute-start.2 = (bf16[96,512]{1,0:T(8,128)(2,1)S(1)}, bf16[96,512]{1,0:T(8,128)(2,1)S(1)}, u32[]{:S(2)}, u32[]{:S(2)}) collective-permute-start(bf16[96,512]{1,0:T(8,128)(2,1)S(1)} %fusion.5), channel_id=1, source_target_pairs={{0,4},{2,6},{4,0},{6,2},{8,12},{10,14},{12,8},{14,10},{16,20},{18,... | collective-permute-start | bytes 294920 | tf_op jit(solution)/shard_map/ppermute | solution.py:10
  21.7 0.0 copy-done.1
  21.7 0.3 fusion.67
  22.1 0.8 %collective-permute-start.4 = (bf16[96,512]{1,0:T(8,128)(2,1)S(1)}, bf16[96,512]{1,0:T(8,128)(2,1)S(1)}, u32[]{:S(2)}, u32[]{:S(2)}) collective-permute-start(bf16[96,512]{1,0:T(8,128)(2,1)S(1)} %get-tuple-element.58), channel_id=1, source_target_pairs={{0,8},{2,10},{4,12},{6,14},{8,0},{10,2},{12,4},{14,6},{16,24},{18,... | collective-permute-start | bytes 294920 | tf_op jit(solution)/shard_map/ppermute | solution.py:10
  22.9 1.1 %collective-permute-start.5 = (bf16[96,512]{1,0:T(8,128)(2,1)S(1)}, bf16[96,512]{1,0:T(8,128)(2,1)S(1)}, u32[]{:S(2)}, u32[]{:S(2)}) collective-permute-start(bf16[96,512]{1,0:T(8,128)(2,1)S(1)} %get-tuple-element.57), channel_id=1, source_target_pairs={{0,16},{2,18},{4,20},{6,22},{8,24},{10,26},{12,28},{14,30},{16,0},... | collective-permute-start | bytes 294920 | tf_op jit(solution)/shard_map/ppermute | solution.py:10
  24.0 0.0 collective-permute-done
  24.0 0.0 collective-permute-done.1
  24.0 1.0 %collective-permute-done.2 = bf16[96,512]{1,0:T(8,128)(2,1)S(1)} collective-permute-done((bf16[96,512]{1,0:T(8,128)(2,1)S(1)}, bf16[96,512]{1,0:T(8,128)(2,1)S(1)}, u32[]{:S(2)}, u32[]{:S(2)}) %collective-permute-start.2) | collective-permute-done | bytes 98336 | tf_op jit(solution)/shard_map/ppermute | solution.py:10
  25.0 0.8 %collective-permute-start.3 = (bf16[96,512]{1,0:T(8,128)(2,1)S(1)}, bf16[96,512]{1,0:T(8,128)(2,1)S(1)}, u32[]{:S(2)}, u32[]{:S(2)}) collective-permute-start(bf16[96,512]{1,0:T(8,128)(2,1)S(1)} %get-tuple-element.27), channel_id=1, source_target_pairs={{0,8},{2,10},{4,12},{6,14},{8,0},{10,2},{12,4},{14,6},{16,24},{18,... | collective-permute-start | bytes 294920 | tf_op jit(solution)/shard_map/ppermute | solution.py:10
  25.8 1.3 %collective-permute-start.7 = (bf16[96,512]{1,0:T(8,128)(2,1)S(1)}, bf16[96,512]{1,0:T(8,128)(2,1)S(1)}, u32[]{:S(2)}, u32[]{:S(2)}) collective-permute-start(bf16[96,512]{1,0:T(8,128)(2,1)S(1)} %get-tuple-element.31), channel_id=1, source_target_pairs={{0,4},{2,6},{4,0},{6,2},{8,12},{10,14},{12,8},{14,10},{16,20},{18,... | collective-permute-start | bytes 294920 | tf_op jit(solution)/shard_map/ppermute | solution.py:10
  27.1 0.6 %collective-permute-start.6 = (bf16[96,512]{1,0:T(8,128)(2,1)S(1)}, bf16[96,512]{1,0:T(8,128)(2,1)S(1)}, u32[]{:S(2)}, u32[]{:S(2)}) collective-permute-start(bf16[96,512]{1,0:T(8,128)(2,1)S(1)} %get-tuple-element.30), channel_id=1, source_target_pairs={{0,2},{2,0},{4,6},{6,4},{8,10},{10,8},{12,14},{14,12},{16,18},{18,... | collective-permute-start | bytes 294920 | tf_op jit(solution)/shard_map/ppermute | solution.py:10
  27.7 0.0 collective-permute-done.4
  27.7 1.9 %collective-permute-done.5 = bf16[96,512]{1,0:T(8,128)(2,1)S(1)} collective-permute-done((bf16[96,512]{1,0:T(8,128)(2,1)S(1)}, bf16[96,512]{1,0:T(8,128)(2,1)S(1)}, u32[]{:S(2)}, u32[]{:S(2)}) %collective-permute-start.5) | collective-permute-done | bytes 98336 | tf_op jit(solution)/shard_map/ppermute | solution.py:10
  29.6 0.8 %collective-permute-done.3 = bf16[96,512]{1,0:T(8,128)(2,1)S(1)} collective-permute-done((bf16[96,512]{1,0:T(8,128)(2,1)S(1)}, bf16[96,512]{1,0:T(8,128)(2,1)S(1)}, u32[]{:S(2)}, u32[]{:S(2)}) %collective-permute-start.3) | collective-permute-done | bytes 98336 | tf_op jit(solution)/shard_map/ppermute | solution.py:10
  30.4 0.7 %collective-permute-start.8 = (bf16[96,512]{1,0:T(8,128)(2,1)S(1)}, bf16[96,512]{1,0:T(8,128)(2,1)S(1)}, u32[]{:S(2)}, u32[]{:S(2)}) collective-permute-start(bf16[96,512]{1,0:T(8,128)(2,1)S(1)} %fusion.7), channel_id=1, source_target_pairs={{0,16},{2,18},{4,20},{6,22},{8,24},{10,26},{12,28},{14,30},{16,0},... | collective-permute-start | bytes 294920 | tf_op jit(solution)/shard_map/ppermute | solution.py:10
  31.1 0.1 fusion.9
  31.2 0.2 fusion.13
  31.4 0.3 collective-permute-done.6
  31.8 0.0 collective-permute-done.7
  31.8 0.2 convolution_add_fusion.3
  32.0 0.2 fusion
  32.2 0.2 convolution_add_fusion.1
  32.4 0.1 collective-permute-start.10
  32.5 4.1 %collective-permute-done.8 = bf16[96,512]{1,0:T(8,128)(2,1)S(1)} collective-permute-done((bf16[96,512]{1,0:T(8,128)(2,1)S(1)}, bf16[96,512]{1,0:T(8,128)(2,1)S(1)}, u32[]{:S(2)}, u32[]{:S(2)}) %collective-permute-start.8) | collective-permute-done | bytes 98336 | tf_op jit(solution)/shard_map/ppermute | solution.py:10
  36.7 0.2 fusion.1
  36.9 0.2 fusion.22
  37.1 0.7 %all_to_all.27 = bf16[16,6,512]{2,1,0:T(8,128)(2,1)} reshape(bf16[96,512]{1,0:T(8,128)(2,1)S(1)} %pad_maximum_fusion.6) | data formatting | bytes 196608 | tf_op jit(solution)/shard_map/all_to_all | solution.py:108
  37.8 3.5 %all-to-all-start.1 = ((bf16[16,6,512]{2,1,0:T(8,128)(2,1)}), bf16[16,6,512]{2,1,0:T(8,128)(2,1)S(1)}, u32[]{:S(2)}, u32[]{:S(2)}) async-start(bf16[16,6,512]{2,1,0:T(8,128)(2,1)} %all_to_all.27), calls=%async_computation.1 | async-start | bytes 262144 | tf_op jit(solution)/shard_map/all_to_all | solution.py:108
  41.3 0.1 collective-permute-start.9
  41.4 0.0 collective-permute-done.10
  41.6 1.1 %convolution_multiply_fusion = f32[640,256]{1,0:T(8,128)} fusion(bf16[96,640]{1,0:T(8,128)(2,1)S(1)} %constant_dynamic-update-slice_fusion.11, bf16[96,640]{1,0:T(8,128)(2,1)S(1)} %get-tuple-element.53, bf16[96,256]{1,0:T(8,128)(2,1)S(1)} %get-tuple-element.46, bf16[96,256]{1,0:T(8,128)(2,1)S(1)} %slice.176), kind=kOutput, calls=%fused_computation | convolution fusion | flops 63766528 | bytes 999424 | tf_op jit(solution)/shard_map/dot_general | solution.py:32
  42.7 0.0 collective-permute-done.9
  42.7 0.9 %convolution_multiply_fusion.1 = f32[128,256]{1,0:T(8,128)} fusion(bf16[96,256]{1,0:T(8,128)(2,1)S(1)} %get-tuple-element.46, bf16[96,256]{1,0:T(8,128)(2,1)S(1)} %slice.176, bf16[96,128]{1,0:T(8,128)(2,1)S(1)} %get-tuple-element.55, bf16[96,128]{1,0:T(8,128)(2,1)S(1)} %get-tuple-element.49), kind=kOutput, calls=%fused_computation.1 | convolution fusion | flops 12910592 | bytes 278528 | tf_op jit(solution)/shard_map/dot_general | solution.py:32
  43.6 0.9 %convolution_multiply_fusion.2 = f32[256,128]{1,0:T(8,128)} fusion(bf16[96,256]{1,0:T(8,128)(2,1)S(1)} %get-tuple-element.45, bf16[96,256]{1,0:T(8,128)(2,1)S(1)} %fusion.27, bf16[96,128]{1,0:T(8,128)(2,1)S(1)} %get-tuple-element.56, bf16[96,128]{1,0:T(8,128)(2,1)S(1)} %get-tuple-element.51), kind=kOutput, calls=%fused_computation.2 | convolution fusion | flops 12910592 | bytes 278528 | tf_op jit(solution)/shard_map/dot_general | solution.py:32
  44.4 4.7 %all-to-all-done.1 = bf16[16,6,512]{2,1,0:T(8,128)(2,1)S(1)} async-done(((bf16[16,6,512]{2,1,0:T(8,128)(2,1)}), bf16[16,6,512]{2,1,0:T(8,128)(2,1)S(1)}, u32[]{:S(2)}, u32[]{:S(2)}) %all-to-all-start.1) | async-done | bytes 98336 | tf_op jit(solution)/shard_map/all_to_all | solution.py:108
  49.1 0.7 %fusion.65 = (bf16[6,16,256]{2,0,1:T(8,128)(2,1)}, bf16[6,16,256]{2,0,1:T(8,128)(2,1)}) fusion(bf16[6,16,512]{2,0,1:T(8,128)(2,1)S(1)} %bitcast.31), kind=kLoop, calls=%fused_computation.109 | loop fusion | bytes 196608 | tf_op jit(solution)/shard_map/slice | solution.py:111
  (29 shorter events, 0.6 us)
Async XLA Ops:
  0.6 17.1 %copy-start = (bf16[256,256]{1,0:T(8,128)(2,1)S(1)}, bf16[256,256]{1,0:T(8,128)(2,1)}, u32[]{:S(2)}) copy-start(bf16[256,256]{1,0:T(8,128)(2,1)} %param.8) | copy-start | bytes 393220
  1.6 16.3 %copy-start.2 = (bf16[256,256]{1,0:T(8,128)(2,1)S(1)}, bf16[256,256]{1,0:T(8,128)(2,1)}, u32[]{:S(2)}) copy-start(bf16[256,256]{1,0:T(8,128)(2,1)} %param.7) | copy-start | bytes 393220
  17.6 4.0 %copy-start.1 = (bf16[1,5,256,256]{3,2,1,0:T(8,128)(2,1)S(1)}, bf16[1,5,256,256]{3,2,1,0:T(8,128)(2,1)}, u32[]{:S(2)}) copy-start(bf16[1,5,256,256]{3,2,1,0:T(8,128)(2,1)} %param.6) | copy-start | bytes 1966084
  18.1 5.9 %collective-permute-start = (bf16[96,512]{1,0:T(8,128)(2,1)S(1)}, bf16[96,512]{1,0:T(8,128)(2,1)S(1)}, u32[]{:S(2)}, u32[]{:S(2)}) collective-permute-start(bf16[96,512]{1,0:T(8,128)(2,1)S(1)} %fusion.5), channel_id=1, source_target_pairs={{0,6},{2,4},{4,2},{6,0},{8,14},{10,12},{12,10},{14,8},{16,22},{18,... | collective-permute-start | bytes 294920 | tf_op jit(solution)/shard_map/ppermute | solution.py:10
  18.9 5.1 %collective-permute-start.1 = (bf16[96,512]{1,0:T(8,128)(2,1)S(1)}, bf16[96,512]{1,0:T(8,128)(2,1)S(1)}, u32[]{:S(2)}, u32[]{:S(2)}) collective-permute-start(bf16[96,512]{1,0:T(8,128)(2,1)S(1)} %fusion.5), channel_id=1, source_target_pairs={{0,2},{2,0},{4,6},{6,4},{8,10},{10,8},{12,14},{14,12},{16,18},{18,... | collective-permute-start | bytes 294920 | tf_op jit(solution)/shard_map/ppermute | solution.py:10
  20.4 4.6 %collective-permute-start.2 = (bf16[96,512]{1,0:T(8,128)(2,1)S(1)}, bf16[96,512]{1,0:T(8,128)(2,1)S(1)}, u32[]{:S(2)}, u32[]{:S(2)}) collective-permute-start(bf16[96,512]{1,0:T(8,128)(2,1)S(1)} %fusion.5), channel_id=1, source_target_pairs={{0,4},{2,6},{4,0},{6,2},{8,12},{10,14},{12,8},{14,10},{16,20},{18,... | collective-permute-start | bytes 294920 | tf_op jit(solution)/shard_map/ppermute | solution.py:10
  22.1 5.6 %collective-permute-start.4 = (bf16[96,512]{1,0:T(8,128)(2,1)S(1)}, bf16[96,512]{1,0:T(8,128)(2,1)S(1)}, u32[]{:S(2)}, u32[]{:S(2)}) collective-permute-start(bf16[96,512]{1,0:T(8,128)(2,1)S(1)} %get-tuple-element.58), channel_id=1, source_target_pairs={{0,8},{2,10},{4,12},{6,14},{8,0},{10,2},{12,4},{14,6},{16,24},{18,... | collective-permute-start | bytes 294920 | tf_op jit(solution)/shard_map/ppermute | solution.py:10
  22.9 6.7 %collective-permute-start.5 = (bf16[96,512]{1,0:T(8,128)(2,1)S(1)}, bf16[96,512]{1,0:T(8,128)(2,1)S(1)}, u32[]{:S(2)}, u32[]{:S(2)}) collective-permute-start(bf16[96,512]{1,0:T(8,128)(2,1)S(1)} %get-tuple-element.57), channel_id=1, source_target_pairs={{0,16},{2,18},{4,20},{6,22},{8,24},{10,26},{12,28},{14,30},{16,0},... | collective-permute-start | bytes 294920 | tf_op jit(solution)/shard_map/ppermute | solution.py:10
  25.0 5.3 %collective-permute-start.3 = (bf16[96,512]{1,0:T(8,128)(2,1)S(1)}, bf16[96,512]{1,0:T(8,128)(2,1)S(1)}, u32[]{:S(2)}, u32[]{:S(2)}) collective-permute-start(bf16[96,512]{1,0:T(8,128)(2,1)S(1)} %get-tuple-element.27), channel_id=1, source_target_pairs={{0,8},{2,10},{4,12},{6,14},{8,0},{10,2},{12,4},{14,6},{16,24},{18,... | collective-permute-start | bytes 294920 | tf_op jit(solution)/shard_map/ppermute | solution.py:10
  25.8 5.9 %collective-permute-start.7 = (bf16[96,512]{1,0:T(8,128)(2,1)S(1)}, bf16[96,512]{1,0:T(8,128)(2,1)S(1)}, u32[]{:S(2)}, u32[]{:S(2)}) collective-permute-start(bf16[96,512]{1,0:T(8,128)(2,1)S(1)} %get-tuple-element.31), channel_id=1, source_target_pairs={{0,4},{2,6},{4,0},{6,2},{8,12},{10,14},{12,8},{14,10},{16,20},{18,... | collective-permute-start | bytes 294920 | tf_op jit(solution)/shard_map/ppermute | solution.py:10
  27.1 4.6 %collective-permute-start.6 = (bf16[96,512]{1,0:T(8,128)(2,1)S(1)}, bf16[96,512]{1,0:T(8,128)(2,1)S(1)}, u32[]{:S(2)}, u32[]{:S(2)}) collective-permute-start(bf16[96,512]{1,0:T(8,128)(2,1)S(1)} %get-tuple-element.30), channel_id=1, source_target_pairs={{0,2},{2,0},{4,6},{6,4},{8,10},{10,8},{12,14},{14,12},{16,18},{18,... | collective-permute-start | bytes 294920 | tf_op jit(solution)/shard_map/ppermute | solution.py:10
  30.4 6.3 %collective-permute-start.8 = (bf16[96,512]{1,0:T(8,128)(2,1)S(1)}, bf16[96,512]{1,0:T(8,128)(2,1)S(1)}, u32[]{:S(2)}, u32[]{:S(2)}) collective-permute-start(bf16[96,512]{1,0:T(8,128)(2,1)S(1)} %fusion.7), channel_id=1, source_target_pairs={{0,16},{2,18},{4,20},{6,22},{8,24},{10,26},{12,28},{14,30},{16,0},... | collective-permute-start | bytes 294920 | tf_op jit(solution)/shard_map/ppermute | solution.py:10
  32.4 9.0 %collective-permute-start.10 = (bf16[96,1024]{1,0:T(8,128)(2,1)S(1)}, bf16[96,1024]{1,0:T(8,128)(2,1)S(1)}, u32[]{:S(2)}, u32[]{:S(2)}) collective-permute-start(bf16[96,1024]{1,0:T(8,128)(2,1)S(1)} %constant_dynamic-update-slice_fusion.5), channel_id=1, source_target_pairs={{0,1},{1,0},{2,3},{3,2},{4,5},{5,4},{6,7},{7,6},{8,9},{9,8},{10,11... | collective-permute-start | bytes 589832 | tf_op jit(solution)/shard_map/ppermute | solution.py:14
  37.8 11.3 %all-to-all-start.1 = ((bf16[16,6,512]{2,1,0:T(8,128)(2,1)}), bf16[16,6,512]{2,1,0:T(8,128)(2,1)S(1)}, u32[]{:S(2)}, u32[]{:S(2)}) async-start(bf16[16,6,512]{2,1,0:T(8,128)(2,1)} %all_to_all.27), calls=%async_computation.1 | async-start | bytes 262144 | tf_op jit(solution)/shard_map/all_to_all | solution.py:108
  41.3 1.4 %collective-permute-start.9 = (bf16[96,256]{1,0:T(8,128)(2,1)S(1)}, bf16[96,256]{1,0:T(8,128)(2,1)S(1)}, u32[]{:S(2)}, u32[]{:S(2)}) collective-permute-start(bf16[96,256]{1,0:T(8,128)(2,1)S(1)} %pad_maximum_fusion.10), channel_id=1, source_target_pairs={{0,1},{1,0},{2,3},{3,2},{4,5},{5,4},{6,7},{7,6},{8,9},{9,8},{10,11... | collective-permute-start | bytes 147464 | tf_op jit(solution)/shard_map/ppermute | solution.py:14

commit v15 on v14

--- a/solution.py
+++ b/solution.py
@@ -52,8 +52,8 @@
         got = [exchange(sent, mask) for mask in masks]
         far = far | {mask: exchange(beside[mask], mask) for mask in beside}
         if at == 1:
-            got, early = lax.optimization_barrier((got, early))
-            far = far | early
+            got, blocks_early = lax.optimization_barrier((got, list(early.values())))
+            far = far | dict(zip(early, blocks_early))
         else:
             got = lax.optimization_barrier(got)
         total = total + sum(x.astype(jnp.float32) for x in got)

time: 50 us -> 50.6 us (1.012)
  starting transfers between devices: 12.4 us -> 13.7 us
  waiting for transfers between devices: 12.8 us -> 12.1 us
    all_to_all x1, starting transfers between devices: 3.51 us -> 4.32 us  [on_device(): lax.all_to_all(results, 'hid', split_axis=0, concat_axis=1, tiled=True)]
    ppermute x9, waiting for transfers between devices: 8.11 us -> 7.46 us  [exchange(): lax.ppermute(x, 'hid', [(i, i ^ mask) for i in range(lax.axis_size('hid'))])]
where the time goes in v15:
time: 50.6 us; the launch traced here: 50.4 us
  blocking collectives  16 us (32%)
  starting transfers between devices  13.7 us (27%)
  waiting for transfers between devices  12.1 us (24%)
  matrix products  4.7 us (9%)
  local copies, waits for them, and re-layouts  1.54 us (3%)
  other arithmetic  1.33 us (3%)
  between operations  0.94 us (2%)
    all_to_all x1, blocking collectives, on_device(): rows = lax.all_to_all(both, 'hid', split_axis=1, concat_axis=0, tiled=True)  16 us
    ppermute x9, starting transfers between devices, exchange(): lax.ppermute(x, 'hid', [(i, i ^ mask) for i in range(lax.axis_size('hid'))])  9.25 us
    ppermute x9, waiting for transfers between devices, exchange(): lax.ppermute(x, 'hid', [(i, i ^ mask) for i in range(lax.axis_size('hid'))])  7.46 us
    all_to_all x1, waiting for transfers between devices, on_device(): lax.all_to_all(results, 'hid', split_axis=0, concat_axis=1, tiled=True)  4.67 us
    all_to_all x1, starting transfers between devices, on_device(): lax.all_to_all(results, 'hid', split_axis=0, concat_axis=1, tiled=True)  4.32 us
    dot_general x3, matrix products, inner_rows(): lax.dot_general(left, right, (((0,), (0,)), ((), ())), preferred_element_...  2.88 us
    dot_general x7, matrix products, dot(): return jnp.dot(left, right, preferred_element_type=jnp.float32)  1.1 us
  transfers between devices with their start and end apart: 12, of which 6 were waited for; matrix products, arithmetic and copies ran while one was open for 10% of the time, Pallas kernels for 0%

profile of v15, /device:TPU:0, one launch (start us, length us, event | category | flops | bytes accessed | tf_op | source)
XLA Modules:
  0.0 50.4 jit_solution(8328886678489347642)
XLA Ops:
  0.6 0.0 copy-start
  0.7 0.9 %pad_maximum_fusion.5 = bf16[6,16,512]{2,0,1:T(8,128)(2,1)S(1)} fusion(bf16[6,16,256]{2,0,1:T(8,128)(2,1)} %bitcast.32, bf16[6,16,256]{2,0,1:T(8,128)(2,1)} %bitcast.33), kind=kLoop, calls=%fused_computation.28 | loop fusion | flops 196608 | bytes 196608 | tf_op jit(solution)/shard_map/concatenate | solution.py:79
  1.6 0.0 copy-start.2
  1.6 16.0 %all_to_all.32 = bf16[6,16,512]{2,0,1:T(8,128)(2,1)S(1)} all-to-all(bf16[6,16,512]{2,0,1:T(8,128)(2,1)S(1)} %pad_maximum_fusion.5), channel_id=1, replica_groups=mesh['hid'=16,'seq'=2] {'hid'}, dimensions={1} | all-to-all | bytes 196608 | tf_op jit(solution)/shard_map/all_to_all | solution.py:82
  17.6 0.0 copy-start.1
  17.7 0.0 copy-done
  17.7 0.2 fusion.58
  17.9 0.0 copy-done.2
  17.9 0.2 fusion.60
  18.1 0.8 %collective-permute-start = (bf16[96,512]{1,0:T(8,128)(2,1)S(1)}, bf16[96,512]{1,0:T(8,128)(2,1)S(1)}, u32[]{:S(2)}, u32[]{:S(2)}) collective-permute-start(bf16[96,512]{1,0:T(8,128)(2,1)S(1)} %fusion.5), channel_id=1, source_target_pairs={{0,6},{2,4},{4,2},{6,0},{8,14},{10,12},{12,10},{14,8},{16,22},{18,... | collective-permute-start | bytes 294920 | tf_op jit(solution)/shard_map/ppermute | solution.py:10
  18.9 1.5 %collective-permute-start.1 = (bf16[96,512]{1,0:T(8,128)(2,1)S(1)}, bf16[96,512]{1,0:T(8,128)(2,1)S(1)}, u32[]{:S(2)}, u32[]{:S(2)}) collective-permute-start(bf16[96,512]{1,0:T(8,128)(2,1)S(1)} %fusion.5), channel_id=1, source_target_pairs={{0,2},{2,0},{4,6},{6,4},{8,10},{10,8},{12,14},{14,12},{16,18},{18,... | collective-permute-start | bytes 294920 | tf_op jit(solution)/shard_map/ppermute | solution.py:10
  20.4 1.3 %collective-permute-start.2 = (bf16[96,512]{1,0:T(8,128)(2,1)S(1)}, bf16[96,512]{1,0:T(8,128)(2,1)S(1)}, u32[]{:S(2)}, u32[]{:S(2)}) collective-permute-start(bf16[96,512]{1,0:T(8,128)(2,1)S(1)} %fusion.5), channel_id=1, source_target_pairs={{0,4},{2,6},{4,0},{6,2},{8,12},{10,14},{12,8},{14,10},{16,20},{18,... | collective-permute-start | bytes 294920 | tf_op jit(solution)/shard_map/ppermute | solution.py:10
  21.7 0.0 copy-done.1
  21.7 0.3 fusion.67
  22.1 1.0 %collective-permute-start.4 = (bf16[96,512]{1,0:T(8,128)(2,1)S(1)}, bf16[96,512]{1,0:T(8,128)(2,1)S(1)}, u32[]{:S(2)}, u32[]{:S(2)}) collective-permute-start(bf16[96,512]{1,0:T(8,128)(2,1)S(1)} %get-tuple-element.58), channel_id=1, source_target_pairs={{0,16},{2,18},{4,20},{6,22},{8,24},{10,26},{12,28},{14,30},{16,0},... | collective-permute-start | bytes 294920 | tf_op jit(solution)/shard_map/ppermute | solution.py:10
  23.1 0.9 %collective-permute-start.5 = (bf16[96,512]{1,0:T(8,128)(2,1)S(1)}, bf16[96,512]{1,0:T(8,128)(2,1)S(1)}, u32[]{:S(2)}, u32[]{:S(2)}) collective-permute-start(bf16[96,512]{1,0:T(8,128)(2,1)S(1)} %get-tuple-element.57), channel_id=1, source_target_pairs={{0,8},{2,10},{4,12},{6,14},{8,0},{10,2},{12,4},{14,6},{16,24},{18,... | collective-permute-start | bytes 294920 | tf_op jit(solution)/shard_map/ppermute | solution.py:10
  24.0 0.0 collective-permute-done
  24.0 0.0 collective-permute-done.1
  24.0 1.0 %collective-permute-done.2 = bf16[96,512]{1,0:T(8,128)(2,1)S(1)} collective-permute-done((bf16[96,512]{1,0:T(8,128)(2,1)S(1)}, bf16[96,512]{1,0:T(8,128)(2,1)S(1)}, u32[]{:S(2)}, u32[]{:S(2)}) %collective-permute-start.2) | collective-permute-done | bytes 98336 | tf_op jit(solution)/shard_map/ppermute | solution.py:10
  25.0 0.8 %collective-permute-start.3 = (bf16[96,512]{1,0:T(8,128)(2,1)S(1)}, bf16[96,512]{1,0:T(8,128)(2,1)S(1)}, u32[]{:S(2)}, u32[]{:S(2)}) collective-permute-start(bf16[96,512]{1,0:T(8,128)(2,1)S(1)} %get-tuple-element.27), channel_id=1, source_target_pairs={{0,8},{2,10},{4,12},{6,14},{8,0},{10,2},{12,4},{14,6},{16,24},{18,... | collective-permute-start | bytes 294920 | tf_op jit(solution)/shard_map/ppermute | solution.py:10
  25.8 1.3 %collective-permute-start.7 = (bf16[96,512]{1,0:T(8,128)(2,1)S(1)}, bf16[96,512]{1,0:T(8,128)(2,1)S(1)}, u32[]{:S(2)}, u32[]{:S(2)}) collective-permute-start(bf16[96,512]{1,0:T(8,128)(2,1)S(1)} %get-tuple-element.31), channel_id=1, source_target_pairs={{0,4},{2,6},{4,0},{6,2},{8,12},{10,14},{12,8},{14,10},{16,20},{18,... | collective-permute-start | bytes 294920 | tf_op jit(solution)/shard_map/ppermute | solution.py:10
  27.1 0.6 %collective-permute-start.6 = (bf16[96,512]{1,0:T(8,128)(2,1)S(1)}, bf16[96,512]{1,0:T(8,128)(2,1)S(1)}, u32[]{:S(2)}, u32[]{:S(2)}) collective-permute-start(bf16[96,512]{1,0:T(8,128)(2,1)S(1)} %get-tuple-element.30), channel_id=1, source_target_pairs={{0,2},{2,0},{4,6},{6,4},{8,10},{10,8},{12,14},{14,12},{16,18},{18,... | collective-permute-start | bytes 294920 | tf_op jit(solution)/shard_map/ppermute | solution.py:10
  27.7 1.1 %collective-permute-done.4 = bf16[96,512]{1,0:T(8,128)(2,1)S(1)} collective-permute-done((bf16[96,512]{1,0:T(8,128)(2,1)S(1)}, bf16[96,512]{1,0:T(8,128)(2,1)S(1)}, u32[]{:S(2)}, u32[]{:S(2)}) %collective-permute-start.4) | collective-permute-done | bytes 98336 | tf_op jit(solution)/shard_map/ppermute | solution.py:10
  28.8 0.0 collective-permute-done.5
  28.8 1.0 %collective-permute-done.3 = bf16[96,512]{1,0:T(8,128)(2,1)S(1)} collective-permute-done((bf16[96,512]{1,0:T(8,128)(2,1)S(1)}, bf16[96,512]{1,0:T(8,128)(2,1)S(1)}, u32[]{:S(2)}, u32[]{:S(2)}) %collective-permute-start.3) | collective-permute-done | bytes 98336 | tf_op jit(solution)/shard_map/ppermute | solution.py:10
  29.8 1.1 %collective-permute-start.8 = (bf16[96,512]{1,0:T(8,128)(2,1)S(1)}, bf16[96,512]{1,0:T(8,128)(2,1)S(1)}, u32[]{:S(2)}, u32[]{:S(2)}) collective-permute-start(bf16[96,512]{1,0:T(8,128)(2,1)S(1)} %fusion.7), channel_id=1, source_target_pairs={{0,16},{2,18},{4,20},{6,22},{8,24},{10,26},{12,28},{14,30},{16,0},... | collective-permute-start | bytes 294920 | tf_op jit(solution)/shard_map/ppermute | solution.py:10
  31.0 0.1 fusion.9
  31.1 0.2 fusion.13
  31.3 0.4 collective-permute-done.6
  31.8 0.0 collective-permute-done.7
  31.8 0.2 convolution_add_fusion.3
  32.0 0.2 fusion
  32.2 0.2 convolution_add_fusion.1
  32.4 0.1 collective-permute-start.10
  32.5 3.9 %collective-permute-done.8 = bf16[96,512]{1,0:T(8,128)(2,1)S(1)} collective-permute-done((bf16[96,512]{1,0:T(8,128)(2,1)S(1)}, bf16[96,512]{1,0:T(8,128)(2,1)S(1)}, u32[]{:S(2)}, u32[]{:S(2)}) %collective-permute-start.8) | collective-permute-done | bytes 98336 | tf_op jit(solution)/shard_map/ppermute | solution.py:10
  36.5 0.2 fusion.1
  36.7 0.2 fusion.22
  36.9 0.7 %all_to_all.27 = bf16[16,6,512]{2,1,0:T(8,128)(2,1)} reshape(bf16[96,512]{1,0:T(8,128)(2,1)S(1)} %pad_maximum_fusion.6) | data formatting | bytes 196608 | tf_op jit(solution)/shard_map/all_to_all | solution.py:108
  37.6 4.3 %all-to-all-start.1 = ((bf16[16,6,512]{2,1,0:T(8,128)(2,1)}), bf16[16,6,512]{2,1,0:T(8,128)(2,1)S(1)}, u32[]{:S(2)}, u32[]{:S(2)}) async-start(bf16[16,6,512]{2,1,0:T(8,128)(2,1)} %all_to_all.27), calls=%async_computation.1 | async-start | bytes 262144 | tf_op jit(solution)/shard_map/all_to_all | solution.py:108
  42.0 0.1 collective-permute-start.9
  42.0 0.0 collective-permute-done.10
  42.2 1.1 %convolution_multiply_fusion = f32[640,256]{1,0:T(8,128)} fusion(bf16[96,640]{1,0:T(8,128)(2,1)S(1)} %constant_dynamic-update-slice_fusion.11, bf16[96,640]{1,0:T(8,128)(2,1)S(1)} %get-tuple-element.53, bf16[96,256]{1,0:T(8,128)(2,1)S(1)} %get-tuple-element.46, bf16[96,256]{1,0:T(8,128)(2,1)S(1)} %slice.176), kind=kOutput, calls=%fused_computation | convolution fusion | flops 63766528 | bytes 999424 | tf_op jit(solution)/shard_map/dot_general | solution.py:32
  43.3 0.0 collective-permute-done.9
  43.3 0.9 %convolution_multiply_fusion.1 = f32[128,256]{1,0:T(8,128)} fusion(bf16[96,256]{1,0:T(8,128)(2,1)S(1)} %get-tuple-element.46, bf16[96,256]{1,0:T(8,128)(2,1)S(1)} %slice.176, bf16[96,128]{1,0:T(8,128)(2,1)S(1)} %get-tuple-element.55, bf16[96,128]{1,0:T(8,128)(2,1)S(1)} %get-tuple-element.49), kind=kOutput, calls=%fused_computation.1 | convolution fusion | flops 12910592 | bytes 278528 | tf_op jit(solution)/shard_map/dot_general | solution.py:32
  44.2 0.9 %convolution_multiply_fusion.2 = f32[256,128]{1,0:T(8,128)} fusion(bf16[96,256]{1,0:T(8,128)(2,1)S(1)} %get-tuple-element.45, bf16[96,256]{1,0:T(8,128)(2,1)S(1)} %fusion.27, bf16[96,128]{1,0:T(8,128)(2,1)S(1)} %get-tuple-element.56, bf16[96,128]{1,0:T(8,128)(2,1)S(1)} %get-tuple-element.51), kind=kOutput, calls=%fused_computation.2 | convolution fusion | flops 12910592 | bytes 278528 | tf_op jit(solution)/shard_map/dot_general | solution.py:32
  45.1 4.7 %all-to-all-done.1 = bf16[16,6,512]{2,1,0:T(8,128)(2,1)S(1)} async-done(((bf16[16,6,512]{2,1,0:T(8,128)(2,1)}), bf16[16,6,512]{2,1,0:T(8,128)(2,1)S(1)}, u32[]{:S(2)}, u32[]{:S(2)}) %all-to-all-start.1) | async-done | bytes 98336 | tf_op jit(solution)/shard_map/all_to_all | solution.py:108
  49.7 0.7 %fusion.65 = (bf16[6,16,256]{2,0,1:T(8,128)(2,1)}, bf16[6,16,256]{2,0,1:T(8,128)(2,1)}) fusion(bf16[6,16,512]{2,0,1:T(8,128)(2,1)S(1)} %bitcast.31), kind=kLoop, calls=%fused_computation.109 | loop fusion | bytes 196608 | tf_op jit(solution)/shard_map/slice | solution.py:111
  (29 shorter events, 0.6 us)
Async XLA Ops:
  0.6 17.1 %copy-start = (bf16[256,256]{1,0:T(8,128)(2,1)S(1)}, bf16[256,256]{1,0:T(8,128)(2,1)}, u32[]{:S(2)}) copy-start(bf16[256,256]{1,0:T(8,128)(2,1)} %param.8) | copy-start | bytes 393220
  1.6 16.3 %copy-start.2 = (bf16[256,256]{1,0:T(8,128)(2,1)S(1)}, bf16[256,256]{1,0:T(8,128)(2,1)}, u32[]{:S(2)}) copy-start(bf16[256,256]{1,0:T(8,128)(2,1)} %param.7) | copy-start | bytes 393220
  17.6 4.0 %copy-start.1 = (bf16[1,5,256,256]{3,2,1,0:T(8,128)(2,1)S(1)}, bf16[1,5,256,256]{3,2,1,0:T(8,128)(2,1)}, u32[]{:S(2)}) copy-start(bf16[1,5,256,256]{3,2,1,0:T(8,128)(2,1)} %param.6) | copy-start | bytes 1966084
  18.1 5.9 %collective-permute-start = (bf16[96,512]{1,0:T(8,128)(2,1)S(1)}, bf16[96,512]{1,0:T(8,128)(2,1)S(1)}, u32[]{:S(2)}, u32[]{:S(2)}) collective-permute-start(bf16[96,512]{1,0:T(8,128)(2,1)S(1)} %fusion.5), channel_id=1, source_target_pairs={{0,6},{2,4},{4,2},{6,0},{8,14},{10,12},{12,10},{14,8},{16,22},{18,... | collective-permute-start | bytes 294920 | tf_op jit(solution)/shard_map/ppermute | solution.py:10
  18.9 5.1 %collective-permute-start.1 = (bf16[96,512]{1,0:T(8,128)(2,1)S(1)}, bf16[96,512]{1,0:T(8,128)(2,1)S(1)}, u32[]{:S(2)}, u32[]{:S(2)}) collective-permute-start(bf16[96,512]{1,0:T(8,128)(2,1)S(1)} %fusion.5), channel_id=1, source_target_pairs={{0,2},{2,0},{4,6},{6,4},{8,10},{10,8},{12,14},{14,12},{16,18},{18,... | collective-permute-start | bytes 294920 | tf_op jit(solution)/shard_map/ppermute | solution.py:10
  20.4 4.6 %collective-permute-start.2 = (bf16[96,512]{1,0:T(8,128)(2,1)S(1)}, bf16[96,512]{1,0:T(8,128)(2,1)S(1)}, u32[]{:S(2)}, u32[]{:S(2)}) collective-permute-start(bf16[96,512]{1,0:T(8,128)(2,1)S(1)} %fusion.5), channel_id=1, source_target_pairs={{0,4},{2,6},{4,0},{6,2},{8,12},{10,14},{12,8},{14,10},{16,20},{18,... | collective-permute-start | bytes 294920 | tf_op jit(solution)/shard_map/ppermute | solution.py:10
  22.1 6.6 %collective-permute-start.4 = (bf16[96,512]{1,0:T(8,128)(2,1)S(1)}, bf16[96,512]{1,0:T(8,128)(2,1)S(1)}, u32[]{:S(2)}, u32[]{:S(2)}) collective-permute-start(bf16[96,512]{1,0:T(8,128)(2,1)S(1)} %get-tuple-element.58), channel_id=1, source_target_pairs={{0,16},{2,18},{4,20},{6,22},{8,24},{10,26},{12,28},{14,30},{16,0},... | collective-permute-start | bytes 294920 | tf_op jit(solution)/shard_map/ppermute | solution.py:10
  23.1 5.7 %collective-permute-start.5 = (bf16[96,512]{1,0:T(8,128)(2,1)S(1)}, bf16[96,512]{1,0:T(8,128)(2,1)S(1)}, u32[]{:S(2)}, u32[]{:S(2)}) collective-permute-start(bf16[96,512]{1,0:T(8,128)(2,1)S(1)} %get-tuple-element.57), channel_id=1, source_target_pairs={{0,8},{2,10},{4,12},{6,14},{8,0},{10,2},{12,4},{14,6},{16,24},{18,... | collective-permute-start | bytes 294920 | tf_op jit(solution)/shard_map/ppermute | solution.py:10
  25.0 4.8 %collective-permute-start.3 = (bf16[96,512]{1,0:T(8,128)(2,1)S(1)}, bf16[96,512]{1,0:T(8,128)(2,1)S(1)}, u32[]{:S(2)}, u32[]{:S(2)}) collective-permute-start(bf16[96,512]{1,0:T(8,128)(2,1)S(1)} %get-tuple-element.27), channel_id=1, source_target_pairs={{0,8},{2,10},{4,12},{6,14},{8,0},{10,2},{12,4},{14,6},{16,24},{18,... | collective-permute-start | bytes 294920 | tf_op jit(solution)/shard_map/ppermute | solution.py:10
  25.8 5.9 %collective-permute-start.7 = (bf16[96,512]{1,0:T(8,128)(2,1)S(1)}, bf16[96,512]{1,0:T(8,128)(2,1)S(1)}, u32[]{:S(2)}, u32[]{:S(2)}) collective-permute-start(bf16[96,512]{1,0:T(8,128)(2,1)S(1)} %get-tuple-element.31), channel_id=1, source_target_pairs={{0,4},{2,6},{4,0},{6,2},{8,12},{10,14},{12,8},{14,10},{16,20},{18,... | collective-permute-start | bytes 294920 | tf_op jit(solution)/shard_map/ppermute | solution.py:10
  27.1 4.6 %collective-permute-start.6 = (bf16[96,512]{1,0:T(8,128)(2,1)S(1)}, bf16[96,512]{1,0:T(8,128)(2,1)S(1)}, u32[]{:S(2)}, u32[]{:S(2)}) collective-permute-start(bf16[96,512]{1,0:T(8,128)(2,1)S(1)} %get-tuple-element.30), channel_id=1, source_target_pairs={{0,2},{2,0},{4,6},{6,4},{8,10},{10,8},{12,14},{14,12},{16,18},{18,... | collective-permute-start | bytes 294920 | tf_op jit(solution)/shard_map/ppermute | solution.py:10
  29.8 6.6 %collective-permute-start.8 = (bf16[96,512]{1,0:T(8,128)(2,1)S(1)}, bf16[96,512]{1,0:T(8,128)(2,1)S(1)}, u32[]{:S(2)}, u32[]{:S(2)}) collective-permute-start(bf16[96,512]{1,0:T(8,128)(2,1)S(1)} %fusion.7), channel_id=1, source_target_pairs={{0,16},{2,18},{4,20},{6,22},{8,24},{10,26},{12,28},{14,30},{16,0},... | collective-permute-start | bytes 294920 | tf_op jit(solution)/shard_map/ppermute | solution.py:10
  32.4 9.6 %collective-permute-start.10 = (bf16[96,1024]{1,0:T(8,128)(2,1)S(1)}, bf16[96,1024]{1,0:T(8,128)(2,1)S(1)}, u32[]{:S(2)}, u32[]{:S(2)}) collective-permute-start(bf16[96,1024]{1,0:T(8,128)(2,1)S(1)} %constant_dynamic-update-slice_fusion.5), channel_id=1, source_target_pairs={{0,1},{1,0},{2,3},{3,2},{4,5},{5,4},{6,7},{7,6},{8,9},{9,8},{10,11... | collective-permute-start | bytes 589832 | tf_op jit(solution)/shard_map/ppermute | solution.py:14
  37.6 12.1 %all-to-all-start.1 = ((bf16[16,6,512]{2,1,0:T(8,128)(2,1)}), bf16[16,6,512]{2,1,0:T(8,128)(2,1)S(1)}, u32[]{:S(2)}, u32[]{:S(2)}) async-start(bf16[16,6,512]{2,1,0:T(8,128)(2,1)} %all_to_all.27), calls=%async_computation.1 | async-start | bytes 262144 | tf_op jit(solution)/shard_map/all_to_all | solution.py:108
  42.0 1.4 %collective-permute-start.9 = (bf16[96,256]{1,0:T(8,128)(2,1)S(1)}, bf16[96,256]{1,0:T(8,128)(2,1)S(1)}, u32[]{:S(2)}, u32[]{:S(2)}) collective-permute-start(bf16[96,256]{1,0:T(8,128)(2,1)S(1)} %pad_maximum_fusion.10), channel_id=1, source_target_pairs={{0,1},{1,0},{2,3},{3,2},{4,5},{5,4},{6,7},{7,6},{8,9},{9,8},{10,11... | collective-permute-start | bytes 147464 | tf_op jit(solution)/shard_map/ppermute | solution.py:14

commit v16 on v15

--- a/solution.py
+++ b/solution.py
@@ -41,7 +41,7 @@
     for at, masks in enumerate(rounds):
         sent = total.astype(jnp.bfloat16)
         if at == 0:
-            beside = {mask: blocks[mask] for mask in sorted(blocks, reverse=True) if mask > 3}
+            beside = {max(blocks): blocks[max(blocks)]}
         elif at == 1:
             early, beside = far, {mask: blocks[mask] for mask in blocks if mask not in far}
             sent, beside = lax.optimization_barrier((sent, beside))

time: 50.6 us -> 50.6 us (level)
  starting transfers between devices: 13.7 us -> 14.3 us
  waiting for transfers between devices: 12.1 us -> 11.5 us
    ppermute x9, waiting for transfers between devices: 7.46 us -> 6.82 us  [exchange(): lax.ppermute(x, 'hid', [(i, i ^ mask) for i in range(lax.axis_size('hid'))])]
    ppermute x9, starting transfers between devices: 9.25 us -> 9.88 us  [exchange(): lax.ppermute(x, 'hid', [(i, i ^ mask) for i in range(lax.axis_size('hid'))])]
  transfers between devices with their start and end apart: 12 -> 12, of which waited for: 6 -> 7; matrix products, arithmetic and copies ran while one was open for 10% -> 10% of each run, Pallas kernels for 0% -> 0%
where the time goes in v16:
time: 50.6 us; the launch traced here: 50.4 us
  blocking collectives  16 us (32%)
  starting transfers between devices  14.3 us (28%)
  waiting for transfers between devices  11.5 us (23%)
  matrix products  4.7 us (9%)
  local copies, waits for them, and re-layouts  1.54 us (3%)
  other arithmetic  1.33 us (3%)
  between operations  0.94 us (2%)
    all_to_all x1, blocking collectives, on_device(): rows = lax.all_to_all(both, 'hid', split_axis=1, concat_axis=0, tiled=True)  16 us
    ppermute x9, starting transfers between devices, exchange(): lax.ppermute(x, 'hid', [(i, i ^ mask) for i in range(lax.axis_size('hid'))])  9.88 us
    ppermute x9, waiting for transfers between devices, exchange(): lax.ppermute(x, 'hid', [(i, i ^ mask) for i in range(lax.axis_size('hid'))])  6.82 us
    all_to_all x1, waiting for transfers between devices, on_device(): lax.all_to_all(results, 'hid', split_axis=0, concat_axis=1, tiled=True)  4.67 us
    all_to_all x1, starting transfers between devices, on_device(): lax.all_to_all(results, 'hid', split_axis=0, concat_axis=1, tiled=True)  4.32 us
    dot_general x3, matrix products, inner_rows(): lax.dot_general(left, right, (((0,), (0,)), ((), ())), preferred_element_...  2.88 us
    dot_general x7, matrix products, dot(): return jnp.dot(left, right, preferred_element_type=jnp.float32)  1.1 us
  transfers between devices with their start and end apart: 12, of which 7 were waited for; matrix products, arithmetic and copies ran while one was open for 10% of the time, Pallas kernels for 0%

profile of v16, /device:TPU:0, one launch (start us, length us, event | category | flops | bytes accessed | tf_op | source)
XLA Modules:
  0.0 50.4 jit_solution(8805641979247425309)
XLA Ops:
  0.6 0.0 copy-start
  0.7 0.9 %pad_maximum_fusion.5 = bf16[6,16,512]{2,0,1:T(8,128)(2,1)S(1)} fusion(bf16[6,16,256]{2,0,1:T(8,128)(2,1)} %bitcast.32, bf16[6,16,256]{2,0,1:T(8,128)(2,1)} %bitcast.33), kind=kLoop, calls=%fused_computation.28 | loop fusion | flops 196608 | bytes 196608 | tf_op jit(solution)/shard_map/concatenate | solution.py:79
  1.6 0.0 copy-start.2
  1.6 16.0 %all_to_all.32 = bf16[6,16,512]{2,0,1:T(8,128)(2,1)S(1)} all-to-all(bf16[6,16,512]{2,0,1:T(8,128)(2,1)S(1)} %pad_maximum_fusion.5), channel_id=1, replica_groups=mesh['hid'=16,'seq'=2] {'hid'}, dimensions={1} | all-to-all | bytes 196608 | tf_op jit(solution)/shard_map/all_to_all | solution.py:82
  17.6 0.0 copy-start.1
  17.7 0.0 copy-done
  17.7 0.2 fusion.60
  17.9 0.0 copy-done.2
  17.9 0.2 fusion.62
  18.1 0.8 %collective-permute-start = (bf16[96,512]{1,0:T(8,128)(2,1)S(1)}, bf16[96,512]{1,0:T(8,128)(2,1)S(1)}, u32[]{:S(2)}, u32[]{:S(2)}) collective-permute-start(bf16[96,512]{1,0:T(8,128)(2,1)S(1)} %fusion.6), channel_id=1, source_target_pairs={{0,6},{2,4},{4,2},{6,0},{8,14},{10,12},{12,10},{14,8},{16,22},{18,... | collective-permute-start | bytes 294920 | tf_op jit(solution)/shard_map/ppermute | solution.py:10
  18.9 1.5 %collective-permute-start.1 = (bf16[96,512]{1,0:T(8,128)(2,1)S(1)}, bf16[96,512]{1,0:T(8,128)(2,1)S(1)}, u32[]{:S(2)}, u32[]{:S(2)}) collective-permute-start(bf16[96,512]{1,0:T(8,128)(2,1)S(1)} %fusion.6), channel_id=1, source_target_pairs={{0,2},{2,0},{4,6},{6,4},{8,10},{10,8},{12,14},{14,12},{16,18},{18,... | collective-permute-start | bytes 294920 | tf_op jit(solution)/shard_map/ppermute | solution.py:10
  20.4 1.3 %collective-permute-start.2 = (bf16[96,512]{1,0:T(8,128)(2,1)S(1)}, bf16[96,512]{1,0:T(8,128)(2,1)S(1)}, u32[]{:S(2)}, u32[]{:S(2)}) collective-permute-start(bf16[96,512]{1,0:T(8,128)(2,1)S(1)} %fusion.6), channel_id=1, source_target_pairs={{0,4},{2,6},{4,0},{6,2},{8,12},{10,14},{12,8},{14,10},{16,20},{18,... | collective-permute-start | bytes 294920 | tf_op jit(solution)/shard_map/ppermute | solution.py:10
  21.7 0.0 copy-done.1
  21.7 0.3 fusion.69
  22.1 1.0 %collective-permute-start.4 = (bf16[96,512]{1,0:T(8,128)(2,1)S(1)}, bf16[96,512]{1,0:T(8,128)(2,1)S(1)}, u32[]{:S(2)}, u32[]{:S(2)}) collective-permute-start(bf16[96,512]{1,0:T(8,128)(2,1)S(1)} %get-tuple-element.57), channel_id=1, source_target_pairs={{0,16},{2,18},{4,20},{6,22},{8,24},{10,26},{12,28},{14,30},{16,0},... | collective-permute-start | bytes 294920 | tf_op jit(solution)/shard_map/ppermute | solution.py:10
  23.1 0.6 %collective-permute-done = bf16[96,512]{1,0:T(8,128)(2,1)S(1)} collective-permute-done((bf16[96,512]{1,0:T(8,128)(2,1)S(1)}, bf16[96,512]{1,0:T(8,128)(2,1)S(1)}, u32[]{:S(2)}, u32[]{:S(2)}) %collective-permute-start) | collective-permute-done | bytes 98336 | tf_op jit(solution)/shard_map/ppermute | solution.py:10
  23.7 0.3 collective-permute-done.1
  24.0 1.0 %collective-permute-done.2 = bf16[96,512]{1,0:T(8,128)(2,1)S(1)} collective-permute-done((bf16[96,512]{1,0:T(8,128)(2,1)S(1)}, bf16[96,512]{1,0:T(8,128)(2,1)S(1)}, u32[]{:S(2)}, u32[]{:S(2)}) %collective-permute-start.2) | collective-permute-done | bytes 98336 | tf_op jit(solution)/shard_map/ppermute | solution.py:10
  25.0 0.8 %collective-permute-start.3 = (bf16[96,512]{1,0:T(8,128)(2,1)S(1)}, bf16[96,512]{1,0:T(8,128)(2,1)S(1)}, u32[]{:S(2)}, u32[]{:S(2)}) collective-permute-start(bf16[96,512]{1,0:T(8,128)(2,1)S(1)} %get-tuple-element.27), channel_id=1, source_target_pairs={{0,8},{2,10},{4,12},{6,14},{8,0},{10,2},{12,4},{14,6},{16,24},{18,... | collective-permute-start | bytes 294920 | tf_op jit(solution)/shard_map/ppermute | solution.py:10
  25.8 1.3 %collective-permute-start.7 = (bf16[96,512]{1,0:T(8,128)(2,1)S(1)}, bf16[96,512]{1,0:T(8,128)(2,1)S(1)}, u32[]{:S(2)}, u32[]{:S(2)}) collective-permute-start(bf16[96,512]{1,0:T(8,128)(2,1)S(1)} %get-tuple-element.32), channel_id=1, source_target_pairs={{0,8},{2,10},{4,12},{6,14},{8,0},{10,2},{12,4},{14,6},{16,24},{18,... | collective-permute-start | bytes 294920 | tf_op jit(solution)/shard_map/ppermute | solution.py:10
  27.1 1.3 %collective-permute-start.6 = (bf16[96,512]{1,0:T(8,128)(2,1)S(1)}, bf16[96,512]{1,0:T(8,128)(2,1)S(1)}, u32[]{:S(2)}, u32[]{:S(2)}) collective-permute-start(bf16[96,512]{1,0:T(8,128)(2,1)S(1)} %get-tuple-element.31), channel_id=1, source_target_pairs={{0,4},{2,6},{4,0},{6,2},{8,12},{10,14},{12,8},{14,10},{16,20},{18,... | collective-permute-start | bytes 294920 | tf_op jit(solution)/shard_map/ppermute | solution.py:10
  28.4 1.1 %collective-permute-start.5 = (bf16[96,512]{1,0:T(8,128)(2,1)S(1)}, bf16[96,512]{1,0:T(8,128)(2,1)S(1)}, u32[]{:S(2)}, u32[]{:S(2)}) collective-permute-start(bf16[96,512]{1,0:T(8,128)(2,1)S(1)} %get-tuple-element.30), channel_id=1, source_target_pairs={{0,2},{2,0},{4,6},{6,4},{8,10},{10,8},{12,14},{14,12},{16,18},{18,... | collective-permute-start | bytes 294920 | tf_op jit(solution)/shard_map/ppermute | solution.py:10
  29.5 0.0 collective-permute-done.4
  29.5 0.3 collective-permute-done.3
  29.8 0.9 %collective-permute-start.8 = (bf16[96,512]{1,0:T(8,128)(2,1)S(1)}, bf16[96,512]{1,0:T(8,128)(2,1)S(1)}, u32[]{:S(2)}, u32[]{:S(2)}) collective-permute-start(bf16[96,512]{1,0:T(8,128)(2,1)S(1)} %fusion.8), channel_id=1, source_target_pairs={{0,16},{2,18},{4,20},{6,22},{8,24},{10,26},{12,28},{14,30},{16,0},... | collective-permute-start | bytes 294920 | tf_op jit(solution)/shard_map/ppermute | solution.py:10
  30.7 0.1 fusion.9
  30.8 0.2 fusion.15
  31.0 2.0 %collective-permute-done.5 = bf16[96,512]{1,0:T(8,128)(2,1)S(1)} collective-permute-done((bf16[96,512]{1,0:T(8,128)(2,1)S(1)}, bf16[96,512]{1,0:T(8,128)(2,1)S(1)}, u32[]{:S(2)}, u32[]{:S(2)}) %collective-permute-start.5) | collective-permute-done | bytes 98336 | tf_op jit(solution)/shard_map/ppermute | solution.py:10
  33.1 0.0 collective-permute-done.6
  33.1 0.0 collective-permute-done.7
  33.2 0.1 collective-permute-start.10
  33.3 0.1 fusion.11
  33.5 0.2 convolution_add_fusion.2
  33.6 0.2 fusion.1
  33.8 2.6 %collective-permute-done.8 = bf16[96,512]{1,0:T(8,128)(2,1)S(1)} collective-permute-done((bf16[96,512]{1,0:T(8,128)(2,1)S(1)}, bf16[96,512]{1,0:T(8,128)(2,1)S(1)}, u32[]{:S(2)}, u32[]{:S(2)}) %collective-permute-start.8) | collective-permute-done | bytes 98336 | tf_op jit(solution)/shard_map/ppermute | solution.py:10
  36.5 0.2 fusion.2
  36.7 0.2 fusion.24
  36.9 0.7 %all_to_all.27 = bf16[16,6,512]{2,1,0:T(8,128)(2,1)} reshape(bf16[96,512]{1,0:T(8,128)(2,1)S(1)} %pad_maximum_fusion.6) | data formatting | bytes 196608 | tf_op jit(solution)/shard_map/all_to_all | solution.py:108
  37.6 4.3 %all-to-all-start.1 = ((bf16[16,6,512]{2,1,0:T(8,128)(2,1)}), bf16[16,6,512]{2,1,0:T(8,128)(2,1)S(1)}, u32[]{:S(2)}, u32[]{:S(2)}) async-start(bf16[16,6,512]{2,1,0:T(8,128)(2,1)} %all_to_all.27), calls=%async_computation.1 | async-start | bytes 262144 | tf_op jit(solution)/shard_map/all_to_all | solution.py:108
  42.0 0.1 collective-permute-start.9
  42.0 0.0 collective-permute-done.10
  42.2 1.1 %convolution_multiply_fusion = f32[640,256]{1,0:T(8,128)} fusion(bf16[96,640]{1,0:T(8,128)(2,1)S(1)} %constant_dynamic-update-slice_fusion.11, bf16[96,640]{1,0:T(8,128)(2,1)S(1)} %get-tuple-element.53, bf16[96,256]{1,0:T(8,128)(2,1)S(1)} %get-tuple-element.46, bf16[96,256]{1,0:T(8,128)(2,1)S(1)} %slice.176), kind=kOutput, calls=%fused_computation | convolution fusion | flops 63766528 | bytes 999424 | tf_op jit(solution)/shard_map/dot_general | solution.py:32
  43.3 0.0 collective-permute-done.9
  43.3 0.9 %convolution_multiply_fusion.1 = f32[128,256]{1,0:T(8,128)} fusion(bf16[96,256]{1,0:T(8,128)(2,1)S(1)} %get-tuple-element.46, bf16[96,256]{1,0:T(8,128)(2,1)S(1)} %slice.176, bf16[96,128]{1,0:T(8,128)(2,1)S(1)} %get-tuple-element.55, bf16[96,128]{1,0:T(8,128)(2,1)S(1)} %get-tuple-element.49), kind=kOutput, calls=%fused_computation.1 | convolution fusion | flops 12910592 | bytes 278528 | tf_op jit(solution)/shard_map/dot_general | solution.py:32
  44.2 0.9 %convolution_multiply_fusion.2 = f32[256,128]{1,0:T(8,128)} fusion(bf16[96,256]{1,0:T(8,128)(2,1)S(1)} %get-tuple-element.45, bf16[96,256]{1,0:T(8,128)(2,1)S(1)} %fusion.29, bf16[96,128]{1,0:T(8,128)(2,1)S(1)} %get-tuple-element.56, bf16[96,128]{1,0:T(8,128)(2,1)S(1)} %get-tuple-element.51), kind=kOutput, calls=%fused_computation.2 | convolution fusion | flops 12910592 | bytes 278528 | tf_op jit(solution)/shard_map/dot_general | solution.py:32
  45.1 4.7 %all-to-all-done.1 = bf16[16,6,512]{2,1,0:T(8,128)(2,1)S(1)} async-done(((bf16[16,6,512]{2,1,0:T(8,128)(2,1)}), bf16[16,6,512]{2,1,0:T(8,128)(2,1)S(1)}, u32[]{:S(2)}, u32[]{:S(2)}) %all-to-all-start.1) | async-done | bytes 98336 | tf_op jit(solution)/shard_map/all_to_all | solution.py:108
  49.7 0.7 %fusion.67 = (bf16[6,16,256]{2,0,1:T(8,128)(2,1)}, bf16[6,16,256]{2,0,1:T(8,128)(2,1)}) fusion(bf16[6,16,512]{2,0,1:T(8,128)(2,1)S(1)} %bitcast.31), kind=kLoop, calls=%fused_computation.110 | loop fusion | bytes 196608 | tf_op jit(solution)/shard_map/slice | solution.py:111
  (29 shorter events, 0.6 us)
Async XLA Ops:
  0.6 17.1 %copy-start = (bf16[256,256]{1,0:T(8,128)(2,1)S(1)}, bf16[256,256]{1,0:T(8,128)(2,1)}, u32[]{:S(2)}) copy-start(bf16[256,256]{1,0:T(8,128)(2,1)} %param.8) | copy-start | bytes 393220
  1.6 16.3 %copy-start.2 = (bf16[256,256]{1,0:T(8,128)(2,1)S(1)}, bf16[256,256]{1,0:T(8,128)(2,1)}, u32[]{:S(2)}) copy-start(bf16[256,256]{1,0:T(8,128)(2,1)} %param.7) | copy-start | bytes 393220
  17.6 4.0 %copy-start.1 = (bf16[1,5,256,256]{3,2,1,0:T(8,128)(2,1)S(1)}, bf16[1,5,256,256]{3,2,1,0:T(8,128)(2,1)}, u32[]{:S(2)}) copy-start(bf16[1,5,256,256]{3,2,1,0:T(8,128)(2,1)} %param.6) | copy-start | bytes 1966084
  18.1 5.6 %collective-permute-start = (bf16[96,512]{1,0:T(8,128)(2,1)S(1)}, bf16[96,512]{1,0:T(8,128)(2,1)S(1)}, u32[]{:S(2)}, u32[]{:S(2)}) collective-permute-start(bf16[96,512]{1,0:T(8,128)(2,1)S(1)} %fusion.6), channel_id=1, source_target_pairs={{0,6},{2,4},{4,2},{6,0},{8,14},{10,12},{12,10},{14,8},{16,22},{18,... | collective-permute-start | bytes 294920 | tf_op jit(solution)/shard_map/ppermute | solution.py:10
  18.9 5.1 %collective-permute-start.1 = (bf16[96,512]{1,0:T(8,128)(2,1)S(1)}, bf16[96,512]{1,0:T(8,128)(2,1)S(1)}, u32[]{:S(2)}, u32[]{:S(2)}) collective-permute-start(bf16[96,512]{1,0:T(8,128)(2,1)S(1)} %fusion.6), channel_id=1, source_target_pairs={{0,2},{2,0},{4,6},{6,4},{8,10},{10,8},{12,14},{14,12},{16,18},{18,... | collective-permute-start | bytes 294920 | tf_op jit(solution)/shard_map/ppermute | solution.py:10
  20.4 4.6 %collective-permute-start.2 = (bf16[96,512]{1,0:T(8,128)(2,1)S(1)}, bf16[96,512]{1,0:T(8,128)(2,1)S(1)}, u32[]{:S(2)}, u32[]{:S(2)}) collective-permute-start(bf16[96,512]{1,0:T(8,128)(2,1)S(1)} %fusion.6), channel_id=1, source_target_pairs={{0,4},{2,6},{4,0},{6,2},{8,12},{10,14},{12,8},{14,10},{16,20},{18,... | collective-permute-start | bytes 294920 | tf_op jit(solution)/shard_map/ppermute | solution.py:10
  22.1 7.4 %collective-permute-start.4 = (bf16[96,512]{1,0:T(8,128)(2,1)S(1)}, bf16[96,512]{1,0:T(8,128)(2,1)S(1)}, u32[]{:S(2)}, u32[]{:S(2)}) collective-permute-start(bf16[96,512]{1,0:T(8,128)(2,1)S(1)} %get-tuple-element.57), channel_id=1, source_target_pairs={{0,16},{2,18},{4,20},{6,22},{8,24},{10,26},{12,28},{14,30},{16,0},... | collective-permute-start | bytes 294920 | tf_op jit(solution)/shard_map/ppermute | solution.py:10
  25.0 4.8 %collective-permute-start.3 = (bf16[96,512]{1,0:T(8,128)(2,1)S(1)}, bf16[96,512]{1,0:T(8,128)(2,1)S(1)}, u32[]{:S(2)}, u32[]{:S(2)}) collective-permute-start(bf16[96,512]{1,0:T(8,128)(2,1)S(1)} %get-tuple-element.27), channel_id=1, source_target_pairs={{0,8},{2,10},{4,12},{6,14},{8,0},{10,2},{12,4},{14,6},{16,24},{18,... | collective-permute-start | bytes 294920 | tf_op jit(solution)/shard_map/ppermute | solution.py:10
  25.8 7.3 %collective-permute-start.7 = (bf16[96,512]{1,0:T(8,128)(2,1)S(1)}, bf16[96,512]{1,0:T(8,128)(2,1)S(1)}, u32[]{:S(2)}, u32[]{:S(2)}) collective-permute-start(bf16[96,512]{1,0:T(8,128)(2,1)S(1)} %get-tuple-element.32), channel_id=1, source_target_pairs={{0,8},{2,10},{4,12},{6,14},{8,0},{10,2},{12,4},{14,6},{16,24},{18,... | collective-permute-start | bytes 294920 | tf_op jit(solution)/shard_map/ppermute | solution.py:10
  27.1 5.9 %collective-permute-start.6 = (bf16[96,512]{1,0:T(8,128)(2,1)S(1)}, bf16[96,512]{1,0:T(8,128)(2,1)S(1)}, u32[]{:S(2)}, u32[]{:S(2)}) collective-permute-start(bf16[96,512]{1,0:T(8,128)(2,1)S(1)} %get-tuple-element.31), channel_id=1, source_target_pairs={{0,4},{2,6},{4,0},{6,2},{8,12},{10,14},{12,8},{14,10},{16,20},{18,... | collective-permute-start | bytes 294920 | tf_op jit(solution)/shard_map/ppermute | solution.py:10
  28.4 4.6 %collective-permute-start.5 = (bf16[96,512]{1,0:T(8,128)(2,1)S(1)}, bf16[96,512]{1,0:T(8,128)(2,1)S(1)}, u32[]{:S(2)}, u32[]{:S(2)}) collective-permute-start(bf16[96,512]{1,0:T(8,128)(2,1)S(1)} %get-tuple-element.30), channel_id=1, source_target_pairs={{0,2},{2,0},{4,6},{6,4},{8,10},{10,8},{12,14},{14,12},{16,18},{18,... | collective-permute-start | bytes 294920 | tf_op jit(solution)/shard_map/ppermute | solution.py:10
  29.8 6.6 %collective-permute-start.8 = (bf16[96,512]{1,0:T(8,128)(2,1)S(1)}, bf16[96,512]{1,0:T(8,128)(2,1)S(1)}, u32[]{:S(2)}, u32[]{:S(2)}) collective-permute-start(bf16[96,512]{1,0:T(8,128)(2,1)S(1)} %fusion.8), channel_id=1, source_target_pairs={{0,16},{2,18},{4,20},{6,22},{8,24},{10,26},{12,28},{14,30},{16,0},... | collective-permute-start | bytes 294920 | tf_op jit(solution)/shard_map/ppermute | solution.py:10
  33.2 8.8 %collective-permute-start.10 = (bf16[96,1024]{1,0:T(8,128)(2,1)S(1)}, bf16[96,1024]{1,0:T(8,128)(2,1)S(1)}, u32[]{:S(2)}, u32[]{:S(2)}) collective-permute-start(bf16[96,1024]{1,0:T(8,128)(2,1)S(1)} %constant_dynamic-update-slice_fusion.5), channel_id=1, source_target_pairs={{0,1},{1,0},{2,3},{3,2},{4,5},{5,4},{6,7},{7,6},{8,9},{9,8},{10,11... | collective-permute-start | bytes 589832 | tf_op jit(solution)/shard_map/ppermute | solution.py:14
  37.6 12.1 %all-to-all-start.1 = ((bf16[16,6,512]{2,1,0:T(8,128)(2,1)}), bf16[16,6,512]{2,1,0:T(8,128)(2,1)S(1)}, u32[]{:S(2)}, u32[]{:S(2)}) async-start(bf16[16,6,512]{2,1,0:T(8,128)(2,1)} %all_to_all.27), calls=%async_computation.1 | async-start | bytes 262144 | tf_op jit(solution)/shard_map/all_to_all | solution.py:108
  42.0 1.4 %collective-permute-start.9 = (bf16[96,256]{1,0:T(8,128)(2,1)S(1)}, bf16[96,256]{1,0:T(8,128)(2,1)S(1)}, u32[]{:S(2)}, u32[]{:S(2)}) collective-permute-start(bf16[96,256]{1,0:T(8,128)(2,1)S(1)} %pad_maximum_fusion.10), channel_id=1, source_target_pairs={{0,1},{1,0},{2,3},{3,2},{4,5},{5,4},{6,7},{7,6},{8,9},{9,8},{10,11... | collective-permute-start | bytes 147464 | tf_op jit(solution)/shard_map/ppermute | solution.py:14

commit v17 on v16

--- a/solution.py
+++ b/solution.py
@@ -36,7 +36,7 @@
 
 def sum_over_hid(part, blocks, data):
     bits = (lax.axis_size("hid") - 1).bit_length()
-    rounds = [(3, 1, 2)] + [(1 << bit,) for bit in range(2, bits)]
+    rounds = [(5, 1, 4), (10, 8, 2)] + [(1 << bit,) for bit in range(4, bits)]
     total, far = part, {}
     for at, masks in enumerate(rounds):
         sent = total.astype(jnp.bfloat16)

time: 50.6 us -> 57.3 us (1.13)
  waiting for transfers between devices: 11.5 us -> 17.1 us
  starting transfers between devices: 14.3 us -> 15.4 us
    ppermute x9 -> x10, waiting for transfers between devices: 6.82 us -> 10.1 us  [exchange(): lax.ppermute(x, 'hid', [(i, i ^ mask) for i in range(lax.axis_size('hid'))])]
    all_to_all x1, waiting for transfers between devices: 4.67 us -> 6.93 us  [on_device(): lax.all_to_all(results, 'hid', split_axis=0, concat_axis=1, tiled=True)]
    ppermute x9 -> x10, starting transfers between devices: 9.88 us -> 11.3 us  [exchange(): lax.ppermute(x, 'hid', [(i, i ^ mask) for i in range(lax.axis_size('hid'))])]
    all_to_all x1, starting transfers between devices: 4.32 us -> 3.51 us  [on_device(): lax.all_to_all(results, 'hid', split_axis=0, concat_axis=1, tiled=True)]
  transfers between devices with their start and end apart: 12 -> 13, of which waited for: 7 -> 8; matrix products, arithmetic and copies ran while one was open for 10% -> 6% of each run, Pallas kernels for 0% -> 0%
where the time goes in v17:
time: 57.3 us; the launch traced here: 57.1 us
  waiting for transfers between devices  17.1 us (30%)
  blocking collectives  16 us (28%)
  starting transfers between devices  15.4 us (27%)
  matrix products  4.67 us (8%)
  local copies, waits for them, and re-layouts  1.55 us (3%)
  other arithmetic  1.37 us (2%)
  between operations  0.92 us (2%)
    all_to_all x1, blocking collectives, on_device(): rows = lax.all_to_all(both, 'hid', split_axis=1, concat_axis=0, tiled=True)  16 us
    ppermute x10, starting transfers between devices, exchange(): lax.ppermute(x, 'hid', [(i, i ^ mask) for i in range(lax.axis_size('hid'))])  11.3 us
    ppermute x10, waiting for transfers between devices, exchange(): lax.ppermute(x, 'hid', [(i, i ^ mask) for i in range(lax.axis_size('hid'))])  10.1 us
    all_to_all x1, waiting for transfers between devices, on_device(): lax.all_to_all(results, 'hid', split_axis=0, concat_axis=1, tiled=True)  6.93 us
    all_to_all x1, starting transfers between devices, on_device(): lax.all_to_all(results, 'hid', split_axis=0, concat_axis=1, tiled=True)  3.51 us
    dot_general x3, matrix products, inner_rows(): lax.dot_general(left, right, (((0,), (0,)), ((), ())), preferred_element_...  2.88 us
  transfers between devices with their start and end apart: 13, of which 8 were waited for; matrix products, arithmetic and copies ran while one was open for 6% of the time, Pallas kernels for 0%

profile of v17, /device:TPU:0, one launch (start us, length us, event | category | flops | bytes accessed | tf_op | source)
XLA Modules:
  0.0 57.1 jit_solution(6700171801615058205)
XLA Ops:
  0.6 0.0 copy-start
  0.7 0.9 %pad_maximum_fusion.5 = bf16[6,16,512]{2,0,1:T(8,128)(2,1)S(1)} fusion(bf16[6,16,256]{2,0,1:T(8,128)(2,1)} %bitcast.32, bf16[6,16,256]{2,0,1:T(8,128)(2,1)} %bitcast.33), kind=kLoop, calls=%fused_computation.26 | loop fusion | flops 196608 | bytes 196608 | tf_op jit(solution)/shard_map/concatenate | solution.py:79
  1.6 0.0 copy-start.2
  1.6 16.0 %all_to_all.32 = bf16[6,16,512]{2,0,1:T(8,128)(2,1)S(1)} all-to-all(bf16[6,16,512]{2,0,1:T(8,128)(2,1)S(1)} %pad_maximum_fusion.5), channel_id=1, replica_groups=mesh['hid'=16,'seq'=2] {'hid'}, dimensions={1} | all-to-all | bytes 196608 | tf_op jit(solution)/shard_map/all_to_all | solution.py:82
  17.6 0.0 copy-start.1
  17.7 0.0 copy-done
  17.7 0.2 fusion.59
  17.9 0.0 copy-done.2
  17.9 0.2 fusion.62
  18.1 0.8 %collective-permute-start = (bf16[96,512]{1,0:T(8,128)(2,1)S(1)}, bf16[96,512]{1,0:T(8,128)(2,1)S(1)}, u32[]{:S(2)}, u32[]{:S(2)}) collective-permute-start(bf16[96,512]{1,0:T(8,128)(2,1)S(1)} %fusion.6), channel_id=1, source_target_pairs={{0,10},{2,8},{4,14},{6,12},{8,2},{10,0},{12,6},{14,4},{16,26},{18,... | collective-permute-start | bytes 294920 | tf_op jit(solution)/shard_map/ppermute | solution.py:10
  18.9 1.5 %collective-permute-start.1 = (bf16[96,512]{1,0:T(8,128)(2,1)S(1)}, bf16[96,512]{1,0:T(8,128)(2,1)S(1)}, u32[]{:S(2)}, u32[]{:S(2)}) collective-permute-start(bf16[96,512]{1,0:T(8,128)(2,1)S(1)} %fusion.6), channel_id=1, source_target_pairs={{0,2},{2,0},{4,6},{6,4},{8,10},{10,8},{12,14},{14,12},{16,18},{18,... | collective-permute-start | bytes 294920 | tf_op jit(solution)/shard_map/ppermute | solution.py:10
  20.4 1.3 %collective-permute-start.2 = (bf16[96,512]{1,0:T(8,128)(2,1)S(1)}, bf16[96,512]{1,0:T(8,128)(2,1)S(1)}, u32[]{:S(2)}, u32[]{:S(2)}) collective-permute-start(bf16[96,512]{1,0:T(8,128)(2,1)S(1)} %fusion.6), channel_id=1, source_target_pairs={{0,8},{2,10},{4,12},{6,14},{8,0},{10,2},{12,4},{14,6},{16,24},{18,... | collective-permute-start | bytes 294920 | tf_op jit(solution)/shard_map/ppermute | solution.py:10
  21.7 0.0 copy-done.1
  21.7 0.3 fusion.68
  22.1 1.0 %collective-permute-start.9 = (bf16[96,512]{1,0:T(8,128)(2,1)S(1)}, bf16[96,512]{1,0:T(8,128)(2,1)S(1)}, u32[]{:S(2)}, u32[]{:S(2)}) collective-permute-start(bf16[96,512]{1,0:T(8,128)(2,1)S(1)} %get-tuple-element.59), channel_id=1, source_target_pairs={{0,16},{2,18},{4,20},{6,22},{8,24},{10,26},{12,28},{14,30},{16,0},... | collective-permute-start | bytes 294920 | tf_op jit(solution)/shard_map/ppermute | solution.py:10
  23.1 0.7 %collective-permute-done = bf16[96,512]{1,0:T(8,128)(2,1)S(1)} collective-permute-done((bf16[96,512]{1,0:T(8,128)(2,1)S(1)}, bf16[96,512]{1,0:T(8,128)(2,1)S(1)}, u32[]{:S(2)}, u32[]{:S(2)}) %collective-permute-start) | collective-permute-done | bytes 98336 | tf_op jit(solution)/shard_map/ppermute | solution.py:10
  23.8 0.8 %collective-permute-done.1 = bf16[96,512]{1,0:T(8,128)(2,1)S(1)} collective-permute-done((bf16[96,512]{1,0:T(8,128)(2,1)S(1)}, bf16[96,512]{1,0:T(8,128)(2,1)S(1)}, u32[]{:S(2)}, u32[]{:S(2)}) %collective-permute-start.1) | collective-permute-done | bytes 98336 | tf_op jit(solution)/shard_map/ppermute | solution.py:10
  24.6 1.1 %collective-permute-done.2 = bf16[96,512]{1,0:T(8,128)(2,1)S(1)} collective-permute-done((bf16[96,512]{1,0:T(8,128)(2,1)S(1)}, bf16[96,512]{1,0:T(8,128)(2,1)S(1)}, u32[]{:S(2)}, u32[]{:S(2)}) %collective-permute-start.2) | collective-permute-done | bytes 98336 | tf_op jit(solution)/shard_map/ppermute | solution.py:10
  25.7 0.9 %collective-permute-start.6 = (bf16[96,512]{1,0:T(8,128)(2,1)S(1)}, bf16[96,512]{1,0:T(8,128)(2,1)S(1)}, u32[]{:S(2)}, u32[]{:S(2)}) collective-permute-start(bf16[96,512]{1,0:T(8,128)(2,1)S(1)} %fusion.61), channel_id=1, source_target_pairs={{0,20},{2,22},{4,16},{6,18},{8,28},{10,30},{12,24},{14,26},{16,4},... | collective-permute-start | bytes 294920 | tf_op jit(solution)/shard_map/ppermute | solution.py:10
  26.6 2.4 %collective-permute-start.7 = (bf16[96,512]{1,0:T(8,128)(2,1)S(1)}, bf16[96,512]{1,0:T(8,128)(2,1)S(1)}, u32[]{:S(2)}, u32[]{:S(2)}) collective-permute-start(bf16[96,512]{1,0:T(8,128)(2,1)S(1)} %fusion.61), channel_id=1, source_target_pairs={{0,16},{2,18},{4,20},{6,22},{8,24},{10,26},{12,28},{14,30},{16,0},... | collective-permute-start | bytes 294920 | tf_op jit(solution)/shard_map/ppermute | solution.py:10
  29.0 1.2 %collective-permute-start.8 = (bf16[96,512]{1,0:T(8,128)(2,1)S(1)}, bf16[96,512]{1,0:T(8,128)(2,1)S(1)}, u32[]{:S(2)}, u32[]{:S(2)}) collective-permute-start(bf16[96,512]{1,0:T(8,128)(2,1)S(1)} %fusion.61), channel_id=1, source_target_pairs={{0,4},{2,6},{4,0},{6,2},{8,12},{10,14},{12,8},{14,10},{16,20},{18,... | collective-permute-start | bytes 294920 | tf_op jit(solution)/shard_map/ppermute | solution.py:10
  30.2 0.9 %collective-permute-start.5 = (bf16[96,512]{1,0:T(8,128)(2,1)S(1)}, bf16[96,512]{1,0:T(8,128)(2,1)S(1)}, u32[]{:S(2)}, u32[]{:S(2)}) collective-permute-start(bf16[96,512]{1,0:T(8,128)(2,1)S(1)} %get-tuple-element.33), channel_id=1, source_target_pairs={{0,8},{2,10},{4,12},{6,14},{8,0},{10,2},{12,4},{14,6},{16,24},{18,... | collective-permute-start | bytes 294920 | tf_op jit(solution)/shard_map/ppermute | solution.py:10
  31.0 0.1 fusion.14
  31.2 2.8 %collective-permute-done.9 = bf16[96,512]{1,0:T(8,128)(2,1)S(1)} collective-permute-done((bf16[96,512]{1,0:T(8,128)(2,1)S(1)}, bf16[96,512]{1,0:T(8,128)(2,1)S(1)}, u32[]{:S(2)}, u32[]{:S(2)}) %collective-permute-start.9) | collective-permute-done | bytes 98336 | tf_op jit(solution)/shard_map/ppermute | solution.py:10
  34.0 0.7 %collective-permute-start.4 = (bf16[96,512]{1,0:T(8,128)(2,1)S(1)}, bf16[96,512]{1,0:T(8,128)(2,1)S(1)}, u32[]{:S(2)}, u32[]{:S(2)}) collective-permute-start(bf16[96,512]{1,0:T(8,128)(2,1)S(1)} %get-tuple-element.32), channel_id=1, source_target_pairs={{0,4},{2,6},{4,0},{6,2},{8,12},{10,14},{12,8},{14,10},{16,20},{18,... | collective-permute-start | bytes 294920 | tf_op jit(solution)/shard_map/ppermute | solution.py:10
  34.7 1.3 %collective-permute-done.6 = bf16[96,512]{1,0:T(8,128)(2,1)S(1)} collective-permute-done((bf16[96,512]{1,0:T(8,128)(2,1)S(1)}, bf16[96,512]{1,0:T(8,128)(2,1)S(1)}, u32[]{:S(2)}, u32[]{:S(2)}) %collective-permute-start.6) | collective-permute-done | bytes 98336 | tf_op jit(solution)/shard_map/ppermute | solution.py:10
  36.0 0.8 %collective-permute-start.3 = (bf16[96,512]{1,0:T(8,128)(2,1)S(1)}, bf16[96,512]{1,0:T(8,128)(2,1)S(1)}, u32[]{:S(2)}, u32[]{:S(2)}) collective-permute-start(bf16[96,512]{1,0:T(8,128)(2,1)S(1)} %get-tuple-element.31), channel_id=1, source_target_pairs={{0,2},{2,0},{4,6},{6,4},{8,10},{10,8},{12,14},{14,12},{16,18},{18,... | collective-permute-start | bytes 294920 | tf_op jit(solution)/shard_map/ppermute | solution.py:10
  36.8 0.0 collective-permute-done.7
  36.8 0.0 collective-permute-done.8
  36.8 0.1 add_convert_fusion
  36.9 0.1 fusion.8
  37.0 0.6 %collective-permute-done.5 = bf16[96,512]{1,0:T(8,128)(2,1)S(1)} collective-permute-done((bf16[96,512]{1,0:T(8,128)(2,1)S(1)}, bf16[96,512]{1,0:T(8,128)(2,1)S(1)}, u32[]{:S(2)}, u32[]{:S(2)}) %collective-permute-start.5) | collective-permute-done | bytes 98336 | tf_op jit(solution)/shard_map/ppermute | solution.py:10
  37.6 0.1 fusion.10
  37.8 2.9 %collective-permute-done.3 = bf16[96,512]{1,0:T(8,128)(2,1)S(1)} collective-permute-done((bf16[96,512]{1,0:T(8,128)(2,1)S(1)}, bf16[96,512]{1,0:T(8,128)(2,1)S(1)}, u32[]{:S(2)}, u32[]{:S(2)}) %collective-permute-start.3) | collective-permute-done | bytes 98336 | tf_op jit(solution)/shard_map/ppermute | solution.py:10
  40.6 0.2 convolution_add_fusion.2
  40.8 0.0 collective-permute-done.4
  40.8 0.2 fusion.1
  41.0 0.2 fusion.2
  41.2 0.2 fusion.23
  41.4 0.7 %all_to_all.27 = bf16[16,6,512]{2,1,0:T(8,128)(2,1)} reshape(bf16[96,512]{1,0:T(8,128)(2,1)S(1)} %pad_maximum_fusion.6) | data formatting | bytes 196608 | tf_op jit(solution)/shard_map/all_to_all | solution.py:108
  42.1 3.5 %all-to-all-start.1 = ((bf16[16,6,512]{2,1,0:T(8,128)(2,1)}), bf16[16,6,512]{2,1,0:T(8,128)(2,1)S(1)}, u32[]{:S(2)}, u32[]{:S(2)}) async-start(bf16[16,6,512]{2,1,0:T(8,128)(2,1)} %all_to_all.27), calls=%async_computation.1 | async-start | bytes 262144 | tf_op jit(solution)/shard_map/all_to_all | solution.py:108
  45.7 0.1 collective-permute-start.10
  45.9 0.6 collective-permute-start.11
  46.5 6.9 %all-to-all-done.1 = bf16[16,6,512]{2,1,0:T(8,128)(2,1)S(1)} async-done(((bf16[16,6,512]{2,1,0:T(8,128)(2,1)}), bf16[16,6,512]{2,1,0:T(8,128)(2,1)S(1)}, u32[]{:S(2)}, u32[]{:S(2)}) %all-to-all-start.1) | async-done | bytes 98336 | tf_op jit(solution)/shard_map/all_to_all | solution.py:108
  53.4 0.7 %fusion.66 = (bf16[6,16,256]{2,0,1:T(8,128)(2,1)}, bf16[6,16,256]{2,0,1:T(8,128)(2,1)}) fusion(bf16[6,16,512]{2,0,1:T(8,128)(2,1)S(1)} %bitcast.31), kind=kLoop, calls=%fused_computation.108 | loop fusion | bytes 196608 | tf_op jit(solution)/shard_map/slice | solution.py:111
  54.1 0.0 collective-permute-done.11
  54.2 1.1 %convolution_multiply_fusion = f32[640,256]{1,0:T(8,128)} fusion(bf16[96,640]{1,0:T(8,128)(2,1)S(1)} %constant_dynamic-update-slice_fusion.11, bf16[96,640]{1,0:T(8,128)(2,1)S(1)} %get-tuple-element.55, bf16[96,256]{1,0:T(8,128)(2,1)S(1)} %get-tuple-element.48, bf16[96,256]{1,0:T(8,128)(2,1)S(1)} %slice.176), kind=kOutput, calls=%fused_computation | convolution fusion | flops 63766528 | bytes 999424 | tf_op jit(solution)/shard_map/dot_general | solution.py:32
  55.3 0.0 collective-permute-done.10
  55.3 0.9 %convolution_multiply_fusion.1 = f32[128,256]{1,0:T(8,128)} fusion(bf16[96,256]{1,0:T(8,128)(2,1)S(1)} %get-tuple-element.48, bf16[96,256]{1,0:T(8,128)(2,1)S(1)} %slice.176, bf16[96,128]{1,0:T(8,128)(2,1)S(1)} %get-tuple-element.57, bf16[96,128]{1,0:T(8,128)(2,1)S(1)} %get-tuple-element.51), kind=kOutput, calls=%fused_computation.1 | convolution fusion | flops 12910592 | bytes 278528 | tf_op jit(solution)/shard_map/dot_general | solution.py:32
  56.2 0.9 %convolution_multiply_fusion.2 = f32[256,128]{1,0:T(8,128)} fusion(bf16[96,256]{1,0:T(8,128)(2,1)S(1)} %get-tuple-element.47, bf16[96,256]{1,0:T(8,128)(2,1)S(1)} %fusion.28, bf16[96,128]{1,0:T(8,128)(2,1)S(1)} %get-tuple-element.58, bf16[96,128]{1,0:T(8,128)(2,1)S(1)} %get-tuple-element.53), kind=kOutput, calls=%fused_computation.2 | convolution fusion | flops 12910592 | bytes 278528 | tf_op jit(solution)/shard_map/dot_general | solution.py:32
  (27 shorter events, 0.5 us)
Async XLA Ops:
  0.6 17.1 %copy-start = (bf16[256,256]{1,0:T(8,128)(2,1)S(1)}, bf16[256,256]{1,0:T(8,128)(2,1)}, u32[]{:S(2)}) copy-start(bf16[256,256]{1,0:T(8,128)(2,1)} %param.8) | copy-start | bytes 393220
  1.6 16.3 %copy-start.2 = (bf16[256,256]{1,0:T(8,128)(2,1)S(1)}, bf16[256,256]{1,0:T(8,128)(2,1)}, u32[]{:S(2)}) copy-start(bf16[256,256]{1,0:T(8,128)(2,1)} %param.7) | copy-start | bytes 393220
  17.6 4.1 %copy-start.1 = (bf16[1,5,256,256]{3,2,1,0:T(8,128)(2,1)S(1)}, bf16[1,5,256,256]{3,2,1,0:T(8,128)(2,1)}, u32[]{:S(2)}) copy-start(bf16[1,5,256,256]{3,2,1,0:T(8,128)(2,1)} %param.6) | copy-start | bytes 1966084
  18.1 5.7 %collective-permute-start = (bf16[96,512]{1,0:T(8,128)(2,1)S(1)}, bf16[96,512]{1,0:T(8,128)(2,1)S(1)}, u32[]{:S(2)}, u32[]{:S(2)}) collective-permute-start(bf16[96,512]{1,0:T(8,128)(2,1)S(1)} %fusion.6), channel_id=1, source_target_pairs={{0,10},{2,8},{4,14},{6,12},{8,2},{10,0},{12,6},{14,4},{16,26},{18,... | collective-permute-start | bytes 294920 | tf_op jit(solution)/shard_map/ppermute | solution.py:10
  18.9 5.7 %collective-permute-start.1 = (bf16[96,512]{1,0:T(8,128)(2,1)S(1)}, bf16[96,512]{1,0:T(8,128)(2,1)S(1)}, u32[]{:S(2)}, u32[]{:S(2)}) collective-permute-start(bf16[96,512]{1,0:T(8,128)(2,1)S(1)} %fusion.6), channel_id=1, source_target_pairs={{0,2},{2,0},{4,6},{6,4},{8,10},{10,8},{12,14},{14,12},{16,18},{18,... | collective-permute-start | bytes 294920 | tf_op jit(solution)/shard_map/ppermute | solution.py:10
  20.4 5.3 %collective-permute-start.2 = (bf16[96,512]{1,0:T(8,128)(2,1)S(1)}, bf16[96,512]{1,0:T(8,128)(2,1)S(1)}, u32[]{:S(2)}, u32[]{:S(2)}) collective-permute-start(bf16[96,512]{1,0:T(8,128)(2,1)S(1)} %fusion.6), channel_id=1, source_target_pairs={{0,8},{2,10},{4,12},{6,14},{8,0},{10,2},{12,4},{14,6},{16,24},{18,... | collective-permute-start | bytes 294920 | tf_op jit(solution)/shard_map/ppermute | solution.py:10
  22.1 11.9 %collective-permute-start.9 = (bf16[96,512]{1,0:T(8,128)(2,1)S(1)}, bf16[96,512]{1,0:T(8,128)(2,1)S(1)}, u32[]{:S(2)}, u32[]{:S(2)}) collective-permute-start(bf16[96,512]{1,0:T(8,128)(2,1)S(1)} %get-tuple-element.59), channel_id=1, source_target_pairs={{0,16},{2,18},{4,20},{6,22},{8,24},{10,26},{12,28},{14,30},{16,0},... | collective-permute-start | bytes 294920 | tf_op jit(solution)/shard_map/ppermute | solution.py:10
  25.7 10.3 %collective-permute-start.6 = (bf16[96,512]{1,0:T(8,128)(2,1)S(1)}, bf16[96,512]{1,0:T(8,128)(2,1)S(1)}, u32[]{:S(2)}, u32[]{:S(2)}) collective-permute-start(bf16[96,512]{1,0:T(8,128)(2,1)S(1)} %fusion.61), channel_id=1, source_target_pairs={{0,20},{2,22},{4,16},{6,18},{8,28},{10,30},{12,24},{14,26},{16,4},... | collective-permute-start | bytes 294920 | tf_op jit(solution)/shard_map/ppermute | solution.py:10
  26.6 10.2 %collective-permute-start.7 = (bf16[96,512]{1,0:T(8,128)(2,1)S(1)}, bf16[96,512]{1,0:T(8,128)(2,1)S(1)}, u32[]{:S(2)}, u32[]{:S(2)}) collective-permute-start(bf16[96,512]{1,0:T(8,128)(2,1)S(1)} %fusion.61), channel_id=1, source_target_pairs={{0,16},{2,18},{4,20},{6,22},{8,24},{10,26},{12,28},{14,30},{16,0},... | collective-permute-start | bytes 294920 | tf_op jit(solution)/shard_map/ppermute | solution.py:10
  29.0 7.8 %collective-permute-start.8 = (bf16[96,512]{1,0:T(8,128)(2,1)S(1)}, bf16[96,512]{1,0:T(8,128)(2,1)S(1)}, u32[]{:S(2)}, u32[]{:S(2)}) collective-permute-start(bf16[96,512]{1,0:T(8,128)(2,1)S(1)} %fusion.61), channel_id=1, source_target_pairs={{0,4},{2,6},{4,0},{6,2},{8,12},{10,14},{12,8},{14,10},{16,20},{18,... | collective-permute-start | bytes 294920 | tf_op jit(solution)/shard_map/ppermute | solution.py:10
  30.2 7.4 %collective-permute-start.5 = (bf16[96,512]{1,0:T(8,128)(2,1)S(1)}, bf16[96,512]{1,0:T(8,128)(2,1)S(1)}, u32[]{:S(2)}, u32[]{:S(2)}) collective-permute-start(bf16[96,512]{1,0:T(8,128)(2,1)S(1)} %get-tuple-element.33), channel_id=1, source_target_pairs={{0,8},{2,10},{4,12},{6,14},{8,0},{10,2},{12,4},{14,6},{16,24},{18,... | collective-permute-start | bytes 294920 | tf_op jit(solution)/shard_map/ppermute | solution.py:10
  34.0 6.8 %collective-permute-start.4 = (bf16[96,512]{1,0:T(8,128)(2,1)S(1)}, bf16[96,512]{1,0:T(8,128)(2,1)S(1)}, u32[]{:S(2)}, u32[]{:S(2)}) collective-permute-start(bf16[96,512]{1,0:T(8,128)(2,1)S(1)} %get-tuple-element.32), channel_id=1, source_target_pairs={{0,4},{2,6},{4,0},{6,2},{8,12},{10,14},{12,8},{14,10},{16,20},{18,... | collective-permute-start | bytes 294920 | tf_op jit(solution)/shard_map/ppermute | solution.py:10
  36.0 4.6 %collective-permute-start.3 = (bf16[96,512]{1,0:T(8,128)(2,1)S(1)}, bf16[96,512]{1,0:T(8,128)(2,1)S(1)}, u32[]{:S(2)}, u32[]{:S(2)}) collective-permute-start(bf16[96,512]{1,0:T(8,128)(2,1)S(1)} %get-tuple-element.31), channel_id=1, source_target_pairs={{0,2},{2,0},{4,6},{6,4},{8,10},{10,8},{12,14},{14,12},{16,18},{18,... | collective-permute-start | bytes 294920 | tf_op jit(solution)/shard_map/ppermute | solution.py:10
  42.1 11.3 %all-to-all-start.1 = ((bf16[16,6,512]{2,1,0:T(8,128)(2,1)}), bf16[16,6,512]{2,1,0:T(8,128)(2,1)S(1)}, u32[]{:S(2)}, u32[]{:S(2)}) async-start(bf16[16,6,512]{2,1,0:T(8,128)(2,1)} %all_to_all.27), calls=%async_computation.1 | async-start | bytes 262144 | tf_op jit(solution)/shard_map/all_to_all | solution.py:108
  45.7 9.7 %collective-permute-start.10 = (bf16[96,256]{1,0:T(8,128)(2,1)S(1)}, bf16[96,256]{1,0:T(8,128)(2,1)S(1)}, u32[]{:S(2)}, u32[]{:S(2)}) collective-permute-start(bf16[96,256]{1,0:T(8,128)(2,1)S(1)} %pad_maximum_fusion.10), channel_id=1, source_target_pairs={{0,1},{1,0},{2,3},{3,2},{4,5},{5,4},{6,7},{7,6},{8,9},{9,8},{10,11... | collective-permute-start | bytes 147464 | tf_op jit(solution)/shard_map/ppermute | solution.py:14
  45.9 8.2 %collective-permute-start.11 = (bf16[96,1024]{1,0:T(8,128)(2,1)S(1)}, bf16[96,1024]{1,0:T(8,128)(2,1)S(1)}, u32[]{:S(2)}, u32[]{:S(2)}) collective-permute-start(bf16[96,1024]{1,0:T(8,128)(2,1)S(1)} %constant_dynamic-update-slice_fusion.5), channel_id=1, source_target_pairs={{0,1},{1,0},{2,3},{3,2},{4,5},{5,4},{6,7},{7,6},{8,9},{9,8},{10,11... | collective-permute-start | bytes 589832 | tf_op jit(solution)/shard_map/ppermute | solution.py:14

commit v18 on v14

--- a/solution.py
+++ b/solution.py
@@ -36,7 +36,7 @@
 
 def sum_over_hid(part, blocks, data):
     bits = (lax.axis_size("hid") - 1).bit_length()
-    rounds = [(3, 1, 2)] + [(1 << bit,) for bit in range(2, bits)]
+    rounds = [(3, 2, 1)] + [(1 << bit,) for bit in range(2, bits)]
     total, far = part, {}
     for at, masks in enumerate(rounds):
         sent = total.astype(jnp.bfloat16)

time: 50 us -> 50 us (level)
  transfers between devices with their start and end apart: 12 -> 12, of which waited for: 6 -> 7; matrix products, arithmetic and copies ran while one was open for 10% -> 10% of each run, Pallas kernels for 0% -> 0%
where the time goes in v18:
time: 50 us; the launch traced here: 49.7 us
  blocking collectives  16 us (32%)
  waiting for transfers between devices  12.9 us (26%)
  starting transfers between devices  12.2 us (24%)
  matrix products  4.7 us (9%)
  local copies, waits for them, and re-layouts  1.54 us (3%)
  other arithmetic  1.33 us (3%)
  between operations  0.95 us (2%)
    all_to_all x1, blocking collectives, on_device(): rows = lax.all_to_all(both, 'hid', split_axis=1, concat_axis=0, tiled=True)  16 us
    ppermute x9, starting transfers between devices, exchange(): lax.ppermute(x, 'hid', [(i, i ^ mask) for i in range(lax.axis_size('hid'))])  8.52 us
    ppermute x9, waiting for transfers between devices, exchange(): lax.ppermute(x, 'hid', [(i, i ^ mask) for i in range(lax.axis_size('hid'))])  8.3 us
    all_to_all x1, waiting for transfers between devices, on_device(): lax.all_to_all(results, 'hid', split_axis=0, concat_axis=1, tiled=True)  4.65 us
    all_to_all x1, starting transfers between devices, on_device(): lax.all_to_all(results, 'hid', split_axis=0, concat_axis=1, tiled=True)  3.51 us
    dot_general x3, matrix products, inner_rows(): lax.dot_general(left, right, (((0,), (0,)), ((), ())), preferred_element_...  2.87 us
    dot_general x7, matrix products, dot(): return jnp.dot(left, right, preferred_element_type=jnp.float32)  1.1 us
  transfers between devices with their start and end apart: 12, of which 7 were waited for; matrix products, arithmetic and copies ran while one was open for 10% of the time, Pallas kernels for 0%

profile of v18, /device:TPU:0, one launch (start us, length us, event | category | flops | bytes accessed | tf_op | source)
XLA Modules:
  0.0 49.7 jit_solution(5577462437061651188)
XLA Ops:
  0.6 0.0 copy-start
  0.7 0.9 %pad_maximum_fusion.5 = bf16[6,16,512]{2,0,1:T(8,128)(2,1)S(1)} fusion(bf16[6,16,256]{2,0,1:T(8,128)(2,1)} %bitcast.32, bf16[6,16,256]{2,0,1:T(8,128)(2,1)} %bitcast.33), kind=kLoop, calls=%fused_computation.28 | loop fusion | flops 196608 | bytes 196608 | tf_op jit(solution)/shard_map/concatenate | solution.py:79
  1.6 0.0 copy-start.2
  1.6 16.0 %all_to_all.32 = bf16[6,16,512]{2,0,1:T(8,128)(2,1)S(1)} all-to-all(bf16[6,16,512]{2,0,1:T(8,128)(2,1)S(1)} %pad_maximum_fusion.5), channel_id=1, replica_groups=mesh['hid'=16,'seq'=2] {'hid'}, dimensions={1} | all-to-all | bytes 196608 | tf_op jit(solution)/shard_map/all_to_all | solution.py:82
  17.6 0.0 copy-start.1
  17.7 0.0 copy-done
  17.7 0.2 fusion.58
  17.9 0.0 copy-done.2
  17.9 0.2 fusion.60
  18.1 0.8 %collective-permute-start = (bf16[96,512]{1,0:T(8,128)(2,1)S(1)}, bf16[96,512]{1,0:T(8,128)(2,1)S(1)}, u32[]{:S(2)}, u32[]{:S(2)}) collective-permute-start(bf16[96,512]{1,0:T(8,128)(2,1)S(1)} %fusion.5), channel_id=1, source_target_pairs={{0,6},{2,4},{4,2},{6,0},{8,14},{10,12},{12,10},{14,8},{16,22},{18,... | collective-permute-start | bytes 294920 | tf_op jit(solution)/shard_map/ppermute | solution.py:10
  18.9 1.8 %collective-permute-start.1 = (bf16[96,512]{1,0:T(8,128)(2,1)S(1)}, bf16[96,512]{1,0:T(8,128)(2,1)S(1)}, u32[]{:S(2)}, u32[]{:S(2)}) collective-permute-start(bf16[96,512]{1,0:T(8,128)(2,1)S(1)} %fusion.5), channel_id=1, source_target_pairs={{0,4},{2,6},{4,0},{6,2},{8,12},{10,14},{12,8},{14,10},{16,20},{18,... | collective-permute-start | bytes 294920 | tf_op jit(solution)/shard_map/ppermute | solution.py:10
  20.7 0.9 %collective-permute-start.2 = (bf16[96,512]{1,0:T(8,128)(2,1)S(1)}, bf16[96,512]{1,0:T(8,128)(2,1)S(1)}, u32[]{:S(2)}, u32[]{:S(2)}) collective-permute-start(bf16[96,512]{1,0:T(8,128)(2,1)S(1)} %fusion.5), channel_id=1, source_target_pairs={{0,2},{2,0},{4,6},{6,4},{8,10},{10,8},{12,14},{14,12},{16,18},{18,... | collective-permute-start | bytes 294920 | tf_op jit(solution)/shard_map/ppermute | solution.py:10
  21.7 0.0 copy-done.1
  21.7 0.3 fusion.67
  22.1 0.8 %collective-permute-start.4 = (bf16[96,512]{1,0:T(8,128)(2,1)S(1)}, bf16[96,512]{1,0:T(8,128)(2,1)S(1)}, u32[]{:S(2)}, u32[]{:S(2)}) collective-permute-start(bf16[96,512]{1,0:T(8,128)(2,1)S(1)} %get-tuple-element.58), channel_id=1, source_target_pairs={{0,8},{2,10},{4,12},{6,14},{8,0},{10,2},{12,4},{14,6},{16,24},{18,... | collective-permute-start | bytes 294920 | tf_op jit(solution)/shard_map/ppermute | solution.py:10
  22.9 1.1 %collective-permute-start.5 = (bf16[96,512]{1,0:T(8,128)(2,1)S(1)}, bf16[96,512]{1,0:T(8,128)(2,1)S(1)}, u32[]{:S(2)}, u32[]{:S(2)}) collective-permute-start(bf16[96,512]{1,0:T(8,128)(2,1)S(1)} %get-tuple-element.57), channel_id=1, source_target_pairs={{0,16},{2,18},{4,20},{6,22},{8,24},{10,26},{12,28},{14,30},{16,0},... | collective-permute-start | bytes 294920 | tf_op jit(solution)/shard_map/ppermute | solution.py:10
  24.0 0.0 collective-permute-done
  24.0 0.6 %collective-permute-done.1 = bf16[96,512]{1,0:T(8,128)(2,1)S(1)} collective-permute-done((bf16[96,512]{1,0:T(8,128)(2,1)S(1)}, bf16[96,512]{1,0:T(8,128)(2,1)S(1)}, u32[]{:S(2)}, u32[]{:S(2)}) %collective-permute-start.1) | collective-permute-done | bytes 98336 | tf_op jit(solution)/shard_map/ppermute | solution.py:10
  24.6 0.8 %collective-permute-done.2 = bf16[96,512]{1,0:T(8,128)(2,1)S(1)} collective-permute-done((bf16[96,512]{1,0:T(8,128)(2,1)S(1)}, bf16[96,512]{1,0:T(8,128)(2,1)S(1)}, u32[]{:S(2)}, u32[]{:S(2)}) %collective-permute-start.2) | collective-permute-done | bytes 98336 | tf_op jit(solution)/shard_map/ppermute | solution.py:10
  25.4 0.3 collective-permute-start.3
  25.7 0.7 %collective-permute-start.7 = (bf16[96,512]{1,0:T(8,128)(2,1)S(1)}, bf16[96,512]{1,0:T(8,128)(2,1)S(1)}, u32[]{:S(2)}, u32[]{:S(2)}) collective-permute-start(bf16[96,512]{1,0:T(8,128)(2,1)S(1)} %get-tuple-element.31), channel_id=1, source_target_pairs={{0,4},{2,6},{4,0},{6,2},{8,12},{10,14},{12,8},{14,10},{16,20},{18,... | collective-permute-start | bytes 294920 | tf_op jit(solution)/shard_map/ppermute | solution.py:10
  26.4 1.5 %collective-permute-start.6 = (bf16[96,512]{1,0:T(8,128)(2,1)S(1)}, bf16[96,512]{1,0:T(8,128)(2,1)S(1)}, u32[]{:S(2)}, u32[]{:S(2)}) collective-permute-start(bf16[96,512]{1,0:T(8,128)(2,1)S(1)} %get-tuple-element.30), channel_id=1, source_target_pairs={{0,2},{2,0},{4,6},{6,4},{8,10},{10,8},{12,14},{14,12},{16,18},{18,... | collective-permute-start | bytes 294920 | tf_op jit(solution)/shard_map/ppermute | solution.py:10
  27.9 0.8 %collective-permute-done.4 = bf16[96,512]{1,0:T(8,128)(2,1)S(1)} collective-permute-done((bf16[96,512]{1,0:T(8,128)(2,1)S(1)}, bf16[96,512]{1,0:T(8,128)(2,1)S(1)}, u32[]{:S(2)}, u32[]{:S(2)}) %collective-permute-start.4) | collective-permute-done | bytes 98336 | tf_op jit(solution)/shard_map/ppermute | solution.py:10
  28.7 0.9 %collective-permute-done.5 = bf16[96,512]{1,0:T(8,128)(2,1)S(1)} collective-permute-done((bf16[96,512]{1,0:T(8,128)(2,1)S(1)}, bf16[96,512]{1,0:T(8,128)(2,1)S(1)}, u32[]{:S(2)}, u32[]{:S(2)}) %collective-permute-start.5) | collective-permute-done | bytes 98336 | tf_op jit(solution)/shard_map/ppermute | solution.py:10
  29.6 0.7 %collective-permute-done.3 = bf16[96,512]{1,0:T(8,128)(2,1)S(1)} collective-permute-done((bf16[96,512]{1,0:T(8,128)(2,1)S(1)}, bf16[96,512]{1,0:T(8,128)(2,1)S(1)}, u32[]{:S(2)}, u32[]{:S(2)}) %collective-permute-start.3) | collective-permute-done | bytes 98336 | tf_op jit(solution)/shard_map/ppermute | solution.py:10
  30.3 0.6 %collective-permute-start.8 = (bf16[96,512]{1,0:T(8,128)(2,1)S(1)}, bf16[96,512]{1,0:T(8,128)(2,1)S(1)}, u32[]{:S(2)}, u32[]{:S(2)}) collective-permute-start(bf16[96,512]{1,0:T(8,128)(2,1)S(1)} %fusion.7), channel_id=1, source_target_pairs={{0,16},{2,18},{4,20},{6,22},{8,24},{10,26},{12,28},{14,30},{16,0},... | collective-permute-start | bytes 294920 | tf_op jit(solution)/shard_map/ppermute | solution.py:10
  30.9 0.1 fusion.9
  31.0 0.2 fusion.13
  31.2 0.0 collective-permute-done.6
  31.3 0.0 collective-permute-done.7
  31.4 0.2 convolution_add_fusion.3
  31.5 0.2 fusion
  31.7 0.2 convolution_add_fusion.1
  32.0 0.1 collective-permute-start.10
  32.0 4.5 %collective-permute-done.8 = bf16[96,512]{1,0:T(8,128)(2,1)S(1)} collective-permute-done((bf16[96,512]{1,0:T(8,128)(2,1)S(1)}, bf16[96,512]{1,0:T(8,128)(2,1)S(1)}, u32[]{:S(2)}, u32[]{:S(2)}) %collective-permute-start.8) | collective-permute-done | bytes 98336 | tf_op jit(solution)/shard_map/ppermute | solution.py:10
  36.6 0.2 fusion.1
  36.8 0.2 fusion.22
  37.1 0.7 %all_to_all.27 = bf16[16,6,512]{2,1,0:T(8,128)(2,1)} reshape(bf16[96,512]{1,0:T(8,128)(2,1)S(1)} %pad_maximum_fusion.6) | data formatting | bytes 196608 | tf_op jit(solution)/shard_map/all_to_all | solution.py:108
  37.7 3.5 %all-to-all-start.1 = ((bf16[16,6,512]{2,1,0:T(8,128)(2,1)}), bf16[16,6,512]{2,1,0:T(8,128)(2,1)S(1)}, u32[]{:S(2)}, u32[]{:S(2)}) async-start(bf16[16,6,512]{2,1,0:T(8,128)(2,1)} %all_to_all.27), calls=%async_computation.1 | async-start | bytes 262144 | tf_op jit(solution)/shard_map/all_to_all | solution.py:108
  41.3 0.1 collective-permute-start.9
  41.3 0.0 collective-permute-done.10
  41.5 1.1 %convolution_multiply_fusion = f32[640,256]{1,0:T(8,128)} fusion(bf16[96,640]{1,0:T(8,128)(2,1)S(1)} %constant_dynamic-update-slice_fusion.11, bf16[96,640]{1,0:T(8,128)(2,1)S(1)} %get-tuple-element.53, bf16[96,256]{1,0:T(8,128)(2,1)S(1)} %get-tuple-element.46, bf16[96,256]{1,0:T(8,128)(2,1)S(1)} %slice.176), kind=kOutput, calls=%fused_computation | convolution fusion | flops 63766528 | bytes 999424 | tf_op jit(solution)/shard_map/dot_general | solution.py:32
  42.6 0.0 collective-permute-done.9
  42.6 0.9 %convolution_multiply_fusion.1 = f32[128,256]{1,0:T(8,128)} fusion(bf16[96,256]{1,0:T(8,128)(2,1)S(1)} %get-tuple-element.46, bf16[96,256]{1,0:T(8,128)(2,1)S(1)} %slice.176, bf16[96,128]{1,0:T(8,128)(2,1)S(1)} %get-tuple-element.55, bf16[96,128]{1,0:T(8,128)(2,1)S(1)} %get-tuple-element.49), kind=kOutput, calls=%fused_computation.1 | convolution fusion | flops 12910592 | bytes 278528 | tf_op jit(solution)/shard_map/dot_general | solution.py:32
  43.5 0.9 %convolution_multiply_fusion.2 = f32[256,128]{1,0:T(8,128)} fusion(bf16[96,256]{1,0:T(8,128)(2,1)S(1)} %get-tuple-element.45, bf16[96,256]{1,0:T(8,128)(2,1)S(1)} %fusion.27, bf16[96,128]{1,0:T(8,128)(2,1)S(1)} %get-tuple-element.56, bf16[96,128]{1,0:T(8,128)(2,1)S(1)} %get-tuple-element.51), kind=kOutput, calls=%fused_computation.2 | convolution fusion | flops 12910592 | bytes 278528 | tf_op jit(solution)/shard_map/dot_general | solution.py:32
  44.4 4.6 %all-to-all-done.1 = bf16[16,6,512]{2,1,0:T(8,128)(2,1)S(1)} async-done(((bf16[16,6,512]{2,1,0:T(8,128)(2,1)}), bf16[16,6,512]{2,1,0:T(8,128)(2,1)S(1)}, u32[]{:S(2)}, u32[]{:S(2)}) %all-to-all-start.1) | async-done | bytes 98336 | tf_op jit(solution)/shard_map/all_to_all | solution.py:108
  49.0 0.7 %fusion.65 = (bf16[6,16,256]{2,0,1:T(8,128)(2,1)}, bf16[6,16,256]{2,0,1:T(8,128)(2,1)}) fusion(bf16[6,16,512]{2,0,1:T(8,128)(2,1)S(1)} %bitcast.31), kind=kLoop, calls=%fused_computation.109 | loop fusion | bytes 196608 | tf_op jit(solution)/shard_map/slice | solution.py:111
  (29 shorter events, 0.6 us)
Async XLA Ops:
  0.6 17.1 %copy-start = (bf16[256,256]{1,0:T(8,128)(2,1)S(1)}, bf16[256,256]{1,0:T(8,128)(2,1)}, u32[]{:S(2)}) copy-start(bf16[256,256]{1,0:T(8,128)(2,1)} %param.8) | copy-start | bytes 393220
  1.6 16.3 %copy-start.2 = (bf16[256,256]{1,0:T(8,128)(2,1)S(1)}, bf16[256,256]{1,0:T(8,128)(2,1)}, u32[]{:S(2)}) copy-start(bf16[256,256]{1,0:T(8,128)(2,1)} %param.7) | copy-start | bytes 393220
  17.6 4.0 %copy-start.1 = (bf16[1,5,256,256]{3,2,1,0:T(8,128)(2,1)S(1)}, bf16[1,5,256,256]{3,2,1,0:T(8,128)(2,1)}, u32[]{:S(2)}) copy-start(bf16[1,5,256,256]{3,2,1,0:T(8,128)(2,1)} %param.6) | copy-start | bytes 1966084
  18.1 5.9 %collective-permute-start = (bf16[96,512]{1,0:T(8,128)(2,1)S(1)}, bf16[96,512]{1,0:T(8,128)(2,1)S(1)}, u32[]{:S(2)}, u32[]{:S(2)}) collective-permute-start(bf16[96,512]{1,0:T(8,128)(2,1)S(1)} %fusion.5), channel_id=1, source_target_pairs={{0,6},{2,4},{4,2},{6,0},{8,14},{10,12},{12,10},{14,8},{16,22},{18,... | collective-permute-start | bytes 294920 | tf_op jit(solution)/shard_map/ppermute | solution.py:10
  18.9 5.7 %collective-permute-start.1 = (bf16[96,512]{1,0:T(8,128)(2,1)S(1)}, bf16[96,512]{1,0:T(8,128)(2,1)S(1)}, u32[]{:S(2)}, u32[]{:S(2)}) collective-permute-start(bf16[96,512]{1,0:T(8,128)(2,1)S(1)} %fusion.5), channel_id=1, source_target_pairs={{0,4},{2,6},{4,0},{6,2},{8,12},{10,14},{12,8},{14,10},{16,20},{18,... | collective-permute-start | bytes 294920 | tf_op jit(solution)/shard_map/ppermute | solution.py:10
  20.7 4.6 %collective-permute-start.2 = (bf16[96,512]{1,0:T(8,128)(2,1)S(1)}, bf16[96,512]{1,0:T(8,128)(2,1)S(1)}, u32[]{:S(2)}, u32[]{:S(2)}) collective-permute-start(bf16[96,512]{1,0:T(8,128)(2,1)S(1)} %fusion.5), channel_id=1, source_target_pairs={{0,2},{2,0},{4,6},{6,4},{8,10},{10,8},{12,14},{14,12},{16,18},{18,... | collective-permute-start | bytes 294920 | tf_op jit(solution)/shard_map/ppermute | solution.py:10
  22.1 6.6 %collective-permute-start.4 = (bf16[96,512]{1,0:T(8,128)(2,1)S(1)}, bf16[96,512]{1,0:T(8,128)(2,1)S(1)}, u32[]{:S(2)}, u32[]{:S(2)}) collective-permute-start(bf16[96,512]{1,0:T(8,128)(2,1)S(1)} %get-tuple-element.58), channel_id=1, source_target_pairs={{0,8},{2,10},{4,12},{6,14},{8,0},{10,2},{12,4},{14,6},{16,24},{18,... | collective-permute-start | bytes 294920 | tf_op jit(solution)/shard_map/ppermute | solution.py:10
  22.9 6.7 %collective-permute-start.5 = (bf16[96,512]{1,0:T(8,128)(2,1)S(1)}, bf16[96,512]{1,0:T(8,128)(2,1)S(1)}, u32[]{:S(2)}, u32[]{:S(2)}) collective-permute-start(bf16[96,512]{1,0:T(8,128)(2,1)S(1)} %get-tuple-element.57), channel_id=1, source_target_pairs={{0,16},{2,18},{4,20},{6,22},{8,24},{10,26},{12,28},{14,30},{16,0},... | collective-permute-start | bytes 294920 | tf_op jit(solution)/shard_map/ppermute | solution.py:10
  25.4 4.9 %collective-permute-start.3 = (bf16[96,512]{1,0:T(8,128)(2,1)S(1)}, bf16[96,512]{1,0:T(8,128)(2,1)S(1)}, u32[]{:S(2)}, u32[]{:S(2)}) collective-permute-start(bf16[96,512]{1,0:T(8,128)(2,1)S(1)} %get-tuple-element.27), channel_id=1, source_target_pairs={{0,8},{2,10},{4,12},{6,14},{8,0},{10,2},{12,4},{14,6},{16,24},{18,... | collective-permute-start | bytes 294920 | tf_op jit(solution)/shard_map/ppermute | solution.py:10
  25.7 5.6 %collective-permute-start.7 = (bf16[96,512]{1,0:T(8,128)(2,1)S(1)}, bf16[96,512]{1,0:T(8,128)(2,1)S(1)}, u32[]{:S(2)}, u32[]{:S(2)}) collective-permute-start(bf16[96,512]{1,0:T(8,128)(2,1)S(1)} %get-tuple-element.31), channel_id=1, source_target_pairs={{0,4},{2,6},{4,0},{6,2},{8,12},{10,14},{12,8},{14,10},{16,20},{18,... | collective-permute-start | bytes 294920 | tf_op jit(solution)/shard_map/ppermute | solution.py:10
  26.4 4.8 %collective-permute-start.6 = (bf16[96,512]{1,0:T(8,128)(2,1)S(1)}, bf16[96,512]{1,0:T(8,128)(2,1)S(1)}, u32[]{:S(2)}, u32[]{:S(2)}) collective-permute-start(bf16[96,512]{1,0:T(8,128)(2,1)S(1)} %get-tuple-element.30), channel_id=1, source_target_pairs={{0,2},{2,0},{4,6},{6,4},{8,10},{10,8},{12,14},{14,12},{16,18},{18,... | collective-permute-start | bytes 294920 | tf_op jit(solution)/shard_map/ppermute | solution.py:10
  30.3 6.3 %collective-permute-start.8 = (bf16[96,512]{1,0:T(8,128)(2,1)S(1)}, bf16[96,512]{1,0:T(8,128)(2,1)S(1)}, u32[]{:S(2)}, u32[]{:S(2)}) collective-permute-start(bf16[96,512]{1,0:T(8,128)(2,1)S(1)} %fusion.7), channel_id=1, source_target_pairs={{0,16},{2,18},{4,20},{6,22},{8,24},{10,26},{12,28},{14,30},{16,0},... | collective-permute-start | bytes 294920 | tf_op jit(solution)/shard_map/ppermute | solution.py:10
  32.0 9.4 %collective-permute-start.10 = (bf16[96,1024]{1,0:T(8,128)(2,1)S(1)}, bf16[96,1024]{1,0:T(8,128)(2,1)S(1)}, u32[]{:S(2)}, u32[]{:S(2)}) collective-permute-start(bf16[96,1024]{1,0:T(8,128)(2,1)S(1)} %constant_dynamic-update-slice_fusion.5), channel_id=1, source_target_pairs={{0,1},{1,0},{2,3},{3,2},{4,5},{5,4},{6,7},{7,6},{8,9},{9,8},{10,11... | collective-permute-start | bytes 589832 | tf_op jit(solution)/shard_map/ppermute | solution.py:14
  37.7 11.3 %all-to-all-start.1 = ((bf16[16,6,512]{2,1,0:T(8,128)(2,1)}), bf16[16,6,512]{2,1,0:T(8,128)(2,1)S(1)}, u32[]{:S(2)}, u32[]{:S(2)}) async-start(bf16[16,6,512]{2,1,0:T(8,128)(2,1)} %all_to_all.27), calls=%async_computation.1 | async-start | bytes 262144 | tf_op jit(solution)/shard_map/all_to_all | solution.py:108
  41.3 1.4 %collective-permute-start.9 = (bf16[96,256]{1,0:T(8,128)(2,1)S(1)}, bf16[96,256]{1,0:T(8,128)(2,1)S(1)}, u32[]{:S(2)}, u32[]{:S(2)}) collective-permute-start(bf16[96,256]{1,0:T(8,128)(2,1)S(1)} %pad_maximum_fusion.10), channel_id=1, source_target_pairs={{0,1},{1,0},{2,3},{3,2},{4,5},{5,4},{6,7},{7,6},{8,9},{9,8},{10,11... | collective-permute-start | bytes 147464 | tf_op jit(solution)/shard_map/ppermute | solution.py:14

commit v19 on v18

--- a/solution.py
+++ b/solution.py
@@ -41,7 +41,7 @@
     for at, masks in enumerate(rounds):
         sent = total.astype(jnp.bfloat16)
         if at == 0:
-            beside = {mask: blocks[mask] for mask in sorted(blocks, reverse=True) if mask > 3}
+            beside = {mask: blocks[mask] for mask in blocks if 3 < mask < max(blocks)}
         elif at == 1:
             early, beside = far, {mask: blocks[mask] for mask in blocks if mask not in far}
             sent, beside = lax.optimization_barrier((sent, beside))

time: 50 us -> 50.6 us (1.012)
  starting transfers between devices: 12.2 us -> 12.8 us
where the time goes in v19:
time: 50.6 us; the launch traced here: 50.3 us
  blocking collectives  16 us (32%)
  waiting for transfers between devices  13 us (26%)
  starting transfers between devices  12.8 us (25%)
  matrix products  4.69 us (9%)
  local copies, waits for them, and re-layouts  1.54 us (3%)
  other arithmetic  1.34 us (3%)
  between operations  0.94 us (2%)
    all_to_all x1, blocking collectives, on_device(): rows = lax.all_to_all(both, 'hid', split_axis=1, concat_axis=0, tiled=True)  16 us
    ppermute x9, starting transfers between devices, exchange(): lax.ppermute(x, 'hid', [(i, i ^ mask) for i in range(lax.axis_size('hid'))])  8.72 us
    ppermute x9, waiting for transfers between devices, exchange(): lax.ppermute(x, 'hid', [(i, i ^ mask) for i in range(lax.axis_size('hid'))])  8.31 us
    all_to_all x1, waiting for transfers between devices, on_device(): lax.all_to_all(results, 'hid', split_axis=0, concat_axis=1, tiled=True)  4.67 us
    all_to_all x1, starting transfers between devices, on_device(): lax.all_to_all(results, 'hid', split_axis=0, concat_axis=1, tiled=True)  3.9 us
    dot_general x3, matrix products, inner_rows(): lax.dot_general(left, right, (((0,), (0,)), ((), ())), preferred_element_...  2.88 us
    dot_general x7, matrix products, dot(): return jnp.dot(left, right, preferred_element_type=jnp.float32)  1.08 us
  transfers between devices with their start and end apart: 12, of which 7 were waited for; matrix products, arithmetic and copies ran while one was open for 10% of the time, Pallas kernels for 0%

profile of v19, /device:TPU:0, one launch (start us, length us, event | category | flops | bytes accessed | tf_op | source)
XLA Modules:
  0.0 50.3 jit_solution(18288615500452952874)
XLA Ops:
  0.6 0.0 copy-start
  0.7 0.9 %pad_maximum_fusion.5 = bf16[6,16,512]{2,0,1:T(8,128)(2,1)S(1)} fusion(bf16[6,16,256]{2,0,1:T(8,128)(2,1)} %bitcast.32, bf16[6,16,256]{2,0,1:T(8,128)(2,1)} %bitcast.33), kind=kLoop, calls=%fused_computation.28 | loop fusion | flops 196608 | bytes 196608 | tf_op jit(solution)/shard_map/concatenate | solution.py:79
  1.6 0.0 copy-start.2
  1.6 16.0 %all_to_all.32 = bf16[6,16,512]{2,0,1:T(8,128)(2,1)S(1)} all-to-all(bf16[6,16,512]{2,0,1:T(8,128)(2,1)S(1)} %pad_maximum_fusion.5), channel_id=1, replica_groups=mesh['hid'=16,'seq'=2] {'hid'}, dimensions={1} | all-to-all | bytes 196608 | tf_op jit(solution)/shard_map/all_to_all | solution.py:82
  17.6 0.0 copy-start.1
  17.7 0.0 copy-done
  17.7 0.2 fusion.60
  17.9 0.0 copy-done.2
  17.9 0.2 fusion.62
  18.1 0.8 %collective-permute-start = (bf16[96,512]{1,0:T(8,128)(2,1)S(1)}, bf16[96,512]{1,0:T(8,128)(2,1)S(1)}, u32[]{:S(2)}, u32[]{:S(2)}) collective-permute-start(bf16[96,512]{1,0:T(8,128)(2,1)S(1)} %fusion.6), channel_id=1, source_target_pairs={{0,6},{2,4},{4,2},{6,0},{8,14},{10,12},{12,10},{14,8},{16,22},{18,... | collective-permute-start | bytes 294920 | tf_op jit(solution)/shard_map/ppermute | solution.py:10
  18.9 1.8 %collective-permute-start.1 = (bf16[96,512]{1,0:T(8,128)(2,1)S(1)}, bf16[96,512]{1,0:T(8,128)(2,1)S(1)}, u32[]{:S(2)}, u32[]{:S(2)}) collective-permute-start(bf16[96,512]{1,0:T(8,128)(2,1)S(1)} %fusion.6), channel_id=1, source_target_pairs={{0,4},{2,6},{4,0},{6,2},{8,12},{10,14},{12,8},{14,10},{16,20},{18,... | collective-permute-start | bytes 294920 | tf_op jit(solution)/shard_map/ppermute | solution.py:10
  20.7 0.9 %collective-permute-start.2 = (bf16[96,512]{1,0:T(8,128)(2,1)S(1)}, bf16[96,512]{1,0:T(8,128)(2,1)S(1)}, u32[]{:S(2)}, u32[]{:S(2)}) collective-permute-start(bf16[96,512]{1,0:T(8,128)(2,1)S(1)} %fusion.6), channel_id=1, source_target_pairs={{0,2},{2,0},{4,6},{6,4},{8,10},{10,8},{12,14},{14,12},{16,18},{18,... | collective-permute-start | bytes 294920 | tf_op jit(solution)/shard_map/ppermute | solution.py:10
  21.7 0.0 copy-done.1
  21.7 0.3 fusion.69
  22.1 0.8 %collective-permute-start.4 = (bf16[96,512]{1,0:T(8,128)(2,1)S(1)}, bf16[96,512]{1,0:T(8,128)(2,1)S(1)}, u32[]{:S(2)}, u32[]{:S(2)}) collective-permute-start(bf16[96,512]{1,0:T(8,128)(2,1)S(1)} %get-tuple-element.57), channel_id=1, source_target_pairs={{0,8},{2,10},{4,12},{6,14},{8,0},{10,2},{12,4},{14,6},{16,24},{18,... | collective-permute-start | bytes 294920 | tf_op jit(solution)/shard_map/ppermute | solution.py:10
  22.9 0.9 %collective-permute-done = bf16[96,512]{1,0:T(8,128)(2,1)S(1)} collective-permute-done((bf16[96,512]{1,0:T(8,128)(2,1)S(1)}, bf16[96,512]{1,0:T(8,128)(2,1)S(1)}, u32[]{:S(2)}, u32[]{:S(2)}) %collective-permute-start) | collective-permute-done | bytes 98336 | tf_op jit(solution)/shard_map/ppermute | solution.py:10
  23.8 0.8 %collective-permute-done.1 = bf16[96,512]{1,0:T(8,128)(2,1)S(1)} collective-permute-done((bf16[96,512]{1,0:T(8,128)(2,1)S(1)}, bf16[96,512]{1,0:T(8,128)(2,1)S(1)}, u32[]{:S(2)}, u32[]{:S(2)}) %collective-permute-start.1) | collective-permute-done | bytes 98336 | tf_op jit(solution)/shard_map/ppermute | solution.py:10
  24.6 0.8 %collective-permute-done.2 = bf16[96,512]{1,0:T(8,128)(2,1)S(1)} collective-permute-done((bf16[96,512]{1,0:T(8,128)(2,1)S(1)}, bf16[96,512]{1,0:T(8,128)(2,1)S(1)}, u32[]{:S(2)}, u32[]{:S(2)}) %collective-permute-start.2) | collective-permute-done | bytes 98336 | tf_op jit(solution)/shard_map/ppermute | solution.py:10
  25.4 0.3 collective-permute-start.3
  25.7 1.1 %collective-permute-start.7 = (bf16[96,512]{1,0:T(8,128)(2,1)S(1)}, bf16[96,512]{1,0:T(8,128)(2,1)S(1)}, u32[]{:S(2)}, u32[]{:S(2)}) collective-permute-start(bf16[96,512]{1,0:T(8,128)(2,1)S(1)} %get-tuple-element.33), channel_id=1, source_target_pairs={{0,16},{2,18},{4,20},{6,22},{8,24},{10,26},{12,28},{14,30},{16,0},... | collective-permute-start | bytes 294920 | tf_op jit(solution)/shard_map/ppermute | solution.py:10
  26.7 0.7 %collective-permute-start.6 = (bf16[96,512]{1,0:T(8,128)(2,1)S(1)}, bf16[96,512]{1,0:T(8,128)(2,1)S(1)}, u32[]{:S(2)}, u32[]{:S(2)}) collective-permute-start(bf16[96,512]{1,0:T(8,128)(2,1)S(1)} %get-tuple-element.31), channel_id=1, source_target_pairs={{0,4},{2,6},{4,0},{6,2},{8,12},{10,14},{12,8},{14,10},{16,20},{18,... | collective-permute-start | bytes 294920 | tf_op jit(solution)/shard_map/ppermute | solution.py:10
  27.4 1.5 %collective-permute-start.5 = (bf16[96,512]{1,0:T(8,128)(2,1)S(1)}, bf16[96,512]{1,0:T(8,128)(2,1)S(1)}, u32[]{:S(2)}, u32[]{:S(2)}) collective-permute-start(bf16[96,512]{1,0:T(8,128)(2,1)S(1)} %get-tuple-element.30), channel_id=1, source_target_pairs={{0,2},{2,0},{4,6},{6,4},{8,10},{10,8},{12,14},{14,12},{16,18},{18,... | collective-permute-start | bytes 294920 | tf_op jit(solution)/shard_map/ppermute | solution.py:10
  28.9 0.0 collective-permute-done.4
  28.9 1.1 %collective-permute-done.3 = bf16[96,512]{1,0:T(8,128)(2,1)S(1)} collective-permute-done((bf16[96,512]{1,0:T(8,128)(2,1)S(1)}, bf16[96,512]{1,0:T(8,128)(2,1)S(1)}, u32[]{:S(2)}, u32[]{:S(2)}) %collective-permute-start.3) | collective-permute-done | bytes 98336 | tf_op jit(solution)/shard_map/ppermute | solution.py:10
  30.1 0.8 %collective-permute-start.8 = (bf16[96,512]{1,0:T(8,128)(2,1)S(1)}, bf16[96,512]{1,0:T(8,128)(2,1)S(1)}, u32[]{:S(2)}, u32[]{:S(2)}) collective-permute-start(bf16[96,512]{1,0:T(8,128)(2,1)S(1)} %fusion.8), channel_id=1, source_target_pairs={{0,16},{2,18},{4,20},{6,22},{8,24},{10,26},{12,28},{14,30},{16,0},... | collective-permute-start | bytes 294920 | tf_op jit(solution)/shard_map/ppermute | solution.py:10
  30.9 0.1 fusion.10
  31.0 0.2 fusion.14
  31.2 0.8 %collective-permute-done.5 = bf16[96,512]{1,0:T(8,128)(2,1)S(1)} collective-permute-done((bf16[96,512]{1,0:T(8,128)(2,1)S(1)}, bf16[96,512]{1,0:T(8,128)(2,1)S(1)}, u32[]{:S(2)}, u32[]{:S(2)}) %collective-permute-start.5) | collective-permute-done | bytes 98336 | tf_op jit(solution)/shard_map/ppermute | solution.py:10
  32.0 0.0 collective-permute-done.6
  32.1 0.0 collective-permute-done.7
  32.2 0.1 collective-permute-start.10
  32.3 0.2 convolution_add_fusion.2
  32.5 0.2 fusion
  32.7 4.0 %collective-permute-done.8 = bf16[96,512]{1,0:T(8,128)(2,1)S(1)} collective-permute-done((bf16[96,512]{1,0:T(8,128)(2,1)S(1)}, bf16[96,512]{1,0:T(8,128)(2,1)S(1)}, u32[]{:S(2)}, u32[]{:S(2)}) %collective-permute-start.8) | collective-permute-done | bytes 98336 | tf_op jit(solution)/shard_map/ppermute | solution.py:10
  36.7 0.1 fusion.43
  36.8 0.2 fusion.23
  37.1 0.2 fusion.2
  37.3 0.7 %all_to_all.27 = bf16[16,6,512]{2,1,0:T(8,128)(2,1)} reshape(bf16[96,512]{1,0:T(8,128)(2,1)S(1)} %pad_maximum_fusion.6) | data formatting | bytes 196608 | tf_op jit(solution)/shard_map/all_to_all | solution.py:108
  37.9 3.9 %all-to-all-start.1 = ((bf16[16,6,512]{2,1,0:T(8,128)(2,1)}), bf16[16,6,512]{2,1,0:T(8,128)(2,1)S(1)}, u32[]{:S(2)}, u32[]{:S(2)}) async-start(bf16[16,6,512]{2,1,0:T(8,128)(2,1)} %all_to_all.27), calls=%async_computation.1 | async-start | bytes 262144 | tf_op jit(solution)/shard_map/all_to_all | solution.py:108
  41.9 0.1 collective-permute-start.9
  41.9 0.0 collective-permute-done.10
  42.1 1.1 %convolution_multiply_fusion = f32[640,256]{1,0:T(8,128)} fusion(bf16[96,640]{1,0:T(8,128)(2,1)S(1)} %constant_dynamic-update-slice_fusion.11, bf16[96,640]{1,0:T(8,128)(2,1)S(1)} %get-tuple-element.53, bf16[96,256]{1,0:T(8,128)(2,1)S(1)} %get-tuple-element.46, bf16[96,256]{1,0:T(8,128)(2,1)S(1)} %slice.176), kind=kOutput, calls=%fused_computation | convolution fusion | flops 63766528 | bytes 999424 | tf_op jit(solution)/shard_map/dot_general | solution.py:32
  43.2 0.0 collective-permute-done.9
  43.2 0.9 %convolution_multiply_fusion.1 = f32[128,256]{1,0:T(8,128)} fusion(bf16[96,256]{1,0:T(8,128)(2,1)S(1)} %get-tuple-element.46, bf16[96,256]{1,0:T(8,128)(2,1)S(1)} %slice.176, bf16[96,128]{1,0:T(8,128)(2,1)S(1)} %get-tuple-element.55, bf16[96,128]{1,0:T(8,128)(2,1)S(1)} %get-tuple-element.49), kind=kOutput, calls=%fused_computation.1 | convolution fusion | flops 12910592 | bytes 278528 | tf_op jit(solution)/shard_map/dot_general | solution.py:32
  44.1 0.9 %convolution_multiply_fusion.2 = f32[256,128]{1,0:T(8,128)} fusion(bf16[96,256]{1,0:T(8,128)(2,1)S(1)} %get-tuple-element.45, bf16[96,256]{1,0:T(8,128)(2,1)S(1)} %fusion.28, bf16[96,128]{1,0:T(8,128)(2,1)S(1)} %get-tuple-element.56, bf16[96,128]{1,0:T(8,128)(2,1)S(1)} %get-tuple-element.51), kind=kOutput, calls=%fused_computation.2 | convolution fusion | flops 12910592 | bytes 278528 | tf_op jit(solution)/shard_map/dot_general | solution.py:32
  45.0 4.7 %all-to-all-done.1 = bf16[16,6,512]{2,1,0:T(8,128)(2,1)S(1)} async-done(((bf16[16,6,512]{2,1,0:T(8,128)(2,1)}), bf16[16,6,512]{2,1,0:T(8,128)(2,1)S(1)}, u32[]{:S(2)}, u32[]{:S(2)}) %all-to-all-start.1) | async-done | bytes 98336 | tf_op jit(solution)/shard_map/all_to_all | solution.py:108
  49.6 0.7 %fusion.67 = (bf16[6,16,256]{2,0,1:T(8,128)(2,1)}, bf16[6,16,256]{2,0,1:T(8,128)(2,1)}) fusion(bf16[6,16,512]{2,0,1:T(8,128)(2,1)S(1)} %bitcast.31), kind=kLoop, calls=%fused_computation.110 | loop fusion | bytes 196608 | tf_op jit(solution)/shard_map/slice | solution.py:111
  (29 shorter events, 0.6 us)
Async XLA Ops:
  0.6 17.1 %copy-start = (bf16[256,256]{1,0:T(8,128)(2,1)S(1)}, bf16[256,256]{1,0:T(8,128)(2,1)}, u32[]{:S(2)}) copy-start(bf16[256,256]{1,0:T(8,128)(2,1)} %param.8) | copy-start | bytes 393220
  1.6 16.3 %copy-start.2 = (bf16[256,256]{1,0:T(8,128)(2,1)S(1)}, bf16[256,256]{1,0:T(8,128)(2,1)}, u32[]{:S(2)}) copy-start(bf16[256,256]{1,0:T(8,128)(2,1)} %param.7) | copy-start | bytes 393220
  17.6 4.0 %copy-start.1 = (bf16[1,5,256,256]{3,2,1,0:T(8,128)(2,1)S(1)}, bf16[1,5,256,256]{3,2,1,0:T(8,128)(2,1)}, u32[]{:S(2)}) copy-start(bf16[1,5,256,256]{3,2,1,0:T(8,128)(2,1)} %param.6) | copy-start | bytes 1966084
  18.1 5.7 %collective-permute-start = (bf16[96,512]{1,0:T(8,128)(2,1)S(1)}, bf16[96,512]{1,0:T(8,128)(2,1)S(1)}, u32[]{:S(2)}, u32[]{:S(2)}) collective-permute-start(bf16[96,512]{1,0:T(8,128)(2,1)S(1)} %fusion.6), channel_id=1, source_target_pairs={{0,6},{2,4},{4,2},{6,0},{8,14},{10,12},{12,10},{14,8},{16,22},{18,... | collective-permute-start | bytes 294920 | tf_op jit(solution)/shard_map/ppermute | solution.py:10
  18.9 5.7 %collective-permute-start.1 = (bf16[96,512]{1,0:T(8,128)(2,1)S(1)}, bf16[96,512]{1,0:T(8,128)(2,1)S(1)}, u32[]{:S(2)}, u32[]{:S(2)}) collective-permute-start(bf16[96,512]{1,0:T(8,128)(2,1)S(1)} %fusion.6), channel_id=1, source_target_pairs={{0,4},{2,6},{4,0},{6,2},{8,12},{10,14},{12,8},{14,10},{16,20},{18,... | collective-permute-start | bytes 294920 | tf_op jit(solution)/shard_map/ppermute | solution.py:10
  20.7 4.6 %collective-permute-start.2 = (bf16[96,512]{1,0:T(8,128)(2,1)S(1)}, bf16[96,512]{1,0:T(8,128)(2,1)S(1)}, u32[]{:S(2)}, u32[]{:S(2)}) collective-permute-start(bf16[96,512]{1,0:T(8,128)(2,1)S(1)} %fusion.6), channel_id=1, source_target_pairs={{0,2},{2,0},{4,6},{6,4},{8,10},{10,8},{12,14},{14,12},{16,18},{18,... | collective-permute-start | bytes 294920 | tf_op jit(solution)/shard_map/ppermute | solution.py:10
  22.1 6.8 %collective-permute-start.4 = (bf16[96,512]{1,0:T(8,128)(2,1)S(1)}, bf16[96,512]{1,0:T(8,128)(2,1)S(1)}, u32[]{:S(2)}, u32[]{:S(2)}) collective-permute-start(bf16[96,512]{1,0:T(8,128)(2,1)S(1)} %get-tuple-element.57), channel_id=1, source_target_pairs={{0,8},{2,10},{4,12},{6,14},{8,0},{10,2},{12,4},{14,6},{16,24},{18,... | collective-permute-start | bytes 294920 | tf_op jit(solution)/shard_map/ppermute | solution.py:10
  25.4 4.7 %collective-permute-start.3 = (bf16[96,512]{1,0:T(8,128)(2,1)S(1)}, bf16[96,512]{1,0:T(8,128)(2,1)S(1)}, u32[]{:S(2)}, u32[]{:S(2)}) collective-permute-start(bf16[96,512]{1,0:T(8,128)(2,1)S(1)} %get-tuple-element.27), channel_id=1, source_target_pairs={{0,8},{2,10},{4,12},{6,14},{8,0},{10,2},{12,4},{14,6},{16,24},{18,... | collective-permute-start | bytes 294920 | tf_op jit(solution)/shard_map/ppermute | solution.py:10
  25.7 6.5 %collective-permute-start.7 = (bf16[96,512]{1,0:T(8,128)(2,1)S(1)}, bf16[96,512]{1,0:T(8,128)(2,1)S(1)}, u32[]{:S(2)}, u32[]{:S(2)}) collective-permute-start(bf16[96,512]{1,0:T(8,128)(2,1)S(1)} %get-tuple-element.33), channel_id=1, source_target_pairs={{0,16},{2,18},{4,20},{6,22},{8,24},{10,26},{12,28},{14,30},{16,0},... | collective-permute-start | bytes 294920 | tf_op jit(solution)/shard_map/ppermute | solution.py:10
  26.7 5.3 %collective-permute-start.6 = (bf16[96,512]{1,0:T(8,128)(2,1)S(1)}, bf16[96,512]{1,0:T(8,128)(2,1)S(1)}, u32[]{:S(2)}, u32[]{:S(2)}) collective-permute-start(bf16[96,512]{1,0:T(8,128)(2,1)S(1)} %get-tuple-element.31), channel_id=1, source_target_pairs={{0,4},{2,6},{4,0},{6,2},{8,12},{10,14},{12,8},{14,10},{16,20},{18,... | collective-permute-start | bytes 294920 | tf_op jit(solution)/shard_map/ppermute | solution.py:10
  27.4 4.6 %collective-permute-start.5 = (bf16[96,512]{1,0:T(8,128)(2,1)S(1)}, bf16[96,512]{1,0:T(8,128)(2,1)S(1)}, u32[]{:S(2)}, u32[]{:S(2)}) collective-permute-start(bf16[96,512]{1,0:T(8,128)(2,1)S(1)} %get-tuple-element.30), channel_id=1, source_target_pairs={{0,2},{2,0},{4,6},{6,4},{8,10},{10,8},{12,14},{14,12},{16,18},{18,... | collective-permute-start | bytes 294920 | tf_op jit(solution)/shard_map/ppermute | solution.py:10
  30.1 6.6 %collective-permute-start.8 = (bf16[96,512]{1,0:T(8,128)(2,1)S(1)}, bf16[96,512]{1,0:T(8,128)(2,1)S(1)}, u32[]{:S(2)}, u32[]{:S(2)}) collective-permute-start(bf16[96,512]{1,0:T(8,128)(2,1)S(1)} %fusion.8), channel_id=1, source_target_pairs={{0,16},{2,18},{4,20},{6,22},{8,24},{10,26},{12,28},{14,30},{16,0},... | collective-permute-start | bytes 294920 | tf_op jit(solution)/shard_map/ppermute | solution.py:10
  32.2 9.7 %collective-permute-start.10 = (bf16[96,1024]{1,0:T(8,128)(2,1)S(1)}, bf16[96,1024]{1,0:T(8,128)(2,1)S(1)}, u32[]{:S(2)}, u32[]{:S(2)}) collective-permute-start(bf16[96,1024]{1,0:T(8,128)(2,1)S(1)} %constant_dynamic-update-slice_fusion.5), channel_id=1, source_target_pairs={{0,1},{1,0},{2,3},{3,2},{4,5},{5,4},{6,7},{7,6},{8,9},{9,8},{10,11... | collective-permute-start | bytes 589832 | tf_op jit(solution)/shard_map/ppermute | solution.py:14
  37.9 11.7 %all-to-all-start.1 = ((bf16[16,6,512]{2,1,0:T(8,128)(2,1)}), bf16[16,6,512]{2,1,0:T(8,128)(2,1)S(1)}, u32[]{:S(2)}, u32[]{:S(2)}) async-start(bf16[16,6,512]{2,1,0:T(8,128)(2,1)} %all_to_all.27), calls=%async_computation.1 | async-start | bytes 262144 | tf_op jit(solution)/shard_map/all_to_all | solution.py:108
  41.9 1.4 %collective-permute-start.9 = (bf16[96,256]{1,0:T(8,128)(2,1)S(1)}, bf16[96,256]{1,0:T(8,128)(2,1)S(1)}, u32[]{:S(2)}, u32[]{:S(2)}) collective-permute-start(bf16[96,256]{1,0:T(8,128)(2,1)S(1)} %pad_maximum_fusion.10), channel_id=1, source_target_pairs={{0,1},{1,0},{2,3},{3,2},{4,5},{5,4},{6,7},{7,6},{8,9},{9,8},{10,11... | collective-permute-start | bytes 147464 | tf_op jit(solution)/shard_map/ppermute | solution.py:14

commit v20 on v19

--- a/solution.py
+++ b/solution.py
@@ -36,7 +36,7 @@
 
 def sum_over_hid(part, blocks, data):
     bits = (lax.axis_size("hid") - 1).bit_length()
-    rounds = [(3, 2, 1)] + [(1 << bit,) for bit in range(2, bits)]
+    rounds = [(3, 2, 1), (8,), (4,)] + [(1 << bit,) for bit in range(4, bits)]
     total, far = part, {}
     for at, masks in enumerate(rounds):
         sent = total.astype(jnp.bfloat16)

time: 50.6 us -> 52 us (1.028)
  waiting for transfers between devices: 13 us -> 14 us
    ppermute x9, waiting for transfers between devices: 8.31 us -> 9.33 us  [exchange(): lax.ppermute(x, 'hid', [(i, i ^ mask) for i in range(lax.axis_size('hid'))])]
  transfers between devices with their start and end apart: 12 -> 12, of which waited for: 7 -> 7; matrix products, arithmetic and copies ran while one was open for 10% -> 9% of each run, Pallas kernels for 0% -> 0%
where the time goes in v20:
time: 52 us; the launch traced here: 51.7 us
  blocking collectives  16 us (31%)
  waiting for transfers between devices  14 us (27%)
  starting transfers between devices  13.1 us (25%)
  matrix products  4.69 us (9%)
  local copies, waits for them, and re-layouts  1.54 us (3%)
  other arithmetic  1.34 us (3%)
  between operations  0.94 us (2%)
    all_to_all x1, blocking collectives, on_device(): rows = lax.all_to_all(both, 'hid', split_axis=1, concat_axis=0, tiled=True)  16 us
    ppermute x9, waiting for transfers between devices, exchange(): lax.ppermute(x, 'hid', [(i, i ^ mask) for i in range(lax.axis_size('hid'))])  9.33 us
    ppermute x9, starting transfers between devices, exchange(): lax.ppermute(x, 'hid', [(i, i ^ mask) for i in range(lax.axis_size('hid'))])  9.09 us
    all_to_all x1, waiting for transfers between devices, on_device(): lax.all_to_all(results, 'hid', split_axis=0, concat_axis=1, tiled=True)  4.68 us
    all_to_all x1, starting transfers between devices, on_device(): lax.all_to_all(results, 'hid', split_axis=0, concat_axis=1, tiled=True)  3.91 us
    dot_general x3, matrix products, inner_rows(): lax.dot_general(left, right, (((0,), (0,)), ((), ())), preferred_element_...  2.88 us
    dot_general x7, matrix products, dot(): return jnp.dot(left, right, preferred_element_type=jnp.float32)  1.09 us
  transfers between devices with their start and end apart: 12, of which 7 were waited for; matrix products, arithmetic and copies ran while one was open for 9% of the time, Pallas kernels for 0%

profile of v20, /device:TPU:0, one launch (start us, length us, event | category | flops | bytes accessed | tf_op | source)
XLA Modules:
  0.0 51.7 jit_solution(14650355117831322526)
XLA Ops:
  0.6 0.0 copy-start
  0.7 0.9 %pad_maximum_fusion.5 = bf16[6,16,512]{2,0,1:T(8,128)(2,1)S(1)} fusion(bf16[6,16,256]{2,0,1:T(8,128)(2,1)} %bitcast.32, bf16[6,16,256]{2,0,1:T(8,128)(2,1)} %bitcast.33), kind=kLoop, calls=%fused_computation.28 | loop fusion | flops 196608 | bytes 196608 | tf_op jit(solution)/shard_map/concatenate | solution.py:79
  1.6 0.0 copy-start.2
  1.6 16.0 %all_to_all.32 = bf16[6,16,512]{2,0,1:T(8,128)(2,1)S(1)} all-to-all(bf16[6,16,512]{2,0,1:T(8,128)(2,1)S(1)} %pad_maximum_fusion.5), channel_id=1, replica_groups=mesh['hid'=16,'seq'=2] {'hid'}, dimensions={1} | all-to-all | bytes 196608 | tf_op jit(solution)/shard_map/all_to_all | solution.py:82
  17.6 0.0 copy-start.1
  17.7 0.0 copy-done
  17.7 0.2 fusion.60
  17.9 0.0 copy-done.2
  17.9 0.2 fusion.62
  18.1 0.8 %collective-permute-start = (bf16[96,512]{1,0:T(8,128)(2,1)S(1)}, bf16[96,512]{1,0:T(8,128)(2,1)S(1)}, u32[]{:S(2)}, u32[]{:S(2)}) collective-permute-start(bf16[96,512]{1,0:T(8,128)(2,1)S(1)} %fusion.6), channel_id=1, source_target_pairs={{0,6},{2,4},{4,2},{6,0},{8,14},{10,12},{12,10},{14,8},{16,22},{18,... | collective-permute-start | bytes 294920 | tf_op jit(solution)/shard_map/ppermute | solution.py:10
  18.9 1.8 %collective-permute-start.1 = (bf16[96,512]{1,0:T(8,128)(2,1)S(1)}, bf16[96,512]{1,0:T(8,128)(2,1)S(1)}, u32[]{:S(2)}, u32[]{:S(2)}) collective-permute-start(bf16[96,512]{1,0:T(8,128)(2,1)S(1)} %fusion.6), channel_id=1, source_target_pairs={{0,4},{2,6},{4,0},{6,2},{8,12},{10,14},{12,8},{14,10},{16,20},{18,... | collective-permute-start | bytes 294920 | tf_op jit(solution)/shard_map/ppermute | solution.py:10
  20.7 0.9 %collective-permute-start.2 = (bf16[96,512]{1,0:T(8,128)(2,1)S(1)}, bf16[96,512]{1,0:T(8,128)(2,1)S(1)}, u32[]{:S(2)}, u32[]{:S(2)}) collective-permute-start(bf16[96,512]{1,0:T(8,128)(2,1)S(1)} %fusion.6), channel_id=1, source_target_pairs={{0,2},{2,0},{4,6},{6,4},{8,10},{10,8},{12,14},{14,12},{16,18},{18,... | collective-permute-start | bytes 294920 | tf_op jit(solution)/shard_map/ppermute | solution.py:10
  21.7 0.0 copy-done.1
  21.7 0.3 fusion.69
  22.1 0.8 %collective-permute-start.4 = (bf16[96,512]{1,0:T(8,128)(2,1)S(1)}, bf16[96,512]{1,0:T(8,128)(2,1)S(1)}, u32[]{:S(2)}, u32[]{:S(2)}) collective-permute-start(bf16[96,512]{1,0:T(8,128)(2,1)S(1)} %get-tuple-element.57), channel_id=1, source_target_pairs={{0,8},{2,10},{4,12},{6,14},{8,0},{10,2},{12,4},{14,6},{16,24},{18,... | collective-permute-start | bytes 294920 | tf_op jit(solution)/shard_map/ppermute | solution.py:10
  22.9 0.9 %collective-permute-done = bf16[96,512]{1,0:T(8,128)(2,1)S(1)} collective-permute-done((bf16[96,512]{1,0:T(8,128)(2,1)S(1)}, bf16[96,512]{1,0:T(8,128)(2,1)S(1)}, u32[]{:S(2)}, u32[]{:S(2)}) %collective-permute-start) | collective-permute-done | bytes 98336 | tf_op jit(solution)/shard_map/ppermute | solution.py:10
  23.8 0.8 %collective-permute-done.1 = bf16[96,512]{1,0:T(8,128)(2,1)S(1)} collective-permute-done((bf16[96,512]{1,0:T(8,128)(2,1)S(1)}, bf16[96,512]{1,0:T(8,128)(2,1)S(1)}, u32[]{:S(2)}, u32[]{:S(2)}) %collective-permute-start.1) | collective-permute-done | bytes 98336 | tf_op jit(solution)/shard_map/ppermute | solution.py:10
  24.6 0.8 %collective-permute-done.2 = bf16[96,512]{1,0:T(8,128)(2,1)S(1)} collective-permute-done((bf16[96,512]{1,0:T(8,128)(2,1)S(1)}, bf16[96,512]{1,0:T(8,128)(2,1)S(1)}, u32[]{:S(2)}, u32[]{:S(2)}) %collective-permute-start.2) | collective-permute-done | bytes 98336 | tf_op jit(solution)/shard_map/ppermute | solution.py:10
  25.4 0.5 collective-permute-start.3
  25.8 2.5 %collective-permute-start.7 = (bf16[96,512]{1,0:T(8,128)(2,1)S(1)}, bf16[96,512]{1,0:T(8,128)(2,1)S(1)}, u32[]{:S(2)}, u32[]{:S(2)}) collective-permute-start(bf16[96,512]{1,0:T(8,128)(2,1)S(1)} %get-tuple-element.33), channel_id=1, source_target_pairs={{0,16},{2,18},{4,20},{6,22},{8,24},{10,26},{12,28},{14,30},{16,0},... | collective-permute-start | bytes 294920 | tf_op jit(solution)/shard_map/ppermute | solution.py:10
  28.4 0.6 %collective-permute-start.6 = (bf16[96,512]{1,0:T(8,128)(2,1)S(1)}, bf16[96,512]{1,0:T(8,128)(2,1)S(1)}, u32[]{:S(2)}, u32[]{:S(2)}) collective-permute-start(bf16[96,512]{1,0:T(8,128)(2,1)S(1)} %get-tuple-element.31), channel_id=1, source_target_pairs={{0,4},{2,6},{4,0},{6,2},{8,12},{10,14},{12,8},{14,10},{16,20},{18,... | collective-permute-start | bytes 294920 | tf_op jit(solution)/shard_map/ppermute | solution.py:10
  28.9 1.1 %collective-permute-start.5 = (bf16[96,512]{1,0:T(8,128)(2,1)S(1)}, bf16[96,512]{1,0:T(8,128)(2,1)S(1)}, u32[]{:S(2)}, u32[]{:S(2)}) collective-permute-start(bf16[96,512]{1,0:T(8,128)(2,1)S(1)} %get-tuple-element.30), channel_id=1, source_target_pairs={{0,2},{2,0},{4,6},{6,4},{8,10},{10,8},{12,14},{14,12},{16,18},{18,... | collective-permute-start | bytes 294920 | tf_op jit(solution)/shard_map/ppermute | solution.py:10
  30.0 0.0 collective-permute-done.4
  30.0 3.3 %collective-permute-done.3 = bf16[96,512]{1,0:T(8,128)(2,1)S(1)} collective-permute-done((bf16[96,512]{1,0:T(8,128)(2,1)S(1)}, bf16[96,512]{1,0:T(8,128)(2,1)S(1)}, u32[]{:S(2)}, u32[]{:S(2)}) %collective-permute-start.3) | collective-permute-done | bytes 98336 | tf_op jit(solution)/shard_map/ppermute | solution.py:10
  33.3 0.1 collective-permute-start.8
  33.4 0.1 fusion.10
  33.6 0.2 fusion.14
  33.8 0.0 collective-permute-done.5
  33.8 0.0 collective-permute-done.6
  33.9 0.5 collective-permute-done.7
  34.5 0.1 collective-permute-start.10
  34.6 0.2 convolution_add_fusion.2
  34.7 0.2 fusion
  34.9 3.1 %collective-permute-done.8 = bf16[96,512]{1,0:T(8,128)(2,1)S(1)} collective-permute-done((bf16[96,512]{1,0:T(8,128)(2,1)S(1)}, bf16[96,512]{1,0:T(8,128)(2,1)S(1)}, u32[]{:S(2)}, u32[]{:S(2)}) %collective-permute-start.8) | collective-permute-done | bytes 98336 | tf_op jit(solution)/shard_map/ppermute | solution.py:10
  38.1 0.1 fusion.43
  38.2 0.2 fusion.23
  38.5 0.2 fusion.2
  38.7 0.7 %all_to_all.27 = bf16[16,6,512]{2,1,0:T(8,128)(2,1)} reshape(bf16[96,512]{1,0:T(8,128)(2,1)S(1)} %pad_maximum_fusion.6) | data formatting | bytes 196608 | tf_op jit(solution)/shard_map/all_to_all | solution.py:108
  39.3 3.9 %all-to-all-start.1 = ((bf16[16,6,512]{2,1,0:T(8,128)(2,1)}), bf16[16,6,512]{2,1,0:T(8,128)(2,1)S(1)}, u32[]{:S(2)}, u32[]{:S(2)}) async-start(bf16[16,6,512]{2,1,0:T(8,128)(2,1)} %all_to_all.27), calls=%async_computation.1 | async-start | bytes 262144 | tf_op jit(solution)/shard_map/all_to_all | solution.py:108
  43.3 0.1 collective-permute-start.9
  43.3 0.0 collective-permute-done.10
  43.5 1.1 %convolution_multiply_fusion = f32[640,256]{1,0:T(8,128)} fusion(bf16[96,640]{1,0:T(8,128)(2,1)S(1)} %constant_dynamic-update-slice_fusion.11, bf16[96,640]{1,0:T(8,128)(2,1)S(1)} %get-tuple-element.53, bf16[96,256]{1,0:T(8,128)(2,1)S(1)} %get-tuple-element.46, bf16[96,256]{1,0:T(8,128)(2,1)S(1)} %slice.176), kind=kOutput, calls=%fused_computation | convolution fusion | flops 63766528 | bytes 999424 | tf_op jit(solution)/shard_map/dot_general | solution.py:32
  44.6 0.0 collective-permute-done.9
  44.6 0.9 %convolution_multiply_fusion.1 = f32[128,256]{1,0:T(8,128)} fusion(bf16[96,256]{1,0:T(8,128)(2,1)S(1)} %get-tuple-element.46, bf16[96,256]{1,0:T(8,128)(2,1)S(1)} %slice.176, bf16[96,128]{1,0:T(8,128)(2,1)S(1)} %get-tuple-element.55, bf16[96,128]{1,0:T(8,128)(2,1)S(1)} %get-tuple-element.49), kind=kOutput, calls=%fused_computation.1 | convolution fusion | flops 12910592 | bytes 278528 | tf_op jit(solution)/shard_map/dot_general | solution.py:32
  45.5 0.9 %convolution_multiply_fusion.2 = f32[256,128]{1,0:T(8,128)} fusion(bf16[96,256]{1,0:T(8,128)(2,1)S(1)} %get-tuple-element.45, bf16[96,256]{1,0:T(8,128)(2,1)S(1)} %fusion.28, bf16[96,128]{1,0:T(8,128)(2,1)S(1)} %get-tuple-element.56, bf16[96,128]{1,0:T(8,128)(2,1)S(1)} %get-tuple-element.51), kind=kOutput, calls=%fused_computation.2 | convolution fusion | flops 12910592 | bytes 278528 | tf_op jit(solution)/shard_map/dot_general | solution.py:32
  46.4 4.7 %all-to-all-done.1 = bf16[16,6,512]{2,1,0:T(8,128)(2,1)S(1)} async-done(((bf16[16,6,512]{2,1,0:T(8,128)(2,1)}), bf16[16,6,512]{2,1,0:T(8,128)(2,1)S(1)}, u32[]{:S(2)}, u32[]{:S(2)}) %all-to-all-start.1) | async-done | bytes 98336 | tf_op jit(solution)/shard_map/all_to_all | solution.py:108
  51.0 0.7 %fusion.67 = (bf16[6,16,256]{2,0,1:T(8,128)(2,1)}, bf16[6,16,256]{2,0,1:T(8,128)(2,1)}) fusion(bf16[6,16,512]{2,0,1:T(8,128)(2,1)S(1)} %bitcast.31), kind=kLoop, calls=%fused_computation.110 | loop fusion | bytes 196608 | tf_op jit(solution)/shard_map/slice | solution.py:111
  (29 shorter events, 0.6 us)
Async XLA Ops:
  0.6 17.1 %copy-start = (bf16[256,256]{1,0:T(8,128)(2,1)S(1)}, bf16[256,256]{1,0:T(8,128)(2,1)}, u32[]{:S(2)}) copy-start(bf16[256,256]{1,0:T(8,128)(2,1)} %param.8) | copy-start | bytes 393220
  1.6 16.3 %copy-start.2 = (bf16[256,256]{1,0:T(8,128)(2,1)S(1)}, bf16[256,256]{1,0:T(8,128)(2,1)}, u32[]{:S(2)}) copy-start(bf16[256,256]{1,0:T(8,128)(2,1)} %param.7) | copy-start | bytes 393220
  17.6 4.0 %copy-start.1 = (bf16[1,5,256,256]{3,2,1,0:T(8,128)(2,1)S(1)}, bf16[1,5,256,256]{3,2,1,0:T(8,128)(2,1)}, u32[]{:S(2)}) copy-start(bf16[1,5,256,256]{3,2,1,0:T(8,128)(2,1)} %param.6) | copy-start | bytes 1966084
  18.1 5.7 %collective-permute-start = (bf16[96,512]{1,0:T(8,128)(2,1)S(1)}, bf16[96,512]{1,0:T(8,128)(2,1)S(1)}, u32[]{:S(2)}, u32[]{:S(2)}) collective-permute-start(bf16[96,512]{1,0:T(8,128)(2,1)S(1)} %fusion.6), channel_id=1, source_target_pairs={{0,6},{2,4},{4,2},{6,0},{8,14},{10,12},{12,10},{14,8},{16,22},{18,... | collective-permute-start | bytes 294920 | tf_op jit(solution)/shard_map/ppermute | solution.py:10
  18.9 5.7 %collective-permute-start.1 = (bf16[96,512]{1,0:T(8,128)(2,1)S(1)}, bf16[96,512]{1,0:T(8,128)(2,1)S(1)}, u32[]{:S(2)}, u32[]{:S(2)}) collective-permute-start(bf16[96,512]{1,0:T(8,128)(2,1)S(1)} %fusion.6), channel_id=1, source_target_pairs={{0,4},{2,6},{4,0},{6,2},{8,12},{10,14},{12,8},{14,10},{16,20},{18,... | collective-permute-start | bytes 294920 | tf_op jit(solution)/shard_map/ppermute | solution.py:10
  20.7 4.6 %collective-permute-start.2 = (bf16[96,512]{1,0:T(8,128)(2,1)S(1)}, bf16[96,512]{1,0:T(8,128)(2,1)S(1)}, u32[]{:S(2)}, u32[]{:S(2)}) collective-permute-start(bf16[96,512]{1,0:T(8,128)(2,1)S(1)} %fusion.6), channel_id=1, source_target_pairs={{0,2},{2,0},{4,6},{6,4},{8,10},{10,8},{12,14},{14,12},{16,18},{18,... | collective-permute-start | bytes 294920 | tf_op jit(solution)/shard_map/ppermute | solution.py:10
  22.1 7.9 %collective-permute-start.4 = (bf16[96,512]{1,0:T(8,128)(2,1)S(1)}, bf16[96,512]{1,0:T(8,128)(2,1)S(1)}, u32[]{:S(2)}, u32[]{:S(2)}) collective-permute-start(bf16[96,512]{1,0:T(8,128)(2,1)S(1)} %get-tuple-element.57), channel_id=1, source_target_pairs={{0,8},{2,10},{4,12},{6,14},{8,0},{10,2},{12,4},{14,6},{16,24},{18,... | collective-permute-start | bytes 294920 | tf_op jit(solution)/shard_map/ppermute | solution.py:10
  25.4 8.0 %collective-permute-start.3 = (bf16[96,512]{1,0:T(8,128)(2,1)S(1)}, bf16[96,512]{1,0:T(8,128)(2,1)S(1)}, u32[]{:S(2)}, u32[]{:S(2)}) collective-permute-start(bf16[96,512]{1,0:T(8,128)(2,1)S(1)} %get-tuple-element.27), channel_id=1, source_target_pairs={{0,16},{2,18},{4,20},{6,22},{8,24},{10,26},{12,28},{14,30},{16,0},... | collective-permute-start | bytes 294920 | tf_op jit(solution)/shard_map/ppermute | solution.py:10
  25.8 8.6 %collective-permute-start.7 = (bf16[96,512]{1,0:T(8,128)(2,1)S(1)}, bf16[96,512]{1,0:T(8,128)(2,1)S(1)}, u32[]{:S(2)}, u32[]{:S(2)}) collective-permute-start(bf16[96,512]{1,0:T(8,128)(2,1)S(1)} %get-tuple-element.33), channel_id=1, source_target_pairs={{0,16},{2,18},{4,20},{6,22},{8,24},{10,26},{12,28},{14,30},{16,0},... | collective-permute-start | bytes 294920 | tf_op jit(solution)/shard_map/ppermute | solution.py:10
  28.4 5.4 %collective-permute-start.6 = (bf16[96,512]{1,0:T(8,128)(2,1)S(1)}, bf16[96,512]{1,0:T(8,128)(2,1)S(1)}, u32[]{:S(2)}, u32[]{:S(2)}) collective-permute-start(bf16[96,512]{1,0:T(8,128)(2,1)S(1)} %get-tuple-element.31), channel_id=1, source_target_pairs={{0,4},{2,6},{4,0},{6,2},{8,12},{10,14},{12,8},{14,10},{16,20},{18,... | collective-permute-start | bytes 294920 | tf_op jit(solution)/shard_map/ppermute | solution.py:10
  28.9 4.8 %collective-permute-start.5 = (bf16[96,512]{1,0:T(8,128)(2,1)S(1)}, bf16[96,512]{1,0:T(8,128)(2,1)S(1)}, u32[]{:S(2)}, u32[]{:S(2)}) collective-permute-start(bf16[96,512]{1,0:T(8,128)(2,1)S(1)} %get-tuple-element.30), channel_id=1, source_target_pairs={{0,2},{2,0},{4,6},{6,4},{8,10},{10,8},{12,14},{14,12},{16,18},{18,... | collective-permute-start | bytes 294920 | tf_op jit(solution)/shard_map/ppermute | solution.py:10
  33.3 4.7 %collective-permute-start.8 = (bf16[96,512]{1,0:T(8,128)(2,1)S(1)}, bf16[96,512]{1,0:T(8,128)(2,1)S(1)}, u32[]{:S(2)}, u32[]{:S(2)}) collective-permute-start(bf16[96,512]{1,0:T(8,128)(2,1)S(1)} %fusion.8), channel_id=1, source_target_pairs={{0,8},{2,10},{4,12},{6,14},{8,0},{10,2},{12,4},{14,6},{16,24},{18,... | collective-permute-start | bytes 294920 | tf_op jit(solution)/shard_map/ppermute | solution.py:10
  34.5 8.9 %collective-permute-start.10 = (bf16[96,1024]{1,0:T(8,128)(2,1)S(1)}, bf16[96,1024]{1,0:T(8,128)(2,1)S(1)}, u32[]{:S(2)}, u32[]{:S(2)}) collective-permute-start(bf16[96,1024]{1,0:T(8,128)(2,1)S(1)} %constant_dynamic-update-slice_fusion.5), channel_id=1, source_target_pairs={{0,1},{1,0},{2,3},{3,2},{4,5},{5,4},{6,7},{7,6},{8,9},{9,8},{10,11... | collective-permute-start | bytes 589832 | tf_op jit(solution)/shard_map/ppermute | solution.py:14
  39.3 11.7 %all-to-all-start.1 = ((bf16[16,6,512]{2,1,0:T(8,128)(2,1)}), bf16[16,6,512]{2,1,0:T(8,128)(2,1)S(1)}, u32[]{:S(2)}, u32[]{:S(2)}) async-start(bf16[16,6,512]{2,1,0:T(8,128)(2,1)} %all_to_all.27), calls=%async_computation.1 | async-start | bytes 262144 | tf_op jit(solution)/shard_map/all_to_all | solution.py:108
  43.3 1.4 %collective-permute-start.9 = (bf16[96,256]{1,0:T(8,128)(2,1)S(1)}, bf16[96,256]{1,0:T(8,128)(2,1)S(1)}, u32[]{:S(2)}, u32[]{:S(2)}) collective-permute-start(bf16[96,256]{1,0:T(8,128)(2,1)S(1)} %pad_maximum_fusion.10), channel_id=1, source_target_pairs={{0,1},{1,0},{2,3},{3,2},{4,5},{5,4},{6,7},{7,6},{8,9},{9,8},{10,11... | collective-permute-start | bytes 147464 | tf_op jit(solution)/shard_map/ppermute | solution.py:14

commit v21 on v18

--- a/solution.py
+++ b/solution.py
@@ -51,7 +51,7 @@
             sent, data = lax.optimization_barrier((sent, data))
         got = [exchange(sent, mask) for mask in masks]
         far = far | {mask: exchange(beside[mask], mask) for mask in beside}
-        if at == 1:
+        if at == len(rounds) - 1:
             got, early = lax.optimization_barrier((got, early))
             far = far | early
         else:

time: 50 us -> 54.4 us (1.088)
  waiting for transfers between devices: 12.9 us -> 16.5 us
  starting transfers between devices: 12.2 us -> 13.1 us
    all_to_all x1, waiting for transfers between devices: 4.65 us -> 7.02 us  [on_device(): lax.all_to_all(results, 'hid', split_axis=0, concat_axis=1, tiled=True)]
    ppermute x9, waiting for transfers between devices: 8.3 us -> 9.49 us  [exchange(): lax.ppermute(x, 'hid', [(i, i ^ mask) for i in range(lax.axis_size('hid'))])]
  transfers between devices with their start and end apart: 12 -> 12, of which waited for: 7 -> 8; matrix products, arithmetic and copies ran while one was open for 10% -> 5% of each run, Pallas kernels for 0% -> 0%
where the time goes in v21:
time: 54.4 us; the launch traced here: 54.1 us
  waiting for transfers between devices  16.5 us (30%)
  blocking collectives  16 us (29%)
  starting transfers between devices  13.1 us (24%)
  matrix products  4.69 us (9%)
  local copies, waits for them, and re-layouts  1.55 us (3%)
  other arithmetic  1.34 us (2%)
  between operations  0.93 us (2%)
    all_to_all x1, blocking collectives, on_device(): rows = lax.all_to_all(both, 'hid', split_axis=1, concat_axis=0, tiled=True)  16 us
    ppermute x9, waiting for transfers between devices, exchange(): lax.ppermute(x, 'hid', [(i, i ^ mask) for i in range(lax.axis_size('hid'))])  9.49 us
    ppermute x9, starting transfers between devices, exchange(): lax.ppermute(x, 'hid', [(i, i ^ mask) for i in range(lax.axis_size('hid'))])  8.71 us
    all_to_all x1, waiting for transfers between devices, on_device(): lax.all_to_all(results, 'hid', split_axis=0, concat_axis=1, tiled=True)  7.02 us
    all_to_all x1, starting transfers between devices, on_device(): lax.all_to_all(results, 'hid', split_axis=0, concat_axis=1, tiled=True)  3.74 us
    dot_general x3, matrix products, inner_rows(): lax.dot_general(left, right, (((0,), (0,)), ((), ())), preferred_element_...  2.88 us
  transfers between devices with their start and end apart: 12, of which 8 were waited for; matrix products, arithmetic and copies ran while one was open for 5% of the time, Pallas kernels for 0%

profile of v21, /device:TPU:0, one launch (start us, length us, event | category | flops | bytes accessed | tf_op | source)
XLA Modules:
  0.0 54.1 jit_solution(15972686518200334601)
XLA Ops:
  0.6 0.0 copy-start
  0.7 0.9 %pad_maximum_fusion.5 = bf16[6,16,512]{2,0,1:T(8,128)(2,1)S(1)} fusion(bf16[6,16,256]{2,0,1:T(8,128)(2,1)} %bitcast.32, bf16[6,16,256]{2,0,1:T(8,128)(2,1)} %bitcast.33), kind=kLoop, calls=%fused_computation.28 | loop fusion | flops 196608 | bytes 196608 | tf_op jit(solution)/shard_map/concatenate | solution.py:79
  1.6 0.0 copy-start.2
  1.6 16.0 %all_to_all.32 = bf16[6,16,512]{2,0,1:T(8,128)(2,1)S(1)} all-to-all(bf16[6,16,512]{2,0,1:T(8,128)(2,1)S(1)} %pad_maximum_fusion.5), channel_id=1, replica_groups=mesh['hid'=16,'seq'=2] {'hid'}, dimensions={1} | all-to-all | bytes 196608 | tf_op jit(solution)/shard_map/all_to_all | solution.py:82
  17.6 0.0 copy-start.1
  17.7 0.0 copy-done
  17.7 0.2 fusion.58
  17.9 0.0 copy-done.2
  17.9 0.2 fusion.60
  18.1 0.8 %collective-permute-start = (bf16[96,512]{1,0:T(8,128)(2,1)S(1)}, bf16[96,512]{1,0:T(8,128)(2,1)S(1)}, u32[]{:S(2)}, u32[]{:S(2)}) collective-permute-start(bf16[96,512]{1,0:T(8,128)(2,1)S(1)} %fusion.5), channel_id=1, source_target_pairs={{0,6},{2,4},{4,2},{6,0},{8,14},{10,12},{12,10},{14,8},{16,22},{18,... | collective-permute-start | bytes 294920 | tf_op jit(solution)/shard_map/ppermute | solution.py:10
  18.9 1.8 %collective-permute-start.1 = (bf16[96,512]{1,0:T(8,128)(2,1)S(1)}, bf16[96,512]{1,0:T(8,128)(2,1)S(1)}, u32[]{:S(2)}, u32[]{:S(2)}) collective-permute-start(bf16[96,512]{1,0:T(8,128)(2,1)S(1)} %fusion.5), channel_id=1, source_target_pairs={{0,4},{2,6},{4,0},{6,2},{8,12},{10,14},{12,8},{14,10},{16,20},{18,... | collective-permute-start | bytes 294920 | tf_op jit(solution)/shard_map/ppermute | solution.py:10
  20.7 0.9 %collective-permute-start.2 = (bf16[96,512]{1,0:T(8,128)(2,1)S(1)}, bf16[96,512]{1,0:T(8,128)(2,1)S(1)}, u32[]{:S(2)}, u32[]{:S(2)}) collective-permute-start(bf16[96,512]{1,0:T(8,128)(2,1)S(1)} %fusion.5), channel_id=1, source_target_pairs={{0,2},{2,0},{4,6},{6,4},{8,10},{10,8},{12,14},{14,12},{16,18},{18,... | collective-permute-start | bytes 294920 | tf_op jit(solution)/shard_map/ppermute | solution.py:10
  21.7 0.0 copy-done.1
  21.7 0.3 fusion.67
  22.1 1.7 %collective-permute-done = bf16[96,512]{1,0:T(8,128)(2,1)S(1)} collective-permute-done((bf16[96,512]{1,0:T(8,128)(2,1)S(1)}, bf16[96,512]{1,0:T(8,128)(2,1)S(1)}, u32[]{:S(2)}, u32[]{:S(2)}) %collective-permute-start) | collective-permute-done | bytes 98336 | tf_op jit(solution)/shard_map/ppermute | solution.py:10
  23.8 0.8 %collective-permute-done.1 = bf16[96,512]{1,0:T(8,128)(2,1)S(1)} collective-permute-done((bf16[96,512]{1,0:T(8,128)(2,1)S(1)}, bf16[96,512]{1,0:T(8,128)(2,1)S(1)}, u32[]{:S(2)}, u32[]{:S(2)}) %collective-permute-start.1) | collective-permute-done | bytes 98336 | tf_op jit(solution)/shard_map/ppermute | solution.py:10
  24.6 0.8 %collective-permute-done.2 = bf16[96,512]{1,0:T(8,128)(2,1)S(1)} collective-permute-done((bf16[96,512]{1,0:T(8,128)(2,1)S(1)}, bf16[96,512]{1,0:T(8,128)(2,1)S(1)}, u32[]{:S(2)}, u32[]{:S(2)}) %collective-permute-start.2) | collective-permute-done | bytes 98336 | tf_op jit(solution)/shard_map/ppermute | solution.py:10
  25.4 0.3 collective-permute-start.3
  25.7 1.8 %collective-permute-start.7 = (bf16[96,512]{1,0:T(8,128)(2,1)S(1)}, bf16[96,512]{1,0:T(8,128)(2,1)S(1)}, u32[]{:S(2)}, u32[]{:S(2)}) collective-permute-start(bf16[96,512]{1,0:T(8,128)(2,1)S(1)} %get-tuple-element.58), channel_id=1, source_target_pairs={{0,8},{2,10},{4,12},{6,14},{8,0},{10,2},{12,4},{14,6},{16,24},{18,... | collective-permute-start | bytes 294920 | tf_op jit(solution)/shard_map/ppermute | solution.py:10
  27.5 0.4 collective-permute-start.8
  27.9 0.7 %collective-permute-start.5 = (bf16[96,512]{1,0:T(8,128)(2,1)S(1)}, bf16[96,512]{1,0:T(8,128)(2,1)S(1)}, u32[]{:S(2)}, u32[]{:S(2)}) collective-permute-start(bf16[96,512]{1,0:T(8,128)(2,1)S(1)} %get-tuple-element.30), channel_id=1, source_target_pairs={{0,4},{2,6},{4,0},{6,2},{8,12},{10,14},{12,8},{14,10},{16,20},{18,... | collective-permute-start | bytes 294920 | tf_op jit(solution)/shard_map/ppermute | solution.py:10
  28.6 1.5 %collective-permute-start.4 = (bf16[96,512]{1,0:T(8,128)(2,1)S(1)}, bf16[96,512]{1,0:T(8,128)(2,1)S(1)}, u32[]{:S(2)}, u32[]{:S(2)}) collective-permute-start(bf16[96,512]{1,0:T(8,128)(2,1)S(1)} %get-tuple-element.29), channel_id=1, source_target_pairs={{0,2},{2,0},{4,6},{6,4},{8,10},{10,8},{12,14},{14,12},{16,18},{18,... | collective-permute-start | bytes 294920 | tf_op jit(solution)/shard_map/ppermute | solution.py:10
  30.1 1.6 %collective-permute-done.3 = bf16[96,512]{1,0:T(8,128)(2,1)S(1)} collective-permute-done((bf16[96,512]{1,0:T(8,128)(2,1)S(1)}, bf16[96,512]{1,0:T(8,128)(2,1)S(1)}, u32[]{:S(2)}, u32[]{:S(2)}) %collective-permute-start.3) | collective-permute-done | bytes 98336 | tf_op jit(solution)/shard_map/ppermute | solution.py:10
  31.7 0.5 collective-permute-start.6
  32.2 0.1 fusion.13
  32.3 0.9 %collective-permute-done.4 = bf16[96,512]{1,0:T(8,128)(2,1)S(1)} collective-permute-done((bf16[96,512]{1,0:T(8,128)(2,1)S(1)}, bf16[96,512]{1,0:T(8,128)(2,1)S(1)}, u32[]{:S(2)}, u32[]{:S(2)}) %collective-permute-start.4) | collective-permute-done | bytes 98336 | tf_op jit(solution)/shard_map/ppermute | solution.py:10
  33.2 0.2 convolution_add_fusion.3
  33.4 0.0 collective-permute-done.5
  33.5 0.0 collective-permute-done.7
  33.5 1.2 %collective-permute-done.8 = bf16[96,512]{1,0:T(8,128)(2,1)S(1)} collective-permute-done((bf16[96,512]{1,0:T(8,128)(2,1)S(1)}, bf16[96,512]{1,0:T(8,128)(2,1)S(1)}, u32[]{:S(2)}, u32[]{:S(2)}) %collective-permute-start.8) | collective-permute-done | bytes 98336 | tf_op jit(solution)/shard_map/ppermute | solution.py:10
  34.7 2.6 %collective-permute-done.6 = bf16[96,512]{1,0:T(8,128)(2,1)S(1)} collective-permute-done((bf16[96,512]{1,0:T(8,128)(2,1)S(1)}, bf16[96,512]{1,0:T(8,128)(2,1)S(1)}, u32[]{:S(2)}, u32[]{:S(2)}) %collective-permute-start.6) | collective-permute-done | bytes 98336 | tf_op jit(solution)/shard_map/ppermute | solution.py:10
  37.3 0.1 fusion.9
  37.5 0.2 fusion
  37.7 0.2 convolution_add_fusion.1
  37.8 0.2 fusion.1
  38.0 0.2 fusion.22
  38.2 0.7 %all_to_all.27 = bf16[16,6,512]{2,1,0:T(8,128)(2,1)} reshape(bf16[96,512]{1,0:T(8,128)(2,1)S(1)} %pad_maximum_fusion.6) | data formatting | bytes 196608 | tf_op jit(solution)/shard_map/all_to_all | solution.py:108
  38.9 3.7 %all-to-all-start.1 = ((bf16[16,6,512]{2,1,0:T(8,128)(2,1)}), bf16[16,6,512]{2,1,0:T(8,128)(2,1)S(1)}, u32[]{:S(2)}, u32[]{:S(2)}) async-start(bf16[16,6,512]{2,1,0:T(8,128)(2,1)} %all_to_all.27), calls=%async_computation.1 | async-start | bytes 262144 | tf_op jit(solution)/shard_map/all_to_all | solution.py:108
  42.7 0.1 collective-permute-start.9
  42.9 0.6 %collective-permute-start.10 = (bf16[96,1024]{1,0:T(8,128)(2,1)S(1)}, bf16[96,1024]{1,0:T(8,128)(2,1)S(1)}, u32[]{:S(2)}, u32[]{:S(2)}) collective-permute-start(bf16[96,1024]{1,0:T(8,128)(2,1)S(1)} %constant_dynamic-update-slice_fusion.5), channel_id=1, source_target_pairs={{0,1},{1,0},{2,3},{3,2},{4,5},{5,4},{6,7},{7,6},{8,9},{9,8},{10,11... | collective-permute-start | bytes 589832 | tf_op jit(solution)/shard_map/ppermute | solution.py:14
  43.5 7.0 %all-to-all-done.1 = bf16[16,6,512]{2,1,0:T(8,128)(2,1)S(1)} async-done(((bf16[16,6,512]{2,1,0:T(8,128)(2,1)}), bf16[16,6,512]{2,1,0:T(8,128)(2,1)S(1)}, u32[]{:S(2)}, u32[]{:S(2)}) %all-to-all-start.1) | async-done | bytes 98336 | tf_op jit(solution)/shard_map/all_to_all | solution.py:108
  50.5 0.7 %fusion.65 = (bf16[6,16,256]{2,0,1:T(8,128)(2,1)}, bf16[6,16,256]{2,0,1:T(8,128)(2,1)}) fusion(bf16[6,16,512]{2,0,1:T(8,128)(2,1)S(1)} %bitcast.31), kind=kLoop, calls=%fused_computation.109 | loop fusion | bytes 196608 | tf_op jit(solution)/shard_map/slice | solution.py:111
  51.1 0.0 collective-permute-done.10
  51.3 1.1 %convolution_multiply_fusion = f32[640,256]{1,0:T(8,128)} fusion(bf16[96,640]{1,0:T(8,128)(2,1)S(1)} %constant_dynamic-update-slice_fusion.11, bf16[96,640]{1,0:T(8,128)(2,1)S(1)} %get-tuple-element.53, bf16[96,256]{1,0:T(8,128)(2,1)S(1)} %get-tuple-element.46, bf16[96,256]{1,0:T(8,128)(2,1)S(1)} %slice.176), kind=kOutput, calls=%fused_computation | convolution fusion | flops 63766528 | bytes 999424 | tf_op jit(solution)/shard_map/dot_general | solution.py:32
  52.4 0.0 collective-permute-done.9
  52.4 0.9 %convolution_multiply_fusion.1 = f32[128,256]{1,0:T(8,128)} fusion(bf16[96,256]{1,0:T(8,128)(2,1)S(1)} %get-tuple-element.46, bf16[96,256]{1,0:T(8,128)(2,1)S(1)} %slice.176, bf16[96,128]{1,0:T(8,128)(2,1)S(1)} %get-tuple-element.55, bf16[96,128]{1,0:T(8,128)(2,1)S(1)} %get-tuple-element.49), kind=kOutput, calls=%fused_computation.1 | convolution fusion | flops 12910592 | bytes 278528 | tf_op jit(solution)/shard_map/dot_general | solution.py:32
  53.3 0.9 %convolution_multiply_fusion.2 = f32[256,128]{1,0:T(8,128)} fusion(bf16[96,256]{1,0:T(8,128)(2,1)S(1)} %get-tuple-element.45, bf16[96,256]{1,0:T(8,128)(2,1)S(1)} %fusion.27, bf16[96,128]{1,0:T(8,128)(2,1)S(1)} %get-tuple-element.56, bf16[96,128]{1,0:T(8,128)(2,1)S(1)} %get-tuple-element.51), kind=kOutput, calls=%fused_computation.2 | convolution fusion | flops 12910592 | bytes 278528 | tf_op jit(solution)/shard_map/dot_general | solution.py:32
  (29 shorter events, 0.6 us)
Async XLA Ops:
  0.6 17.1 %copy-start = (bf16[256,256]{1,0:T(8,128)(2,1)S(1)}, bf16[256,256]{1,0:T(8,128)(2,1)}, u32[]{:S(2)}) copy-start(bf16[256,256]{1,0:T(8,128)(2,1)} %param.8) | copy-start | bytes 393220
  1.6 16.3 %copy-start.2 = (bf16[256,256]{1,0:T(8,128)(2,1)S(1)}, bf16[256,256]{1,0:T(8,128)(2,1)}, u32[]{:S(2)}) copy-start(bf16[256,256]{1,0:T(8,128)(2,1)} %param.7) | copy-start | bytes 393220
  17.6 4.0 %copy-start.1 = (bf16[1,5,256,256]{3,2,1,0:T(8,128)(2,1)S(1)}, bf16[1,5,256,256]{3,2,1,0:T(8,128)(2,1)}, u32[]{:S(2)}) copy-start(bf16[1,5,256,256]{3,2,1,0:T(8,128)(2,1)} %param.6) | copy-start | bytes 1966084
  18.1 5.7 %collective-permute-start = (bf16[96,512]{1,0:T(8,128)(2,1)S(1)}, bf16[96,512]{1,0:T(8,128)(2,1)S(1)}, u32[]{:S(2)}, u32[]{:S(2)}) collective-permute-start(bf16[96,512]{1,0:T(8,128)(2,1)S(1)} %fusion.5), channel_id=1, source_target_pairs={{0,6},{2,4},{4,2},{6,0},{8,14},{10,12},{12,10},{14,8},{16,22},{18,... | collective-permute-start | bytes 294920 | tf_op jit(solution)/shard_map/ppermute | solution.py:10
  18.9 5.7 %collective-permute-start.1 = (bf16[96,512]{1,0:T(8,128)(2,1)S(1)}, bf16[96,512]{1,0:T(8,128)(2,1)S(1)}, u32[]{:S(2)}, u32[]{:S(2)}) collective-permute-start(bf16[96,512]{1,0:T(8,128)(2,1)S(1)} %fusion.5), channel_id=1, source_target_pairs={{0,4},{2,6},{4,0},{6,2},{8,12},{10,14},{12,8},{14,10},{16,20},{18,... | collective-permute-start | bytes 294920 | tf_op jit(solution)/shard_map/ppermute | solution.py:10
  20.7 4.6 %collective-permute-start.2 = (bf16[96,512]{1,0:T(8,128)(2,1)S(1)}, bf16[96,512]{1,0:T(8,128)(2,1)S(1)}, u32[]{:S(2)}, u32[]{:S(2)}) collective-permute-start(bf16[96,512]{1,0:T(8,128)(2,1)S(1)} %fusion.5), channel_id=1, source_target_pairs={{0,2},{2,0},{4,6},{6,4},{8,10},{10,8},{12,14},{14,12},{16,18},{18,... | collective-permute-start | bytes 294920 | tf_op jit(solution)/shard_map/ppermute | solution.py:10
  25.4 6.3 %collective-permute-start.3 = (bf16[96,512]{1,0:T(8,128)(2,1)S(1)}, bf16[96,512]{1,0:T(8,128)(2,1)S(1)}, u32[]{:S(2)}, u32[]{:S(2)}) collective-permute-start(bf16[96,512]{1,0:T(8,128)(2,1)S(1)} %get-tuple-element.27), channel_id=1, source_target_pairs={{0,8},{2,10},{4,12},{6,14},{8,0},{10,2},{12,4},{14,6},{16,24},{18,... | collective-permute-start | bytes 294920 | tf_op jit(solution)/shard_map/ppermute | solution.py:10
  25.7 7.8 %collective-permute-start.7 = (bf16[96,512]{1,0:T(8,128)(2,1)S(1)}, bf16[96,512]{1,0:T(8,128)(2,1)S(1)}, u32[]{:S(2)}, u32[]{:S(2)}) collective-permute-start(bf16[96,512]{1,0:T(8,128)(2,1)S(1)} %get-tuple-element.58), channel_id=1, source_target_pairs={{0,8},{2,10},{4,12},{6,14},{8,0},{10,2},{12,4},{14,6},{16,24},{18,... | collective-permute-start | bytes 294920 | tf_op jit(solution)/shard_map/ppermute | solution.py:10
  27.5 7.2 %collective-permute-start.8 = (bf16[96,512]{1,0:T(8,128)(2,1)S(1)}, bf16[96,512]{1,0:T(8,128)(2,1)S(1)}, u32[]{:S(2)}, u32[]{:S(2)}) collective-permute-start(bf16[96,512]{1,0:T(8,128)(2,1)S(1)} %get-tuple-element.57), channel_id=1, source_target_pairs={{0,16},{2,18},{4,20},{6,22},{8,24},{10,26},{12,28},{14,30},{16,0},... | collective-permute-start | bytes 294920 | tf_op jit(solution)/shard_map/ppermute | solution.py:10
  27.9 5.6 %collective-permute-start.5 = (bf16[96,512]{1,0:T(8,128)(2,1)S(1)}, bf16[96,512]{1,0:T(8,128)(2,1)S(1)}, u32[]{:S(2)}, u32[]{:S(2)}) collective-permute-start(bf16[96,512]{1,0:T(8,128)(2,1)S(1)} %get-tuple-element.30), channel_id=1, source_target_pairs={{0,4},{2,6},{4,0},{6,2},{8,12},{10,14},{12,8},{14,10},{16,20},{18,... | collective-permute-start | bytes 294920 | tf_op jit(solution)/shard_map/ppermute | solution.py:10
  28.6 4.6 %collective-permute-start.4 = (bf16[96,512]{1,0:T(8,128)(2,1)S(1)}, bf16[96,512]{1,0:T(8,128)(2,1)S(1)}, u32[]{:S(2)}, u32[]{:S(2)}) collective-permute-start(bf16[96,512]{1,0:T(8,128)(2,1)S(1)} %get-tuple-element.29), channel_id=1, source_target_pairs={{0,2},{2,0},{4,6},{6,4},{8,10},{10,8},{12,14},{14,12},{16,18},{18,... | collective-permute-start | bytes 294920 | tf_op jit(solution)/shard_map/ppermute | solution.py:10
  31.7 5.6 %collective-permute-start.6 = (bf16[96,512]{1,0:T(8,128)(2,1)S(1)}, bf16[96,512]{1,0:T(8,128)(2,1)S(1)}, u32[]{:S(2)}, u32[]{:S(2)}) collective-permute-start(bf16[96,512]{1,0:T(8,128)(2,1)S(1)} %fusion.7), channel_id=1, source_target_pairs={{0,16},{2,18},{4,20},{6,22},{8,24},{10,26},{12,28},{14,30},{16,0},... | collective-permute-start | bytes 294920 | tf_op jit(solution)/shard_map/ppermute | solution.py:10
  38.9 11.5 %all-to-all-start.1 = ((bf16[16,6,512]{2,1,0:T(8,128)(2,1)}), bf16[16,6,512]{2,1,0:T(8,128)(2,1)S(1)}, u32[]{:S(2)}, u32[]{:S(2)}) async-start(bf16[16,6,512]{2,1,0:T(8,128)(2,1)} %all_to_all.27), calls=%async_computation.1 | async-start | bytes 262144 | tf_op jit(solution)/shard_map/all_to_all | solution.py:108
  42.7 9.7 %collective-permute-start.9 = (bf16[96,256]{1,0:T(8,128)(2,1)S(1)}, bf16[96,256]{1,0:T(8,128)(2,1)S(1)}, u32[]{:S(2)}, u32[]{:S(2)}) collective-permute-start(bf16[96,256]{1,0:T(8,128)(2,1)S(1)} %pad_maximum_fusion.10), channel_id=1, source_target_pairs={{0,1},{1,0},{2,3},{3,2},{4,5},{5,4},{6,7},{7,6},{8,9},{9,8},{10,11... | collective-permute-start | bytes 147464 | tf_op jit(solution)/shard_map/ppermute | solution.py:14
  42.9 8.2 %collective-permute-start.10 = (bf16[96,1024]{1,0:T(8,128)(2,1)S(1)}, bf16[96,1024]{1,0:T(8,128)(2,1)S(1)}, u32[]{:S(2)}, u32[]{:S(2)}) collective-permute-start(bf16[96,1024]{1,0:T(8,128)(2,1)S(1)} %constant_dynamic-update-slice_fusion.5), channel_id=1, source_target_pairs={{0,1},{1,0},{2,3},{3,2},{4,5},{5,4},{6,7},{7,6},{8,9},{9,8},{10,11... | collective-permute-start | bytes 589832 | tf_op jit(solution)/shard_map/ppermute | solution.py:14

commit v22 on v14

--- a/solution.py
+++ b/solution.py
@@ -104,8 +104,10 @@
     output_rows = (total + dot(latent, low_v)).astype(jnp.bfloat16)
     grad_act = (back + dot_t(dlatent, low_u)).astype(jnp.bfloat16)
     grad_pre_rows = pullback(grad_act.astype(jnp.float32))[0].astype(jnp.bfloat16)
-    results = jnp.concatenate([output_rows, grad_pre_rows], axis=1)
-    results = lax.all_to_all(results, "hid", split_axis=0, concat_axis=1, tiled=True)
+    results = jnp.concatenate(
+        [x.reshape(hid, tokens, side) for x in (output_rows, grad_pre_rows)], axis=2
+    )
+    results = lax.all_to_all(results, "hid", 0, 0, tiled=True).transpose(1, 0, 2)
     results = results.reshape(tokens, hid, 2 * side)
     output = results[:, :, :side].reshape(tokens, hid * side)
     grad_pre = results[:, :, side:].reshape(tokens, hid * side)

time: 50 us -> 50 us (level)
  other arithmetic: 1.33 us -> 1.99 us
  local copies, waits for them, and re-layouts: 1.54 us -> 0.9 us
    all_to_all x1 -> x0, local copies, waits for them, and re-layouts: 0.68 us -> none  [on_device(): lax.all_to_all(results, 'hid', split_axis=0, concat_axis=1, tiled=True)]
    concatenate x1, other arithmetic: 0.01 us -> 0.67 us  [on_device(): jnp.concatenate([x.reshape(hid, tokens, side) for x in (output_rows, grad...]
  transfers between devices with their start and end apart: 12 -> 12, of which waited for: 6 -> 6; matrix products, arithmetic and copies ran while one was open for 10% -> 11% of each run, Pallas kernels for 0% -> 0%
where the time goes in v22:
time: 50 us; the launch traced here: 49.8 us
  blocking collectives  16 us (32%)
  waiting for transfers between devices  12.8 us (26%)
  starting transfers between devices  12.4 us (25%)
  matrix products  4.7 us (9%)
  other arithmetic  1.99 us (4%)
  between operations  0.94 us (2%)
  local copies, waits for them, and re-layouts  0.9 us (2%)
    all_to_all x1, blocking collectives, on_device(): rows = lax.all_to_all(both, 'hid', split_axis=1, concat_axis=0, tiled=True)  16 us
    ppermute x9, starting transfers between devices, exchange(): lax.ppermute(x, 'hid', [(i, i ^ mask) for i in range(lax.axis_size('hid'))])  8.78 us
    ppermute x9, waiting for transfers between devices, exchange(): lax.ppermute(x, 'hid', [(i, i ^ mask) for i in range(lax.axis_size('hid'))])  8.12 us
    all_to_all x1, waiting for transfers between devices, on_device(): lax.all_to_all(results, 'hid', 0, 0, tiled=True).transpose(1, 0, 2)  4.66 us
    all_to_all x1, starting transfers between devices, on_device(): lax.all_to_all(results, 'hid', 0, 0, tiled=True).transpose(1, 0, 2)  3.51 us
    dot_general x3, matrix products, inner_rows(): lax.dot_general(left, right, (((0,), (0,)), ((), ())), preferred_element_...  2.88 us
    dot_general x7, matrix products, dot(): return jnp.dot(left, right, preferred_element_type=jnp.float32)  1.09 us
  transfers between devices with their start and end apart: 12, of which 6 were waited for; matrix products, arithmetic and copies ran while one was open for 11% of the time, Pallas kernels for 0%

profile of v22, /device:TPU:0, one launch (start us, length us, event | category | flops | bytes accessed | tf_op | source)
XLA Modules:
  0.0 49.8 jit_solution(7768857692413970763)
XLA Ops:
  0.6 0.0 copy-start
  0.7 0.9 %pad_maximum_fusion.5 = bf16[6,16,512]{2,0,1:T(8,128)(2,1)S(1)} fusion(bf16[6,16,256]{2,0,1:T(8,128)(2,1)} %bitcast.32, bf16[6,16,256]{2,0,1:T(8,128)(2,1)} %bitcast.33), kind=kLoop, calls=%fused_computation.28 | loop fusion | flops 196608 | bytes 196608 | tf_op jit(solution)/shard_map/concatenate | solution.py:79
  1.6 0.0 copy-start.2
  1.6 16.0 %all_to_all.21 = bf16[6,16,512]{2,0,1:T(8,128)(2,1)S(1)} all-to-all(bf16[6,16,512]{2,0,1:T(8,128)(2,1)S(1)} %pad_maximum_fusion.5), channel_id=1, replica_groups=mesh['hid'=16,'seq'=2] {'hid'}, dimensions={1} | all-to-all | bytes 196608 | tf_op jit(solution)/shard_map/all_to_all | solution.py:82
  17.6 0.0 copy-start.1
  17.7 0.0 copy-done.2
  17.7 0.2 fusion.58
  17.9 0.0 copy-done
  17.9 0.2 fusion.60
  18.1 0.8 %collective-permute-start = (bf16[96,512]{1,0:T(8,128)(2,1)S(1)}, bf16[96,512]{1,0:T(8,128)(2,1)S(1)}, u32[]{:S(2)}, u32[]{:S(2)}) collective-permute-start(bf16[96,512]{1,0:T(8,128)(2,1)S(1)} %fusion.5), channel_id=1, source_target_pairs={{0,6},{2,4},{4,2},{6,0},{8,14},{10,12},{12,10},{14,8},{16,22},{18,... | collective-permute-start | bytes 294920 | tf_op jit(solution)/shard_map/ppermute | solution.py:10
  18.9 1.5 %collective-permute-start.1 = (bf16[96,512]{1,0:T(8,128)(2,1)S(1)}, bf16[96,512]{1,0:T(8,128)(2,1)S(1)}, u32[]{:S(2)}, u32[]{:S(2)}) collective-permute-start(bf16[96,512]{1,0:T(8,128)(2,1)S(1)} %fusion.5), channel_id=1, source_target_pairs={{0,2},{2,0},{4,6},{6,4},{8,10},{10,8},{12,14},{14,12},{16,18},{18,... | collective-permute-start | bytes 294920 | tf_op jit(solution)/shard_map/ppermute | solution.py:10
  20.4 1.3 %collective-permute-start.2 = (bf16[96,512]{1,0:T(8,128)(2,1)S(1)}, bf16[96,512]{1,0:T(8,128)(2,1)S(1)}, u32[]{:S(2)}, u32[]{:S(2)}) collective-permute-start(bf16[96,512]{1,0:T(8,128)(2,1)S(1)} %fusion.5), channel_id=1, source_target_pairs={{0,4},{2,6},{4,0},{6,2},{8,12},{10,14},{12,8},{14,10},{16,20},{18,... | collective-permute-start | bytes 294920 | tf_op jit(solution)/shard_map/ppermute | solution.py:10
  21.7 0.0 copy-done.1
  21.7 0.3 fusion.67
  22.1 0.8 %collective-permute-start.4 = (bf16[96,512]{1,0:T(8,128)(2,1)S(1)}, bf16[96,512]{1,0:T(8,128)(2,1)S(1)}, u32[]{:S(2)}, u32[]{:S(2)}) collective-permute-start(bf16[96,512]{1,0:T(8,128)(2,1)S(1)} %get-tuple-element.58), channel_id=1, source_target_pairs={{0,8},{2,10},{4,12},{6,14},{8,0},{10,2},{12,4},{14,6},{16,24},{18,... | collective-permute-start | bytes 294920 | tf_op jit(solution)/shard_map/ppermute | solution.py:10
  22.9 1.1 %collective-permute-start.5 = (bf16[96,512]{1,0:T(8,128)(2,1)S(1)}, bf16[96,512]{1,0:T(8,128)(2,1)S(1)}, u32[]{:S(2)}, u32[]{:S(2)}) collective-permute-start(bf16[96,512]{1,0:T(8,128)(2,1)S(1)} %get-tuple-element.57), channel_id=1, source_target_pairs={{0,16},{2,18},{4,20},{6,22},{8,24},{10,26},{12,28},{14,30},{16,0},... | collective-permute-start | bytes 294920 | tf_op jit(solution)/shard_map/ppermute | solution.py:10
  24.0 0.0 collective-permute-done
  24.0 0.0 collective-permute-done.1
  24.0 1.0 %collective-permute-done.2 = bf16[96,512]{1,0:T(8,128)(2,1)S(1)} collective-permute-done((bf16[96,512]{1,0:T(8,128)(2,1)S(1)}, bf16[96,512]{1,0:T(8,128)(2,1)S(1)}, u32[]{:S(2)}, u32[]{:S(2)}) %collective-permute-start.2) | collective-permute-done | bytes 98336 | tf_op jit(solution)/shard_map/ppermute | solution.py:10
  25.0 0.8 %collective-permute-start.3 = (bf16[96,512]{1,0:T(8,128)(2,1)S(1)}, bf16[96,512]{1,0:T(8,128)(2,1)S(1)}, u32[]{:S(2)}, u32[]{:S(2)}) collective-permute-start(bf16[96,512]{1,0:T(8,128)(2,1)S(1)} %get-tuple-element.27), channel_id=1, source_target_pairs={{0,8},{2,10},{4,12},{6,14},{8,0},{10,2},{12,4},{14,6},{16,24},{18,... | collective-permute-start | bytes 294920 | tf_op jit(solution)/shard_map/ppermute | solution.py:10
  25.8 1.3 %collective-permute-start.7 = (bf16[96,512]{1,0:T(8,128)(2,1)S(1)}, bf16[96,512]{1,0:T(8,128)(2,1)S(1)}, u32[]{:S(2)}, u32[]{:S(2)}) collective-permute-start(bf16[96,512]{1,0:T(8,128)(2,1)S(1)} %get-tuple-element.31), channel_id=1, source_target_pairs={{0,4},{2,6},{4,0},{6,2},{8,12},{10,14},{12,8},{14,10},{16,20},{18,... | collective-permute-start | bytes 294920 | tf_op jit(solution)/shard_map/ppermute | solution.py:10
  27.1 0.6 %collective-permute-start.6 = (bf16[96,512]{1,0:T(8,128)(2,1)S(1)}, bf16[96,512]{1,0:T(8,128)(2,1)S(1)}, u32[]{:S(2)}, u32[]{:S(2)}) collective-permute-start(bf16[96,512]{1,0:T(8,128)(2,1)S(1)} %get-tuple-element.30), channel_id=1, source_target_pairs={{0,2},{2,0},{4,6},{6,4},{8,10},{10,8},{12,14},{14,12},{16,18},{18,... | collective-permute-start | bytes 294920 | tf_op jit(solution)/shard_map/ppermute | solution.py:10
  27.7 0.0 collective-permute-done.4
  27.7 1.9 %collective-permute-done.5 = bf16[96,512]{1,0:T(8,128)(2,1)S(1)} collective-permute-done((bf16[96,512]{1,0:T(8,128)(2,1)S(1)}, bf16[96,512]{1,0:T(8,128)(2,1)S(1)}, u32[]{:S(2)}, u32[]{:S(2)}) %collective-permute-start.5) | collective-permute-done | bytes 98336 | tf_op jit(solution)/shard_map/ppermute | solution.py:10
  29.6 0.8 %collective-permute-done.3 = bf16[96,512]{1,0:T(8,128)(2,1)S(1)} collective-permute-done((bf16[96,512]{1,0:T(8,128)(2,1)S(1)}, bf16[96,512]{1,0:T(8,128)(2,1)S(1)}, u32[]{:S(2)}, u32[]{:S(2)}) %collective-permute-start.3) | collective-permute-done | bytes 98336 | tf_op jit(solution)/shard_map/ppermute | solution.py:10
  30.4 0.7 %collective-permute-start.8 = (bf16[96,512]{1,0:T(8,128)(2,1)S(1)}, bf16[96,512]{1,0:T(8,128)(2,1)S(1)}, u32[]{:S(2)}, u32[]{:S(2)}) collective-permute-start(bf16[96,512]{1,0:T(8,128)(2,1)S(1)} %fusion.7), channel_id=1, source_target_pairs={{0,16},{2,18},{4,20},{6,22},{8,24},{10,26},{12,28},{14,30},{16,0},... | collective-permute-start | bytes 294920 | tf_op jit(solution)/shard_map/ppermute | solution.py:10
  31.1 0.1 fusion.9
  31.2 0.2 fusion.13
  31.4 0.3 collective-permute-done.6
  31.8 0.0 collective-permute-done.7
  31.8 0.2 convolution_add_fusion.3
  32.0 0.2 fusion
  32.2 0.2 convolution_add_fusion.1
  32.4 0.1 collective-permute-start.10
  32.5 4.1 %collective-permute-done.8 = bf16[96,512]{1,0:T(8,128)(2,1)S(1)} collective-permute-done((bf16[96,512]{1,0:T(8,128)(2,1)S(1)}, bf16[96,512]{1,0:T(8,128)(2,1)S(1)}, u32[]{:S(2)}, u32[]{:S(2)}) %collective-permute-start.8) | collective-permute-done | bytes 98336 | tf_op jit(solution)/shard_map/ppermute | solution.py:10
  36.7 0.2 fusion.22
  37.0 0.2 fusion.1
  37.2 0.7 %pad_maximum_fusion.6 = bf16[16,6,512]{2,1,0:T(8,128)(2,1)} fusion(bf16[16,6,256]{2,1,0:T(8,128)(2,1)S(1)} %reshape.43, bf16[16,6,256]{2,1,0:T(8,128)(2,1)S(1)} %reshape.42), kind=kLoop, calls=%fused_computation.29 | loop fusion | flops 196608 | bytes 196608 | tf_op jit(solution)/shard_map/concatenate | solution.py:107
  37.8 3.5 %all-to-all-start.1 = ((bf16[16,6,512]{2,1,0:T(8,128)(2,1)}), bf16[16,6,512]{2,1,0:T(8,128)(2,1)S(1)}, u32[]{:S(2)}, u32[]{:S(2)}) async-start(bf16[16,6,512]{2,1,0:T(8,128)(2,1)} %pad_maximum_fusion.6), calls=%async_computation.1 | async-start | bytes 262144 | tf_op jit(solution)/shard_map/all_to_all | solution.py:110
  41.4 0.1 collective-permute-start.9
  41.4 0.0 collective-permute-done.10
  41.6 1.1 %convolution_multiply_fusion = f32[640,256]{1,0:T(8,128)} fusion(bf16[96,640]{1,0:T(8,128)(2,1)S(1)} %constant_dynamic-update-slice_fusion.11, bf16[96,640]{1,0:T(8,128)(2,1)S(1)} %get-tuple-element.53, bf16[96,256]{1,0:T(8,128)(2,1)S(1)} %get-tuple-element.46, bf16[96,256]{1,0:T(8,128)(2,1)S(1)} %slice.176), kind=kOutput, calls=%fused_computation | convolution fusion | flops 63766528 | bytes 999424 | tf_op jit(solution)/shard_map/dot_general | solution.py:32
  42.7 0.0 collective-permute-done.9
  42.7 0.9 %convolution_multiply_fusion.1 = f32[128,256]{1,0:T(8,128)} fusion(bf16[96,256]{1,0:T(8,128)(2,1)S(1)} %get-tuple-element.46, bf16[96,256]{1,0:T(8,128)(2,1)S(1)} %slice.176, bf16[96,128]{1,0:T(8,128)(2,1)S(1)} %get-tuple-element.55, bf16[96,128]{1,0:T(8,128)(2,1)S(1)} %get-tuple-element.49), kind=kOutput, calls=%fused_computation.1 | convolution fusion | flops 12910592 | bytes 278528 | tf_op jit(solution)/shard_map/dot_general | solution.py:32
  43.6 0.9 %convolution_multiply_fusion.2 = f32[256,128]{1,0:T(8,128)} fusion(bf16[96,256]{1,0:T(8,128)(2,1)S(1)} %get-tuple-element.45, bf16[96,256]{1,0:T(8,128)(2,1)S(1)} %fusion.27, bf16[96,128]{1,0:T(8,128)(2,1)S(1)} %get-tuple-element.56, bf16[96,128]{1,0:T(8,128)(2,1)S(1)} %get-tuple-element.51), kind=kOutput, calls=%fused_computation.2 | convolution fusion | flops 12910592 | bytes 278528 | tf_op jit(solution)/shard_map/dot_general | solution.py:32
  44.5 4.7 %all-to-all-done.1 = bf16[16,6,512]{2,1,0:T(8,128)(2,1)S(1)} async-done(((bf16[16,6,512]{2,1,0:T(8,128)(2,1)}), bf16[16,6,512]{2,1,0:T(8,128)(2,1)S(1)}, u32[]{:S(2)}, u32[]{:S(2)}) %all-to-all-start.1) | async-done | bytes 98336 | tf_op jit(solution)/shard_map/all_to_all | solution.py:110
  49.1 0.7 %fusion.65 = (bf16[6,16,256]{2,0,1:T(8,128)(2,1)}, bf16[6,16,256]{2,0,1:T(8,128)(2,1)}) fusion(bf16[6,16,512]{2,0,1:T(8,128)(2,1)S(1)} %bitcast.31), kind=kLoop, calls=%fused_computation.109 | loop fusion | bytes 196608 | tf_op jit(solution)/shard_map/slice | solution.py:113
  (30 shorter events, 0.6 us)
Async XLA Ops:
  0.6 17.3 %copy-start = (bf16[256,256]{1,0:T(8,128)(2,1)S(1)}, bf16[256,256]{1,0:T(8,128)(2,1)}, u32[]{:S(2)}) copy-start(bf16[256,256]{1,0:T(8,128)(2,1)} %param.7) | copy-start | bytes 393220
  1.6 16.1 %copy-start.2 = (bf16[256,256]{1,0:T(8,128)(2,1)S(1)}, bf16[256,256]{1,0:T(8,128)(2,1)}, u32[]{:S(2)}) copy-start(bf16[256,256]{1,0:T(8,128)(2,1)} %param.8) | copy-start | bytes 393220
  17.6 4.0 %copy-start.1 = (bf16[1,5,256,256]{3,2,1,0:T(8,128)(2,1)S(1)}, bf16[1,5,256,256]{3,2,1,0:T(8,128)(2,1)}, u32[]{:S(2)}) copy-start(bf16[1,5,256,256]{3,2,1,0:T(8,128)(2,1)} %param.6) | copy-start | bytes 1966084
  18.1 5.9 %collective-permute-start = (bf16[96,512]{1,0:T(8,128)(2,1)S(1)}, bf16[96,512]{1,0:T(8,128)(2,1)S(1)}, u32[]{:S(2)}, u32[]{:S(2)}) collective-permute-start(bf16[96,512]{1,0:T(8,128)(2,1)S(1)} %fusion.5), channel_id=1, source_target_pairs={{0,6},{2,4},{4,2},{6,0},{8,14},{10,12},{12,10},{14,8},{16,22},{18,... | collective-permute-start | bytes 294920 | tf_op jit(solution)/shard_map/ppermute | solution.py:10
  18.9 5.1 %collective-permute-start.1 = (bf16[96,512]{1,0:T(8,128)(2,1)S(1)}, bf16[96,512]{1,0:T(8,128)(2,1)S(1)}, u32[]{:S(2)}, u32[]{:S(2)}) collective-permute-start(bf16[96,512]{1,0:T(8,128)(2,1)S(1)} %fusion.5), channel_id=1, source_target_pairs={{0,2},{2,0},{4,6},{6,4},{8,10},{10,8},{12,14},{14,12},{16,18},{18,... | collective-permute-start | bytes 294920 | tf_op jit(solution)/shard_map/ppermute | solution.py:10
  20.4 4.6 %collective-permute-start.2 = (bf16[96,512]{1,0:T(8,128)(2,1)S(1)}, bf16[96,512]{1,0:T(8,128)(2,1)S(1)}, u32[]{:S(2)}, u32[]{:S(2)}) collective-permute-start(bf16[96,512]{1,0:T(8,128)(2,1)S(1)} %fusion.5), channel_id=1, source_target_pairs={{0,4},{2,6},{4,0},{6,2},{8,12},{10,14},{12,8},{14,10},{16,20},{18,... | collective-permute-start | bytes 294920 | tf_op jit(solution)/shard_map/ppermute | solution.py:10
  22.1 5.6 %collective-permute-start.4 = (bf16[96,512]{1,0:T(8,128)(2,1)S(1)}, bf16[96,512]{1,0:T(8,128)(2,1)S(1)}, u32[]{:S(2)}, u32[]{:S(2)}) collective-permute-start(bf16[96,512]{1,0:T(8,128)(2,1)S(1)} %get-tuple-element.58), channel_id=1, source_target_pairs={{0,8},{2,10},{4,12},{6,14},{8,0},{10,2},{12,4},{14,6},{16,24},{18,... | collective-permute-start | bytes 294920 | tf_op jit(solution)/shard_map/ppermute | solution.py:10
  22.9 6.7 %collective-permute-start.5 = (bf16[96,512]{1,0:T(8,128)(2,1)S(1)}, bf16[96,512]{1,0:T(8,128)(2,1)S(1)}, u32[]{:S(2)}, u32[]{:S(2)}) collective-permute-start(bf16[96,512]{1,0:T(8,128)(2,1)S(1)} %get-tuple-element.57), channel_id=1, source_target_pairs={{0,16},{2,18},{4,20},{6,22},{8,24},{10,26},{12,28},{14,30},{16,0},... | collective-permute-start | bytes 294920 | tf_op jit(solution)/shard_map/ppermute | solution.py:10
  25.0 5.3 %collective-permute-start.3 = (bf16[96,512]{1,0:T(8,128)(2,1)S(1)}, bf16[96,512]{1,0:T(8,128)(2,1)S(1)}, u32[]{:S(2)}, u32[]{:S(2)}) collective-permute-start(bf16[96,512]{1,0:T(8,128)(2,1)S(1)} %get-tuple-element.27), channel_id=1, source_target_pairs={{0,8},{2,10},{4,12},{6,14},{8,0},{10,2},{12,4},{14,6},{16,24},{18,... | collective-permute-start | bytes 294920 | tf_op jit(solution)/shard_map/ppermute | solution.py:10
  25.8 5.9 %collective-permute-start.7 = (bf16[96,512]{1,0:T(8,128)(2,1)S(1)}, bf16[96,512]{1,0:T(8,128)(2,1)S(1)}, u32[]{:S(2)}, u32[]{:S(2)}) collective-permute-start(bf16[96,512]{1,0:T(8,128)(2,1)S(1)} %get-tuple-element.31), channel_id=1, source_target_pairs={{0,4},{2,6},{4,0},{6,2},{8,12},{10,14},{12,8},{14,10},{16,20},{18,... | collective-permute-start | bytes 294920 | tf_op jit(solution)/shard_map/ppermute | solution.py:10
  27.1 4.6 %collective-permute-start.6 = (bf16[96,512]{1,0:T(8,128)(2,1)S(1)}, bf16[96,512]{1,0:T(8,128)(2,1)S(1)}, u32[]{:S(2)}, u32[]{:S(2)}) collective-permute-start(bf16[96,512]{1,0:T(8,128)(2,1)S(1)} %get-tuple-element.30), channel_id=1, source_target_pairs={{0,2},{2,0},{4,6},{6,4},{8,10},{10,8},{12,14},{14,12},{16,18},{18,... | collective-permute-start | bytes 294920 | tf_op jit(solution)/shard_map/ppermute | solution.py:10
  30.4 6.3 %collective-permute-start.8 = (bf16[96,512]{1,0:T(8,128)(2,1)S(1)}, bf16[96,512]{1,0:T(8,128)(2,1)S(1)}, u32[]{:S(2)}, u32[]{:S(2)}) collective-permute-start(bf16[96,512]{1,0:T(8,128)(2,1)S(1)} %fusion.7), channel_id=1, source_target_pairs={{0,16},{2,18},{4,20},{6,22},{8,24},{10,26},{12,28},{14,30},{16,0},... | collective-permute-start | bytes 294920 | tf_op jit(solution)/shard_map/ppermute | solution.py:10
  32.4 9.0 %collective-permute-start.10 = (bf16[96,1024]{1,0:T(8,128)(2,1)S(1)}, bf16[96,1024]{1,0:T(8,128)(2,1)S(1)}, u32[]{:S(2)}, u32[]{:S(2)}) collective-permute-start(bf16[96,1024]{1,0:T(8,128)(2,1)S(1)} %constant_dynamic-update-slice_fusion.5), channel_id=1, source_target_pairs={{0,1},{1,0},{2,3},{3,2},{4,5},{5,4},{6,7},{7,6},{8,9},{9,8},{10,11... | collective-permute-start | bytes 589832 | tf_op jit(solution)/shard_map/ppermute | solution.py:14
  37.8 11.3 %all-to-all-start.1 = ((bf16[16,6,512]{2,1,0:T(8,128)(2,1)}), bf16[16,6,512]{2,1,0:T(8,128)(2,1)S(1)}, u32[]{:S(2)}, u32[]{:S(2)}) async-start(bf16[16,6,512]{2,1,0:T(8,128)(2,1)} %pad_maximum_fusion.6), calls=%async_computation.1 | async-start | bytes 262144 | tf_op jit(solution)/shard_map/all_to_all | solution.py:110
  41.4 1.4 %collective-permute-start.9 = (bf16[96,256]{1,0:T(8,128)(2,1)S(1)}, bf16[96,256]{1,0:T(8,128)(2,1)S(1)}, u32[]{:S(2)}, u32[]{:S(2)}) collective-permute-start(bf16[96,256]{1,0:T(8,128)(2,1)S(1)} %pad_maximum_fusion.10), channel_id=1, source_target_pairs={{0,1},{1,0},{2,3},{3,2},{4,5},{5,4},{6,7},{7,6},{8,9},{9,8},{10,11... | collective-permute-start | bytes 147464 | tf_op jit(solution)/shard_map/ppermute | solution.py:14
